TPU v7x, 32 devices: a whole 2x2x4 slice. The times are simulated.
32 devices in a mesh: wide: 8 (over y, x, core), narrow: 4 (over z).
Axes of the slice: x: 2, y: 2, z: 4, core: 2. Of those that a mesh axis runs over, the one named last changes fastest.
Arguments:
- populations: float32 [19, 4, 256, 1024], P(None, None, ('wide', 'narrow')), as said below
- phase: int32 [4, 256, 1024], P(None, ('wide', 'narrow')), may hold values from 0 to 2, as said below
- porosity: float32 [4, 256, 1024], P(None, ('wide', 'narrow')), may hold values from 0 to 1, as said below
- napl: float32 [4, 256, 1024], P(None, ('wide', 'narrow')), may hold values from 0 to 0.9, as said below
- concentration: float32 [4, 256, 1024], P(None, ('wide', 'narrow')), may hold values from 0 to 1
- flags: int32 [2, 4, 1024], replicated, may hold values 0 or 1
Outputs:
- populations_out: float32 [19, 4, 256, 1024], P(None, None, ('wide', 'narrow'))
- concentration_out: float32 [4, 256, 1024], P(None, 'wide', 'narrow')
- napl_out: float32 [4, 256, 1024], P(None, 'wide', 'narrow')
Inputs may be any that keep to these rules, and one draw needn't show every extreme that they name: `phase`: 0 open pore, 1 pore holding NAPL, 2 solid. `porosity`: exactly 0 on voxels of phase 2 and 0.35 or more elsewhere. `napl`: above 0 exactly on voxels of phase 1, 0 elsewhere. `populations`: every entry positive.
All inputs are finite; a program needn't handle non-finite values.
Results may differ from a plain program's by a relative error of at most 0.0003.
Values sent between devices are 32-bit elements; how exact they have to be, the bound alone decides.
No kernel may reach another device: no remote copies, remote signals or barrier semaphores. Data moves between devices by JAX's collectives and lax.ppermute only.
A program may use at most 128 MiB of HBM per device.

v0:
```python
import functools

import jax
import jax.numpy as jnp
import numpy as np
from jax import lax
from jax.experimental import pallas as pl
from jax.experimental.pallas import tpu as pltpu
from jax.sharding import PartitionSpec as P

LBM_STEPS = 4
F32 = jnp.float32

DIRS = [
    (0, 0, 0), (1, 0, 0), (-1, 0, 0), (0, 1, 0), (0, -1, 0), (0, 0, 1), (0, 0, -1),
    (1, 1, 0), (-1, -1, 0), (1, -1, 0), (-1, 1, 0), (1, 0, 1), (-1, 0, -1), (1, 0, -1),
    (-1, 0, 1), (0, 1, 1), (0, -1, -1), (0, 1, -1), (0, -1, 1),
]
OPP = [0, 2, 1, 4, 3, 6, 5, 8, 7, 10, 9, 12, 11, 14, 13, 16, 15, 18, 17]
UP = [1, 7, 9, 11, 13]
DOWN = [2, 8, 10, 12, 14]
DIFFUSION = 0.15
TRANSFER = 0.3
DEPLETION = 0.5
FLOOR = 0.3
SUBS = 8
LANES = 128
VMEM_LIMIT = 16 * 1024 * 1024


def to_view(array):
    *lead, rows, width = array.shape
    n = len(lead)
    t = array.reshape(*lead, rows // SUBS, SUBS, width // LANES, LANES)
    t = t.transpose(*range(n), n, n + 2, n + 1, n + 3)
    return t.reshape(*lead[:-1], lead[-1] * rows * width // LANES, LANES)


def from_view(view, shape):
    *lead, rows, width = shape
    n = len(lead)
    t = view.reshape(*lead, rows // SUBS, width // LANES, SUBS, LANES)
    t = t.transpose(*range(n), n, n + 2, n + 1, n + 3)
    return t.reshape(shape)


def iotas():
    lane = lax.broadcasted_iota(jnp.int32, (SUBS, LANES), 1)
    sub = lax.broadcasted_iota(jnp.int32, (SUBS, LANES), 0)
    return lane, sub


def cut(c):
    return slice(c * LANES, (c + 1) * LANES)


def strided(tiles, c, x):
    return pl.ds(c * SUBS + x, SUBS, stride=tiles * SUBS)


def collide(f, fac):
    s = [f[2 * p + 1] + f[2 * p + 2] for p in range(9)]
    d = [f[2 * p + 1] - f[2 * p + 2] for p in range(9)]
    rho = f[0] + (((s[0] + s[1]) + (s[2] + s[3])) + ((s[4] + s[5]) + (s[6] + s[7])) + s[8])
    jx = d[0] + ((d[3] + d[4]) + (d[5] + d[6]))
    jy = d[1] + ((d[3] - d[4]) + (d[7] + d[8]))
    jz = d[2] + ((d[5] - d[6]) + (d[7] - d[8]))
    inv = fac / rho
    vx, vy, vz = jx * inv, jy * inv, jz * inv
    w1 = rho * np.float32(1.25 / 18)
    w2 = rho * np.float32(1.25 / 36)
    w4 = rho * np.float32(1.25 / 72)
    a1 = w1 - w1 * ((vx * vx + vy * vy + vz * vz) * np.float32(1.0 / 6))
    a2 = a1 * np.float32(0.5)
    post = [a1 * np.float32(6.0) - f[0] * np.float32(0.25)]
    axes = [vx, vy, vz, vx + vy, vx - vy, vx + vz, vx - vz, vy + vz, vy - vz]
    for p, v in enumerate(axes):
        wa, wh, base = (w1, w2, a1) if p < 3 else (w2, w4, a2)
        even = (base + (wh * v) * v) - s[p] * np.float32(0.125)
        odd = wa * v - d[p] * np.float32(0.125)
        post += [even + odd, even - odd]
    return post


def pull(load, q, c, tiles, halves, lane, sub):
    _, cross, layer = DIRS[q]
    v = load(q, c)
    if cross == 1:
        if c > 0:
            side = load(q, c - 1)
        else:
            side = jnp.where(sub % halves == 0, jnp.nan, pltpu.roll(load(q, tiles - 1), 1, 0))
        v = pltpu.roll(jnp.where(lane == LANES - 1, side, v), 1, 1)
    elif cross == -1:
        if c < tiles - 1:
            side = load(q, c + 1)
        else:
            side = jnp.where(sub % halves == halves - 1, jnp.nan, pltpu.roll(load(q, 0), SUBS - 1, 0))
        v = pltpu.roll(jnp.where(lane == 0, side, v), LANES - 1, 1)
    if layer:
        v = pltpu.roll(v, (layer * halves) % SUBS, 0)
    return v


def stream(g, lo, hi, x, c, tiles, halves, lane, sub, place):
    def load(q, cc):
        flow = DIRS[q][0]
        if flow == 1 and place == "first":
            return lo[UP.index(q), :, cut(cc)]
        if flow == -1 and place == "last":
            return hi[DOWN.index(q), :, cut(cc)]
        return g[q, x - flow, :, cut(cc)]

    f = [g[0, x, :, cut(c)]]
    for q in range(1, 19):
        v = pull(load, q, c, tiles, halves, lane, sub)
        f.append(jnp.where(v != v, g[OPP[q], x, :, cut(c)], v))
    return f


def first_edge_kernel(
    tiles, pop_h, phase_h, conc_h, napl_h, poro_h, flags_h,
    pop, phase, conc, napl, poro, flags, ge, up, down, sems,
):
    small = [
        pltpu.make_async_copy(a, b, sems.at[tiles + i])
        for i, (a, b) in enumerate(
            ((phase_h, phase), (conc_h, conc), (poro_h, poro), (napl_h, napl), (flags_h, flags))
        )
    ]
    small[0].start()
    parts = [pltpu.make_async_copy(pop_h.at[:, :, c], pop.at[:, :, c], sems.at[c]) for c in range(tiles)]
    for copy in parts:
        copy.start()
    for copy in small[1:]:
        copy.start()
    flat = pop.reshape(pop.shape[0], SUBS * tiles * SUBS, LANES)
    rows = SUBS
    small[0].wait()
    for c in range(tiles):
        parts[c].wait()
        for k, x in enumerate((0, rows - 1)):
            at = strided(tiles, c, x)
            post = collide([flat[q, at, :] for q in range(19)], drag(phase[at, :]))
            for q in range(19):
                ge[q, k, :, cut(c)] = post[q]
            for i, q in enumerate(DOWN if k == 0 else UP):
                (down if k == 0 else up)[i, :, cut(c)] = post[q]
    for copy in small[1:]:
        copy.wait()
    for n, (ref, r) in enumerate(((conc, 0), (conc, 1), (poro, 0))):
        for c in range(tiles):
            down[5 + n, :, cut(c)] = ref[strided(tiles, c, r), :]
            up[5 + n, :, cut(c)] = ref[strided(tiles, c, rows - 1 - r), :]


def drag(ph):
    return jnp.where(ph == 2, jnp.nan, jnp.where(ph == 1, np.float32(1.5), np.float32(3.0)))


def first_inner_kernel(tiles, halves, pop, phase, conc, napl, poro, flags, ge, g, fac, start, slabs, open_ends):
    rows = g.shape[1]
    length = tiles * LANES
    for k in range(2):
        for z in range(SUBS // halves):
            for h in range(halves):
                line = flags[k, z : z + 1, h * length : (h + 1) * length]
                open_ends[k, z * halves + h : z * halves + h + 1, :] = line.astype(F32)

    def row(x, inner):
        for c in range(tiles):
            at = strided(tiles, c, x)
            fc = drag(phase[at, :])
            fac[x, :, cut(c)] = fc
            f = [pop[q, at, :] for q in range(19)]
            post = collide(f, fc) if inner else None
            for q in range(19):
                start[q, x, :, cut(c)] = f[q]
                g[q, x, :, cut(c)] = post[q] if inner else ge[q, 0 if x == 0 else 1, :, cut(c)]
            for k, ref in enumerate((conc, napl, poro)):
                slabs[k, x, :, cut(c)] = ref[at, :]
        return 0

    row(0, False)
    lax.fori_loop(1, rows - 1, lambda x, _: row(x, True), 0)
    row(rows - 1, False)


def edge_kernel(tiles, halves, g, fac, lo, hi, ge, up, down):
    rows = g.shape[1]
    lane, sub = iotas()
    for k, (x, place) in enumerate(((0, "first"), (rows - 1, "last"))):
        for c in range(tiles):
            f = stream(g, lo, hi, x, c, tiles, halves, lane, sub, place)
            post = collide(f, fac[x, :, cut(c)])
            for q in range(19):
                ge[q, k, :, cut(c)] = post[q]
            for i, q in enumerate(DOWN if k == 0 else UP):
                (down if k == 0 else up)[i, :, cut(c)] = post[q]


def inner_kernel(tiles, halves, g, ge, fac, out):
    rows = g.shape[1]
    lane, sub = iotas()

    def row(x, _):
        for c in range(tiles):
            f = stream(g, None, None, x, c, tiles, halves, lane, sub, "mid")
            post = collide(f, fac[x, :, cut(c)])
            for q in range(19):
                out[q, x, :, cut(c)] = post[q]
        return 0

    lax.fori_loop(1, rows - 1, row, 0)
    for q in range(19):
        out[q, 0] = ge[q, 0]
        out[q, rows - 1] = ge[q, 1]


def speed(f, fc):
    s = [f[2 * p + 1] + f[2 * p + 2] for p in range(9)]
    d = [f[2 * p + 1] - f[2 * p + 2] for p in range(9)]
    rho = f[0] + (((s[0] + s[1]) + (s[2] + s[3])) + ((s[4] + s[5]) + (s[6] + s[7])) + s[8])
    jx = d[0] + ((d[3] + d[4]) + (d[5] + d[6]))
    jy = d[1] + ((d[3] - d[4]) + (d[7] + d[8]))
    jz = d[2] + ((d[5] - d[6]) + (d[7] - d[8]))
    inv = np.float32(1.0) / rho
    return [jnp.where(fc != fc, np.float32(0.0), j * inv) for j in (jz, jx, jy)]


def edge_speed_kernel(tiles, halves, g, fac, lo, hi, ue, up, down):
    rows = g.shape[1]
    lane, sub = iotas()
    for k, (x, place) in enumerate(((0, "first"), (rows - 1, "last"))):
        for c in range(tiles):
            f = stream(g, lo, hi, x, c, tiles, halves, lane, sub, place)
            for i, v in enumerate(speed(f, fac[x, :, cut(c)])):
                ue[i, k, :, cut(c)] = v
                if i == 1:
                    (down if k == 0 else up)[:, cut(c)] = v


def inner_speed_kernel(tiles, halves, g, fac, ue, u):
    rows = g.shape[1]
    lane, sub = iotas()

    def row(x, _):
        for c in range(tiles):
            f = stream(g, None, None, x, c, tiles, halves, lane, sub, "mid")
            for i, v in enumerate(speed(f, fac[x, :, cut(c)])):
                u[i, x, :, cut(c)] = v
        return 0

    lax.fori_loop(1, rows - 1, row, 0)
    for i in range(3):
        u[i, 0] = ue[i, 0]
        u[i, rows - 1] = ue[i, 1]


def swap_tile(v, sub):
    v = list(v)
    for k in (4, 2, 1):
        low = sub & k == 0
        for i in range(SUBS):
            if not i & k:
                a, b = v[i], v[i + k]
                v[i] = jnp.where(low, a, pltpu.roll(b, k, 0))
                v[i + k] = jnp.where(low, pltpu.roll(a, SUBS - k, 0), b)
    return v


def final_kernel(tiles, halves, g, fac, lo, hi, start, out, buf, sems):
    rows = g.shape[1]
    lane, sub = iotas()

    def row_of(q, x):
        at = x - DIRS[q][0]
        if at < 0:
            return lambda qq, cc: lo[UP.index(qq), :, cut(cc)]
        if at >= rows:
            return lambda qq, cc: hi[DOWN.index(qq), :, cut(cc)]
        return lambda qq, cc: g[qq, at, :, cut(cc)]

    copies = []
    for q in range(19):
        for c in range(tiles):
            new = []
            for x in range(rows):
                fc = fac[x, :, cut(c)]
                if q == 0:
                    v = g[0, x, :, cut(c)]
                else:
                    v = pull(row_of(q, x), q, c, tiles, halves, lane, sub)
                    v = jnp.where(v != v, g[OPP[q], x, :, cut(c)], v)
                new.append(jnp.where(fc != fc, start[q, x, :, cut(c)], v))
            for i, t in enumerate(swap_tile(new, sub)):
                first = (i * tiles + c) * SUBS
                buf[q, first : first + SUBS, :] = t
        copy = pltpu.make_async_copy(buf.at[q], out.at[q], sems.at[q])
        copy.start()
        copies.append(copy)
    for copy in copies:
        copy.wait()


def slope(p, q):
    return np.float32(0.5) * (
        jnp.maximum(jnp.minimum(p, q), np.float32(0.0)) + jnp.minimum(jnp.maximum(p, q), np.float32(0.0))
    )


def loss(s, c):
    return [np.float32(TRANSFER) * a * (np.float32(1.0) - b) for a, b in zip(s, c)]


def ends_of(parts, strips):
    place = lax.axis_index("wide") * parts + lax.axis_index("narrow")
    return place == 0, place == strips - 1


class Row:
    def __init__(self, tiles, halves):
        self.tiles, self.halves = tiles, halves
        self.lane, self.sub = iotas()

    def read(self, slab):
        return [slab[:, cut(c)] for c in range(self.tiles)]

    def after(self, v):
        out = []
        for c in range(self.tiles):
            if c < self.tiles - 1:
                side = v[c + 1]
            else:
                edge = self.sub % self.halves == self.halves - 1
                side = jnp.where(edge, np.float32(0.0), pltpu.roll(v[0], SUBS - 1, 0))
            out.append(pltpu.roll(jnp.where(self.lane == 0, side, v[c]), LANES - 1, 1))
        return out

    def before(self, v):
        out = []
        for c in range(self.tiles):
            if c > 0:
                side = v[c - 1]
            else:
                edge = self.sub % self.halves == 0
                side = jnp.where(edge, np.float32(0.0), pltpu.roll(v[self.tiles - 1], 1, 0))
            out.append(pltpu.roll(jnp.where(self.lane == LANES - 1, side, v[c]), 1, 1))
        return out

    def above(self, v):
        return [pltpu.roll(t, SUBS - self.halves, 0) for t in v]

    def below(self, v):
        return [pltpu.roll(t, self.halves, 0) for t in v]

    def step(self, r, conc, poro, flow, u, s):
        def each(f, *lists):
            return [f(*t) for t in zip(*lists)]

        def less(a, b):
            return each(lambda x, y: x - y, a, b)

        def times(a, b):
            return each(lambda x, y: x * y, a, b)

        def slopes(a, b):
            return each(slope, a, b)

        def face(w, va, vb, c, cn, sl, sn, dn):
            a = each(lambda w, x, y: w * np.float32(0.5) * (x + y), w, va, vb)
            return each(
                lambda a, w, c, cn, sl, sn, dn: a * jnp.where(a > 0, c + sl, cn - sn)
                - np.float32(DIFFUSION) * w * dn,
                a, w, c, cn, sl, sn, dn,
            )

        cm2, cm1, c, cp1, cp2 = (conc(r + k) for k in (-2, -1, 0, 1, 2))
        pm, p, pn = (poro(r + k) for k in (-1, 0, 1))
        vm, v0, vn = (flow(r + k) for k in (-1, 0, 1))
        d0, d1, d2, d3 = less(cm1, cm2), less(c, cm1), less(cp1, c), less(cp2, cp1)
        sm, s0, sp = slopes(d0, d1), slopes(d1, d2), slopes(d2, d3)
        change = less(
            face(times(pm, p), vm, v0, cm1, c, sm, s0, d1), face(times(p, pn), v0, vn, c, cp1, s0, sp, d2)
        )
        for after, before, vel, open_ends in (
            (self.after, self.before, u[1], True), (self.above, self.below, u[0], False),
        ):
            cn = after(c)
            dn = less(cn, c)
            dm = less(c, before(c)) if open_ends else before(dn)
            s0 = slopes(dm, dn)
            flux = face(times(p, after(p)), vel, after(vel), c, cn, s0, after(s0), dn)
            change = each(lambda t, a, b: t + (a - b), change, before(flux), flux)
        rate = loss(s, c)
        cnew = each(
            lambda c, t, k, p: c + (t + k) / jnp.maximum(p, np.float32(FLOOR)), c, change, rate, p
        )
        return cnew, each(lambda s, k: s - np.float32(DEPLETION) * k, s, rate)


def row_readers(row, rows, ends, conc_at, lo_c, hi_c, slabs, lo1, hi1, flags, u, ulo, uhi):
    first, last = ends_of(*ends)

    def pick(flag, a, b):
        there = [np.float32(0.0)] * row.tiles if a is None else row.read(a)
        return [jnp.where(flag, x, y) for x, y in zip(there, row.read(b))]

    def conc(r):
        if r < 0:
            return pick(first, None, lo_c(-1 - r))
        if r >= rows:
            return pick(last, conc_at(rows - 1), hi_c(r - rows))
        return row.read(conc_at(r))

    def poro(r):
        if r < 0:
            return pick(first, flags.at[0], lo1.at[7])
        if r >= rows:
            return pick(last, flags.at[1], hi1.at[7])
        return row.read(slabs.at[2, r])

    def flow(r):
        if r < 0:
            return pick(first, u.at[1, 0], ulo)
        if r >= rows:
            return pick(last, u.at[1, rows - 1], uhi)
        return row.read(u.at[1, r])

    return conc, poro, flow


def early_kernel(tiles, halves, ends, slabs, lo1, hi1, u, flags, cs):
    rows = u.shape[1]
    row = Row(tiles, halves)
    conc, poro, flow = row_readers(
        row, rows, ends, lambda r: slabs.at[0, r], lambda k: lo1.at[5 + k], lambda k: hi1.at[5 + k],
        slabs, lo1, hi1, flags, u, None, None,
    )
    for r in range(1, rows - 1):
        new = row.step(r, conc, poro, flow, (row.read(u.at[0, r]), row.read(u.at[2, r])), row.read(slabs.at[1, r]))
        for k in range(2):
            for c in range(tiles):
                cs[k, r - 1, :, cut(c)] = new[k][c]


def rim_kernel(tiles, halves, ends, slabs, lo1, hi1, u, flags, ulo, uhi, inner, cs, up, down):
    rows = u.shape[1]
    row = Row(tiles, halves)
    conc, poro, flow = row_readers(
        row, rows, ends, lambda r: slabs.at[0, r], lambda k: lo1.at[5 + k], lambda k: hi1.at[5 + k],
        slabs, lo1, hi1, flags, u, ulo, uhi,
    )
    for i, r in enumerate((0, rows - 1)):
        new = row.step(r, conc, poro, flow, (row.read(u.at[0, r]), row.read(u.at[2, r])), row.read(slabs.at[1, r]))
        for k in range(2):
            for c in range(tiles):
                cs[k, i, :, cut(c)] = new[k][c]
        for c in range(tiles):
            (down if i == 0 else up)[0, :, cut(c)] = new[0][c]
    down[1] = inner[0, 0]
    up[1] = inner[0, rows - 3]


def late_rows(tiles, halves, ends, which, slabs, lo1, hi1, u, flags, ulo, uhi, inner, rim, clo, chi, store):
    rows = u.shape[1]
    row = Row(tiles, halves)

    def state(k, r):
        return rim.at[k, 0 if r == 0 else 1] if r in (0, rows - 1) else inner.at[k, r - 1]

    conc, poro, flow = row_readers(
        row, rows, ends, lambda r: state(0, r), lambda k: clo.at[k], lambda k: chi.at[k],
        slabs, lo1, hi1, flags, u, ulo, uhi,
    )
    for r in which:
        new = row.step(r, conc, poro, flow, (row.read(u.at[0, r]), row.read(u.at[2, r])), row.read(state(1, r)))
        for c in range(tiles):
            store(r, c, new[0][c])


def middle_kernel(tiles, halves, ends, slabs, lo1, hi1, u, flags, inner, rim, out):
    def store(r, c, v):
        out[r - 2, :, cut(c)] = v

    late_rows(
        tiles, halves, ends, range(2, u.shape[1] - 2), slabs, lo1, hi1, u, flags, None, None, inner, rim,
        None, None, store,
    )


def deal(tiles, halves, parts, natural, blocks):
    depth = halves * tiles * SUBS
    run = depth // parts
    for k in range(parts):
        dest = lax.axis_index("narrow") ^ k
        for z in range(SUBS // halves):
            at = pl.multiple_of(z * depth + dest * run, SUBS)
            blocks[k][z] = natural[pl.ds(at, run), :]


def napl_kernel(tiles, halves, parts, inner, rim, *refs):
    *blocks, natural = refs
    rows = inner.shape[1] + 2
    for r in range(rows):
        for c in range(tiles):
            if r in (0, rows - 1):
                cc, ss = (rim[k, 0 if r == 0 else 1, :, cut(c)] for k in range(2))
            else:
                cc, ss = (inner[k, r - 1, :, cut(c)] for k in range(2))
            natural[strided(tiles, c, r), :] = ss - np.float32(DEPLETION) * loss([ss], [cc])[0]
    deal(tiles, halves, parts, natural, blocks)


def last_kernel(
    tiles, halves, ends, parts, slabs, lo1, hi1, u, flags, ulo, uhi, inner, rim, clo, chi, mid, *refs
):
    *blocks, natural = refs
    rows = u.shape[1]

    def store(r, c, v):
        natural[strided(tiles, c, r), :] = v

    for r in range(2, rows - 2):
        for c in range(tiles):
            store(r, c, mid[r - 2, :, cut(c)])
    late_rows(
        tiles, halves, ends, (0, 1, rows - 2, rows - 1), slabs, lo1, hi1, u, flags, ulo, uhi, inner, rim,
        clo, chi, store,
    )
    deal(tiles, halves, parts, natural, blocks)


def gather_kernel(parts, *refs):
    conc, napl, sems = refs[2 * parts :]
    copies = []
    for k in range(parts):
        origin = lax.axis_index("narrow") ^ k
        for i, (blocks, out) in enumerate(((refs[:parts], conc), (refs[parts : 2 * parts], napl))):
            copies.append(pltpu.make_async_copy(blocks[k], out.at[:, origin], sems.at[i * parts + k]))
            copies[-1].start()
    for copy in copies:
        copy.wait()


def call(kernel, out_shape, scratch=(), hbm=(), hbm_out=False, name=None, flops=0, n_in=0):
    specs = [pl.BlockSpec(memory_space=pltpu.HBM if i in hbm else pltpu.VMEM) for i in range(n_in)]
    if hbm_out:
        out_specs = jax.tree.map(lambda _: pl.BlockSpec(memory_space=pltpu.HBM), out_shape)
    else:
        out_specs = jax.tree.map(lambda _: pl.BlockSpec(memory_space=pltpu.VMEM), out_shape)
    return pl.pallas_call(
        kernel,
        out_shape=out_shape,
        in_specs=specs,
        out_specs=out_specs,
        scratch_shapes=list(scratch),
        name=name,
        compiler_params=pltpu.CompilerParams(vmem_limit_bytes=VMEM_LIMIT),
        cost_estimate=pl.CostEstimate(flops=flops, bytes_accessed=flops // 10, transcendentals=0),
    )


def local(populations, phase, porosity, napl, concentration, flags):
    layers, rows, width = phase.shape
    halves = SUBS // layers
    length = width // halves
    tiles = length // LANES
    parts = lax.axis_size("narrow")
    strips = lax.axis_size("wide") * parts
    both = ("wide", "narrow")
    ahead = [(i, (i + 1) % strips) for i in range(strips)]
    back = [(j, i) for i, j in ahead]
    cells = rows * SUBS * length
    slab = (SUBS, length)
    ends = (parts, strips)
    run = width // LANES * SUBS // parts

    def hold(*shape, dtype=F32):
        return pltpu.VMEM(shape, dtype)

    def exchange(up, down):
        return lax.ppermute(up, both, ahead), lax.ppermute(down, both, back)

    def pairwise(blocks):
        out = [blocks[0]] * parts
        for k in reversed(range(1, parts)):
            out[k] = lax.ppermute(blocks[k], "narrow", [(i, i ^ k) for i in range(parts)])
        return out

    pop = to_view(populations).reshape(19, SUBS, tiles, SUBS, LANES)
    views = [to_view(a) for a in (phase, concentration, napl, porosity)]
    flat = views[0].shape
    given = [pltpu.with_memory_space_constraint(a, pltpu.HBM) for a in (pop, *views, flags)]
    popv, phv, cov, nav, pov, flv, ge, up, down = call(
        functools.partial(first_edge_kernel, tiles),
        (
            hold(*pop.shape), hold(*flat, dtype=jnp.int32), hold(*flat), hold(*flat), hold(*flat),
            hold(*flags.shape, dtype=jnp.int32), hold(19, 2, *slab), hold(8, *slab), hold(8, *slab),
        ),
        scratch=(pltpu.SemaphoreType.DMA((tiles + 5,)),),
        hbm=range(6), name="first_edge", flops=100 * cells, n_in=6,
    )(*given)
    lo, hi = lo1, hi1 = exchange(up, down)
    g, fac, start, slabs, open_ends = call(
        functools.partial(first_inner_kernel, tiles, halves),
        (
            hold(19, rows, *slab), hold(rows, *slab), hold(19, rows, *slab), hold(3, rows, *slab),
            hold(2, *slab),
        ),
        name="first_inner", flops=400 * cells, n_in=7,
    )(popv.reshape(19, *flat), phv, cov, nav, pov, flv, ge)
    for _ in range(1, LBM_STEPS):
        ge, up, down = call(
            functools.partial(edge_kernel, tiles, halves),
            (hold(19, 2, *slab), hold(5, *slab), hold(5, *slab)),
            name="edge", flops=60 * cells, n_in=4,
        )(g, fac, lo, hi)
        lo, hi = exchange(up, down)
        g = call(
            functools.partial(inner_kernel, tiles, halves),
            hold(19, rows, *slab), name="inner", flops=250 * cells, n_in=3,
        )(g, ge, fac)
    ue, up, down = call(
        functools.partial(edge_speed_kernel, tiles, halves),
        (hold(3, 2, *slab), hold(*slab), hold(*slab)),
        name="edge_speed", flops=40 * cells, n_in=4,
    )(g, fac, lo, hi)
    ulo, uhi = exchange(up, down)
    u = call(
        functools.partial(inner_speed_kernel, tiles, halves),
        hold(3, rows, *slab), name="inner_speed", flops=150 * cells, n_in=3,
    )(g, fac, ue)
    inner = call(
        functools.partial(early_kernel, tiles, halves, ends),
        hold(2, rows - 2, *slab), name="early", flops=100 * cells, n_in=5,
    )(slabs, lo1, hi1, u, open_ends)
    rim, up, down = call(
        functools.partial(rim_kernel, tiles, halves, ends),
        (hold(2, 2, *slab), hold(2, *slab), hold(2, *slab)),
        name="rim", flops=30 * cells, n_in=8,
    )(slabs, lo1, hi1, u, open_ends, ulo, uhi, inner)
    clo, chi = exchange(up, down)
    blocks = call(
        functools.partial(napl_kernel, tiles, halves, parts),
        tuple(hold(layers, run, LANES) for _ in range(parts)),
        scratch=(pltpu.VMEM(flat, F32),), name="napl", flops=20 * cells, n_in=2,
    )(inner, rim)
    napl_blocks = pairwise(blocks)
    mid = call(
        functools.partial(middle_kernel, tiles, halves, ends),
        hold(rows - 4, *slab), name="middle", flops=60 * cells, n_in=7,
    )(slabs, lo1, hi1, u, open_ends, inner, rim)
    blocks = call(
        functools.partial(last_kernel, tiles, halves, ends, parts),
        tuple(hold(layers, run, LANES) for _ in range(parts)),
        scratch=(pltpu.VMEM(flat, F32),), name="last", flops=60 * cells, n_in=12,
    )(slabs, lo1, hi1, u, open_ends, ulo, uhi, inner, rim, clo, chi, mid)
    conc_blocks = pairwise(blocks)
    out = call(
        functools.partial(final_kernel, tiles, halves),
        jax.ShapeDtypeStruct((19, *flat), F32),
        scratch=(pltpu.VMEM((19, *flat), F32), pltpu.SemaphoreType.DMA((19,))),
        hbm_out=True, name="final", flops=400 * cells, n_in=5,
    )(g, fac, lo, hi, start)
    tile = (layers, parts, run, LANES)
    conc_out, napl_out = call(
        functools.partial(gather_kernel, parts),
        (jax.ShapeDtypeStruct(tile, F32), jax.ShapeDtypeStruct(tile, F32)),
        scratch=(pltpu.SemaphoreType.DMA((2 * parts,)),),
        hbm_out=True, name="gather", flops=10 * cells, n_in=2 * parts,
    )(*conc_blocks, *napl_blocks)
    shape = (layers, rows * parts, width // parts)

    def tile_of(a):
        return from_view(a.reshape(layers * parts * run, LANES), shape)

    return from_view(out, populations.shape), tile_of(conc_out), tile_of(napl_out)


def solution(mesh):
    strip = P(None, ("wide", "narrow"), None)
    in_specs = (P(None, None, ("wide", "narrow"), None), strip, strip, strip, strip, P())
    tile = P(None, "wide", "narrow")
    out_specs = (P(None, None, ("wide", "narrow"), None), tile, tile)
    return jax.shard_map(local, mesh=mesh, in_specs=in_specs, out_specs=out_specs, check_vma=False)
```

profile of v0, /device:TPU:0, one launch (start us, length us, event | category | flops | bytes accessed | tf_op | source)
XLA Modules:
  0.0 64.3 jit_solution(1157948480592945548)
XLA Ops:
  0.6 2.2 %first_edge.1 = (f32[19,8,4,8,128]{4,3,2,1,0:T(8,128)S(1)}, s32[256,128]{1,0:T(8,128)S(1)}, f32[256,128]{1,0:T(8,128)S(1)}, f32[256,128]{1,0:T(8,128)S(1)}, f32[...) custom-call(f32[19,8,4,8,128]{4,3,2,1,0:T(8,128)} %bitcast.42, ...), custom_call_target="tpu_custom_call" | custom-call | flops 3276800 | bytes 327680 | tf_op jit(solution)/shard_map/first_edge/pallas_call | solution.py:595
  2.8 3.1 %collective-permute-start = (f32[8,8,512]{2,1,0:T(8,128)S(1)}, f32[8,8,512]{2,1,0:T(8,128)S(1)}, u32[]{:S(2)}, u32[]{:S(2)}) collective-permute-start(f32[8,8,512]{2,1,0:T(8,128)S(1)} %get-tuple-element.51), channel_id=1, source_target_pairs={{0,1},{1,2},{2,3},{3,4},{4,5},{5,6},{6,7},{7,8},{8,9},{9,10},{10,1... | collective-permute-start | bytes 393224 | tf_op jit(solution)/shard_map/ppermute | solution.py:583
  5.9 3.4 %collective-permute-start.1 = (f32[8,8,512]{2,1,0:T(8,128)S(1)}, f32[8,8,512]{2,1,0:T(8,128)S(1)}, u32[]{:S(2)}, u32[]{:S(2)}) collective-permute-start(f32[8,8,512]{2,1,0:T(8,128)S(1)} %get-tuple-element.52), channel_id=1, source_target_pairs={{1,0},{2,1},{3,2},{4,3},{5,4},{6,5},{7,6},{8,7},{9,8},{10,9},{11,1... | collective-permute-start | bytes 393224 | tf_op jit(solution)/shard_map/ppermute | solution.py:583
  9.3 3.2 %first_inner.1 = (f32[19,8,8,512]{3,2,1,0:T(8,128)S(1)}, f32[8,8,512]{2,1,0:T(8,128)S(1)}, f32[19,8,8,512]{3,2,1,0:T(8,128)S(1)}, f32[3,8,8,512]{3,2,1,0:T(8,128)S(1)}, f32[2,8,512]{2,1,0:T(8,128)S(1)}) custom-call(f32[19,256,128]{2,1,0:T(8,128)S(1)} %bitcast.41, s32[256,128]{1,0:T(8,128)S(1)} %get-tuple-element.43.phase, ...), custom_call_target="tpu_custom_call" | custom-call | flops 13107200 | bytes 1310720 | tf_op jit(solution)/shard_map/first_inner/pallas_call | solution.py:605
  12.6 1.1 %collective-permute-done.1.hi.hi1 = f32[8,8,512]{2,1,0:T(8,128)S(1)} collective-permute-done((f32[8,8,512]{2,1,0:T(8,128)S(1)}, f32[8,8,512]{2,1,0:T(8,128)S(1)}, u32[]{:S(2)}, u32[]{:S(2)}) %collective-permute-start.1) | collective-permute-done | bytes 131104 | tf_op jit(solution)/shard_map/ppermute | solution.py:583
  14.0 1.6 %collective-permute-start.2 = (f32[5,8,512]{2,1,0:T(8,128)S(1)}, f32[5,8,512]{2,1,0:T(8,128)S(1)}, u32[]{:S(2)}, u32[]{:S(2)}) collective-permute-start(f32[5,8,512]{2,1,0:T(8,128)S(1)} %get-tuple-element.54), channel_id=1, source_target_pairs={{0,1},{1,2},{2,3},{3,4},{4,5},{5,6},{6,7},{7,8},{8,9},{9,10},{10,1... | collective-permute-start | bytes 245768 | tf_op jit(solution)/shard_map/ppermute | solution.py:583
  15.6 3.8 %collective-permute-start.3 = (f32[5,8,512]{2,1,0:T(8,128)S(1)}, f32[5,8,512]{2,1,0:T(8,128)S(1)}, u32[]{:S(2)}, u32[]{:S(2)}) collective-permute-start(f32[5,8,512]{2,1,0:T(8,128)S(1)} %get-tuple-element.55), channel_id=1, source_target_pairs={{1,0},{2,1},{3,2},{4,3},{5,4},{6,5},{7,6},{8,7},{9,8},{10,9},{11,1... | collective-permute-start | bytes 245768 | tf_op jit(solution)/shard_map/ppermute | solution.py:583
  19.4 1.3 %inner.3.g = f32[19,8,8,512]{3,2,1,0:T(8,128)S(1)} custom-call(f32[19,8,8,512]{3,2,1,0:T(8,128)S(1)} %get-tuple-element.49.g, f32[19,2,8,512]{3,2,1,0:T(8,128)S(1)} %get-tuple-element.53.ge, f32[8,8,512]{2,1,0:T(8,128)S(1)} %get-tuple-element.50.fac), custom_call_target="tpu_custom_call" | custom-call | flops 8192000 | bytes 819200 | tf_op jit(solution)/shard_map/inner/pallas_call | solution.py:620
  20.7 1.6 %collective-permute-done.2.lo = f32[5,8,512]{2,1,0:T(8,128)S(1)} collective-permute-done((f32[5,8,512]{2,1,0:T(8,128)S(1)}, f32[5,8,512]{2,1,0:T(8,128)S(1)}, u32[]{:S(2)}, u32[]{:S(2)}) %collective-permute-start.2) | collective-permute-done | bytes 81952 | tf_op jit(solution)/shard_map/ppermute | solution.py:583
  22.7 5.4 %collective-permute-start.5 = (f32[5,8,512]{2,1,0:T(8,128)S(1)}, f32[5,8,512]{2,1,0:T(8,128)S(1)}, u32[]{:S(2)}, u32[]{:S(2)}) collective-permute-start(f32[5,8,512]{2,1,0:T(8,128)S(1)} %get-tuple-element.58), channel_id=1, source_target_pairs={{1,0},{2,1},{3,2},{4,3},{5,4},{6,5},{7,6},{8,7},{9,8},{10,9},{11,1... | collective-permute-start | bytes 245768 | tf_op jit(solution)/shard_map/ppermute | solution.py:583
  28.1 1.3 %inner.4.g = f32[19,8,8,512]{3,2,1,0:T(8,128)S(1)} custom-call(f32[19,8,8,512]{3,2,1,0:T(8,128)S(1)} %inner.3.g, f32[19,2,8,512]{3,2,1,0:T(8,128)S(1)} %get-tuple-element.56.ge, f32[8,8,512]{2,1,0:T(8,128)S(1)} %get-tuple-element.50.fac), custom_call_target="tpu_custom_call" | custom-call | flops 8192000 | bytes 819200 | tf_op jit(solution)/shard_map/inner/pallas_call | solution.py:620
  29.4 0.9 %collective-permute-done.4.lo = f32[5,8,512]{2,1,0:T(8,128)S(1)} collective-permute-done((f32[5,8,512]{2,1,0:T(8,128)S(1)}, f32[5,8,512]{2,1,0:T(8,128)S(1)}, u32[]{:S(2)}, u32[]{:S(2)}) %collective-permute-start.4) | collective-permute-done | bytes 81952 | tf_op jit(solution)/shard_map/ppermute | solution.py:583
  31.0 5.6 %collective-permute-start.7 = (f32[5,8,512]{2,1,0:T(8,128)S(1)}, f32[5,8,512]{2,1,0:T(8,128)S(1)}, u32[]{:S(2)}, u32[]{:S(2)}) collective-permute-start(f32[5,8,512]{2,1,0:T(8,128)S(1)} %get-tuple-element.61), channel_id=1, source_target_pairs={{1,0},{2,1},{3,2},{4,3},{5,4},{6,5},{7,6},{8,7},{9,8},{10,9},{11,1... | collective-permute-start | bytes 245768 | tf_op jit(solution)/shard_map/ppermute | solution.py:583
  36.6 1.3 %inner.5.g = f32[19,8,8,512]{3,2,1,0:T(8,128)S(1)} custom-call(f32[19,8,8,512]{3,2,1,0:T(8,128)S(1)} %inner.4.g, f32[19,2,8,512]{3,2,1,0:T(8,128)S(1)} %get-tuple-element.59.ge, f32[8,8,512]{2,1,0:T(8,128)S(1)} %get-tuple-element.50.fac), custom_call_target="tpu_custom_call" | custom-call | flops 8192000 | bytes 819200 | tf_op jit(solution)/shard_map/inner/pallas_call | solution.py:620
  37.8 0.9 %collective-permute-done.6.lo = f32[5,8,512]{2,1,0:T(8,128)S(1)} collective-permute-done((f32[5,8,512]{2,1,0:T(8,128)S(1)}, f32[5,8,512]{2,1,0:T(8,128)S(1)}, u32[]{:S(2)}, u32[]{:S(2)}) %collective-permute-start.6) | collective-permute-done | bytes 81952 | tf_op jit(solution)/shard_map/ppermute | solution.py:583
  38.9 5.4 %collective-permute-start.9 = (f32[8,512]{1,0:T(8,128)S(1)}, f32[8,512]{1,0:T(8,128)S(1)}, u32[]{:S(2)}, u32[]{:S(2)}) collective-permute-start(f32[8,512]{1,0:T(8,128)S(1)} %get-tuple-element.67), channel_id=1, source_target_pairs={{1,0},{2,1},{3,2},{4,3},{5,4},{6,5},{7,6},{8,7},{9,8},{10,9},{11,1... | collective-permute-start | bytes 49160 | tf_op jit(solution)/shard_map/ppermute | solution.py:583
  44.4 0.8 %inner_speed.1.u = f32[3,8,8,512]{3,2,1,0:T(8,128)S(1)} custom-call(f32[19,8,8,512]{3,2,1,0:T(8,128)S(1)} %inner.5.g, f32[8,8,512]{2,1,0:T(8,128)S(1)} %get-tuple-element.50.fac, f32[3,2,8,512]{3,2,1,0:T(8,128)S(1)} %get-tuple-element.64.ue), custom_call_target="tpu_custom_call" | custom-call | flops 4915200 | bytes 491520 | tf_op jit(solution)/shard_map/inner_speed/pallas_call | solution.py:630
  45.1 0.5 early.1.inner
  46.1 5.4 %collective-permute-start.11 = (f32[2,8,512]{2,1,0:T(8,128)S(1)}, f32[2,8,512]{2,1,0:T(8,128)S(1)}, u32[]{:S(2)}, u32[]{:S(2)}) collective-permute-start(f32[2,8,512]{2,1,0:T(8,128)S(1)} %get-tuple-element.70), channel_id=1, source_target_pairs={{1,0},{2,1},{3,2},{4,3},{5,4},{6,5},{7,6},{8,7},{9,8},{10,9},{11,1... | collective-permute-start | bytes 98312 | tf_op jit(solution)/shard_map/ppermute | solution.py:583
  51.8 4.3 %collective-permute-start.17 = (f32[4,16,128]{2,1,0:T(8,128)S(1)}, f32[4,16,128]{2,1,0:T(8,128)S(1)}, u32[]{:S(2)}, u32[]{:S(2)}) collective-permute-start(f32[4,16,128]{2,1,0:T(8,128)S(1)} %get-tuple-element.78), channel_id=1, source_target_pairs={{0,3},{1,2},{2,1},{3,0},{4,7},{5,6},{6,5},{7,4},{8,11},{9,10},{10,... | collective-permute-start | bytes 98312 | tf_op jit(solution)/shard_map/ppermute | solution.py:588
  57.0 0.6 collective-permute-start.13
  57.5 3.8 %collective-permute-start.14 = (f32[4,16,128]{2,1,0:T(8,128)S(1)}, f32[4,16,128]{2,1,0:T(8,128)S(1)}, u32[]{:S(2)}, u32[]{:S(2)}) collective-permute-start(f32[4,16,128]{2,1,0:T(8,128)S(1)} %get-tuple-element.74), channel_id=1, source_target_pairs={{0,3},{1,2},{2,1},{3,0},{4,7},{5,6},{6,5},{7,4},{8,11},{9,10},{10,... | collective-permute-start | bytes 98312 | tf_op jit(solution)/shard_map/ppermute | solution.py:588
  61.3 2.1 %final.1 = f32[19,256,128]{2,1,0:T(8,128)} custom-call(f32[19,8,8,512]{3,2,1,0:T(8,128)S(1)} %inner.5.g, f32[8,8,512]{2,1,0:T(8,128)S(1)} %get-tuple-element.50.fac, f32[5,8,512]{2,1,0:T(8,128)S(1)} %collective-permute-done.6.lo, f32[5,8,512]{2,1,0:T(8,128)S(1)} %collective-permute-done.7.hi, f32[19,8,8,512]{3,2,1,0:T(8,128)S(1)} %get-tuple-element.62.start), custom_call_target="tpu_custom_call" | custom-call | flops 13107200 | bytes 1310720 | tf_op jit(solution)/shard_map/final/pallas_call | solution.py:660
  63.6 0.8 %gather.1 = (f32[4,4,16,128]{3,2,1,0:T(8,128)}, f32[4,4,16,128]{3,2,1,0:T(8,128)}) custom-call(f32[4,16,128]{2,1,0:T(8,128)S(1)} %get-tuple-element.71.refs_0_, f32[4,16,128]{2,1,0:T(8,128)S(1)} %collective-permute-done.12.refs_1_, f32[4,16,128]{2,1,0:T(8,128)S(1)} %collective-permute-done.13.refs_2_, f32[4,16,128]{2,1,0:T(8,128)S(1)} %collective-permute-done.14.refs_3_, ...), custom_call_target="tpu_custom_call" | custom-call | flops 327680 | bytes 32768 | tf_op jit(solution)/shard_map/gather/pallas_call | solution.py:667
  (29 shorter events, 3.6 us)
Async XLA Ops:
  2.8 9.8 %collective-permute-start = (f32[8,8,512]{2,1,0:T(8,128)S(1)}, f32[8,8,512]{2,1,0:T(8,128)S(1)}, u32[]{:S(2)}, u32[]{:S(2)}) collective-permute-start(f32[8,8,512]{2,1,0:T(8,128)S(1)} %get-tuple-element.51), channel_id=1, source_target_pairs={{0,1},{1,2},{2,3},{3,4},{4,5},{5,6},{6,7},{7,8},{8,9},{9,10},{10,1... | collective-permute-start | bytes 393224 | tf_op jit(solution)/shard_map/ppermute | solution.py:583
  5.9 7.8 %collective-permute-start.1 = (f32[8,8,512]{2,1,0:T(8,128)S(1)}, f32[8,8,512]{2,1,0:T(8,128)S(1)}, u32[]{:S(2)}, u32[]{:S(2)}) collective-permute-start(f32[8,8,512]{2,1,0:T(8,128)S(1)} %get-tuple-element.52), channel_id=1, source_target_pairs={{1,0},{2,1},{3,2},{4,3},{5,4},{6,5},{7,6},{8,7},{9,8},{10,9},{11,1... | collective-permute-start | bytes 393224 | tf_op jit(solution)/shard_map/ppermute | solution.py:583
  14.0 8.3 %collective-permute-start.2 = (f32[5,8,512]{2,1,0:T(8,128)S(1)}, f32[5,8,512]{2,1,0:T(8,128)S(1)}, u32[]{:S(2)}, u32[]{:S(2)}) collective-permute-start(f32[5,8,512]{2,1,0:T(8,128)S(1)} %get-tuple-element.54), channel_id=1, source_target_pairs={{0,1},{1,2},{2,3},{3,4},{4,5},{5,6},{6,7},{7,8},{8,9},{9,10},{10,1... | collective-permute-start | bytes 245768 | tf_op jit(solution)/shard_map/ppermute | solution.py:583
  15.6 6.7 %collective-permute-start.3 = (f32[5,8,512]{2,1,0:T(8,128)S(1)}, f32[5,8,512]{2,1,0:T(8,128)S(1)}, u32[]{:S(2)}, u32[]{:S(2)}) collective-permute-start(f32[5,8,512]{2,1,0:T(8,128)S(1)} %get-tuple-element.55), channel_id=1, source_target_pairs={{1,0},{2,1},{3,2},{4,3},{5,4},{6,5},{7,6},{8,7},{9,8},{10,9},{11,1... | collective-permute-start | bytes 245768 | tf_op jit(solution)/shard_map/ppermute | solution.py:583
  22.6 7.6 %collective-permute-start.4 = (f32[5,8,512]{2,1,0:T(8,128)S(1)}, f32[5,8,512]{2,1,0:T(8,128)S(1)}, u32[]{:S(2)}, u32[]{:S(2)}) collective-permute-start(f32[5,8,512]{2,1,0:T(8,128)S(1)} %get-tuple-element.57), channel_id=1, source_target_pairs={{0,1},{1,2},{2,3},{3,4},{4,5},{5,6},{6,7},{7,8},{8,9},{9,10},{10,1... | collective-permute-start | bytes 245768 | tf_op jit(solution)/shard_map/ppermute | solution.py:583
  22.7 7.9 %collective-permute-start.5 = (f32[5,8,512]{2,1,0:T(8,128)S(1)}, f32[5,8,512]{2,1,0:T(8,128)S(1)}, u32[]{:S(2)}, u32[]{:S(2)}) collective-permute-start(f32[5,8,512]{2,1,0:T(8,128)S(1)} %get-tuple-element.58), channel_id=1, source_target_pairs={{1,0},{2,1},{3,2},{4,3},{5,4},{6,5},{7,6},{8,7},{9,8},{10,9},{11,1... | collective-permute-start | bytes 245768 | tf_op jit(solution)/shard_map/ppermute | solution.py:583
  30.9 7.8 %collective-permute-start.6 = (f32[5,8,512]{2,1,0:T(8,128)S(1)}, f32[5,8,512]{2,1,0:T(8,128)S(1)}, u32[]{:S(2)}, u32[]{:S(2)}) collective-permute-start(f32[5,8,512]{2,1,0:T(8,128)S(1)} %get-tuple-element.60), channel_id=1, source_target_pairs={{0,1},{1,2},{2,3},{3,4},{4,5},{5,6},{6,7},{7,8},{8,9},{9,10},{10,1... | collective-permute-start | bytes 245768 | tf_op jit(solution)/shard_map/ppermute | solution.py:583
  31.0 7.7 %collective-permute-start.7 = (f32[5,8,512]{2,1,0:T(8,128)S(1)}, f32[5,8,512]{2,1,0:T(8,128)S(1)}, u32[]{:S(2)}, u32[]{:S(2)}) collective-permute-start(f32[5,8,512]{2,1,0:T(8,128)S(1)} %get-tuple-element.61), channel_id=1, source_target_pairs={{1,0},{2,1},{3,2},{4,3},{5,4},{6,5},{7,6},{8,7},{9,8},{10,9},{11,1... | collective-permute-start | bytes 245768 | tf_op jit(solution)/shard_map/ppermute | solution.py:583
  38.9 6.8 %collective-permute-start.8 = (f32[8,512]{1,0:T(8,128)S(1)}, f32[8,512]{1,0:T(8,128)S(1)}, u32[]{:S(2)}, u32[]{:S(2)}) collective-permute-start(f32[8,512]{1,0:T(8,128)S(1)} %get-tuple-element.66), channel_id=1, source_target_pairs={{0,1},{1,2},{2,3},{3,4},{4,5},{5,6},{6,7},{7,8},{8,9},{9,10},{10,1... | collective-permute-start | bytes 49160 | tf_op jit(solution)/shard_map/ppermute | solution.py:583
  38.9 6.9 %collective-permute-start.9 = (f32[8,512]{1,0:T(8,128)S(1)}, f32[8,512]{1,0:T(8,128)S(1)}, u32[]{:S(2)}, u32[]{:S(2)}) collective-permute-start(f32[8,512]{1,0:T(8,128)S(1)} %get-tuple-element.67), channel_id=1, source_target_pairs={{1,0},{2,1},{3,2},{4,3},{5,4},{6,5},{7,6},{8,7},{9,8},{10,9},{11,1... | collective-permute-start | bytes 49160 | tf_op jit(solution)/shard_map/ppermute | solution.py:583
  46.1 10.4 %collective-permute-start.10 = (f32[2,8,512]{2,1,0:T(8,128)S(1)}, f32[2,8,512]{2,1,0:T(8,128)S(1)}, u32[]{:S(2)}, u32[]{:S(2)}) collective-permute-start(f32[2,8,512]{2,1,0:T(8,128)S(1)} %get-tuple-element.69), channel_id=1, source_target_pairs={{0,1},{1,2},{2,3},{3,4},{4,5},{5,6},{6,7},{7,8},{8,9},{9,10},{10,1... | collective-permute-start | bytes 98312 | tf_op jit(solution)/shard_map/ppermute | solution.py:583
  46.1 10.3 %collective-permute-start.11 = (f32[2,8,512]{2,1,0:T(8,128)S(1)}, f32[2,8,512]{2,1,0:T(8,128)S(1)}, u32[]{:S(2)}, u32[]{:S(2)}) collective-permute-start(f32[2,8,512]{2,1,0:T(8,128)S(1)} %get-tuple-element.70), channel_id=1, source_target_pairs={{1,0},{2,1},{3,2},{4,3},{5,4},{6,5},{7,6},{8,7},{9,8},{10,9},{11,1... | collective-permute-start | bytes 98312 | tf_op jit(solution)/shard_map/ppermute | solution.py:583
  51.6 5.9 %collective-permute-start.15 = (f32[4,16,128]{2,1,0:T(8,128)S(1)}, f32[4,16,128]{2,1,0:T(8,128)S(1)}, u32[]{:S(2)}, u32[]{:S(2)}) collective-permute-start(f32[4,16,128]{2,1,0:T(8,128)S(1)} %get-tuple-element.76), channel_id=1, source_target_pairs={{0,1},{1,0},{2,3},{3,2},{4,5},{5,4},{6,7},{7,6},{8,9},{9,8},{10,11... | collective-permute-start | bytes 98312 | tf_op jit(solution)/shard_map/ppermute | solution.py:588
  51.7 11.7 %collective-permute-start.16 = (f32[4,16,128]{2,1,0:T(8,128)S(1)}, f32[4,16,128]{2,1,0:T(8,128)S(1)}, u32[]{:S(2)}, u32[]{:S(2)}) collective-permute-start(f32[4,16,128]{2,1,0:T(8,128)S(1)} %get-tuple-element.77), channel_id=1, source_target_pairs={{0,2},{1,3},{2,0},{3,1},{4,6},{5,7},{6,4},{7,5},{8,10},{9,11},{10,... | collective-permute-start | bytes 98312 | tf_op jit(solution)/shard_map/ppermute | solution.py:588
  51.8 11.6 %collective-permute-start.17 = (f32[4,16,128]{2,1,0:T(8,128)S(1)}, f32[4,16,128]{2,1,0:T(8,128)S(1)}, u32[]{:S(2)}, u32[]{:S(2)}) collective-permute-start(f32[4,16,128]{2,1,0:T(8,128)S(1)} %get-tuple-element.78), channel_id=1, source_target_pairs={{0,3},{1,2},{2,1},{3,0},{4,7},{5,6},{6,5},{7,4},{8,11},{9,10},{10,... | collective-permute-start | bytes 98312 | tf_op jit(solution)/shard_map/ppermute | solution.py:588
  56.9 6.5 %collective-permute-start.12 = (f32[4,16,128]{2,1,0:T(8,128)S(1)}, f32[4,16,128]{2,1,0:T(8,128)S(1)}, u32[]{:S(2)}, u32[]{:S(2)}) collective-permute-start(f32[4,16,128]{2,1,0:T(8,128)S(1)} %get-tuple-element.72), channel_id=1, source_target_pairs={{0,1},{1,0},{2,3},{3,2},{4,5},{5,4},{6,7},{7,6},{8,9},{9,8},{10,11... | collective-permute-start | bytes 98312 | tf_op jit(solution)/shard_map/ppermute | solution.py:588
  57.0 6.5 %collective-permute-start.13 = (f32[4,16,128]{2,1,0:T(8,128)S(1)}, f32[4,16,128]{2,1,0:T(8,128)S(1)}, u32[]{:S(2)}, u32[]{:S(2)}) collective-permute-start(f32[4,16,128]{2,1,0:T(8,128)S(1)} %get-tuple-element.73), channel_id=1, source_target_pairs={{0,2},{1,3},{2,0},{3,1},{4,6},{5,7},{6,4},{7,5},{8,10},{9,11},{10,... | collective-permute-start | bytes 98312 | tf_op jit(solution)/shard_map/ppermute | solution.py:588
  57.5 6.1 %collective-permute-start.14 = (f32[4,16,128]{2,1,0:T(8,128)S(1)}, f32[4,16,128]{2,1,0:T(8,128)S(1)}, u32[]{:S(2)}, u32[]{:S(2)}) collective-permute-start(f32[4,16,128]{2,1,0:T(8,128)S(1)} %get-tuple-element.74), channel_id=1, source_target_pairs={{0,3},{1,2},{2,1},{3,0},{4,7},{5,6},{6,5},{7,4},{8,11},{9,10},{10,... | collective-permute-start | bytes 98312 | tf_op jit(solution)/shard_map/ppermute | solution.py:588
where the time goes:
time: 64.5 us; the launch traced here: 64.3 us
  starting transfers between devices  42.8 us (66%)
  Pallas kernels  15.4 us (24%)
  waiting for transfers between devices  5.2 us (8%)
  between operations  0.86 us (1%)
    ppermute x12, starting transfers between devices, exchange(): return (lax.ppermute(up, both, ahead), lax.ppermute(down, both, back))  33.9 us
    ppermute x6, starting transfers between devices, pairwise(): lax.ppermute(blocks[k], 'narrow', [(i, i ^ k) for i in range(parts)])  8.88 us
    ppermute x12, waiting for transfers between devices, exchange(): return (lax.ppermute(up, both, ahead), lax.ppermute(down, both, back))  5.06 us
    pallas_call x3, Pallas kernels, local(): call(functools.partial(inner_kernel, tiles, halves), hold(19, rows, *slab...  3.76 us
    pallas_call x1, Pallas kernels, local(): call(functools.partial(first_inner_kernel, tiles, halves), (hold(19, rows...  3.22 us
    pallas_call x1, Pallas kernels, local(): call(functools.partial(first_edge_kernel, tiles), (hold(*pop.shape), hold...  2.18 us
    pallas_call x1, Pallas kernels, local(): call(functools.partial(final_kernel, tiles, halves), jax.ShapeDtypeStruct...  2.05 us
  transfers between devices with their start and end apart: 18, of which 9 were waited for; matrix products, arithmetic and copies ran while one was open for 0% of the time, Pallas kernels for 17%

commit v1 on v0

v1 whole, which is shorter than its diff:
```python
import functools

import jax
import jax.numpy as jnp
import numpy as np
from jax import lax
from jax.experimental import pallas as pl
from jax.experimental.pallas import tpu as pltpu
from jax.sharding import PartitionSpec as P

LBM_STEPS = 4
F32 = jnp.float32

DIRS = [
    (0, 0, 0), (1, 0, 0), (-1, 0, 0), (0, 1, 0), (0, -1, 0), (0, 0, 1), (0, 0, -1),
    (1, 1, 0), (-1, -1, 0), (1, -1, 0), (-1, 1, 0), (1, 0, 1), (-1, 0, -1), (1, 0, -1),
    (-1, 0, 1), (0, 1, 1), (0, -1, -1), (0, 1, -1), (0, -1, 1),
]
OPP = [0, 2, 1, 4, 3, 6, 5, 8, 7, 10, 9, 12, 11, 14, 13, 16, 15, 18, 17]
UP = [1, 7, 9, 11, 13]
DOWN = [2, 8, 10, 12, 14]
DIFFUSION = 0.15
TRANSFER = 0.3
DEPLETION = 0.5
FLOOR = 0.3
SUBS = 8
LANES = 128
VMEM_LIMIT = 16 * 1024 * 1024


def to_view(array):
    *lead, rows, width = array.shape
    n = len(lead)
    t = array.reshape(*lead, rows // SUBS, SUBS, width // LANES, LANES)
    t = t.transpose(*range(n), n, n + 2, n + 1, n + 3)
    return t.reshape(*lead[:-1], lead[-1] * rows * width // LANES, LANES)


def from_view(view, shape):
    *lead, rows, width = shape
    n = len(lead)
    t = view.reshape(*lead, rows // SUBS, width // LANES, SUBS, LANES)
    t = t.transpose(*range(n), n, n + 2, n + 1, n + 3)
    return t.reshape(shape)


def iotas():
    lane = lax.broadcasted_iota(jnp.int32, (SUBS, LANES), 1)
    sub = lax.broadcasted_iota(jnp.int32, (SUBS, LANES), 0)
    return lane, sub


def cut(c):
    return slice(c * LANES, (c + 1) * LANES)


def strided(tiles, c, x):
    return pl.ds(c * SUBS + x, SUBS, stride=tiles * SUBS)


def collide(f, fac):
    s = [f[2 * p + 1] + f[2 * p + 2] for p in range(9)]
    d = [f[2 * p + 1] - f[2 * p + 2] for p in range(9)]
    rho = f[0] + (((s[0] + s[1]) + (s[2] + s[3])) + ((s[4] + s[5]) + (s[6] + s[7])) + s[8])
    jx = d[0] + ((d[3] + d[4]) + (d[5] + d[6]))
    jy = d[1] + ((d[3] - d[4]) + (d[7] + d[8]))
    jz = d[2] + ((d[5] - d[6]) + (d[7] - d[8]))
    inv = fac / rho
    vx, vy, vz = jx * inv, jy * inv, jz * inv
    w1 = rho * np.float32(1.25 / 18)
    w2 = rho * np.float32(1.25 / 36)
    w4 = rho * np.float32(1.25 / 72)
    a1 = w1 - w1 * ((vx * vx + vy * vy + vz * vz) * np.float32(1.0 / 6))
    a2 = a1 * np.float32(0.5)
    post = [a1 * np.float32(6.0) - f[0] * np.float32(0.25)]
    axes = [vx, vy, vz, vx + vy, vx - vy, vx + vz, vx - vz, vy + vz, vy - vz]
    for p, v in enumerate(axes):
        wa, wh, base = (w1, w2, a1) if p < 3 else (w2, w4, a2)
        even = (base + (wh * v) * v) - s[p] * np.float32(0.125)
        odd = wa * v - d[p] * np.float32(0.125)
        post += [even + odd, even - odd]
    return post


def pull(load, q, c, tiles, halves, lane, sub):
    _, cross, layer = DIRS[q]
    v = load(q, c)
    if cross == 1:
        if c > 0:
            side = load(q, c - 1)
        else:
            side = jnp.where(sub % halves == 0, jnp.nan, pltpu.roll(load(q, tiles - 1), 1, 0))
        v = pltpu.roll(jnp.where(lane == LANES - 1, side, v), 1, 1)
    elif cross == -1:
        if c < tiles - 1:
            side = load(q, c + 1)
        else:
            side = jnp.where(sub % halves == halves - 1, jnp.nan, pltpu.roll(load(q, 0), SUBS - 1, 0))
        v = pltpu.roll(jnp.where(lane == 0, side, v), LANES - 1, 1)
    if layer:
        v = pltpu.roll(v, (layer * halves) % SUBS, 0)
    return v


def stream(g, lo, hi, x, c, tiles, halves, lane, sub, place):
    def load(q, cc):
        flow = DIRS[q][0]
        if flow == 1 and place == "first":
            return lo[UP.index(q), :, cut(cc)]
        if flow == -1 and place == "last":
            return hi[DOWN.index(q), :, cut(cc)]
        return g[q, x - flow, :, cut(cc)]

    f = [g[0, x, :, cut(c)]]
    for q in range(1, 19):
        v = pull(load, q, c, tiles, halves, lane, sub)
        f.append(jnp.where(v != v, g[OPP[q], x, :, cut(c)], v))
    return f


def drag(ph):
    return jnp.where(ph == 2, jnp.nan, jnp.where(ph == 1, np.float32(1.5), np.float32(3.0)))


def swap_tile(v, sub):
    v = list(v)
    for k in (4, 2, 1):
        low = sub & k == 0
        for i in range(SUBS):
            if not i & k:
                a, b = v[i], v[i + k]
                v[i] = jnp.where(low, a, pltpu.roll(b, k, 0))
                v[i + k] = jnp.where(low, pltpu.roll(a, SUBS - k, 0), b)
    return v


def upper(chain):
    odd = lax.rem(lax.axis_index("narrow"), 2) == 1
    return odd if chain else jnp.logical_not(odd)


def by_side(chain, side):
    pl.when(upper(chain))(lambda: side(True))
    pl.when(jnp.logical_not(upper(chain)))(lambda: side(False))


def pick(flag, a, b):
    return [jnp.where(flag, x, y) for x, y in zip(a, b)]


def start_face(tiles, chain, pop, phase, conc, poro, row, send):
    up = upper(chain)
    x = jnp.where(up, SUBS - 1, 0)
    beside = jnp.where(up, SUBS - 2, 1)
    for c in range(tiles):
        at = strided(tiles, c, x)
        post = collide([pop[q, at, :] for q in range(19)], drag(phase[at, :]))
        for q in range(19):
            row[q, :, cut(c)] = post[q]
        for i in range(5):
            send[i, :, cut(c)] = jnp.where(up, post[UP[i]], post[DOWN[i]])
        send[5, :, cut(c)] = conc[at, :]
        send[6, :, cut(c)] = conc[strided(tiles, c, beside), :]
        send[7, :, cut(c)] = poro[at, :]


def first_kernel(
    tiles, pop_h, phase_h, conc_h, napl_h, poro_h, flags_h,
    pop, phase, conc, napl, poro, flags, row, send, sems,
):
    small = [
        pltpu.make_async_copy(a, b, sems.at[i])
        for i, (a, b) in enumerate(
            ((phase_h, phase), (conc_h, conc), (poro_h, poro), (napl_h, napl), (flags_h, flags))
        )
    ]
    large = pltpu.make_async_copy(pop_h, pop, sems.at[len(small)])
    large.start()
    for copy in small:
        copy.start()
    for copy in small:
        copy.wait()
    large.wait()
    start_face(tiles, 0, pop, phase, conc, poro, row, send)


def second_kernel(tiles, pop, phase, conc, poro, after, row, send):
    start_face(tiles, 1, pop, phase, conc, poro, row, send)


def merge_rows(out, row0, row1, count):
    rows = out.shape[1]

    def side(up):
        for k in range(count):
            out[k, 0] = (row0 if up else row1)[k]
            out[k, rows - 1] = (row1 if up else row0)[k]

    by_side(1, side)


def first_inner_kernel(
    tiles, halves, pop, phase, conc, napl, poro, flags, row0, row1, g, fac, start, slabs, open_ends
):
    rows = g.shape[1]
    length = tiles * LANES
    _, sub = iotas()

    def to_slabs(read, write):
        for c in range(tiles):
            v = [read(pl.ds((i * tiles + c) * SUBS, SUBS)) for i in range(SUBS)]
            for x, t in enumerate(swap_tile(v, sub)):
                write(x, cut(c), t)

    def store(ref, k):
        def write(x, at, t):
            ref[k, x, :, at] = t

        return write

    def store_fac(x, at, t):
        fac[x, :, at] = t

    to_slabs(lambda at: drag(phase[at, :]), store_fac)

    def direction(q, _):
        to_slabs(lambda at: pop[q, at, :], store(start, q))
        return 0

    lax.fori_loop(0, 19, direction, 0)

    def row(x, _):
        for c in range(tiles):
            post = collide([start[q, x, :, cut(c)] for q in range(19)], fac[x, :, cut(c)])
            for q in range(19):
                g[q, x, :, cut(c)] = post[q]
        return 0

    lax.fori_loop(1, rows - 1, row, 0)
    merge_rows(g, row0, row1, 19)
    for k, ref in enumerate((conc, napl, poro)):
        to_slabs(lambda at, ref=ref: ref[at, :], store(slabs, k))
    for k in range(2):
        for z in range(SUBS // halves):
            for h in range(halves):
                line = flags[k, z : z + 1, h * length : (h + 1) * length]
                open_ends[k, z * halves + h : z * halves + h + 1, :] = line.astype(F32)


def edge_kernel(tiles, halves, chain, g, fac, halo, after, row, send):
    rows = g.shape[1]
    lane, sub = iotas()

    def side(up):
        x = rows - 1 if up else 0
        lo, hi, place = (None, halo, "last") if up else (halo, None, "first")
        for c in range(tiles):
            post = collide(stream(g, lo, hi, x, c, tiles, halves, lane, sub, place), fac[x, :, cut(c)])
            for q in range(19):
                row[q, :, cut(c)] = post[q]
            for i, q in enumerate(UP if up else DOWN):
                send[i, :, cut(c)] = post[q]

    by_side(chain, side)


def inner_kernel(tiles, halves, g, row0, row1, fac, out):
    rows = g.shape[1]
    lane, sub = iotas()

    def row(x, _):
        for c in range(tiles):
            f = stream(g, None, None, x, c, tiles, halves, lane, sub, "mid")
            post = collide(f, fac[x, :, cut(c)])
            for q in range(19):
                out[q, x, :, cut(c)] = post[q]
        return 0

    lax.fori_loop(1, rows - 1, row, 0)
    merge_rows(out, row0, row1, 19)


def speed(f, fc):
    s = [f[2 * p + 1] + f[2 * p + 2] for p in range(9)]
    d = [f[2 * p + 1] - f[2 * p + 2] for p in range(9)]
    rho = f[0] + (((s[0] + s[1]) + (s[2] + s[3])) + ((s[4] + s[5]) + (s[6] + s[7])) + s[8])
    jx = d[0] + ((d[3] + d[4]) + (d[5] + d[6]))
    jy = d[1] + ((d[3] - d[4]) + (d[7] + d[8]))
    jz = d[2] + ((d[5] - d[6]) + (d[7] - d[8]))
    inv = np.float32(1.0) / rho
    return [jnp.where(fc != fc, np.float32(0.0), j * inv) for j in (jz, jx, jy)]


def edge_speed_kernel(tiles, halves, chain, g, fac, halo, after, ue, send):
    rows = g.shape[1]
    lane, sub = iotas()

    def side(up):
        x = rows - 1 if up else 0
        lo, hi, place = (None, halo, "last") if up else (halo, None, "first")
        for c in range(tiles):
            f = stream(g, lo, hi, x, c, tiles, halves, lane, sub, place)
            for i, v in enumerate(speed(f, fac[x, :, cut(c)])):
                ue[i, :, cut(c)] = v
                if i == 1:
                    send[:, cut(c)] = v

    by_side(chain, side)


def inner_speed_kernel(tiles, halves, g, fac, u):
    rows = g.shape[1]
    lane, sub = iotas()
    for i in range(3):
        u[i, 0] = jnp.zeros(u.shape[2:], F32)
        u[i, rows - 1] = jnp.zeros(u.shape[2:], F32)

    def row(x, _):
        for c in range(tiles):
            f = stream(g, None, None, x, c, tiles, halves, lane, sub, "mid")
            for i, v in enumerate(speed(f, fac[x, :, cut(c)])):
                u[i, x, :, cut(c)] = v
        return 0

    lax.fori_loop(1, rows - 1, row, 0)


def final_kernel(tiles, halves, dirs, passed, aliased, *refs):
    g, fac, halo0, halo1, start = refs[:5]
    blocks = refs[5 : 5 + passed]
    out, *through = refs[6 + passed + aliased : 7 + 2 * passed + aliased]
    buf, sems = refs[7 + 2 * passed + aliased :]
    rows = g.shape[1]
    lane, sub = iotas()
    odd = upper(1)
    for a, b in zip(blocks, through):
        b[...] = a[...]

    def row_of(q, x):
        at = x - DIRS[q][0]
        if at < 0:
            return lambda qq, cc: jnp.where(
                odd, halo0[UP.index(qq), :, cut(cc)], halo1[UP.index(qq), :, cut(cc)]
            )
        if at >= rows:
            return lambda qq, cc: jnp.where(
                odd, halo1[DOWN.index(qq), :, cut(cc)], halo0[DOWN.index(qq), :, cut(cc)]
            )
        return lambda qq, cc: g[qq, at, :, cut(cc)]

    copies = []
    for n, q in enumerate(dirs):
        for c in range(tiles):
            new = []
            for x in range(rows):
                fc = fac[x, :, cut(c)]
                if q == 0:
                    v = g[0, x, :, cut(c)]
                else:
                    v = pull(row_of(q, x), q, c, tiles, halves, lane, sub)
                    v = jnp.where(v != v, g[OPP[q], x, :, cut(c)], v)
                new.append(jnp.where(fc != fc, start[q, x, :, cut(c)], v))
            for i, t in enumerate(swap_tile(new, sub)):
                first = (i * tiles + c) * SUBS
                buf[n, first : first + SUBS, :] = t
        copy = pltpu.make_async_copy(buf.at[n], out.at[q], sems.at[n])
        copy.start()
        copies.append(copy)
    for copy in copies:
        copy.wait()


def slope(p, q):
    return np.float32(0.5) * (
        jnp.maximum(jnp.minimum(p, q), np.float32(0.0)) + jnp.minimum(jnp.maximum(p, q), np.float32(0.0))
    )


def loss(s, c):
    return [np.float32(TRANSFER) * a * (np.float32(1.0) - b) for a, b in zip(s, c)]


def ends_of(parts, strips):
    place = lax.axis_index("wide") * parts + lax.axis_index("narrow")
    return place == 0, place == strips - 1


class Row:
    def __init__(self, tiles, halves):
        self.tiles, self.halves = tiles, halves
        self.lane, self.sub = iotas()

    def read(self, slab):
        return [slab[:, cut(c)] for c in range(self.tiles)]

    def after(self, v):
        out = []
        for c in range(self.tiles):
            if c < self.tiles - 1:
                side = v[c + 1]
            else:
                edge = self.sub % self.halves == self.halves - 1
                side = jnp.where(edge, np.float32(0.0), pltpu.roll(v[0], SUBS - 1, 0))
            out.append(pltpu.roll(jnp.where(self.lane == 0, side, v[c]), LANES - 1, 1))
        return out

    def before(self, v):
        out = []
        for c in range(self.tiles):
            if c > 0:
                side = v[c - 1]
            else:
                edge = self.sub % self.halves == 0
                side = jnp.where(edge, np.float32(0.0), pltpu.roll(v[self.tiles - 1], 1, 0))
            out.append(pltpu.roll(jnp.where(self.lane == LANES - 1, side, v[c]), 1, 1))
        return out

    def above(self, v):
        return [pltpu.roll(t, SUBS - self.halves, 0) for t in v]

    def below(self, v):
        return [pltpu.roll(t, self.halves, 0) for t in v]

    def step(self, r, conc, poro, flow, u, s):
        def each(f, *lists):
            return [f(*t) for t in zip(*lists)]

        def less(a, b):
            return each(lambda x, y: x - y, a, b)

        def times(a, b):
            return each(lambda x, y: x * y, a, b)

        def slopes(a, b):
            return each(slope, a, b)

        def face(w, va, vb, c, cn, sl, sn, dn):
            a = each(lambda w, x, y: w * np.float32(0.5) * (x + y), w, va, vb)
            return each(
                lambda a, w, c, cn, sl, sn, dn: a * jnp.where(a > 0, c + sl, cn - sn)
                - np.float32(DIFFUSION) * w * dn,
                a, w, c, cn, sl, sn, dn,
            )

        cm2, cm1, c, cp1, cp2 = (conc(r + k) for k in (-2, -1, 0, 1, 2))
        pm, p, pn = (poro(r + k) for k in (-1, 0, 1))
        vm, v0, vn = (flow(r + k) for k in (-1, 0, 1))
        d0, d1, d2, d3 = less(cm1, cm2), less(c, cm1), less(cp1, c), less(cp2, cp1)
        sm, s0, sp = slopes(d0, d1), slopes(d1, d2), slopes(d2, d3)
        change = less(
            face(times(pm, p), vm, v0, cm1, c, sm, s0, d1), face(times(p, pn), v0, vn, c, cp1, s0, sp, d2)
        )
        for after, before, vel, open_ends in (
            (self.after, self.before, u[1], True), (self.above, self.below, u[0], False),
        ):
            cn = after(c)
            dn = less(cn, c)
            dm = less(c, before(c)) if open_ends else before(dn)
            s0 = slopes(dm, dn)
            flux = face(times(p, after(p)), vel, after(vel), c, cn, s0, after(s0), dn)
            change = each(lambda t, a, b: t + (a - b), change, before(flux), flux)
        rate = loss(s, c)
        cnew = each(
            lambda c, t, k, p: c + (t + k) / jnp.maximum(p, np.float32(FLOOR)), c, change, rate, p
        )
        return cnew, each(lambda s, k: s - np.float32(DEPLETION) * k, s, rate)


ZERO = np.float32(0.0)


def early_kernel(tiles, halves, ends, slabs, still0, still1, inner_u, ue0, ue1, flags, cs, u):
    rows = u.shape[1]
    row = Row(tiles, halves)
    first, last = ends_of(*ends)
    odd = upper(1)
    for k in range(3):
        for r in range(1, rows - 1):
            u[k, r] = inner_u[k, r]
    merge_rows(u, ue0, ue1, 3)

    def conc(r):
        if r < 0:
            return pick(first, [ZERO] * tiles, pick(odd, row.read(still0.at[5]), row.read(still1.at[5])))
        if r >= rows:
            beyond = pick(odd, row.read(still1.at[5]), row.read(still0.at[5]))
            return pick(last, row.read(slabs.at[0, rows - 1]), beyond)
        return row.read(slabs.at[0, r])

    def poro(r):
        return row.read(slabs.at[2, r])

    def flow(r):
        return row.read(u.at[1, r])

    for r in range(1, rows - 1):
        new = row.step(r, conc, poro, flow, (row.read(u.at[0, r]), row.read(u.at[2, r])), row.read(slabs.at[1, r]))
        for k in range(2):
            for c in range(tiles):
                cs[k, r - 1, :, cut(c)] = new[k][c]


def side_step(row, ends, up, which, conc_at, beyond_c, napl_at, slabs, still, u, flags, beyond_u):
    rows = u.shape[1]
    first, last = ends_of(*ends)

    def conc(r):
        if r < 0:
            return pick(first, [ZERO] * row.tiles, row.read(beyond_c(-1 - r)))
        if r >= rows:
            return pick(last, row.read(conc_at(rows - 1)), row.read(beyond_c(r - rows)))
        return row.read(conc_at(r))

    def poro(r):
        if r < 0:
            return pick(first, row.read(flags.at[0]), row.read(still.at[7]))
        if r >= rows:
            return pick(last, row.read(flags.at[1]), row.read(still.at[7]))
        return row.read(slabs.at[2, r])

    def flow(r):
        if r < 0:
            return pick(first, row.read(u.at[1, 0]), row.read(beyond_u))
        if r >= rows:
            return pick(last, row.read(u.at[1, rows - 1]), row.read(beyond_u))
        return row.read(u.at[1, r])

    return [
        row.step(r, conc, poro, flow, (row.read(u.at[0, r]), row.read(u.at[2, r])), row.read(napl_at(r)))
        for r in which
    ]


def rim_kernel(tiles, halves, ends, chain, slabs, still, u, flags, beyond_u, inner, after, cs, send):
    rows = u.shape[1]
    row = Row(tiles, halves)

    def side(up):
        x = rows - 1 if up else 0
        ((c1, s1),) = side_step(
            row, ends, up, (x,), lambda r: slabs.at[0, r], lambda k: still.at[5 + k], lambda r: slabs.at[1, r],
            slabs, still, u, flags, beyond_u,
        )
        for c in range(tiles):
            cs[0, :, cut(c)] = c1[c]
            cs[1, :, cut(c)] = s1[c]
            send[0, :, cut(c)] = c1[c]
        send[1] = inner[0, rows - 3 if up else 0]

    by_side(chain, side)


def middle_kernel(tiles, halves, slabs, u, inner, rim0, rim1, out):
    rows = u.shape[1]
    row = Row(tiles, halves)
    odd = upper(1)

    def conc(r):
        if r == 0:
            return pick(odd, row.read(rim0.at[0]), row.read(rim1.at[0]))
        if r == rows - 1:
            return pick(odd, row.read(rim1.at[0]), row.read(rim0.at[0]))
        return row.read(inner.at[0, r - 1])

    for r in range(2, rows - 2):
        new = row.step(
            r, conc, lambda r: row.read(slabs.at[2, r]), lambda r: row.read(u.at[1, r]),
            (row.read(u.at[0, r]), row.read(u.at[2, r])), row.read(inner.at[1, r - 1]),
        )
        for c in range(tiles):
            out[r - 2, :, cut(c)] = new[0][c]


def late_kernel(tiles, halves, ends, chain, slabs, still, u, flags, beyond_u, inner, rim, beyond_c, after, out):
    rows = u.shape[1]
    row = Row(tiles, halves)

    def side(up):
        def state(k, r):
            return rim.at[k] if r in (0, rows - 1) else inner.at[k, r - 1]

        new = side_step(
            row, ends, up, (rows - 1, rows - 2) if up else (0, 1), lambda r: state(0, r),
            lambda k: beyond_c.at[k], lambda r: state(1, r), slabs, still, u, flags, beyond_u,
        )
        for i in range(2):
            for c in range(tiles):
                out[i, :, cut(c)] = new[i][0][c]

    by_side(chain, side)


def deal_kernel(tiles, halves, parts, inner, rim0, rim1, late0, late1, mid, *refs):
    *blocks, whole = refs
    rows = inner.shape[1] + 2
    odd = upper(1)
    _, sub = iotas()
    for c in range(tiles):

        def ends_pick(a, b):
            return jnp.where(odd, a, b)

        lo = [ends_pick(late0[i, :, cut(c)], late1[i, :, cut(c)]) for i in range(2)]
        hi = [ends_pick(late1[i, :, cut(c)], late0[i, :, cut(c)]) for i in range(2)]
        conc = lo + [mid[r, :, cut(c)] for r in range(rows - 4)] + hi[::-1]
        left = []
        for r in range(rows):
            if r in (0, rows - 1):
                a, b = (rim0, rim1) if r == 0 else (rim1, rim0)
                cc, ss = (ends_pick(a[k, :, cut(c)], b[k, :, cut(c)]) for k in range(2))
            else:
                cc, ss = (inner[k, r - 1, :, cut(c)] for k in range(2))
            left.append(ss - np.float32(DEPLETION) * loss([ss], [cc])[0])
        run = whole.shape[3]
        for k, tile in enumerate((conc, left)):
            for i, t in enumerate(swap_tile(tile, sub)):
                column = (i % halves * tiles + c) * SUBS
                at = column % run
                whole[column // run, k, i // halves, at : at + SUBS, :] = t
    for k in range(parts):
        blocks[k][...] = whole[lax.axis_index("narrow") ^ k]


def gather_kernel(parts, *refs):
    blocks = refs[:parts]
    *outs, sems = refs[parts:]
    copies = []
    for k in range(parts):
        origin = lax.axis_index("narrow") ^ k
        for i, out in enumerate(outs):
            copies.append(pltpu.make_async_copy(blocks[k].at[i], out.at[:, origin], sems.at[i * parts + k]))
            copies[-1].start()
    for copy in copies:
        copy.wait()


def call(kernel, out_shape, args, scratch=(), hbm=(), free=(), hbm_out=(), name=None, flops=0, aliases=None):
    def spec(i, hbm, free=()):
        return pl.BlockSpec(memory_space=pltpu.HBM if i in hbm else pl.ANY if i in free else pltpu.VMEM)

    single = not isinstance(out_shape, tuple)
    shapes = (out_shape,) if single else out_shape
    out = pl.pallas_call(
        kernel,
        out_shape=shapes,
        in_specs=[spec(i, hbm, free) for i in range(len(args))],
        out_specs=tuple(spec(i, hbm_out) for i in range(len(shapes))),
        scratch_shapes=list(scratch),
        name=name,
        input_output_aliases=aliases or {},
        compiler_params=pltpu.CompilerParams(vmem_limit_bytes=VMEM_LIMIT),
        cost_estimate=pl.CostEstimate(flops=flops, bytes_accessed=flops // 10, transcendentals=0),
    )(*args)
    return out[0] if single else out


def local(populations, phase, porosity, napl, concentration, flags):
    layers, rows, width = phase.shape
    halves = SUBS // layers
    length = width // halves
    tiles = length // LANES
    parts = lax.axis_size("narrow")
    strips = lax.axis_size("wide") * parts
    both = ("wide", "narrow")
    pairs = (
        [(i, i ^ 1) for i in range(strips)],
        [(i, (i + 1 if i % 2 else i - 1) % strips) for i in range(strips)],
    )
    cells = rows * SUBS * length
    slab = (SUBS, length)
    ends = (parts, strips)
    run = width // LANES * SUBS // parts

    def hold(*shape, dtype=F32):
        return pltpu.VMEM(shape, dtype)

    def swap(chain, array):
        return lax.ppermute(array, both, pairs[chain])

    pop = to_view(populations)
    views = [to_view(a) for a in (phase, concentration, napl, porosity)]
    flat = views[0].shape
    given = [pltpu.with_memory_space_constraint(a, pltpu.HBM) for a in (pop, *views, flags)]
    popv, phv, cov, nav, pov, flv, row0, send = call(
        functools.partial(first_kernel, tiles),
        (
            hold(*pop.shape), hold(*flat, dtype=jnp.int32), hold(*flat), hold(*flat), hold(*flat),
            hold(*flags.shape, dtype=jnp.int32), hold(19, *slab), hold(8, *slab),
        ),
        given, scratch=(pltpu.SemaphoreType.DMA((6,)),), hbm=range(6), name="first", flops=50 * cells,
    )
    halo0 = still0 = swap(0, send)
    row1, send = call(
        functools.partial(second_kernel, tiles), (hold(19, *slab), hold(8, *slab)),
        (popv, phv, cov, pov, send), free=(4,), name="second", flops=30 * cells,
    )
    halo1 = still1 = swap(1, send)
    g, fac, start, slabs, open_ends = call(
        functools.partial(first_inner_kernel, tiles, halves),
        (
            hold(19, rows, *slab), hold(rows, *slab), hold(19, rows, *slab), hold(3, rows, *slab),
            hold(2, *slab),
        ),
        (popv, phv, cov, nav, pov, flv, row0, row1), name="first_inner", flops=300 * cells,
    )
    for _ in range(1, LBM_STEPS):
        row0, send = call(
            functools.partial(edge_kernel, tiles, halves, 0), (hold(19, *slab), hold(5, *slab)),
            (g, fac, halo0, send), free=(3,), name="edge0", flops=30 * cells,
        )
        halo0 = swap(0, send)
        row1, send = call(
            functools.partial(edge_kernel, tiles, halves, 1), (hold(19, *slab), hold(5, *slab)),
            (g, fac, halo1, send), free=(3,), name="edge1", flops=30 * cells,
        )
        halo1 = swap(1, send)
        g = call(
            functools.partial(inner_kernel, tiles, halves), hold(19, rows, *slab),
            (g, row0, row1, fac), name="inner", flops=250 * cells,
        )
    inner_u = call(
        functools.partial(inner_speed_kernel, tiles, halves), hold(3, rows, *slab), (g, fac),
        name="inner_speed", flops=100 * cells,
    )
    ue0, send = call(
        functools.partial(edge_speed_kernel, tiles, halves, 0), (hold(3, *slab), hold(*slab)),
        (g, fac, halo0, inner_u), free=(3,), name="edge_speed0", flops=20 * cells,
    )
    far0 = swap(0, send)
    ue1, send = call(
        functools.partial(edge_speed_kernel, tiles, halves, 1), (hold(3, *slab), hold(*slab)),
        (g, fac, halo1, send), free=(3,), name="edge_speed1", flops=20 * cells,
    )
    far1 = swap(1, send)
    inner, u = call(
        functools.partial(early_kernel, tiles, halves, ends),
        (hold(2, rows - 2, *slab), hold(3, rows, *slab)),
        (slabs, still0, still1, inner_u, ue0, ue1, open_ends), name="early", flops=100 * cells,
    )
    rim0, send = call(
        functools.partial(rim_kernel, tiles, halves, ends, 0), (hold(2, *slab), hold(2, *slab)),
        (slabs, still0, u, open_ends, far0, inner, send), free=(6,), name="rim0", flops=20 * cells,
    )
    next0 = swap(0, send)
    rim1, send = call(
        functools.partial(rim_kernel, tiles, halves, ends, 1), (hold(2, *slab), hold(2, *slab)),
        (slabs, still1, u, open_ends, far1, inner, send), free=(6,), name="rim1", flops=20 * cells,
    )
    next1 = swap(1, send)
    mid = call(
        functools.partial(middle_kernel, tiles, halves), hold(rows - 4, *slab),
        (slabs, u, inner, rim0, rim1), name="middle", flops=60 * cells,
    )
    late0 = call(
        functools.partial(late_kernel, tiles, halves, ends, 0), hold(2, *slab),
        (slabs, still0, u, open_ends, far0, inner, rim0, next0, mid), free=(8,), name="late0", flops=30 * cells,
    )
    late1 = call(
        functools.partial(late_kernel, tiles, halves, ends, 1), hold(2, *slab),
        (slabs, still1, u, open_ends, far1, inner, rim1, next1, late0), free=(8,), name="late1", flops=30 * cells,
    )
    block = (2, layers, run, LANES)
    blocks = call(
        functools.partial(deal_kernel, tiles, halves, parts), tuple(hold(*block) for _ in range(parts)),
        (inner, rim0, rim1, late0, late1, mid),
        scratch=(pltpu.VMEM((parts, *block), F32),), name="deal", flops=20 * cells,
    )
    blocks = list(blocks)

    def send_blocks(ks):
        for k in ks:
            blocks[k] = lax.ppermute(blocks[k], "narrow", [(i, i ^ k) for i in range(parts)])

    groups = [[int(k) for k in ks] for ks in np.array_split(np.arange(parts - 1, 0, -1), 3)]
    send_blocks(groups[0])
    out = None
    for ks, dirs in ((groups[1], range(0, 10)), (groups[2], range(10, 19))):
        args = [g, fac, halo0, halo1, start, *(blocks[k] for k in ks), blocks[0]]
        n = len(args)
        if out is not None:
            args.append(out)
        out, *passed = call(
            functools.partial(final_kernel, tiles, halves, dirs, len(ks), int(out is not None)),
            (jax.ShapeDtypeStruct((19, *flat), F32), *(hold(*block) for _ in ks)),
            args,
            scratch=(pltpu.VMEM((len(dirs), *flat), F32), pltpu.SemaphoreType.DMA((len(dirs),))),
            hbm=(n,), free=(n - 1,), hbm_out=(0,), name="final", flops=200 * cells,
            aliases={n: 0} if out is not None else None,
        )
        for k, b in zip(ks, passed):
            blocks[k] = b
        send_blocks(ks)
    tile = (layers, parts, run, LANES)
    conc_out, napl_out = call(
        functools.partial(gather_kernel, parts),
        (jax.ShapeDtypeStruct(tile, F32), jax.ShapeDtypeStruct(tile, F32)),
        blocks, scratch=(pltpu.SemaphoreType.DMA((2 * parts,)),), hbm_out=(0, 1), name="gather", flops=10 * cells,
    )
    shape = (layers, rows * parts, width // parts)

    def tile_of(a):
        return from_view(a.reshape(layers * parts * run, LANES), shape)

    return from_view(out, populations.shape), tile_of(conc_out), tile_of(napl_out)


def solution(mesh):
    strip = P(None, ("wide", "narrow"), None)
    in_specs = (P(None, None, ("wide", "narrow"), None), strip, strip, strip, strip, P())
    tile = P(None, "wide", "narrow")
    out_specs = (P(None, None, ("wide", "narrow"), None), tile, tile)
    return jax.shard_map(local, mesh=mesh, in_specs=in_specs, out_specs=out_specs, check_vma=False)
```

time: 64.5 us -> 65.9 us (1.022)
  waiting for transfers between devices: 5.2 us -> 23.7 us
  starting transfers between devices: 42.8 us -> 25.6 us
    ppermute x18 -> x15, waiting for transfers between devices: 5.2 us -> 23.7 us  [the longest x12 20.7 us: swap(): return lax.ppermute(array, both, pairs[chain])]
    ppermute x18 -> x15, starting transfers between devices: 42.8 us -> 25.6 us  [the longest x12 21.1 us: swap(): return lax.ppermute(array, both, pairs[chain])]
    pallas_call x17 -> x25, Pallas kernels: 15.4 us -> 15.6 us  [call(): pl.pallas_call(kernel, out_shape=shapes, in_specs=[spec(i, hbm, free) for...]
  transfers between devices with their start and end apart: 18 -> 15, of which waited for: 9 -> 7; matrix products, arithmetic and copies ran while one was open for 0% -> 0% of each run, Pallas kernels for 17% -> 19%
where the time goes in v1:
time: 65.9 us; the launch traced here: 65.7 us
  starting transfers between devices  25.6 us (39%)
  waiting for transfers between devices  23.7 us (36%)
  Pallas kernels  15.6 us (24%)
  between operations  0.91 us (1%)
    ppermute x12, starting transfers between devices, swap(): return lax.ppermute(array, both, pairs[chain])  21.1 us
    ppermute x12, waiting for transfers between devices, swap(): return lax.ppermute(array, both, pairs[chain])  20.7 us
    pallas_call x25, Pallas kernels, call(): pl.pallas_call(kernel, out_shape=shapes, in_specs=[spec(i, hbm, free) for...  15.6 us
    ppermute x3, starting transfers between devices, send_blocks(): lax.ppermute(blocks[k], 'narrow', [(i, i ^ k) for i in range(parts)])  4.5 us
    ppermute x3, waiting for transfers between devices, send_blocks(): lax.ppermute(blocks[k], 'narrow', [(i, i ^ k) for i in range(parts)])  2.94 us
  transfers between devices with their start and end apart: 15, of which 7 were waited for; matrix products, arithmetic and copies ran while one was open for 0% of the time, Pallas kernels for 19%

profile of v1, /device:TPU:0, one launch (start us, length us, event | category | flops | bytes accessed | tf_op | source)
XLA Modules:
  0.0 65.7 jit_solution(9377380761088071429)
XLA Ops:
  0.6 2.3 %first.1 = (f32[19,256,128]{2,1,0:T(8,128)S(1)}, s32[256,128]{1,0:T(8,128)S(1)}, f32[256,128]{1,0:T(8,128)S(1)}, f32[256,128]{1,0:T(8,128)S(1)}, f32[256,128]{1,...) custom-call(f32[19,256,128]{2,1,0:T(8,128)} %bitcast.40, ...), custom_call_target="tpu_custom_call" | custom-call | flops 1638400 | bytes 163840 | tf_op jit(solution)/shard_map/first/pallas_call | solution.py:643
  2.9 3.1 %collective-permute-start = (f32[8,8,512]{2,1,0:T(8,128)S(1)}, f32[8,8,512]{2,1,0:T(8,128)S(1)}, u32[]{:S(2)}, u32[]{:S(2)}) collective-permute-start(f32[8,8,512]{2,1,0:T(8,128)S(1)} %get-tuple-element.57.after), channel_id=1, source_target_pairs={{0,1},{1,0},{2,3},{3,2},{4,5},{5,4},{6,7},{7,6},{8,9},{9,8},{10,11... | collective-permute-start | bytes 393224 | tf_op jit(solution)/shard_map/ppermute | solution.py:678
  6.4 3.6 %collective-permute-start.1 = (f32[8,8,512]{2,1,0:T(8,128)S(1)}, f32[8,8,512]{2,1,0:T(8,128)S(1)}, u32[]{:S(2)}, u32[]{:S(2)}) collective-permute-start(f32[8,8,512]{2,1,0:T(8,128)S(1)} %get-tuple-element.61.after), channel_id=1, source_target_pairs={{0,31},{1,2},{2,1},{3,4},{4,3},{5,6},{6,5},{7,8},{8,7},{9,10},{10,... | collective-permute-start | bytes 393224 | tf_op jit(solution)/shard_map/ppermute | solution.py:678
  10.0 1.5 %first_inner.1 = (f32[19,8,8,512]{3,2,1,0:T(8,128)S(1)}, f32[8,8,512]{2,1,0:T(8,128)S(1)}, f32[19,8,8,512]{3,2,1,0:T(8,128)S(1)}, f32[3,8,8,512]{3,2,1,0:T(8,128)S(1)}, f32[2,8,512]{2,1,0:T(8,128)S(1)}) custom-call(f32[19,256,128]{2,1,0:T(8,128)S(1)} %get-tuple-element.50.pop, s32[256,128]{1,0:T(8,128)S(1)} %get-tuple-element.51.phase, ...), custom_call_target="tpu_custom_call" | custom-call | flops 9830400 | bytes 983040 | tf_op jit(solution)/shard_map/first_inner/pallas_call | solution.py:643
  11.8 4.3 %collective-permute-done.1.halo.still1.still = f32[8,8,512]{2,1,0:T(8,128)S(1)} collective-permute-done((f32[8,8,512]{2,1,0:T(8,128)S(1)}, f32[8,8,512]{2,1,0:T(8,128)S(1)}, u32[]{:S(2)}, u32[]{:S(2)}) %collective-permute-start.1) | collective-permute-done | bytes 131104 | tf_op jit(solution)/shard_map/ppermute | solution.py:678
  16.3 3.0 %collective-permute-start.3 = (f32[5,8,512]{2,1,0:T(8,128)S(1)}, f32[5,8,512]{2,1,0:T(8,128)S(1)}, u32[]{:S(2)}, u32[]{:S(2)}) collective-permute-start(f32[5,8,512]{2,1,0:T(8,128)S(1)} %get-tuple-element.65.after), channel_id=1, source_target_pairs={{0,31},{1,2},{2,1},{3,4},{4,3},{5,6},{6,5},{7,8},{8,7},{9,10},{10,... | collective-permute-start | bytes 245768 | tf_op jit(solution)/shard_map/ppermute | solution.py:678
  19.3 1.3 %inner.3.g = f32[19,8,8,512]{3,2,1,0:T(8,128)S(1)} custom-call(f32[19,8,8,512]{3,2,1,0:T(8,128)S(1)} %get-tuple-element.59.g, f32[19,8,512]{2,1,0:T(8,128)S(1)} %get-tuple-element.62.row0, f32[19,8,512]{2,1,0:T(8,128)S(1)} %get-tuple-element.64.row1, f32[8,8,512]{2,1,0:T(8,128)S(1)} %get-tuple-element.60.fac.refs_1_), custom_call_target="tpu_custom_call" | custom-call | flops 8192000 | bytes 819200 | tf_op jit(solution)/shard_map/inner/pallas_call | solution.py:643
  20.9 3.1 %collective-permute-done.3.halo = f32[5,8,512]{2,1,0:T(8,128)S(1)} collective-permute-done((f32[5,8,512]{2,1,0:T(8,128)S(1)}, f32[5,8,512]{2,1,0:T(8,128)S(1)}, u32[]{:S(2)}, u32[]{:S(2)}) %collective-permute-start.3) | collective-permute-done | bytes 81952 | tf_op jit(solution)/shard_map/ppermute | solution.py:678
  24.1 3.0 %collective-permute-start.5 = (f32[5,8,512]{2,1,0:T(8,128)S(1)}, f32[5,8,512]{2,1,0:T(8,128)S(1)}, u32[]{:S(2)}, u32[]{:S(2)}) collective-permute-start(f32[5,8,512]{2,1,0:T(8,128)S(1)} %get-tuple-element.69.after), channel_id=1, source_target_pairs={{0,31},{1,2},{2,1},{3,4},{4,3},{5,6},{6,5},{7,8},{8,7},{9,10},{10,... | collective-permute-start | bytes 245768 | tf_op jit(solution)/shard_map/ppermute | solution.py:678
  27.1 1.3 %inner.4.g = f32[19,8,8,512]{3,2,1,0:T(8,128)S(1)} custom-call(f32[19,8,8,512]{3,2,1,0:T(8,128)S(1)} %inner.3.g, f32[19,8,512]{2,1,0:T(8,128)S(1)} %get-tuple-element.66.row0, f32[19,8,512]{2,1,0:T(8,128)S(1)} %get-tuple-element.68.row1, f32[8,8,512]{2,1,0:T(8,128)S(1)} %get-tuple-element.60.fac.refs_1_), custom_call_target="tpu_custom_call" | custom-call | flops 8192000 | bytes 819200 | tf_op jit(solution)/shard_map/inner/pallas_call | solution.py:643
  28.7 3.7 %collective-permute-done.5.halo = f32[5,8,512]{2,1,0:T(8,128)S(1)} collective-permute-done((f32[5,8,512]{2,1,0:T(8,128)S(1)}, f32[5,8,512]{2,1,0:T(8,128)S(1)}, u32[]{:S(2)}, u32[]{:S(2)}) %collective-permute-start.5) | collective-permute-done | bytes 81952 | tf_op jit(solution)/shard_map/ppermute | solution.py:678
  32.6 2.6 %collective-permute-start.7 = (f32[5,8,512]{2,1,0:T(8,128)S(1)}, f32[5,8,512]{2,1,0:T(8,128)S(1)}, u32[]{:S(2)}, u32[]{:S(2)}) collective-permute-start(f32[5,8,512]{2,1,0:T(8,128)S(1)} %get-tuple-element.73), channel_id=1, source_target_pairs={{0,31},{1,2},{2,1},{3,4},{4,3},{5,6},{6,5},{7,8},{8,7},{9,10},{10,... | collective-permute-start | bytes 245768 | tf_op jit(solution)/shard_map/ppermute | solution.py:678
  35.2 1.3 %inner.5.g.refs_0_ = f32[19,8,8,512]{3,2,1,0:T(8,128)S(1)} custom-call(f32[19,8,8,512]{3,2,1,0:T(8,128)S(1)} %inner.4.g, f32[19,8,512]{2,1,0:T(8,128)S(1)} %get-tuple-element.70.row0, f32[19,8,512]{2,1,0:T(8,128)S(1)} %get-tuple-element.72.row1, f32[8,8,512]{2,1,0:T(8,128)S(1)} %get-tuple-element.60.fac.refs_1_), custom_call_target="tpu_custom_call" | custom-call | flops 8192000 | bytes 819200 | tf_op jit(solution)/shard_map/inner/pallas_call | solution.py:643
  36.5 0.8 %inner_speed.1.after.inner_u = f32[3,8,8,512]{3,2,1,0:T(8,128)S(1)} custom-call(f32[19,8,8,512]{3,2,1,0:T(8,128)S(1)} %inner.5.g.refs_0_, f32[8,8,512]{2,1,0:T(8,128)S(1)} %get-tuple-element.60.fac.refs_1_), custom_call_target="tpu_custom_call" | custom-call | flops 3276800 | bytes 327680 | tf_op jit(solution)/shard_map/inner_speed/pallas_call | solution.py:643
  37.5 2.7 %collective-permute-done.7.halo.refs_3_ = f32[5,8,512]{2,1,0:T(8,128)S(1)} collective-permute-done((f32[5,8,512]{2,1,0:T(8,128)S(1)}, f32[5,8,512]{2,1,0:T(8,128)S(1)}, u32[]{:S(2)}, u32[]{:S(2)}) %collective-permute-start.7) | collective-permute-done | bytes 81952 | tf_op jit(solution)/shard_map/ppermute | solution.py:678
  40.4 2.7 %collective-permute-start.9 = (f32[8,512]{1,0:T(8,128)S(1)}, f32[8,512]{1,0:T(8,128)S(1)}, u32[]{:S(2)}, u32[]{:S(2)}) collective-permute-start(f32[8,512]{1,0:T(8,128)S(1)} %get-tuple-element.82.after), channel_id=1, source_target_pairs={{0,31},{1,2},{2,1},{3,4},{4,3},{5,6},{6,5},{7,8},{8,7},{9,10},{10,... | collective-permute-start | bytes 49160 | tf_op jit(solution)/shard_map/ppermute | solution.py:678
  43.9 3.4 %collective-permute-done.9.beyond_u = f32[8,512]{1,0:T(8,128)S(1)} collective-permute-done((f32[8,512]{1,0:T(8,128)S(1)}, f32[8,512]{1,0:T(8,128)S(1)}, u32[]{:S(2)}, u32[]{:S(2)}) %collective-permute-start.9) | collective-permute-done | bytes 16416 | tf_op jit(solution)/shard_map/ppermute | solution.py:678
  47.5 2.8 %collective-permute-start.11 = (f32[2,8,512]{2,1,0:T(8,128)S(1)}, f32[2,8,512]{2,1,0:T(8,128)S(1)}, u32[]{:S(2)}, u32[]{:S(2)}) collective-permute-start(f32[2,8,512]{2,1,0:T(8,128)S(1)} %get-tuple-element.86), channel_id=1, source_target_pairs={{0,31},{1,2},{2,1},{3,4},{4,3},{5,6},{6,5},{7,8},{8,7},{9,10},{10,... | collective-permute-start | bytes 98312 | tf_op jit(solution)/shard_map/ppermute | solution.py:678
  50.9 3.6 %collective-permute-done.11.beyond_c = f32[2,8,512]{2,1,0:T(8,128)S(1)} collective-permute-done((f32[2,8,512]{2,1,0:T(8,128)S(1)}, f32[2,8,512]{2,1,0:T(8,128)S(1)}, u32[]{:S(2)}, u32[]{:S(2)}) %collective-permute-start.11) | collective-permute-done | bytes 32800 | tf_op jit(solution)/shard_map/ppermute | solution.py:678
  54.9 1.3 %final.2 = (f32[19,256,128]{2,1,0:T(8,128)}, f32[2,4,16,128]{3,2,1,0:T(8,128)S(1)}) custom-call(f32[19,8,8,512]{3,2,1,0:T(8,128)S(1)} %inner.5.g.refs_0_, f32[8,8,512]{2,1,0:T(8,128)S(1)} %get-tuple-element.60.fac.refs_1_, f32[5,8,512]{2,1,0:T(8,128)S(1)} %collective-permute-done.6.halo.refs_2_, f32[5,8,512]{2,1,0:T(8,128)S(1)} %collective-permute-done.7.halo.refs_3_, ...), custom_call_target="tpu_custom_call" | custom-call | flops 6553600 | bytes 655360 | tf_op jit(solution)/shard_map/final/pallas_call | solution.py:643
  56.2 1.4 %final.3 = (f32[19,256,128]{2,1,0:T(8,128)}, f32[2,4,16,128]{3,2,1,0:T(8,128)S(1)}) custom-call(f32[19,8,8,512]{3,2,1,0:T(8,128)S(1)} %inner.5.g.refs_0_, f32[8,8,512]{2,1,0:T(8,128)S(1)} %get-tuple-element.60.fac.refs_1_, f32[5,8,512]{2,1,0:T(8,128)S(1)} %collective-permute-done.6.halo.refs_2_, ...), custom_call_target="tpu_custom_call", output_to_operand_aliasing={{0}: (7, {})} | custom-call | flops 6553600 | bytes 655360 | tf_op jit(solution)/shard_map/final/pallas_call | solution.py:643
  57.7 4.4 %collective-permute-start.13 = (f32[2,4,16,128]{3,2,1,0:T(8,128)S(1)}, f32[2,4,16,128]{3,2,1,0:T(8,128)S(1)}, u32[]{:S(2)}, u32[]{:S(2)}) collective-permute-start(f32[2,4,16,128]{3,2,1,0:T(8,128)S(1)} %get-tuple-element.93), channel_id=1, source_target_pairs={{0,2},{1,3},{2,0},{3,1},{4,6},{5,7},{6,4},{7,5},{8,10},{9,11},{10,... | collective-permute-start | bytes 196616 | tf_op jit(solution)/shard_map/ppermute | solution.py:772
  62.0 2.9 %collective-permute-done.13.refs_2_ = f32[2,4,16,128]{3,2,1,0:T(8,128)S(1)} collective-permute-done((f32[2,4,16,128]{3,2,1,0:T(8,128)S(1)}, f32[2,4,16,128]{3,2,1,0:T(8,128)S(1)}, u32[]{:S(2)}, u32[]{:S(2)}) %collective-permute-start.13) | collective-permute-done | bytes 65568 | tf_op jit(solution)/shard_map/ppermute | solution.py:772
  65.0 0.8 %gather.1 = (f32[4,4,16,128]{3,2,1,0:T(8,128)}, f32[4,4,16,128]{3,2,1,0:T(8,128)}) custom-call(f32[2,4,16,128]{3,2,1,0:T(8,128)S(1)} %get-tuple-element.88.refs_6_.refs_0_, f32[2,4,16,128]{3,2,1,0:T(8,128)S(1)} %collective-permute-done.12.refs_1_, f32[2,4,16,128]{3,2,1,0:T(8,128)S(1)} %collective-permute-done.13.refs_2_, ...), custom_call_target="tpu_custom_call" | custom-call | flops 327680 | bytes 32768 | tf_op jit(solution)/shard_map/gather/pallas_call | solution.py:643
  (31 shorter events, 4.4 us)
Async XLA Ops:
  2.9 8.6 %collective-permute-start = (f32[8,8,512]{2,1,0:T(8,128)S(1)}, f32[8,8,512]{2,1,0:T(8,128)S(1)}, u32[]{:S(2)}, u32[]{:S(2)}) collective-permute-start(f32[8,8,512]{2,1,0:T(8,128)S(1)} %get-tuple-element.57.after), channel_id=1, source_target_pairs={{0,1},{1,0},{2,3},{3,2},{4,5},{5,4},{6,7},{7,6},{8,9},{9,8},{10,11... | collective-permute-start | bytes 393224 | tf_op jit(solution)/shard_map/ppermute | solution.py:678
  6.4 9.7 %collective-permute-start.1 = (f32[8,8,512]{2,1,0:T(8,128)S(1)}, f32[8,8,512]{2,1,0:T(8,128)S(1)}, u32[]{:S(2)}, u32[]{:S(2)}) collective-permute-start(f32[8,8,512]{2,1,0:T(8,128)S(1)} %get-tuple-element.61.after), channel_id=1, source_target_pairs={{0,31},{1,2},{2,1},{3,4},{4,3},{5,6},{6,5},{7,8},{8,7},{9,10},{10,... | collective-permute-start | bytes 393224 | tf_op jit(solution)/shard_map/ppermute | solution.py:678
  11.7 8.8 %collective-permute-start.2 = (f32[5,8,512]{2,1,0:T(8,128)S(1)}, f32[5,8,512]{2,1,0:T(8,128)S(1)}, u32[]{:S(2)}, u32[]{:S(2)}) collective-permute-start(f32[5,8,512]{2,1,0:T(8,128)S(1)} %get-tuple-element.63.after), channel_id=1, source_target_pairs={{0,1},{1,0},{2,3},{3,2},{4,5},{5,4},{6,7},{7,6},{8,9},{9,8},{10,11... | collective-permute-start | bytes 245768 | tf_op jit(solution)/shard_map/ppermute | solution.py:678
  16.3 7.6 %collective-permute-start.3 = (f32[5,8,512]{2,1,0:T(8,128)S(1)}, f32[5,8,512]{2,1,0:T(8,128)S(1)}, u32[]{:S(2)}, u32[]{:S(2)}) collective-permute-start(f32[5,8,512]{2,1,0:T(8,128)S(1)} %get-tuple-element.65.after), channel_id=1, source_target_pairs={{0,31},{1,2},{2,1},{3,4},{4,3},{5,6},{6,5},{7,8},{8,7},{9,10},{10,... | collective-permute-start | bytes 245768 | tf_op jit(solution)/shard_map/ppermute | solution.py:678
  20.8 7.6 %collective-permute-start.4 = (f32[5,8,512]{2,1,0:T(8,128)S(1)}, f32[5,8,512]{2,1,0:T(8,128)S(1)}, u32[]{:S(2)}, u32[]{:S(2)}) collective-permute-start(f32[5,8,512]{2,1,0:T(8,128)S(1)} %get-tuple-element.67.after), channel_id=1, source_target_pairs={{0,1},{1,0},{2,3},{3,2},{4,5},{5,4},{6,7},{7,6},{8,9},{9,8},{10,11... | collective-permute-start | bytes 245768 | tf_op jit(solution)/shard_map/ppermute | solution.py:678
  24.1 8.3 %collective-permute-start.5 = (f32[5,8,512]{2,1,0:T(8,128)S(1)}, f32[5,8,512]{2,1,0:T(8,128)S(1)}, u32[]{:S(2)}, u32[]{:S(2)}) collective-permute-start(f32[5,8,512]{2,1,0:T(8,128)S(1)} %get-tuple-element.69.after), channel_id=1, source_target_pairs={{0,31},{1,2},{2,1},{3,4},{4,3},{5,6},{6,5},{7,8},{8,7},{9,10},{10,... | collective-permute-start | bytes 245768 | tf_op jit(solution)/shard_map/ppermute | solution.py:678
  28.6 8.6 %collective-permute-start.6 = (f32[5,8,512]{2,1,0:T(8,128)S(1)}, f32[5,8,512]{2,1,0:T(8,128)S(1)}, u32[]{:S(2)}, u32[]{:S(2)}) collective-permute-start(f32[5,8,512]{2,1,0:T(8,128)S(1)} %get-tuple-element.71.after), channel_id=1, source_target_pairs={{0,1},{1,0},{2,3},{3,2},{4,5},{5,4},{6,7},{7,6},{8,9},{9,8},{10,11... | collective-permute-start | bytes 245768 | tf_op jit(solution)/shard_map/ppermute | solution.py:678
  32.6 7.6 %collective-permute-start.7 = (f32[5,8,512]{2,1,0:T(8,128)S(1)}, f32[5,8,512]{2,1,0:T(8,128)S(1)}, u32[]{:S(2)}, u32[]{:S(2)}) collective-permute-start(f32[5,8,512]{2,1,0:T(8,128)S(1)} %get-tuple-element.73), channel_id=1, source_target_pairs={{0,31},{1,2},{2,1},{3,4},{4,3},{5,6},{6,5},{7,8},{8,7},{9,10},{10,... | collective-permute-start | bytes 245768 | tf_op jit(solution)/shard_map/ppermute | solution.py:678
  37.4 6.1 %collective-permute-start.8 = (f32[8,512]{1,0:T(8,128)S(1)}, f32[8,512]{1,0:T(8,128)S(1)}, u32[]{:S(2)}, u32[]{:S(2)}) collective-permute-start(f32[8,512]{1,0:T(8,128)S(1)} %get-tuple-element.77.after), channel_id=1, source_target_pairs={{0,1},{1,0},{2,3},{3,2},{4,5},{5,4},{6,7},{7,6},{8,9},{9,8},{10,11... | collective-permute-start | bytes 49160 | tf_op jit(solution)/shard_map/ppermute | solution.py:678
  40.4 6.9 %collective-permute-start.9 = (f32[8,512]{1,0:T(8,128)S(1)}, f32[8,512]{1,0:T(8,128)S(1)}, u32[]{:S(2)}, u32[]{:S(2)}) collective-permute-start(f32[8,512]{1,0:T(8,128)S(1)} %get-tuple-element.82.after), channel_id=1, source_target_pairs={{0,31},{1,2},{2,1},{3,4},{4,3},{5,6},{6,5},{7,8},{8,7},{9,10},{10,... | collective-permute-start | bytes 49160 | tf_op jit(solution)/shard_map/ppermute | solution.py:678
  43.8 6.8 %collective-permute-start.10 = (f32[2,8,512]{2,1,0:T(8,128)S(1)}, f32[2,8,512]{2,1,0:T(8,128)S(1)}, u32[]{:S(2)}, u32[]{:S(2)}) collective-permute-start(f32[2,8,512]{2,1,0:T(8,128)S(1)} %get-tuple-element.84.after), channel_id=1, source_target_pairs={{0,1},{1,0},{2,3},{3,2},{4,5},{5,4},{6,7},{7,6},{8,9},{9,8},{10,11... | collective-permute-start | bytes 98312 | tf_op jit(solution)/shard_map/ppermute | solution.py:678
  47.5 7.0 %collective-permute-start.11 = (f32[2,8,512]{2,1,0:T(8,128)S(1)}, f32[2,8,512]{2,1,0:T(8,128)S(1)}, u32[]{:S(2)}, u32[]{:S(2)}) collective-permute-start(f32[2,8,512]{2,1,0:T(8,128)S(1)} %get-tuple-element.86), channel_id=1, source_target_pairs={{0,31},{1,2},{2,1},{3,4},{4,3},{5,6},{6,5},{7,8},{8,7},{9,10},{10,... | collective-permute-start | bytes 98312 | tf_op jit(solution)/shard_map/ppermute | solution.py:678
  54.8 7.2 %collective-permute-start.14 = (f32[2,4,16,128]{3,2,1,0:T(8,128)S(1)}, f32[2,4,16,128]{3,2,1,0:T(8,128)S(1)}, u32[]{:S(2)}, u32[]{:S(2)}) collective-permute-start(f32[2,4,16,128]{3,2,1,0:T(8,128)S(1)} %get-tuple-element.94), channel_id=1, source_target_pairs={{0,3},{1,2},{2,1},{3,0},{4,7},{5,6},{6,5},{7,4},{8,11},{9,10},{10,... | collective-permute-start | bytes 196616 | tf_op jit(solution)/shard_map/ppermute | solution.py:772
  57.6 4.4 %collective-permute-start.12 = (f32[2,4,16,128]{3,2,1,0:T(8,128)S(1)}, f32[2,4,16,128]{3,2,1,0:T(8,128)S(1)}, u32[]{:S(2)}, u32[]{:S(2)}) collective-permute-start(f32[2,4,16,128]{3,2,1,0:T(8,128)S(1)} %get-tuple-element.92), channel_id=1, source_target_pairs={{0,1},{1,0},{2,3},{3,2},{4,5},{5,4},{6,7},{7,6},{8,9},{9,8},{10,11... | collective-permute-start | bytes 196616 | tf_op jit(solution)/shard_map/ppermute | solution.py:772
  57.7 7.3 %collective-permute-start.13 = (f32[2,4,16,128]{3,2,1,0:T(8,128)S(1)}, f32[2,4,16,128]{3,2,1,0:T(8,128)S(1)}, u32[]{:S(2)}, u32[]{:S(2)}) collective-permute-start(f32[2,4,16,128]{3,2,1,0:T(8,128)S(1)} %get-tuple-element.93), channel_id=1, source_target_pairs={{0,2},{1,3},{2,0},{3,1},{4,6},{5,7},{6,4},{7,5},{8,10},{9,11},{10,... | collective-permute-start | bytes 196616 | tf_op jit(solution)/shard_map/ppermute | solution.py:772

commit v2 on v1

--- a/solution.py
+++ b/solution.py
@@ -291,50 +291,24 @@
     return [jnp.where(fc != fc, np.float32(0.0), j * inv) for j in (jz, jx, jy)]
 
 
-def edge_speed_kernel(tiles, halves, chain, g, fac, halo, after, ue, send):
-    rows = g.shape[1]
-    lane, sub = iotas()
-
-    def side(up):
-        x = rows - 1 if up else 0
-        lo, hi, place = (None, halo, "last") if up else (halo, None, "first")
-        for c in range(tiles):
-            f = stream(g, lo, hi, x, c, tiles, halves, lane, sub, place)
-            for i, v in enumerate(speed(f, fac[x, :, cut(c)])):
-                ue[i, :, cut(c)] = v
-                if i == 1:
-                    send[:, cut(c)] = v
-
-    by_side(chain, side)
-
-
 def inner_speed_kernel(tiles, halves, g, fac, u):
     rows = g.shape[1]
     lane, sub = iotas()
-    for i in range(3):
-        u[i, 0] = jnp.zeros(u.shape[2:], F32)
-        u[i, rows - 1] = jnp.zeros(u.shape[2:], F32)
 
     def row(x, _):
         for c in range(tiles):
             f = stream(g, None, None, x, c, tiles, halves, lane, sub, "mid")
             for i, v in enumerate(speed(f, fac[x, :, cut(c)])):
-                u[i, x, :, cut(c)] = v
+                u[i, x - 1, :, cut(c)] = v
         return 0
 
     lax.fori_loop(1, rows - 1, row, 0)
 
 
-def final_kernel(tiles, halves, dirs, passed, aliased, *refs):
-    g, fac, halo0, halo1, start = refs[:5]
-    blocks = refs[5 : 5 + passed]
-    out, *through = refs[6 + passed + aliased : 7 + 2 * passed + aliased]
-    buf, sems = refs[7 + 2 * passed + aliased :]
+def final_kernel(tiles, halves, g, fac, halo0, halo1, start, after, out, buf, sems):
     rows = g.shape[1]
     lane, sub = iotas()
     odd = upper(1)
-    for a, b in zip(blocks, through):
-        b[...] = a[...]
 
     def row_of(q, x):
         at = x - DIRS[q][0]
@@ -349,7 +323,7 @@
         return lambda qq, cc: g[qq, at, :, cut(cc)]
 
     copies = []
-    for n, q in enumerate(dirs):
+    for q in range(19):
         for c in range(tiles):
             new = []
             for x in range(rows):
@@ -362,8 +336,8 @@
                 new.append(jnp.where(fc != fc, start[q, x, :, cut(c)], v))
             for i, t in enumerate(swap_tile(new, sub)):
                 first = (i * tiles + c) * SUBS
-                buf[n, first : first + SUBS, :] = t
-        copy = pltpu.make_async_copy(buf.at[n], out.at[q], sems.at[n])
+                buf[q, first : first + SUBS, :] = t
+        copy = pltpu.make_async_copy(buf.at[q], out.at[q], sems.at[q])
         copy.start()
         copies.append(copy)
     for copy in copies:
@@ -385,13 +359,52 @@
     return place == 0, place == strips - 1
 
 
-class Row:
-    def __init__(self, tiles, halves):
+ZERO = np.float32(0.0)
+
+
+def each(f, *lists):
+    return [f(*t) for t in zip(*lists)]
+
+
+def less(a, b):
+    return each(lambda x, y: x - y, a, b)
+
+
+def times(a, b):
+    return each(lambda x, y: x * y, a, b)
+
+
+def face(w, va, vb, c, cn, sl, sn, dn):
+    a = each(lambda w, x, y: w * np.float32(0.5) * (x + y), w, va, vb)
+    return each(
+        lambda a, w, c, cn, sl, sn, dn: a * jnp.where(a > 0, c + sl, cn - sn) - np.float32(DIFFUSION) * w * dn,
+        a, w, c, cn, sl, sn, dn,
+    )
+
+
+def floored(p):
+    return [jnp.maximum(t, np.float32(FLOOR)) for t in p]
+
+
+class Step:
+    def __init__(self, tiles, halves, conc, poro, flow, cross, napl):
         self.tiles, self.halves = tiles, halves
         self.lane, self.sub = iotas()
-
-    def read(self, slab):
-        return [slab[:, cut(c)] for c in range(self.tiles)]
+        self.conc, self.poro, self.flow = (self.keep(f) for f in (conc, poro, flow))
+        self.cross, self.napl = cross, napl
+        self.gap = self.keep(lambda r: less(self.conc(r + 1), self.conc(r)))
+        self.lean = self.keep(lambda r: each(slope, self.gap(r - 1), self.gap(r)))
+
+    @staticmethod
+    def keep(f):
+        seen = {}
+
+        def get(r):
+            if r not in seen:
+                seen[r] = f(r)
+            return seen[r]
+
+        return get
 
     def after(self, v):
         out = []
@@ -400,7 +413,7 @@
                 side = v[c + 1]
             else:
                 edge = self.sub % self.halves == self.halves - 1
-                side = jnp.where(edge, np.float32(0.0), pltpu.roll(v[0], SUBS - 1, 0))
+                side = jnp.where(edge, ZERO, pltpu.roll(v[0], SUBS - 1, 0))
             out.append(pltpu.roll(jnp.where(self.lane == 0, side, v[c]), LANES - 1, 1))
         return out
 
@@ -411,7 +424,7 @@
                 side = v[c - 1]
             else:
                 edge = self.sub % self.halves == 0
-                side = jnp.where(edge, np.float32(0.0), pltpu.roll(v[self.tiles - 1], 1, 0))
+                side = jnp.where(edge, ZERO, pltpu.roll(v[self.tiles - 1], 1, 0))
             out.append(pltpu.roll(jnp.where(self.lane == LANES - 1, side, v[c]), 1, 1))
         return out
 
@@ -421,178 +434,193 @@
     def below(self, v):
         return [pltpu.roll(t, self.halves, 0) for t in v]
 
-    def step(self, r, conc, poro, flow, u, s):
-        def each(f, *lists):
-            return [f(*t) for t in zip(*lists)]
-
-        def less(a, b):
-            return each(lambda x, y: x - y, a, b)
-
-        def times(a, b):
-            return each(lambda x, y: x * y, a, b)
-
-        def slopes(a, b):
-            return each(slope, a, b)
-
-        def face(w, va, vb, c, cn, sl, sn, dn):
-            a = each(lambda w, x, y: w * np.float32(0.5) * (x + y), w, va, vb)
-            return each(
-                lambda a, w, c, cn, sl, sn, dn: a * jnp.where(a > 0, c + sl, cn - sn)
-                - np.float32(DIFFUSION) * w * dn,
-                a, w, c, cn, sl, sn, dn,
-            )
-
-        cm2, cm1, c, cp1, cp2 = (conc(r + k) for k in (-2, -1, 0, 1, 2))
-        pm, p, pn = (poro(r + k) for k in (-1, 0, 1))
-        vm, v0, vn = (flow(r + k) for k in (-1, 0, 1))
-        d0, d1, d2, d3 = less(cm1, cm2), less(c, cm1), less(cp1, c), less(cp2, cp1)
-        sm, s0, sp = slopes(d0, d1), slopes(d1, d2), slopes(d2, d3)
-        change = less(
-            face(times(pm, p), vm, v0, cm1, c, sm, s0, d1), face(times(p, pn), v0, vn, c, cp1, s0, sp, d2)
+    def flow_face(self, r):
+        return face(
+            times(self.poro(r), self.poro(r + 1)), self.flow(r), self.flow(r + 1), self.conc(r), self.conc(r + 1),
+            self.lean(r), self.lean(r + 1), self.gap(r),
         )
-        for after, before, vel, open_ends in (
-            (self.after, self.before, u[1], True), (self.above, self.below, u[0], False),
+
+    def run(self, r, low=True, high=True):
+        c, p, s = self.conc(r), self.poro(r), self.napl(r)
+        change = None
+        if low:
+            change = self.flow_face(r - 1)
+        if high:
+            out = self.flow_face(r)
+            change = [-t for t in out] if change is None else less(change, out)
+        vel = self.cross(r)
+        for after, before, v, open_ends in (
+            (self.after, self.before, vel[0], True), (self.above, self.below, vel[1], False),
         ):
             cn = after(c)
             dn = less(cn, c)
             dm = less(c, before(c)) if open_ends else before(dn)
-            s0 = slopes(dm, dn)
-            flux = face(times(p, after(p)), vel, after(vel), c, cn, s0, after(s0), dn)
+            s0 = each(slope, dm, dn)
+            flux = face(times(p, after(p)), v, after(v), c, cn, s0, after(s0), dn)
             change = each(lambda t, a, b: t + (a - b), change, before(flux), flux)
         rate = loss(s, c)
-        cnew = each(
-            lambda c, t, k, p: c + (t + k) / jnp.maximum(p, np.float32(FLOOR)), c, change, rate, p
-        )
+        cnew = each(lambda c, t, k, p: c + (t + k) / p, c, change, rate, floored(p))
         return cnew, each(lambda s, k: s - np.float32(DEPLETION) * k, s, rate)
 
 
-ZERO = np.float32(0.0)
-
-
-def early_kernel(tiles, halves, ends, slabs, still0, still1, inner_u, ue0, ue1, flags, cs, u):
-    rows = u.shape[1]
-    row = Row(tiles, halves)
+def read(slab):
+    return [slab[:, cut(c)] for c in range(slab.shape[1] // LANES)]
+
+
+def write(slab, tiles):
+    for c, t in enumerate(tiles):
+        slab[:, cut(c)] = t
+
+
+def early_kernel(tiles, halves, slabs, u, cs):
+    rows = slabs.shape[1]
+    step = Step(
+        tiles, halves, lambda r: read(slabs.at[0, r]), lambda r: read(slabs.at[2, r]),
+        lambda r: read(u.at[1, r - 1]), lambda r: (read(u.at[2, r - 1]), read(u.at[0, r - 1])),
+        lambda r: read(slabs.at[1, r]),
+    )
+    for r in range(2, rows - 2):
+        for k, v in enumerate(step.run(r)):
+            write(cs.at[k, r - 2], v)
+
+
+def static_readers(ends, up, slabs, still, flags):
+    rows = slabs.shape[1]
     first, last = ends_of(*ends)
-    odd = upper(1)
-    for k in range(3):
-        for r in range(1, rows - 1):
-            u[k, r] = inner_u[k, r]
-    merge_rows(u, ue0, ue1, 3)
 
     def conc(r):
         if r < 0:
-            return pick(first, [ZERO] * tiles, pick(odd, row.read(still0.at[5]), row.read(still1.at[5])))
+            return [jnp.where(first, ZERO, t) for t in read(still.at[4 - r])]
         if r >= rows:
-            beyond = pick(odd, row.read(still1.at[5]), row.read(still0.at[5]))
-            return pick(last, row.read(slabs.at[0, rows - 1]), beyond)
-        return row.read(slabs.at[0, r])
+            return pick(last, read(slabs.at[0, rows - 1]), read(still.at[5 + r - rows]))
+        return read(slabs.at[0, r])
 
     def poro(r):
-        return row.read(slabs.at[2, r])
-
-    def flow(r):
-        return row.read(u.at[1, r])
-
-    for r in range(1, rows - 1):
-        new = row.step(r, conc, poro, flow, (row.read(u.at[0, r]), row.read(u.at[2, r])), row.read(slabs.at[1, r]))
-        for k in range(2):
-            for c in range(tiles):
-                cs[k, r - 1, :, cut(c)] = new[k][c]
-
-
-def side_step(row, ends, up, which, conc_at, beyond_c, napl_at, slabs, still, u, flags, beyond_u):
-    rows = u.shape[1]
+        if 0 <= r < rows:
+            return read(slabs.at[2, r])
+        return pick(last if up else first, read(flags.at[1 if up else 0]), read(still.at[7]))
+
+    return conc, poro
+
+
+def rim_kernel(tiles, halves, ends, chain, g, fac, halo, u, slabs, still, flags, after, ue, cs, send):
+    rows = g.shape[1]
+    lane, sub = iotas()
+
+    def side(up):
+        x, beside = (rows - 1, rows - 2) if up else (0, 1)
+        lo, hi, place = (None, halo, "last") if up else (halo, None, "first")
+        for c in range(tiles):
+            f = stream(g, lo, hi, x, c, tiles, halves, lane, sub, place)
+            for i, v in enumerate(speed(f, fac[x, :, cut(c)])):
+                ue[i, :, cut(c)] = v
+        conc, poro = static_readers(ends, up, slabs, still, flags)
+
+        def vel(k, r):
+            return read(ue.at[k] if r == x else u.at[k, r - 1])
+
+        step = Step(
+            tiles, halves, conc, poro, lambda r: vel(1, r), lambda r: (vel(2, r), vel(0, r)),
+            lambda r: read(slabs.at[1, r]),
+        )
+        edge = step.run(x, low=up, high=not up)
+        inward = step.run(beside)
+        for i, new in enumerate((edge, inward)):
+            for k in range(2):
+                write(cs.at[i, k], new[k])
+            write(send.at[1 + i], new[0])
+        send[0] = ue[1]
+
+    by_side(chain, side)
+
+
+def state_reader(rows, edge, inner, rims):
+    def state(k, r):
+        if r in (0, rows - 1):
+            return edge(k, r)
+        if r in (1, rows - 2):
+            return rims(k, r)
+        return read(inner.at[k, r - 2])
+
+    return state
+
+
+def middle_kernel(tiles, halves, slabs, u, inner, rim0, rim1, out):
+    rows = slabs.shape[1]
+    odd = upper(1)
+
+    def rims(k, r):
+        a, b = (rim0, rim1) if r == 1 else (rim1, rim0)
+        return pick(odd, read(a.at[1, k]), read(b.at[1, k]))
+
+    state = state_reader(rows, None, inner, rims)
+    step = Step(
+        tiles, halves, lambda r: state(0, r), lambda r: read(slabs.at[2, r]), lambda r: read(u.at[1, r - 1]),
+        lambda r: (read(u.at[2, r - 1]), read(u.at[0, r - 1])), lambda r: state(1, r),
+    )
+    for r in range(3, rows - 3):
+        write(out.at[r - 3], step.run(r)[0])
+
+
+def late_kernel(
+    tiles, halves, ends, chain, slabs, u, ue, inner, rim, still, flags, there, after, out
+):
+    rows = slabs.shape[1]
     first, last = ends_of(*ends)
-
-    def conc(r):
-        if r < 0:
-            return pick(first, [ZERO] * row.tiles, row.read(beyond_c(-1 - r)))
-        if r >= rows:
-            return pick(last, row.read(conc_at(rows - 1)), row.read(beyond_c(r - rows)))
-        return row.read(conc_at(r))
-
-    def poro(r):
-        if r < 0:
-            return pick(first, row.read(flags.at[0]), row.read(still.at[7]))
-        if r >= rows:
-            return pick(last, row.read(flags.at[1]), row.read(still.at[7]))
-        return row.read(slabs.at[2, r])
-
-    def flow(r):
-        if r < 0:
-            return pick(first, row.read(u.at[1, 0]), row.read(beyond_u))
-        if r >= rows:
-            return pick(last, row.read(u.at[1, rows - 1]), row.read(beyond_u))
-        return row.read(u.at[1, r])
-
-    return [
-        row.step(r, conc, poro, flow, (row.read(u.at[0, r]), row.read(u.at[2, r])), row.read(napl_at(r)))
-        for r in which
-    ]
-
-
-def rim_kernel(tiles, halves, ends, chain, slabs, still, u, flags, beyond_u, inner, after, cs, send):
-    rows = u.shape[1]
-    row = Row(tiles, halves)
 
     def side(up):
         x = rows - 1 if up else 0
-        ((c1, s1),) = side_step(
-            row, ends, up, (x,), lambda r: slabs.at[0, r], lambda k: still.at[5 + k], lambda r: slabs.at[1, r],
-            slabs, still, u, flags, beyond_u,
+        beyond = rows if up else -1
+        ghost = last if up else first
+        conc, poro = static_readers(ends, up, slabs, still, flags)
+
+        def vel(k, r):
+            if r == beyond:
+                return pick(ghost, read(ue.at[1]), read(there.at[0]))
+            return read(ue.at[k] if r == x else u.at[k, r - 1])
+
+        def cross(r):
+            return vel(2, r), vel(0, r)
+
+        one = Step(tiles, halves, conc, poro, lambda r: vel(1, r), cross, None)
+        flux = one.flow_face(x if up else -1)
+        sign = np.float32(-1.0 if up else 1.0)
+        edge = each(lambda c, f, p: c + sign * f / p, read(rim.at[0, 0]), flux, floored(poro(x)))
+        outer = each(lambda c, f, p: c - sign * f / p, read(there.at[1]), flux, floored(poro(beyond)))
+        second = read(there.at[2])
+        if up:
+            outer, second = pick(ghost, edge, outer), pick(ghost, edge, second)
+        else:
+            outer, second = ([jnp.where(ghost, ZERO, t) for t in v] for v in (outer, second))
+        state = state_reader(
+            rows, lambda k, r: read(rim.at[0, k]) if k else edge, inner, lambda k, r: read(rim.at[1, k])
         )
-        for c in range(tiles):
-            cs[0, :, cut(c)] = c1[c]
-            cs[1, :, cut(c)] = s1[c]
-            send[0, :, cut(c)] = c1[c]
-        send[1] = inner[0, rows - 3 if up else 0]
+
+        def after_one(r):
+            if r < 0 or r >= rows:
+                return outer if r == beyond else second
+            return state(0, r)
+
+        two = Step(tiles, halves, after_one, poro, lambda r: vel(1, r), cross, lambda r: state(1, r))
+        for i in range(3):
+            new = two.run(rows - 1 - i if up else i)
+            write(out.at[i], new[0])
+            if i == 0:
+                write(out.at[3], new[1])
 
     by_side(chain, side)
 
 
-def middle_kernel(tiles, halves, slabs, u, inner, rim0, rim1, out):
-    rows = u.shape[1]
-    row = Row(tiles, halves)
-    odd = upper(1)
-
-    def conc(r):
-        if r == 0:
-            return pick(odd, row.read(rim0.at[0]), row.read(rim1.at[0]))
-        if r == rows - 1:
-            return pick(odd, row.read(rim1.at[0]), row.read(rim0.at[0]))
-        return row.read(inner.at[0, r - 1])
-
-    for r in range(2, rows - 2):
-        new = row.step(
-            r, conc, lambda r: row.read(slabs.at[2, r]), lambda r: row.read(u.at[1, r]),
-            (row.read(u.at[0, r]), row.read(u.at[2, r])), row.read(inner.at[1, r - 1]),
-        )
-        for c in range(tiles):
-            out[r - 2, :, cut(c)] = new[0][c]
-
-
-def late_kernel(tiles, halves, ends, chain, slabs, still, u, flags, beyond_u, inner, rim, beyond_c, after, out):
-    rows = u.shape[1]
-    row = Row(tiles, halves)
-
-    def side(up):
-        def state(k, r):
-            return rim.at[k] if r in (0, rows - 1) else inner.at[k, r - 1]
-
-        new = side_step(
-            row, ends, up, (rows - 1, rows - 2) if up else (0, 1), lambda r: state(0, r),
-            lambda k: beyond_c.at[k], lambda r: state(1, r), slabs, still, u, flags, beyond_u,
-        )
-        for i in range(2):
-            for c in range(tiles):
-                out[i, :, cut(c)] = new[i][0][c]
-
-    by_side(chain, side)
+def place_of(parts):
+    me = lax.axis_index("narrow")
+    odd = lax.rem(lax.axis_index("wide"), 2) == 1
+    late = jnp.where(odd, parts - 1, 0)
+    return late, me == late, jnp.where(odd, me, me - 1), jnp.where(odd, 0, 1)
 
 
 def deal_kernel(tiles, halves, parts, inner, rim0, rim1, late0, late1, mid, *refs):
     *blocks, whole = refs
-    rows = inner.shape[1] + 2
+    rows = inner.shape[1] + 4
     odd = upper(1)
     _, sub = iotas()
     for c in range(tiles):
@@ -600,38 +628,60 @@
         def ends_pick(a, b):
             return jnp.where(odd, a, b)
 
-        lo = [ends_pick(late0[i, :, cut(c)], late1[i, :, cut(c)]) for i in range(2)]
-        hi = [ends_pick(late1[i, :, cut(c)], late0[i, :, cut(c)]) for i in range(2)]
-        conc = lo + [mid[r, :, cut(c)] for r in range(rows - 4)] + hi[::-1]
-        left = []
-        for r in range(rows):
-            if r in (0, rows - 1):
-                a, b = (rim0, rim1) if r == 0 else (rim1, rim0)
-                cc, ss = (ends_pick(a[k, :, cut(c)], b[k, :, cut(c)]) for k in range(2))
+        lo = [ends_pick(late0[i, :, cut(c)], late1[i, :, cut(c)]) for i in range(4)]
+        hi = [ends_pick(late1[i, :, cut(c)], late0[i, :, cut(c)]) for i in range(4)]
+        conc = lo[:3] + [mid[r, :, cut(c)] for r in range(rows - 6)] + hi[2::-1]
+        left = [lo[3]]
+        for r in range(1, rows - 1):
+            if r in (1, rows - 2):
+                a, b = (rim0, rim1) if r == 1 else (rim1, rim0)
+                cc, ss = (ends_pick(a[1, k, :, cut(c)], b[1, k, :, cut(c)]) for k in range(2))
             else:
-                cc, ss = (inner[k, r - 1, :, cut(c)] for k in range(2))
+                cc, ss = (inner[k, r - 2, :, cut(c)] for k in range(2))
             left.append(ss - np.float32(DEPLETION) * loss([ss], [cc])[0])
+        left.append(hi[3])
         run = whole.shape[3]
         for k, tile in enumerate((conc, left)):
             for i, t in enumerate(swap_tile(tile, sub)):
                 column = (i % halves * tiles + c) * SUBS
                 at = column % run
                 whole[column // run, k, i // halves, at : at + SUBS, :] = t
-    for k in range(parts):
-        blocks[k][...] = whole[lax.axis_index("narrow") ^ k]
+    late, is_late, place, base = place_of(parts)
+    others = parts - 1
+    blocks[0][...] = whole[lax.axis_index("narrow")]
+    for k in range(1, others):
+        blocks[k][...] = whole[base + lax.rem(place + k + others, others)]
+    for k in range(others):
+        blocks[others + k][...] = whole[jnp.where(is_late, base + k, late)]
 
 
 def gather_kernel(parts, *refs):
-    blocks = refs[:parts]
-    *outs, sems = refs[parts:]
-    copies = []
-    for k in range(parts):
-        origin = lax.axis_index("narrow") ^ k
-        for i, out in enumerate(outs):
-            copies.append(pltpu.make_async_copy(blocks[k].at[i], out.at[:, origin], sems.at[i * parts + k]))
-            copies[-1].start()
-    for copy in copies:
-        copy.wait()
+    *blocks, conc, napl, sems = refs
+    late, is_late, place, base = place_of(parts)
+    others = parts - 1
+
+    def copies(k, origin):
+        return [
+            pltpu.make_async_copy(blocks[k].at[i], out.at[:, origin], sems.at[i, k])
+            for i, out in enumerate((conc, napl))
+        ]
+
+    moves = [(None, copies(0, lax.axis_index("narrow")))]
+    for k in range(1, others):
+        moves.append((jnp.logical_not(is_late), copies(k, base + lax.rem(place - k + 2 * others, others))))
+    for k in range(others):
+        moves.append((is_late | (place == k), copies(others + k, jnp.where(is_late, base + k, late))))
+    for act in ("start", "wait"):
+        for when, pair in moves:
+
+            def go(pair=pair):
+                for copy in pair:
+                    getattr(copy, act)()
+
+            if when is None:
+                go()
+            else:
+                pl.when(when)(go)
 
 
 def call(kernel, out_shape, args, scratch=(), hbm=(), free=(), hbm_out=(), name=None, flops=0, aliases=None):
@@ -718,83 +768,67 @@
             functools.partial(inner_kernel, tiles, halves), hold(19, rows, *slab),
             (g, row0, row1, fac), name="inner", flops=250 * cells,
         )
-    inner_u = call(
-        functools.partial(inner_speed_kernel, tiles, halves), hold(3, rows, *slab), (g, fac),
+    u = call(
+        functools.partial(inner_speed_kernel, tiles, halves), hold(3, rows - 2, *slab), (g, fac),
         name="inner_speed", flops=100 * cells,
     )
-    ue0, send = call(
-        functools.partial(edge_speed_kernel, tiles, halves, 0), (hold(3, *slab), hold(*slab)),
-        (g, fac, halo0, inner_u), free=(3,), name="edge_speed0", flops=20 * cells,
-    )
-    far0 = swap(0, send)
-    ue1, send = call(
-        functools.partial(edge_speed_kernel, tiles, halves, 1), (hold(3, *slab), hold(*slab)),
-        (g, fac, halo1, send), free=(3,), name="edge_speed1", flops=20 * cells,
-    )
-    far1 = swap(1, send)
-    inner, u = call(
-        functools.partial(early_kernel, tiles, halves, ends),
-        (hold(2, rows - 2, *slab), hold(3, rows, *slab)),
-        (slabs, still0, still1, inner_u, ue0, ue1, open_ends), name="early", flops=100 * cells,
-    )
-    rim0, send = call(
-        functools.partial(rim_kernel, tiles, halves, ends, 0), (hold(2, *slab), hold(2, *slab)),
-        (slabs, still0, u, open_ends, far0, inner, send), free=(6,), name="rim0", flops=20 * cells,
-    )
-    next0 = swap(0, send)
-    rim1, send = call(
-        functools.partial(rim_kernel, tiles, halves, ends, 1), (hold(2, *slab), hold(2, *slab)),
-        (slabs, still1, u, open_ends, far1, inner, send), free=(6,), name="rim1", flops=20 * cells,
-    )
-    next1 = swap(1, send)
+    inner = call(
+        functools.partial(early_kernel, tiles, halves), hold(2, rows - 4, *slab), (slabs, u),
+        name="early", flops=60 * cells,
+    )
+    ue0, rim0, send = call(
+        functools.partial(rim_kernel, tiles, halves, ends, 0), (hold(3, *slab), hold(2, 2, *slab), hold(3, *slab)),
+        (g, fac, halo0, u, slabs, still0, open_ends, inner), free=(7,), name="rim0", flops=40 * cells,
+    )
+    there0 = swap(0, send)
+    ue1, rim1, send = call(
+        functools.partial(rim_kernel, tiles, halves, ends, 1), (hold(3, *slab), hold(2, 2, *slab), hold(3, *slab)),
+        (g, fac, halo1, u, slabs, still1, open_ends, send), free=(7,), name="rim1", flops=40 * cells,
+    )
+    there1 = swap(1, send)
     mid = call(
-        functools.partial(middle_kernel, tiles, halves), hold(rows - 4, *slab),
-        (slabs, u, inner, rim0, rim1), name="middle", flops=60 * cells,
+        functools.partial(middle_kernel, tiles, halves), hold(rows - 6, *slab), (slabs, u, inner, rim0, rim1),
+        name="middle", flops=40 * cells,
     )
     late0 = call(
-        functools.partial(late_kernel, tiles, halves, ends, 0), hold(2, *slab),
-        (slabs, still0, u, open_ends, far0, inner, rim0, next0, mid), free=(8,), name="late0", flops=30 * cells,
+        functools.partial(late_kernel, tiles, halves, ends, 0), hold(4, *slab),
+        (slabs, u, ue0, inner, rim0, still0, open_ends, there0, mid), free=(8,), name="late0", flops=30 * cells,
     )
     late1 = call(
-        functools.partial(late_kernel, tiles, halves, ends, 1), hold(2, *slab),
-        (slabs, still1, u, open_ends, far1, inner, rim1, next1, late0), free=(8,), name="late1", flops=30 * cells,
+        functools.partial(late_kernel, tiles, halves, ends, 1), hold(4, *slab),
+        (slabs, u, ue1, inner, rim1, still1, open_ends, there1, late0), free=(8,), name="late1", flops=30 * cells,
     )
     block = (2, layers, run, LANES)
+    others = parts - 1
     blocks = call(
-        functools.partial(deal_kernel, tiles, halves, parts), tuple(hold(*block) for _ in range(parts)),
+        functools.partial(deal_kernel, tiles, halves, parts), tuple(hold(*block) for _ in range(2 * others)),
         (inner, rim0, rim1, late0, late1, mid),
         scratch=(pltpu.VMEM((parts, *block), F32),), name="deal", flops=20 * cells,
     )
-    blocks = list(blocks)
-
-    def send_blocks(ks):
-        for k in ks:
-            blocks[k] = lax.ppermute(blocks[k], "narrow", [(i, i ^ k) for i in range(parts)])
-
-    groups = [[int(k) for k in ks] for ks in np.array_split(np.arange(parts - 1, 0, -1), 3)]
-    send_blocks(groups[0])
-    out = None
-    for ks, dirs in ((groups[1], range(0, 10)), (groups[2], range(10, 19))):
-        args = [g, fac, halo0, halo1, start, *(blocks[k] for k in ks), blocks[0]]
-        n = len(args)
-        if out is not None:
-            args.append(out)
-        out, *passed = call(
-            functools.partial(final_kernel, tiles, halves, dirs, len(ks), int(out is not None)),
-            (jax.ShapeDtypeStruct((19, *flat), F32), *(hold(*block) for _ in ks)),
-            args,
-            scratch=(pltpu.VMEM((len(dirs), *flat), F32), pltpu.SemaphoreType.DMA((len(dirs),))),
-            hbm=(n,), free=(n - 1,), hbm_out=(0,), name="final", flops=200 * cells,
-            aliases={n: 0} if out is not None else None,
-        )
-        for k, b in zip(ks, passed):
-            blocks[k] = b
-        send_blocks(ks)
+    came = [blocks[0]]
+    rings, meets = [[] for _ in range(others)], [[] for _ in range(others)]
+    for w in range(strips // parts):
+        late, base = (parts - 1, 0) if w % 2 else (0, 1)
+        for a in range(others):
+            at = w * parts + base + a
+            for k in range(1, others):
+                rings[k].append((at, w * parts + base + (a + k) % others))
+            meets[a] += [(at, w * parts + late), (w * parts + late, at)]
+    for k in range(1, others):
+        came.append(lax.ppermute(blocks[k], both, rings[k]))
+    for k in range(others):
+        came.append(lax.ppermute(blocks[others + k], both, meets[k]))
+    out = call(
+        functools.partial(final_kernel, tiles, halves), jax.ShapeDtypeStruct((19, *flat), F32),
+        (g, fac, halo0, halo1, start, blocks[0]),
+        scratch=(pltpu.VMEM((19, *flat), F32), pltpu.SemaphoreType.DMA((19,))),
+        free=(5,), hbm_out=(0,), name="final", flops=400 * cells,
+    )
     tile = (layers, parts, run, LANES)
     conc_out, napl_out = call(
         functools.partial(gather_kernel, parts),
         (jax.ShapeDtypeStruct(tile, F32), jax.ShapeDtypeStruct(tile, F32)),
-        blocks, scratch=(pltpu.SemaphoreType.DMA((2 * parts,)),), hbm_out=(0, 1), name="gather", flops=10 * cells,
+        came, scratch=(pltpu.SemaphoreType.DMA((2, 2 * others)),), hbm_out=(0, 1), name="gather", flops=10 * cells,
     )
     shape = (layers, rows * parts, width // parts)
 

time: 65.9 us -> 64.5 us (0.979)
  waiting for transfers between devices: 23.7 us -> 21.2 us
  starting transfers between devices: 25.6 us -> 27.6 us
  Pallas kernels: 15.6 us -> 14.6 us
    ppermute x3 -> x5, starting transfers between devices: 4.5 us -> 9.33 us  [the longest x3 8 us: local(): came.append(lax.ppermute(blocks[others + k], both, meets[k]))]
    ppermute x12 -> x10, waiting for transfers between devices: 20.7 us -> 17.1 us  [swap(): return lax.ppermute(array, both, pairs[chain])]
    ppermute x12 -> x10, starting transfers between devices: 21.1 us -> 18.2 us  [swap(): return lax.ppermute(array, both, pairs[chain])]
    ppermute x3 -> x5, waiting for transfers between devices: 2.94 us -> 4.09 us  [the longest x3 4.08 us: local(): came.append(lax.ppermute(blocks[others + k], both, meets[k]))]
    pallas_call x25 -> x22, Pallas kernels: 15.6 us -> 14.6 us  [call(): pl.pallas_call(kernel, out_shape=shapes, in_specs=[spec(i, hbm, free) for...]
  transfers between devices with their start and end apart: 15 -> 15, of which waited for: 7 -> 7; matrix products, arithmetic and copies ran while one was open for 0% -> 0% of each run, Pallas kernels for 19% -> 17%
where the time goes in v2:
time: 64.5 us; the launch traced here: 64.2 us
  starting transfers between devices  27.6 us (43%)
  waiting for transfers between devices  21.2 us (33%)
  Pallas kernels  14.6 us (23%)
  between operations  0.92 us (1%)
    ppermute x10, starting transfers between devices, swap(): return lax.ppermute(array, both, pairs[chain])  18.2 us
    ppermute x10, waiting for transfers between devices, swap(): return lax.ppermute(array, both, pairs[chain])  17.1 us
    pallas_call x22, Pallas kernels, call(): pl.pallas_call(kernel, out_shape=shapes, in_specs=[spec(i, hbm, free) for...  14.6 us
    ppermute x3, starting transfers between devices, local(): came.append(lax.ppermute(blocks[others + k], both, meets[k]))  8 us
    ppermute x3, waiting for transfers between devices, local(): came.append(lax.ppermute(blocks[others + k], both, meets[k]))  4.08 us
    ppermute x2, starting transfers between devices, local(): came.append(lax.ppermute(blocks[k], both, rings[k]))  1.33 us
  transfers between devices with their start and end apart: 15, of which 7 were waited for; matrix products, arithmetic and copies ran while one was open for 0% of the time, Pallas kernels for 17%

profile of v2, /device:TPU:0, one launch (start us, length us, event | category | flops | bytes accessed | tf_op | source)
XLA Modules:
  0.0 64.2 jit_solution(14462629938155279507)
XLA Ops:
  0.6 2.3 %first.1 = (f32[19,256,128]{2,1,0:T(8,128)S(1)}, s32[256,128]{1,0:T(8,128)S(1)}, f32[256,128]{1,0:T(8,128)S(1)}, f32[256,128]{1,0:T(8,128)S(1)}, f32[256,128]{1,...) custom-call(f32[19,256,128]{2,1,0:T(8,128)} %bitcast.40, ...), custom_call_target="tpu_custom_call" | custom-call | flops 1638400 | bytes 163840 | tf_op jit(solution)/shard_map/first/pallas_call | solution.py:693
  2.9 3.1 %collective-permute-start = (f32[8,8,512]{2,1,0:T(8,128)S(1)}, f32[8,8,512]{2,1,0:T(8,128)S(1)}, u32[]{:S(2)}, u32[]{:S(2)}) collective-permute-start(f32[8,8,512]{2,1,0:T(8,128)S(1)} %get-tuple-element.51.after), channel_id=1, source_target_pairs={{0,1},{1,0},{2,3},{3,2},{4,5},{5,4},{6,7},{7,6},{8,9},{9,8},{10,11... | collective-permute-start | bytes 393224 | tf_op jit(solution)/shard_map/ppermute | solution.py:728
  6.4 3.6 %collective-permute-start.1 = (f32[8,8,512]{2,1,0:T(8,128)S(1)}, f32[8,8,512]{2,1,0:T(8,128)S(1)}, u32[]{:S(2)}, u32[]{:S(2)}) collective-permute-start(f32[8,8,512]{2,1,0:T(8,128)S(1)} %get-tuple-element.55.after), channel_id=1, source_target_pairs={{0,31},{1,2},{2,1},{3,4},{4,3},{5,6},{6,5},{7,8},{8,7},{9,10},{10,... | collective-permute-start | bytes 393224 | tf_op jit(solution)/shard_map/ppermute | solution.py:728
  10.0 1.5 %first_inner.1 = (f32[19,8,8,512]{3,2,1,0:T(8,128)S(1)}, f32[8,8,512]{2,1,0:T(8,128)S(1)}, f32[19,8,8,512]{3,2,1,0:T(8,128)S(1)}, f32[3,8,8,512]{3,2,1,0:T(8,128)S(1)}, f32[2,8,512]{2,1,0:T(8,128)S(1)}) custom-call(f32[19,256,128]{2,1,0:T(8,128)S(1)} %get-tuple-element.44.pop, s32[256,128]{1,0:T(8,128)S(1)} %get-tuple-element.45.phase, ...), custom_call_target="tpu_custom_call" | custom-call | flops 9830400 | bytes 983040 | tf_op jit(solution)/shard_map/first_inner/pallas_call | solution.py:693
  11.8 4.3 %collective-permute-done.1.halo.still = f32[8,8,512]{2,1,0:T(8,128)S(1)} collective-permute-done((f32[8,8,512]{2,1,0:T(8,128)S(1)}, f32[8,8,512]{2,1,0:T(8,128)S(1)}, u32[]{:S(2)}, u32[]{:S(2)}) %collective-permute-start.1) | collective-permute-done | bytes 131104 | tf_op jit(solution)/shard_map/ppermute | solution.py:728
  16.3 3.0 %collective-permute-start.3 = (f32[5,8,512]{2,1,0:T(8,128)S(1)}, f32[5,8,512]{2,1,0:T(8,128)S(1)}, u32[]{:S(2)}, u32[]{:S(2)}) collective-permute-start(f32[5,8,512]{2,1,0:T(8,128)S(1)} %get-tuple-element.59.after), channel_id=1, source_target_pairs={{0,31},{1,2},{2,1},{3,4},{4,3},{5,6},{6,5},{7,8},{8,7},{9,10},{10,... | collective-permute-start | bytes 245768 | tf_op jit(solution)/shard_map/ppermute | solution.py:728
  19.3 1.3 %inner.3.g = f32[19,8,8,512]{3,2,1,0:T(8,128)S(1)} custom-call(f32[19,8,8,512]{3,2,1,0:T(8,128)S(1)} %get-tuple-element.53.g, f32[19,8,512]{2,1,0:T(8,128)S(1)} %get-tuple-element.56.row0, f32[19,8,512]{2,1,0:T(8,128)S(1)} %get-tuple-element.58.row1, f32[8,8,512]{2,1,0:T(8,128)S(1)} %get-tuple-element.54.fac), custom_call_target="tpu_custom_call" | custom-call | flops 8192000 | bytes 819200 | tf_op jit(solution)/shard_map/inner/pallas_call | solution.py:693
  20.8 3.1 %collective-permute-done.3.halo = f32[5,8,512]{2,1,0:T(8,128)S(1)} collective-permute-done((f32[5,8,512]{2,1,0:T(8,128)S(1)}, f32[5,8,512]{2,1,0:T(8,128)S(1)}, u32[]{:S(2)}, u32[]{:S(2)}) %collective-permute-start.3) | collective-permute-done | bytes 81952 | tf_op jit(solution)/shard_map/ppermute | solution.py:728
  24.1 3.0 %collective-permute-start.5 = (f32[5,8,512]{2,1,0:T(8,128)S(1)}, f32[5,8,512]{2,1,0:T(8,128)S(1)}, u32[]{:S(2)}, u32[]{:S(2)}) collective-permute-start(f32[5,8,512]{2,1,0:T(8,128)S(1)} %get-tuple-element.63.after), channel_id=1, source_target_pairs={{0,31},{1,2},{2,1},{3,4},{4,3},{5,6},{6,5},{7,8},{8,7},{9,10},{10,... | collective-permute-start | bytes 245768 | tf_op jit(solution)/shard_map/ppermute | solution.py:728
  27.1 1.3 %inner.4.g = f32[19,8,8,512]{3,2,1,0:T(8,128)S(1)} custom-call(f32[19,8,8,512]{3,2,1,0:T(8,128)S(1)} %inner.3.g, f32[19,8,512]{2,1,0:T(8,128)S(1)} %get-tuple-element.60.row0, f32[19,8,512]{2,1,0:T(8,128)S(1)} %get-tuple-element.62.row1, f32[8,8,512]{2,1,0:T(8,128)S(1)} %get-tuple-element.54.fac), custom_call_target="tpu_custom_call" | custom-call | flops 8192000 | bytes 819200 | tf_op jit(solution)/shard_map/inner/pallas_call | solution.py:693
  28.7 3.7 %collective-permute-done.5.halo = f32[5,8,512]{2,1,0:T(8,128)S(1)} collective-permute-done((f32[5,8,512]{2,1,0:T(8,128)S(1)}, f32[5,8,512]{2,1,0:T(8,128)S(1)}, u32[]{:S(2)}, u32[]{:S(2)}) %collective-permute-start.5) | collective-permute-done | bytes 81952 | tf_op jit(solution)/shard_map/ppermute | solution.py:728
  32.6 2.6 %collective-permute-start.7 = (f32[5,8,512]{2,1,0:T(8,128)S(1)}, f32[5,8,512]{2,1,0:T(8,128)S(1)}, u32[]{:S(2)}, u32[]{:S(2)}) collective-permute-start(f32[5,8,512]{2,1,0:T(8,128)S(1)} %get-tuple-element.67), channel_id=1, source_target_pairs={{0,31},{1,2},{2,1},{3,4},{4,3},{5,6},{6,5},{7,8},{8,7},{9,10},{10,... | collective-permute-start | bytes 245768 | tf_op jit(solution)/shard_map/ppermute | solution.py:728
  35.2 1.3 %inner.5.g = f32[19,8,8,512]{3,2,1,0:T(8,128)S(1)} custom-call(f32[19,8,8,512]{3,2,1,0:T(8,128)S(1)} %inner.4.g, f32[19,8,512]{2,1,0:T(8,128)S(1)} %get-tuple-element.64.row0, f32[19,8,512]{2,1,0:T(8,128)S(1)} %get-tuple-element.66.row1, f32[8,8,512]{2,1,0:T(8,128)S(1)} %get-tuple-element.54.fac), custom_call_target="tpu_custom_call" | custom-call | flops 8192000 | bytes 819200 | tf_op jit(solution)/shard_map/inner/pallas_call | solution.py:693
  36.5 0.8 %inner_speed.1.u = f32[3,6,8,512]{3,2,1,0:T(8,128)S(1)} custom-call(f32[19,8,8,512]{3,2,1,0:T(8,128)S(1)} %inner.5.g, f32[8,8,512]{2,1,0:T(8,128)S(1)} %get-tuple-element.54.fac), custom_call_target="tpu_custom_call" | custom-call | flops 3276800 | bytes 327680 | tf_op jit(solution)/shard_map/inner_speed/pallas_call | solution.py:693
  38.0 2.2 %collective-permute-done.7.halo.halo1 = f32[5,8,512]{2,1,0:T(8,128)S(1)} collective-permute-done((f32[5,8,512]{2,1,0:T(8,128)S(1)}, f32[5,8,512]{2,1,0:T(8,128)S(1)}, u32[]{:S(2)}, u32[]{:S(2)}) %collective-permute-start.7) | collective-permute-done | bytes 81952 | tf_op jit(solution)/shard_map/ppermute | solution.py:728
  40.5 2.7 %collective-permute-start.9 = (f32[3,8,512]{2,1,0:T(8,128)S(1)}, f32[3,8,512]{2,1,0:T(8,128)S(1)}, u32[]{:S(2)}, u32[]{:S(2)}) collective-permute-start(f32[3,8,512]{2,1,0:T(8,128)S(1)} %get-tuple-element.76), channel_id=1, source_target_pairs={{0,31},{1,2},{2,1},{3,4},{4,3},{5,6},{6,5},{7,8},{8,7},{9,10},{10,... | collective-permute-start | bytes 147464 | tf_op jit(solution)/shard_map/ppermute | solution.py:728
  43.8 3.9 %collective-permute-done.9.there = f32[3,8,512]{2,1,0:T(8,128)S(1)} collective-permute-done((f32[3,8,512]{2,1,0:T(8,128)S(1)}, f32[3,8,512]{2,1,0:T(8,128)S(1)}, u32[]{:S(2)}, u32[]{:S(2)}) %collective-permute-start.9) | collective-permute-done | bytes 49184 | tf_op jit(solution)/shard_map/ppermute | solution.py:728
  49.4 4.2 %collective-permute-start.12 = (f32[2,4,16,128]{3,2,1,0:T(8,128)S(1)}, f32[2,4,16,128]{3,2,1,0:T(8,128)S(1)}, u32[]{:S(2)}, u32[]{:S(2)}) collective-permute-start(f32[2,4,16,128]{3,2,1,0:T(8,128)S(1)} %get-tuple-element.80), channel_id=1, source_target_pairs={{1,0},{0,1},{4,7},{7,4},{9,8},{8,9},{12,15},{15,12},{17,16},{16,17... | collective-permute-start | bytes 196616 | tf_op jit(solution)/shard_map/ppermute | solution.py:820
  53.6 1.9 %collective-permute-start.13 = (f32[2,4,16,128]{3,2,1,0:T(8,128)S(1)}, f32[2,4,16,128]{3,2,1,0:T(8,128)S(1)}, u32[]{:S(2)}, u32[]{:S(2)}) collective-permute-start(f32[2,4,16,128]{3,2,1,0:T(8,128)S(1)} %get-tuple-element.81), channel_id=1, source_target_pairs={{2,0},{0,2},{5,7},{7,5},{10,8},{8,10},{13,15},{15,13},{18,16},{16,... | collective-permute-start | bytes 196616 | tf_op jit(solution)/shard_map/ppermute | solution.py:820
  55.5 1.9 %collective-permute-start.14 = (f32[2,4,16,128]{3,2,1,0:T(8,128)S(1)}, f32[2,4,16,128]{3,2,1,0:T(8,128)S(1)}, u32[]{:S(2)}, u32[]{:S(2)}) collective-permute-start(f32[2,4,16,128]{3,2,1,0:T(8,128)S(1)} %get-tuple-element.82), channel_id=1, source_target_pairs={{3,0},{0,3},{6,7},{7,6},{11,8},{8,11},{14,15},{15,14},{19,16},{16,... | collective-permute-start | bytes 196616 | tf_op jit(solution)/shard_map/ppermute | solution.py:820
  57.4 1.9 %final.1 = f32[19,256,128]{2,1,0:T(8,128)} custom-call(f32[19,8,8,512]{3,2,1,0:T(8,128)S(1)} %inner.5.g, f32[8,8,512]{2,1,0:T(8,128)S(1)} %get-tuple-element.54.fac, f32[5,8,512]{2,1,0:T(8,128)S(1)} %collective-permute-done.6.halo.halo0, f32[5,8,512]{2,1,0:T(8,128)S(1)} %collective-permute-done.7.halo.halo1, f32[19,8,8,512]{3,2,1,0:T(8,128)S(1)} %get-tuple-element.68.start, ...), custom_call_target="tpu_custom_call" | custom-call | flops 13107200 | bytes 1310720 | tf_op jit(solution)/shard_map/final/pallas_call | solution.py:693
  59.4 1.3 %collective-permute-done.13.refs_4_ = f32[2,4,16,128]{3,2,1,0:T(8,128)S(1)} collective-permute-done((f32[2,4,16,128]{3,2,1,0:T(8,128)S(1)}, f32[2,4,16,128]{3,2,1,0:T(8,128)S(1)}, u32[]{:S(2)}, u32[]{:S(2)}) %collective-permute-start.13) | collective-permute-done | bytes 65568 | tf_op jit(solution)/shard_map/ppermute | solution.py:820
  60.6 2.8 %collective-permute-done.14.refs_5_ = f32[2,4,16,128]{3,2,1,0:T(8,128)S(1)} collective-permute-done((f32[2,4,16,128]{3,2,1,0:T(8,128)S(1)}, f32[2,4,16,128]{3,2,1,0:T(8,128)S(1)}, u32[]{:S(2)}, u32[]{:S(2)}) %collective-permute-start.14) | collective-permute-done | bytes 65568 | tf_op jit(solution)/shard_map/ppermute | solution.py:820
  63.4 0.8 %gather.1 = (f32[4,4,16,128]{3,2,1,0:T(8,128)}, f32[4,4,16,128]{3,2,1,0:T(8,128)}) custom-call(f32[2,4,16,128]{3,2,1,0:T(8,128)S(1)} %get-tuple-element.77.after.refs_0_, f32[2,4,16,128]{3,2,1,0:T(8,128)S(1)} %collective-permute-done.10.refs_1_, f32[2,4,16,128]{3,2,1,0:T(8,128)S(1)} %collective-permute-done.11.refs_2_, ...), custom_call_target="tpu_custom_call" | custom-call | flops 327680 | bytes 32768 | tf_op jit(solution)/shard_map/gather/pallas_call | solution.py:693
  (28 shorter events, 5.2 us)
Async XLA Ops:
  2.9 8.6 %collective-permute-start = (f32[8,8,512]{2,1,0:T(8,128)S(1)}, f32[8,8,512]{2,1,0:T(8,128)S(1)}, u32[]{:S(2)}, u32[]{:S(2)}) collective-permute-start(f32[8,8,512]{2,1,0:T(8,128)S(1)} %get-tuple-element.51.after), channel_id=1, source_target_pairs={{0,1},{1,0},{2,3},{3,2},{4,5},{5,4},{6,7},{7,6},{8,9},{9,8},{10,11... | collective-permute-start | bytes 393224 | tf_op jit(solution)/shard_map/ppermute | solution.py:728
  6.4 9.7 %collective-permute-start.1 = (f32[8,8,512]{2,1,0:T(8,128)S(1)}, f32[8,8,512]{2,1,0:T(8,128)S(1)}, u32[]{:S(2)}, u32[]{:S(2)}) collective-permute-start(f32[8,8,512]{2,1,0:T(8,128)S(1)} %get-tuple-element.55.after), channel_id=1, source_target_pairs={{0,31},{1,2},{2,1},{3,4},{4,3},{5,6},{6,5},{7,8},{8,7},{9,10},{10,... | collective-permute-start | bytes 393224 | tf_op jit(solution)/shard_map/ppermute | solution.py:728
  11.7 8.8 %collective-permute-start.2 = (f32[5,8,512]{2,1,0:T(8,128)S(1)}, f32[5,8,512]{2,1,0:T(8,128)S(1)}, u32[]{:S(2)}, u32[]{:S(2)}) collective-permute-start(f32[5,8,512]{2,1,0:T(8,128)S(1)} %get-tuple-element.57.after), channel_id=1, source_target_pairs={{0,1},{1,0},{2,3},{3,2},{4,5},{5,4},{6,7},{7,6},{8,9},{9,8},{10,11... | collective-permute-start | bytes 245768 | tf_op jit(solution)/shard_map/ppermute | solution.py:728
  16.3 7.6 %collective-permute-start.3 = (f32[5,8,512]{2,1,0:T(8,128)S(1)}, f32[5,8,512]{2,1,0:T(8,128)S(1)}, u32[]{:S(2)}, u32[]{:S(2)}) collective-permute-start(f32[5,8,512]{2,1,0:T(8,128)S(1)} %get-tuple-element.59.after), channel_id=1, source_target_pairs={{0,31},{1,2},{2,1},{3,4},{4,3},{5,6},{6,5},{7,8},{8,7},{9,10},{10,... | collective-permute-start | bytes 245768 | tf_op jit(solution)/shard_map/ppermute | solution.py:728
  20.8 7.6 %collective-permute-start.4 = (f32[5,8,512]{2,1,0:T(8,128)S(1)}, f32[5,8,512]{2,1,0:T(8,128)S(1)}, u32[]{:S(2)}, u32[]{:S(2)}) collective-permute-start(f32[5,8,512]{2,1,0:T(8,128)S(1)} %get-tuple-element.61.after), channel_id=1, source_target_pairs={{0,1},{1,0},{2,3},{3,2},{4,5},{5,4},{6,7},{7,6},{8,9},{9,8},{10,11... | collective-permute-start | bytes 245768 | tf_op jit(solution)/shard_map/ppermute | solution.py:728
  24.1 8.3 %collective-permute-start.5 = (f32[5,8,512]{2,1,0:T(8,128)S(1)}, f32[5,8,512]{2,1,0:T(8,128)S(1)}, u32[]{:S(2)}, u32[]{:S(2)}) collective-permute-start(f32[5,8,512]{2,1,0:T(8,128)S(1)} %get-tuple-element.63.after), channel_id=1, source_target_pairs={{0,31},{1,2},{2,1},{3,4},{4,3},{5,6},{6,5},{7,8},{8,7},{9,10},{10,... | collective-permute-start | bytes 245768 | tf_op jit(solution)/shard_map/ppermute | solution.py:728
  28.6 9.0 %collective-permute-start.6 = (f32[5,8,512]{2,1,0:T(8,128)S(1)}, f32[5,8,512]{2,1,0:T(8,128)S(1)}, u32[]{:S(2)}, u32[]{:S(2)}) collective-permute-start(f32[5,8,512]{2,1,0:T(8,128)S(1)} %get-tuple-element.65.after), channel_id=1, source_target_pairs={{0,1},{1,0},{2,3},{3,2},{4,5},{5,4},{6,7},{7,6},{8,9},{9,8},{10,11... | collective-permute-start | bytes 245768 | tf_op jit(solution)/shard_map/ppermute | solution.py:728
  32.6 7.5 %collective-permute-start.7 = (f32[5,8,512]{2,1,0:T(8,128)S(1)}, f32[5,8,512]{2,1,0:T(8,128)S(1)}, u32[]{:S(2)}, u32[]{:S(2)}) collective-permute-start(f32[5,8,512]{2,1,0:T(8,128)S(1)} %get-tuple-element.67), channel_id=1, source_target_pairs={{0,31},{1,2},{2,1},{3,4},{4,3},{5,6},{6,5},{7,8},{8,7},{9,10},{10,... | collective-permute-start | bytes 245768 | tf_op jit(solution)/shard_map/ppermute | solution.py:728
  37.9 5.5 %collective-permute-start.8 = (f32[3,8,512]{2,1,0:T(8,128)S(1)}, f32[3,8,512]{2,1,0:T(8,128)S(1)}, u32[]{:S(2)}, u32[]{:S(2)}) collective-permute-start(f32[3,8,512]{2,1,0:T(8,128)S(1)} %get-tuple-element.72.after), channel_id=1, source_target_pairs={{0,1},{1,0},{2,3},{3,2},{4,5},{5,4},{6,7},{7,6},{8,9},{9,8},{10,11... | collective-permute-start | bytes 147464 | tf_op jit(solution)/shard_map/ppermute | solution.py:728
  40.5 7.2 %collective-permute-start.9 = (f32[3,8,512]{2,1,0:T(8,128)S(1)}, f32[3,8,512]{2,1,0:T(8,128)S(1)}, u32[]{:S(2)}, u32[]{:S(2)}) collective-permute-start(f32[3,8,512]{2,1,0:T(8,128)S(1)} %get-tuple-element.76), channel_id=1, source_target_pairs={{0,31},{1,2},{2,1},{3,4},{4,3},{5,6},{6,5},{7,8},{8,7},{9,10},{10,... | collective-permute-start | bytes 147464 | tf_op jit(solution)/shard_map/ppermute | solution.py:728
  48.0 11.3 %collective-permute-start.10 = (f32[2,4,16,128]{3,2,1,0:T(8,128)S(1)}, f32[2,4,16,128]{3,2,1,0:T(8,128)S(1)}, u32[]{:S(2)}, u32[]{:S(2)}) collective-permute-start(f32[2,4,16,128]{3,2,1,0:T(8,128)S(1)} %get-tuple-element.78), channel_id=1, source_target_pairs={{1,2},{2,3},{3,1},{4,5},{5,6},{6,4},{9,10},{10,11},{11,9},{12,13},... | collective-permute-start | bytes 196616 | tf_op jit(solution)/shard_map/ppermute | solution.py:818
  48.7 10.6 %collective-permute-start.11 = (f32[2,4,16,128]{3,2,1,0:T(8,128)S(1)}, f32[2,4,16,128]{3,2,1,0:T(8,128)S(1)}, u32[]{:S(2)}, u32[]{:S(2)}) collective-permute-start(f32[2,4,16,128]{3,2,1,0:T(8,128)S(1)} %get-tuple-element.79), channel_id=1, source_target_pairs={{1,3},{2,1},{3,2},{4,6},{5,4},{6,5},{9,11},{10,9},{11,10},{12,14},... | collective-permute-start | bytes 196616 | tf_op jit(solution)/shard_map/ppermute | solution.py:818
  49.4 10.0 %collective-permute-start.12 = (f32[2,4,16,128]{3,2,1,0:T(8,128)S(1)}, f32[2,4,16,128]{3,2,1,0:T(8,128)S(1)}, u32[]{:S(2)}, u32[]{:S(2)}) collective-permute-start(f32[2,4,16,128]{3,2,1,0:T(8,128)S(1)} %get-tuple-element.80), channel_id=1, source_target_pairs={{1,0},{0,1},{4,7},{7,4},{9,8},{8,9},{12,15},{15,12},{17,16},{16,17... | collective-permute-start | bytes 196616 | tf_op jit(solution)/shard_map/ppermute | solution.py:820
  53.6 7.1 %collective-permute-start.13 = (f32[2,4,16,128]{3,2,1,0:T(8,128)S(1)}, f32[2,4,16,128]{3,2,1,0:T(8,128)S(1)}, u32[]{:S(2)}, u32[]{:S(2)}) collective-permute-start(f32[2,4,16,128]{3,2,1,0:T(8,128)S(1)} %get-tuple-element.81), channel_id=1, source_target_pairs={{2,0},{0,2},{5,7},{7,5},{10,8},{8,10},{13,15},{15,13},{18,16},{16,... | collective-permute-start | bytes 196616 | tf_op jit(solution)/shard_map/ppermute | solution.py:820
  55.5 8.0 %collective-permute-start.14 = (f32[2,4,16,128]{3,2,1,0:T(8,128)S(1)}, f32[2,4,16,128]{3,2,1,0:T(8,128)S(1)}, u32[]{:S(2)}, u32[]{:S(2)}) collective-permute-start(f32[2,4,16,128]{3,2,1,0:T(8,128)S(1)} %get-tuple-element.82), channel_id=1, source_target_pairs={{3,0},{0,3},{6,7},{7,6},{11,8},{8,11},{14,15},{15,14},{19,16},{16,... | collective-permute-start | bytes 196616 | tf_op jit(solution)/shard_map/ppermute | solution.py:820

commit v3 on v2

--- a/solution.py
+++ b/solution.py
@@ -148,44 +148,91 @@
     return [jnp.where(flag, x, y) for x, y in zip(a, b)]
 
 
-def start_face(tiles, chain, pop, phase, conc, poro, row, send):
-    up = upper(chain)
-    x = jnp.where(up, SUBS - 1, 0)
-    beside = jnp.where(up, SUBS - 2, 1)
+def start_row(tiles, pop, phase, x, row, c):
+    at = strided(tiles, c, x)
+    fc = drag(phase[at, :])
+    post = collide([pop[q, at, :] for q in range(19)], fc)
+    for q in range(19):
+        row[q, :, cut(c)] = post[q]
+    return post, fc
+
+
+def start_static(tiles, up, conc, poro, send, n):
+    x, beside = jnp.where(up, SUBS - 1, 0), jnp.where(up, SUBS - 2, 1)
     for c in range(tiles):
-        at = strided(tiles, c, x)
-        post = collide([pop[q, at, :] for q in range(19)], drag(phase[at, :]))
+        send[n, :, cut(c)] = conc[strided(tiles, c, x), :]
+        send[n + 1, :, cut(c)] = conc[strided(tiles, c, beside), :]
+        send[n + 2, :, cut(c)] = poro[strided(tiles, c, x), :]
+
+
+def look_ahead(tiles, halves, up, edge, beside, send):
+    lane, sub = iotas()
+    toward, back = (UP, DOWN) if up else (DOWN, UP)
+    for c in range(tiles):
+        sums = [None] * 4
         for q in range(19):
-            row[q, :, cut(c)] = post[q]
-        for i in range(5):
-            send[i, :, cut(c)] = jnp.where(up, post[UP[i]], post[DOWN[i]])
-        send[5, :, cut(c)] = conc[at, :]
-        send[6, :, cut(c)] = conc[strided(tiles, c, beside), :]
-        send[7, :, cut(c)] = poro[at, :]
+            if q in back:
+                continue
+            if q == 0:
+                f = edge(0, c)
+            else:
+                f = pull(beside if q in toward else edge, q, c, tiles, halves, lane, sub)
+                f = jnp.where(f != f, edge(OPP[q], c), f)
+            for k, e in enumerate((1, *DIRS[q])):
+                if e:
+                    t = f if e > 0 else -f
+                    sums[k] = t if sums[k] is None else sums[k] + t
+            if q in toward:
+                i = toward.index(q)
+                send[i, :, cut(c)] = edge(q, c)
+                send[5 + i, :, cut(c)] = f
+        for k in range(4):
+            send[10 + k, :, cut(c)] = sums[k]
 
 
 def first_kernel(
-    tiles, pop_h, phase_h, conc_h, napl_h, poro_h, flags_h,
-    pop, phase, conc, napl, poro, flags, row, send, sems,
+    tiles, halves, pop_h, phase_h, conc_h, napl_h, poro_h, flags_h,
+    pop, phase, conc, napl, poro, flags, row, send, beside, sems,
 ):
     small = [
-        pltpu.make_async_copy(a, b, sems.at[i])
+        pltpu.make_async_copy(a, b, sems.at[tiles + i])
         for i, (a, b) in enumerate(
             ((phase_h, phase), (conc_h, conc), (poro_h, poro), (napl_h, napl), (flags_h, flags))
         )
     ]
-    large = pltpu.make_async_copy(pop_h, pop, sems.at[len(small)])
-    large.start()
-    for copy in small:
+    large = [pltpu.make_async_copy(pop_h.at[:, :, c], pop.at[:, :, c], sems.at[c]) for c in range(tiles)]
+    small[0].start()
+    for copy in large + small[1:]:
         copy.start()
-    for copy in small:
+    flat = pop.reshape(pop.shape[0], SUBS * tiles * SUBS, LANES)
+    up = upper(1)
+    x, inwards = jnp.where(up, SUBS - 1, 0), jnp.where(up, SUBS - 2, 1)
+    small[0].wait()
+    for c in range(tiles):
+        large[c].wait()
+        _, fc = start_row(tiles, flat, phase, x, row, c)
+        send[14, :, cut(c)] = fc
+        start_row(tiles, flat, phase, inwards, beside, c)
+
+    def side(up):
+        look_ahead(
+            tiles, halves, up, lambda q, c: row[q, :, cut(c)], lambda q, c: beside[q, :, cut(c)], send
+        )
+
+    by_side(1, side)
+    for copy in small[1:]:
         copy.wait()
-    large.wait()
-    start_face(tiles, 0, pop, phase, conc, poro, row, send)
+    start_static(tiles, up, conc, poro, send, 15)
 
 
 def second_kernel(tiles, pop, phase, conc, poro, after, row, send):
-    start_face(tiles, 1, pop, phase, conc, poro, row, send)
+    up = upper(0)
+    x = jnp.where(up, SUBS - 1, 0)
+    for c in range(tiles):
+        post, _ = start_row(tiles, pop, phase, x, row, c)
+        for i in range(5):
+            send[i, :, cut(c)] = jnp.where(up, post[UP[i]], post[DOWN[i]])
+    start_static(tiles, up, conc, poro, send, 5)
 
 
 def merge_rows(out, row0, row1, count):
@@ -264,7 +311,7 @@
     by_side(chain, side)
 
 
-def inner_kernel(tiles, halves, g, row0, row1, fac, out):
+def inner_kernel(tiles, halves, g, fac, after, out):
     rows = g.shape[1]
     lane, sub = iotas()
 
@@ -277,7 +324,68 @@
         return 0
 
     lax.fori_loop(1, rows - 1, row, 0)
+
+
+def put_kernel(inner, row0, row1, out):
     merge_rows(out, row0, row1, 19)
+
+
+def arrive_kernel(tiles, halves, g, fac, halo, still, row0, after, inner, out, ghost):
+    rows = g.shape[1]
+    lane, sub = iotas()
+
+    def side(up):
+        x = rows - 1 if up else 0
+        lo, hi, place = (None, halo, "last") if up else (halo, None, "first")
+        toward, back = (DOWN, UP) if up else (UP, DOWN)
+        for q in range(19):
+            out[q, rows - 1 - x] = row0[q]
+        for c in range(tiles):
+            post = collide(stream(g, lo, hi, x, c, tiles, halves, lane, sub, place), fac[x, :, cut(c)])
+            for q in range(19):
+                out[q, x, :, cut(c)] = post[q]
+            sums = [halo[10 + k, :, cut(c)] for k in range(4)]
+            for i, q in enumerate(back):
+                f = pull(lambda q, cc: g[q, x, :, cut(cc)], q, c, tiles, halves, lane, sub)
+                f = jnp.where(f != f, halo[i, :, cut(c)], f)
+                for k, e in enumerate((1, *DIRS[q])):
+                    if e:
+                        sums[k] = sums[k] + f if e > 0 else sums[k] - f
+            rho = sums[0]
+            inv = still[14, :, cut(c)] / rho
+            v = [j * inv for j in sums[1:]]
+            base = np.float32(1.0) - (v[0] * v[0] + v[1] * v[1] + v[2] * v[2]) * np.float32(1.0 / 6)
+            for i, q in enumerate(toward):
+                along = None
+                for e, t in zip(DIRS[q], v):
+                    if e:
+                        t = t if e > 0 else -t
+                        along = t if along is None else along + t
+                weight = np.float32(1.25 / 18 if sum(map(abs, DIRS[q])) == 1 else 1.25 / 36)
+                feq = (rho * weight) * (base + along * (along * np.float32(0.5) + np.float32(1.0)))
+                ghost[i, :, cut(c)] = feq - halo[5 + i, :, cut(c)] * np.float32(0.25)
+
+    by_side(1, side)
+
+
+def far_kernel(tiles, halves, g, fac, halo, row, send, beside):
+    rows = g.shape[1]
+    lane, sub = iotas()
+
+    def side(up):
+        x, inwards = (rows - 1, rows - 2) if up else (0, 1)
+        lo, hi, place = (None, halo, "last") if up else (halo, None, "first")
+        for c in range(tiles):
+            for at, ref, where in ((x, row, place), (inwards, beside, "mid")):
+                f = stream(g, lo, hi, at, c, tiles, halves, lane, sub, where)
+                post = collide(f, fac[at, :, cut(c)])
+                for q in range(19):
+                    ref[q, :, cut(c)] = post[q]
+        look_ahead(
+            tiles, halves, up, lambda q, c: row[q, :, cut(c)], lambda q, c: beside[q, :, cut(c)], send
+        )
+
+    by_side(1, side)
 
 
 def speed(f, fc):
@@ -291,7 +399,7 @@
     return [jnp.where(fc != fc, np.float32(0.0), j * inv) for j in (jz, jx, jy)]
 
 
-def inner_speed_kernel(tiles, halves, g, fac, u):
+def inner_speed_kernel(tiles, halves, g, fac, after, u):
     rows = g.shape[1]
     lane, sub = iotas()
 
@@ -299,16 +407,17 @@
         for c in range(tiles):
             f = stream(g, None, None, x, c, tiles, halves, lane, sub, "mid")
             for i, v in enumerate(speed(f, fac[x, :, cut(c)])):
-                u[i, x - 1, :, cut(c)] = v
+                u[i, x - 2, :, cut(c)] = v
         return 0
 
-    lax.fori_loop(1, rows - 1, row, 0)
-
-
-def final_kernel(tiles, halves, g, fac, halo0, halo1, start, after, out, buf, sems):
+    lax.fori_loop(2, rows - 2, row, 0)
+
+
+def final_kernel(tiles, halves, g, fac, halo0, halo1, start, after, out, token, buf, sems):
     rows = g.shape[1]
     lane, sub = iotas()
     odd = upper(1)
+    token[...] = jnp.zeros(token.shape, F32)
 
     def row_of(q, x):
         at = x - DIRS[q][0]
@@ -472,52 +581,61 @@
         slab[:, cut(c)] = t
 
 
-def early_kernel(tiles, halves, slabs, u, cs):
+def early_kernel(tiles, halves, slabs, u, ue0, ue1, cs):
     rows = slabs.shape[1]
+    odd = upper(1)
+
+    def flow(r):
+        if r == 1:
+            return pick(odd, read(ue0.at[1, 1]), read(ue1.at[1, 1]))
+        if r == rows - 2:
+            return pick(odd, read(ue1.at[1, 1]), read(ue0.at[1, 1]))
+        return read(u.at[1, r - 2])
+
     step = Step(
-        tiles, halves, lambda r: read(slabs.at[0, r]), lambda r: read(slabs.at[2, r]),
-        lambda r: read(u.at[1, r - 1]), lambda r: (read(u.at[2, r - 1]), read(u.at[0, r - 1])),
-        lambda r: read(slabs.at[1, r]),
+        tiles, halves, lambda r: read(slabs.at[0, r]), lambda r: read(slabs.at[2, r]), flow,
+        lambda r: (read(u.at[2, r - 2]), read(u.at[0, r - 2])), lambda r: read(slabs.at[1, r]),
     )
     for r in range(2, rows - 2):
         for k, v in enumerate(step.run(r)):
             write(cs.at[k, r - 2], v)
 
 
-def static_readers(ends, up, slabs, still, flags):
+def static_readers(ends, up, slabs, still, base, flags):
     rows = slabs.shape[1]
     first, last = ends_of(*ends)
 
     def conc(r):
         if r < 0:
-            return [jnp.where(first, ZERO, t) for t in read(still.at[4 - r])]
+            return [jnp.where(first, ZERO, t) for t in read(still.at[base - 1 - r])]
         if r >= rows:
-            return pick(last, read(slabs.at[0, rows - 1]), read(still.at[5 + r - rows]))
+            return pick(last, read(slabs.at[0, rows - 1]), read(still.at[base + r - rows]))
         return read(slabs.at[0, r])
 
     def poro(r):
         if 0 <= r < rows:
             return read(slabs.at[2, r])
-        return pick(last if up else first, read(flags.at[1 if up else 0]), read(still.at[7]))
+        return pick(last if up else first, read(flags.at[1 if up else 0]), read(still.at[base + 2]))
 
     return conc, poro
 
 
-def rim_kernel(tiles, halves, ends, chain, g, fac, halo, u, slabs, still, flags, after, ue, cs, send):
+def rim_kernel(tiles, halves, ends, chain, base, g, fac, halo, u, slabs, still, flags, after, ue, cs, send):
     rows = g.shape[1]
     lane, sub = iotas()
 
     def side(up):
         x, beside = (rows - 1, rows - 2) if up else (0, 1)
         lo, hi, place = (None, halo, "last") if up else (halo, None, "first")
-        for c in range(tiles):
-            f = stream(g, lo, hi, x, c, tiles, halves, lane, sub, place)
-            for i, v in enumerate(speed(f, fac[x, :, cut(c)])):
-                ue[i, :, cut(c)] = v
-        conc, poro = static_readers(ends, up, slabs, still, flags)
+        for n, (at, where) in enumerate(((x, place), (beside, "mid"))):
+            for c in range(tiles):
+                f = stream(g, lo, hi, at, c, tiles, halves, lane, sub, where)
+                for i, v in enumerate(speed(f, fac[at, :, cut(c)])):
+                    ue[n, i, :, cut(c)] = v
+        conc, poro = static_readers(ends, up, slabs, still, base, flags)
 
         def vel(k, r):
-            return read(ue.at[k] if r == x else u.at[k, r - 1])
+            return read(ue.at[0 if r == x else 1, k] if r in (x, beside) else u.at[k, r - 2])
 
         step = Step(
             tiles, halves, conc, poro, lambda r: vel(1, r), lambda r: (vel(2, r), vel(0, r)),
@@ -529,7 +647,7 @@
             for k in range(2):
                 write(cs.at[i, k], new[k])
             write(send.at[1 + i], new[0])
-        send[0] = ue[1]
+        send[0] = ue[0, 1]
 
     by_side(chain, side)
 
@@ -555,15 +673,15 @@
 
     state = state_reader(rows, None, inner, rims)
     step = Step(
-        tiles, halves, lambda r: state(0, r), lambda r: read(slabs.at[2, r]), lambda r: read(u.at[1, r - 1]),
-        lambda r: (read(u.at[2, r - 1]), read(u.at[0, r - 1])), lambda r: state(1, r),
+        tiles, halves, lambda r: state(0, r), lambda r: read(slabs.at[2, r]), lambda r: read(u.at[1, r - 2]),
+        lambda r: (read(u.at[2, r - 2]), read(u.at[0, r - 2])), lambda r: state(1, r),
     )
     for r in range(3, rows - 3):
         write(out.at[r - 3], step.run(r)[0])
 
 
 def late_kernel(
-    tiles, halves, ends, chain, slabs, u, ue, inner, rim, still, flags, there, after, out
+    tiles, halves, ends, chain, base, slabs, u, ue, inner, rim, still, flags, there, after, out
 ):
     rows = slabs.shape[1]
     first, last = ends_of(*ends)
@@ -572,12 +690,14 @@
         x = rows - 1 if up else 0
         beyond = rows if up else -1
         ghost = last if up else first
-        conc, poro = static_readers(ends, up, slabs, still, flags)
+        conc, poro = static_readers(ends, up, slabs, still, base, flags)
 
         def vel(k, r):
             if r == beyond:
-                return pick(ghost, read(ue.at[1]), read(there.at[0]))
-            return read(ue.at[k] if r == x else u.at[k, r - 1])
+                return pick(ghost, read(ue.at[0, 1]), read(there.at[0]))
+            if r in (x, x - 1 if up else x + 1):
+                return read(ue.at[0 if r == x else 1, k])
+            return read(u.at[k, r - 2])
 
         def cross(r):
             return vel(2, r), vel(0, r)
@@ -609,13 +729,6 @@
                 write(out.at[3], new[1])
 
     by_side(chain, side)
-
-
-def place_of(parts):
-    me = lax.axis_index("narrow")
-    odd = lax.rem(lax.axis_index("wide"), 2) == 1
-    late = jnp.where(odd, parts - 1, 0)
-    return late, me == late, jnp.where(odd, me, me - 1), jnp.where(odd, 0, 1)
 
 
 def deal_kernel(tiles, halves, parts, inner, rim0, rim1, late0, late1, mid, *refs):
@@ -646,42 +759,21 @@
                 column = (i % halves * tiles + c) * SUBS
                 at = column % run
                 whole[column // run, k, i // halves, at : at + SUBS, :] = t
-    late, is_late, place, base = place_of(parts)
-    others = parts - 1
-    blocks[0][...] = whole[lax.axis_index("narrow")]
-    for k in range(1, others):
-        blocks[k][...] = whole[base + lax.rem(place + k + others, others)]
-    for k in range(others):
-        blocks[others + k][...] = whole[jnp.where(is_late, base + k, late)]
-
-
-def gather_kernel(parts, *refs):
-    *blocks, conc, napl, sems = refs
-    late, is_late, place, base = place_of(parts)
-    others = parts - 1
-
-    def copies(k, origin):
-        return [
-            pltpu.make_async_copy(blocks[k].at[i], out.at[:, origin], sems.at[i, k])
-            for i, out in enumerate((conc, napl))
-        ]
-
-    moves = [(None, copies(0, lax.axis_index("narrow")))]
-    for k in range(1, others):
-        moves.append((jnp.logical_not(is_late), copies(k, base + lax.rem(place - k + 2 * others, others))))
-    for k in range(others):
-        moves.append((is_late | (place == k), copies(others + k, jnp.where(is_late, base + k, late))))
-    for act in ("start", "wait"):
-        for when, pair in moves:
-
-            def go(pair=pair):
-                for copy in pair:
-                    getattr(copy, act)()
-
-            if when is None:
-                go()
-            else:
-                pl.when(when)(go)
+    for k in range(parts):
+        blocks[k][...] = whole[lax.axis_index("narrow") ^ k]
+
+
+def gather_kernel(parts, order, *refs):
+    blocks = refs[:parts]
+    *outs, sems = refs[parts:]
+    copies = []
+    for k, block in zip(order, blocks):
+        origin = lax.axis_index("narrow") ^ k
+        for i, out in enumerate(outs):
+            copies.append(pltpu.make_async_copy(block.at[i], out.at[:, origin], sems.at[i, k]))
+            copies[-1].start()
+    for copy in copies:
+        copy.wait()
 
 
 def call(kernel, out_shape, args, scratch=(), hbm=(), free=(), hbm_out=(), name=None, flops=0, aliases=None):
@@ -730,21 +822,24 @@
     pop = to_view(populations)
     views = [to_view(a) for a in (phase, concentration, napl, porosity)]
     flat = views[0].shape
-    given = [pltpu.with_memory_space_constraint(a, pltpu.HBM) for a in (pop, *views, flags)]
-    popv, phv, cov, nav, pov, flv, row0, send = call(
-        functools.partial(first_kernel, tiles),
+    chunks = pop.reshape(19, SUBS, tiles, SUBS, LANES)
+    given = [pltpu.with_memory_space_constraint(a, pltpu.HBM) for a in (chunks, *views, flags)]
+    popv, phv, cov, nav, pov, flv, row1, send = call(
+        functools.partial(first_kernel, tiles, halves),
         (
-            hold(*pop.shape), hold(*flat, dtype=jnp.int32), hold(*flat), hold(*flat), hold(*flat),
-            hold(*flags.shape, dtype=jnp.int32), hold(19, *slab), hold(8, *slab),
+            hold(*chunks.shape), hold(*flat, dtype=jnp.int32), hold(*flat), hold(*flat), hold(*flat),
+            hold(*flags.shape, dtype=jnp.int32), hold(19, *slab), hold(18, *slab),
         ),
-        given, scratch=(pltpu.SemaphoreType.DMA((6,)),), hbm=range(6), name="first", flops=50 * cells,
-    )
-    halo0 = still0 = swap(0, send)
-    row1, send = call(
+        given, scratch=(pltpu.VMEM((19, *slab), F32), pltpu.SemaphoreType.DMA((tiles + 5,))),
+        hbm=range(6), name="first", flops=50 * cells,
+    )
+    popv = popv.reshape(pop.shape)
+    halo1 = still1 = swap(1, send)
+    row0, send = call(
         functools.partial(second_kernel, tiles), (hold(19, *slab), hold(8, *slab)),
         (popv, phv, cov, pov, send), free=(4,), name="second", flops=30 * cells,
     )
-    halo1 = still1 = swap(1, send)
+    halo0 = still0 = swap(0, send)
     g, fac, start, slabs, open_ends = call(
         functools.partial(first_inner_kernel, tiles, halves),
         (
@@ -753,82 +848,92 @@
         ),
         (popv, phv, cov, nav, pov, flv, row0, row1), name="first_inner", flops=300 * cells,
     )
-    for _ in range(1, LBM_STEPS):
+    after = slabs
+    for step in range(1, LBM_STEPS):
+        if step % 2 == 0:
+            row1, send1 = call(
+                functools.partial(far_kernel, tiles, halves), (hold(19, *slab), hold(14, *slab)),
+                (g, fac, ghost), scratch=(pltpu.VMEM((19, *slab), F32),), name="far", flops=60 * cells,
+            )
+            halo1 = swap(1, send1)
+            after = send1
+        new = call(
+            functools.partial(inner_kernel, tiles, halves), hold(19, rows, *slab), (g, fac, after),
+            free=(2,), name="inner", flops=250 * cells,
+        )
+        if step == LBM_STEPS - 1:
+            u = call(
+                functools.partial(inner_speed_kernel, tiles, halves), hold(3, rows - 4, *slab), (new, fac, after),
+                free=(2,), name="inner_speed", flops=100 * cells,
+            )
         row0, send = call(
             functools.partial(edge_kernel, tiles, halves, 0), (hold(19, *slab), hold(5, *slab)),
-            (g, fac, halo0, send), free=(3,), name="edge0", flops=30 * cells,
+            (g, fac, halo0, new), free=(3,), name="edge0", flops=30 * cells,
         )
         halo0 = swap(0, send)
-        row1, send = call(
-            functools.partial(edge_kernel, tiles, halves, 1), (hold(19, *slab), hold(5, *slab)),
-            (g, fac, halo1, send), free=(3,), name="edge1", flops=30 * cells,
-        )
-        halo1 = swap(1, send)
-        g = call(
-            functools.partial(inner_kernel, tiles, halves), hold(19, rows, *slab),
-            (g, row0, row1, fac), name="inner", flops=250 * cells,
-        )
-    u = call(
-        functools.partial(inner_speed_kernel, tiles, halves), hold(3, rows - 2, *slab), (g, fac),
-        name="inner_speed", flops=100 * cells,
-    )
+        if step % 2 == 0:
+            g = call(
+                put_kernel, hold(19, rows, *slab), (new, row0, row1), name="put", flops=10 * cells,
+                aliases={0: 0},
+            )
+            after = g
+        else:
+            g, ghost = call(
+                functools.partial(arrive_kernel, tiles, halves), (hold(19, rows, *slab), hold(5, *slab)),
+                (g, fac, halo1, still1, row0, u if step == LBM_STEPS - 1 else send, new), free=(5,),
+                name="arrive", flops=60 * cells, aliases={6: 0},
+            )
+            after = ghost
+    ue1, rim1, send = call(
+        functools.partial(rim_kernel, tiles, halves, ends, 1, 15),
+        (hold(2, 3, *slab), hold(2, 2, *slab), hold(3, *slab)),
+        (g, fac, ghost, u, slabs, still1, open_ends, u), free=(7,), name="rim1", flops=50 * cells,
+    )
+    there1 = swap(1, send)
+    ue0, rim0, send = call(
+        functools.partial(rim_kernel, tiles, halves, ends, 0, 5),
+        (hold(2, 3, *slab), hold(2, 2, *slab), hold(3, *slab)),
+        (g, fac, halo0, u, slabs, still0, open_ends, send), free=(7,), name="rim0", flops=50 * cells,
+    )
+    there0 = swap(0, send)
     inner = call(
-        functools.partial(early_kernel, tiles, halves), hold(2, rows - 4, *slab), (slabs, u),
+        functools.partial(early_kernel, tiles, halves), hold(2, rows - 4, *slab), (slabs, u, ue0, ue1),
         name="early", flops=60 * cells,
     )
-    ue0, rim0, send = call(
-        functools.partial(rim_kernel, tiles, halves, ends, 0), (hold(3, *slab), hold(2, 2, *slab), hold(3, *slab)),
-        (g, fac, halo0, u, slabs, still0, open_ends, inner), free=(7,), name="rim0", flops=40 * cells,
-    )
-    there0 = swap(0, send)
-    ue1, rim1, send = call(
-        functools.partial(rim_kernel, tiles, halves, ends, 1), (hold(3, *slab), hold(2, 2, *slab), hold(3, *slab)),
-        (g, fac, halo1, u, slabs, still1, open_ends, send), free=(7,), name="rim1", flops=40 * cells,
-    )
-    there1 = swap(1, send)
     mid = call(
         functools.partial(middle_kernel, tiles, halves), hold(rows - 6, *slab), (slabs, u, inner, rim0, rim1),
         name="middle", flops=40 * cells,
     )
     late0 = call(
-        functools.partial(late_kernel, tiles, halves, ends, 0), hold(4, *slab),
+        functools.partial(late_kernel, tiles, halves, ends, 0, 5), hold(4, *slab),
         (slabs, u, ue0, inner, rim0, still0, open_ends, there0, mid), free=(8,), name="late0", flops=30 * cells,
     )
+    out, token = call(
+        functools.partial(final_kernel, tiles, halves),
+        (jax.ShapeDtypeStruct((19, *flat), F32), hold(SUBS, LANES)),
+        (g, fac, halo0, ghost, start, late0),
+        scratch=(pltpu.VMEM((19, *flat), F32), pltpu.SemaphoreType.DMA((19,))),
+        free=(5,), hbm_out=(0,), name="final", flops=400 * cells,
+    )
     late1 = call(
-        functools.partial(late_kernel, tiles, halves, ends, 1), hold(4, *slab),
-        (slabs, u, ue1, inner, rim1, still1, open_ends, there1, late0), free=(8,), name="late1", flops=30 * cells,
+        functools.partial(late_kernel, tiles, halves, ends, 1, 15), hold(4, *slab),
+        (slabs, u, ue1, inner, rim1, still1, open_ends, there1, token), free=(8,), name="late1", flops=30 * cells,
     )
     block = (2, layers, run, LANES)
-    others = parts - 1
     blocks = call(
-        functools.partial(deal_kernel, tiles, halves, parts), tuple(hold(*block) for _ in range(2 * others)),
+        functools.partial(deal_kernel, tiles, halves, parts), tuple(hold(*block) for _ in range(parts)),
         (inner, rim0, rim1, late0, late1, mid),
         scratch=(pltpu.VMEM((parts, *block), F32),), name="deal", flops=20 * cells,
     )
+    order = [0, *range(2, parts), 1]
     came = [blocks[0]]
-    rings, meets = [[] for _ in range(others)], [[] for _ in range(others)]
-    for w in range(strips // parts):
-        late, base = (parts - 1, 0) if w % 2 else (0, 1)
-        for a in range(others):
-            at = w * parts + base + a
-            for k in range(1, others):
-                rings[k].append((at, w * parts + base + (a + k) % others))
-            meets[a] += [(at, w * parts + late), (w * parts + late, at)]
-    for k in range(1, others):
-        came.append(lax.ppermute(blocks[k], both, rings[k]))
-    for k in range(others):
-        came.append(lax.ppermute(blocks[others + k], both, meets[k]))
-    out = call(
-        functools.partial(final_kernel, tiles, halves), jax.ShapeDtypeStruct((19, *flat), F32),
-        (g, fac, halo0, halo1, start, blocks[0]),
-        scratch=(pltpu.VMEM((19, *flat), F32), pltpu.SemaphoreType.DMA((19,))),
-        free=(5,), hbm_out=(0,), name="final", flops=400 * cells,
-    )
+    for k in order[1:]:
+        came.append(lax.ppermute(blocks[k], "narrow", [(i, i ^ k) for i in range(parts)]))
     tile = (layers, parts, run, LANES)
     conc_out, napl_out = call(
-        functools.partial(gather_kernel, parts),
+        functools.partial(gather_kernel, parts, order),
         (jax.ShapeDtypeStruct(tile, F32), jax.ShapeDtypeStruct(tile, F32)),
-        came, scratch=(pltpu.SemaphoreType.DMA((2, 2 * others)),), hbm_out=(0, 1), name="gather", flops=10 * cells,
+        came, scratch=(pltpu.SemaphoreType.DMA((2, parts)),), hbm_out=(0, 1), name="gather", flops=10 * cells,
     )
     shape = (layers, rows * parts, width // parts)
 

time: 64.5 us -> 52.8 us (0.82)
  starting transfers between devices: 27.6 us -> 17.5 us
  waiting for transfers between devices: 21.2 us -> 19.9 us
    ppermute x5 -> x3, starting transfers between devices: 9.33 us -> 3.55 us  [local(): lax.ppermute(blocks[k], 'narrow', [(i, i ^ k) for i in range(parts)])]
    ppermute x10 -> x8, starting transfers between devices: 18.2 us -> 13.9 us  [swap(): return lax.ppermute(array, both, pairs[chain])]
    ppermute x5 -> x3, waiting for transfers between devices: 4.09 us -> 3.37 us  [local(): lax.ppermute(blocks[k], 'narrow', [(i, i ^ k) for i in range(parts)])]
    ppermute x10 -> x8, waiting for transfers between devices: 17.1 us -> 16.5 us  [swap(): return lax.ppermute(array, both, pairs[chain])]
    pallas_call x22 -> x23, Pallas kernels: 14.6 us -> 14.5 us  [call(): pl.pallas_call(kernel, out_shape=shapes, in_specs=[spec(i, hbm, free) for...]
  transfers between devices with their start and end apart: 15 -> 11, of which waited for: 7 -> 8; matrix products, arithmetic and copies ran while one was open for 0% -> 0% of each run, Pallas kernels for 17% -> 20%
where the time goes in v3:
time: 52.8 us; the launch traced here: 52.6 us
  waiting for transfers between devices  19.9 us (38%)
  starting transfers between devices  17.5 us (33%)
  Pallas kernels  14.5 us (27%)
  between operations  0.82 us (2%)
    ppermute x8, waiting for transfers between devices, swap(): return lax.ppermute(array, both, pairs[chain])  16.5 us
    pallas_call x23, Pallas kernels, call(): pl.pallas_call(kernel, out_shape=shapes, in_specs=[spec(i, hbm, free) for...  14.5 us
    ppermute x8, starting transfers between devices, swap(): return lax.ppermute(array, both, pairs[chain])  13.9 us
    ppermute x3, starting transfers between devices, local(): lax.ppermute(blocks[k], 'narrow', [(i, i ^ k) for i in range(parts)])  3.55 us
    ppermute x3, waiting for transfers between devices, local(): lax.ppermute(blocks[k], 'narrow', [(i, i ^ k) for i in range(parts)])  3.37 us
  transfers between devices with their start and end apart: 11, of which 8 were waited for; matrix products, arithmetic and copies ran while one was open for 0% of the time, Pallas kernels for 20%

profile of v3, /device:TPU:0, one launch (start us, length us, event | category | flops | bytes accessed | tf_op | source)
XLA Modules:
  0.0 52.6 jit_solution(15465358307459812575)
XLA Ops:
  0.6 2.2 %first.1 = (f32[19,8,4,8,128]{4,3,2,1,0:T(8,128)S(1)}, s32[256,128]{1,0:T(8,128)S(1)}, f32[256,128]{1,0:T(8,128)S(1)}, f32[256,128]{1,0:T(8,128)S(1)}, f32[256,1...) custom-call(f32[19,8,4,8,128]{4,3,2,1,0:T(8,128)} %bitcast.43, ...), custom_call_target="tpu_custom_call" | custom-call | flops 1638400 | bytes 163840 | tf_op jit(solution)/shard_map/first/pallas_call | solution.py:785
  2.9 6.4 %collective-permute-start = (f32[18,8,512]{2,1,0:T(8,128)S(1)}, f32[18,8,512]{2,1,0:T(8,128)S(1)}, u32[]{:S(2)}, u32[]{:S(2)}) collective-permute-start(f32[18,8,512]{2,1,0:T(8,128)S(1)} %get-tuple-element.50.after), channel_id=1, source_target_pairs={{0,31},{1,2},{2,1},{3,4},{4,3},{5,6},{6,5},{7,8},{8,7},{9,10},{10,... | collective-permute-start | bytes 884744 | tf_op jit(solution)/shard_map/ppermute | solution.py:820
  9.3 0.4 second.1
  9.8 1.5 %first_inner.1 = (f32[19,8,8,512]{3,2,1,0:T(8,128)S(1)}, f32[8,8,512]{2,1,0:T(8,128)S(1)}, f32[19,8,8,512]{3,2,1,0:T(8,128)S(1)}, f32[3,8,8,512]{3,2,1,0:T(8,128)S(1)}, f32[2,8,512]{2,1,0:T(8,128)S(1)}) custom-call(f32[19,256,128]{2,1,0:T(8,128)S(1)} %bitcast.42, s32[256,128]{1,0:T(8,128)S(1)} %get-tuple-element.45.phase, ...), custom_call_target="tpu_custom_call" | custom-call | flops 9830400 | bytes 983040 | tf_op jit(solution)/shard_map/first_inner/pallas_call | solution.py:785
  11.3 1.2 %inner.3.after = f32[19,8,8,512]{3,2,1,0:T(8,128)S(1)} custom-call(f32[19,8,8,512]{3,2,1,0:T(8,128)S(1)} %get-tuple-element.53.g, f32[8,8,512]{2,1,0:T(8,128)S(1)} %get-tuple-element.54.fac, f32[3,8,8,512]{3,2,1,0:T(8,128)S(1)} %get-tuple-element.56.after.slabs), custom_call_target="tpu_custom_call" | custom-call | flops 8192000 | bytes 819200 | tf_op jit(solution)/shard_map/inner/pallas_call | solution.py:785
  12.5 6.2 %collective-permute-done.1.halo.still = f32[8,8,512]{2,1,0:T(8,128)S(1)} collective-permute-done((f32[8,8,512]{2,1,0:T(8,128)S(1)}, f32[8,8,512]{2,1,0:T(8,128)S(1)}, u32[]{:S(2)}, u32[]{:S(2)}) %collective-permute-start.1) | collective-permute-done | bytes 131104 | tf_op jit(solution)/shard_map/ppermute | solution.py:820
  19.0 1.5 %collective-permute-start.2 = (f32[5,8,512]{2,1,0:T(8,128)S(1)}, f32[5,8,512]{2,1,0:T(8,128)S(1)}, u32[]{:S(2)}, u32[]{:S(2)}) collective-permute-start(f32[5,8,512]{2,1,0:T(8,128)S(1)} %get-tuple-element.58.after), channel_id=1, source_target_pairs={{0,1},{1,0},{2,3},{3,2},{4,5},{5,4},{6,7},{7,6},{8,9},{9,8},{10,11... | collective-permute-start | bytes 245768 | tf_op jit(solution)/shard_map/ppermute | solution.py:820
  20.7 0.4 far.1
  21.1 1.4 %collective-permute-start.3 = (f32[14,8,512]{2,1,0:T(8,128)S(1)}, f32[14,8,512]{2,1,0:T(8,128)S(1)}, u32[]{:S(2)}, u32[]{:S(2)}) collective-permute-start(f32[14,8,512]{2,1,0:T(8,128)S(1)} %get-tuple-element.61.after), channel_id=1, source_target_pairs={{0,31},{1,2},{2,1},{3,4},{4,3},{5,6},{6,5},{7,8},{8,7},{9,10},{10,... | collective-permute-start | bytes 688136 | tf_op jit(solution)/shard_map/ppermute | solution.py:820
  22.5 1.2 %inner.4.after = f32[19,8,8,512]{3,2,1,0:T(8,128)S(1)} custom-call(f32[19,8,8,512]{3,2,1,0:T(8,128)S(1)} %get-tuple-element.59.g, f32[8,8,512]{2,1,0:T(8,128)S(1)} %get-tuple-element.54.fac, f32[14,8,512]{2,1,0:T(8,128)S(1)} %get-tuple-element.61.after), custom_call_target="tpu_custom_call" | custom-call | flops 8192000 | bytes 819200 | tf_op jit(solution)/shard_map/inner/pallas_call | solution.py:785
  24.0 1.2 %collective-permute-start.4 = (f32[5,8,512]{2,1,0:T(8,128)S(1)}, f32[5,8,512]{2,1,0:T(8,128)S(1)}, u32[]{:S(2)}, u32[]{:S(2)}) collective-permute-start(f32[5,8,512]{2,1,0:T(8,128)S(1)} %get-tuple-element.64), channel_id=1, source_target_pairs={{0,1},{1,0},{2,3},{3,2},{4,5},{5,4},{6,7},{7,6},{8,9},{9,8},{10,11... | collective-permute-start | bytes 245768 | tf_op jit(solution)/shard_map/ppermute | solution.py:820
  25.2 1.2 %inner.5.after.g = f32[19,8,8,512]{3,2,1,0:T(8,128)S(1)} custom-call(f32[19,8,8,512]{3,2,1,0:T(8,128)S(1)} %put.1.g.after, f32[8,8,512]{2,1,0:T(8,128)S(1)} %get-tuple-element.54.fac, f32[19,8,8,512]{3,2,1,0:T(8,128)S(1)} %put.1.g.after), custom_call_target="tpu_custom_call" | custom-call | flops 8192000 | bytes 819200 | tf_op jit(solution)/shard_map/inner/pallas_call | solution.py:785
  26.4 5.1 %collective-permute-done.4.halo = f32[5,8,512]{2,1,0:T(8,128)S(1)} collective-permute-done((f32[5,8,512]{2,1,0:T(8,128)S(1)}, f32[5,8,512]{2,1,0:T(8,128)S(1)}, u32[]{:S(2)}, u32[]{:S(2)}) %collective-permute-start.4) | collective-permute-done | bytes 81952 | tf_op jit(solution)/shard_map/ppermute | solution.py:820
  32.0 0.5 inner_speed.1.after.u
  33.4 2.9 %collective-permute-done.5.halo.halo0 = f32[5,8,512]{2,1,0:T(8,128)S(1)} collective-permute-done((f32[5,8,512]{2,1,0:T(8,128)S(1)}, f32[5,8,512]{2,1,0:T(8,128)S(1)}, u32[]{:S(2)}, u32[]{:S(2)}) %collective-permute-start.5) | collective-permute-done | bytes 81952 | tf_op jit(solution)/shard_map/ppermute | solution.py:820
  36.9 2.9 %collective-permute-start.7 = (f32[3,8,512]{2,1,0:T(8,128)S(1)}, f32[3,8,512]{2,1,0:T(8,128)S(1)}, u32[]{:S(2)}, u32[]{:S(2)}) collective-permute-start(f32[3,8,512]{2,1,0:T(8,128)S(1)} %get-tuple-element.71.after), channel_id=1, source_target_pairs={{0,31},{1,2},{2,1},{3,4},{4,3},{5,6},{6,5},{7,8},{8,7},{9,10},{10,... | collective-permute-start | bytes 147464 | tf_op jit(solution)/shard_map/ppermute | solution.py:820
  40.4 0.4 collective-permute-done.6.there
  41.1 1.9 %final.1 = (f32[19,256,128]{2,1,0:T(8,128)}, f32[8,128]{1,0:T(8,128)S(1)}) custom-call(f32[19,8,8,512]{3,2,1,0:T(8,128)S(1)} %get-tuple-element.66.g, f32[8,8,512]{2,1,0:T(8,128)S(1)} %get-tuple-element.54.fac, f32[5,8,512]{2,1,0:T(8,128)S(1)} %collective-permute-done.5.halo.halo0, f32[5,8,512]{2,1,0:T(8,128)S(1)} %get-tuple-element.68.halo.halo1, ...), custom_call_target="tpu_custom_call" | custom-call | flops 13107200 | bytes 1310720 | tf_op jit(solution)/shard_map/final/pallas_call | solution.py:785
  43.0 1.6 %collective-permute-done.7.there = f32[3,8,512]{2,1,0:T(8,128)S(1)} collective-permute-done((f32[3,8,512]{2,1,0:T(8,128)S(1)}, f32[3,8,512]{2,1,0:T(8,128)S(1)}, u32[]{:S(2)}, u32[]{:S(2)}) %collective-permute-start.7) | collective-permute-done | bytes 49184 | tf_op jit(solution)/shard_map/ppermute | solution.py:820
  45.0 1.0 %collective-permute-start.9 = (f32[2,4,16,128]{3,2,1,0:T(8,128)S(1)}, f32[2,4,16,128]{3,2,1,0:T(8,128)S(1)}, u32[]{:S(2)}, u32[]{:S(2)}) collective-permute-start(f32[2,4,16,128]{3,2,1,0:T(8,128)S(1)} %get-tuple-element.81), channel_id=1, source_target_pairs={{0,3},{1,2},{2,1},{3,0},{4,7},{5,6},{6,5},{7,4},{8,11},{9,10},{10,... | collective-permute-start | bytes 196616 | tf_op jit(solution)/shard_map/ppermute | solution.py:931
  46.1 2.4 %collective-permute-start.10 = (f32[2,4,16,128]{3,2,1,0:T(8,128)S(1)}, f32[2,4,16,128]{3,2,1,0:T(8,128)S(1)}, u32[]{:S(2)}, u32[]{:S(2)}) collective-permute-start(f32[2,4,16,128]{3,2,1,0:T(8,128)S(1)} %get-tuple-element.82), channel_id=1, source_target_pairs={{0,1},{1,0},{2,3},{3,2},{4,5},{5,4},{6,7},{7,6},{8,9},{9,8},{10,11... | collective-permute-start | bytes 196616 | tf_op jit(solution)/shard_map/ppermute | solution.py:931
  48.5 2.9 %collective-permute-done.8.refs_1_ = f32[2,4,16,128]{3,2,1,0:T(8,128)S(1)} collective-permute-done((f32[2,4,16,128]{3,2,1,0:T(8,128)S(1)}, f32[2,4,16,128]{3,2,1,0:T(8,128)S(1)}, u32[]{:S(2)}, u32[]{:S(2)}) %collective-permute-start.8) | collective-permute-done | bytes 65568 | tf_op jit(solution)/shard_map/ppermute | solution.py:931
  51.4 0.5 collective-permute-done.10.refs_3_
  51.9 0.8 %gather.1 = (f32[4,4,16,128]{3,2,1,0:T(8,128)}, f32[4,4,16,128]{3,2,1,0:T(8,128)}) custom-call(f32[2,4,16,128]{3,2,1,0:T(8,128)S(1)} %get-tuple-element.79.refs_0_, f32[2,4,16,128]{3,2,1,0:T(8,128)S(1)} %collective-permute-done.8.refs_1_, f32[2,4,16,128]{3,2,1,0:T(8,128)S(1)} %collective-permute-done.9.refs_2_, ...), custom_call_target="tpu_custom_call" | custom-call | flops 327680 | bytes 32768 | tf_op jit(solution)/shard_map/gather/pallas_call | solution.py:785
  (21 shorter events, 4.0 us)
Async XLA Ops:
  2.9 17.6 %collective-permute-start = (f32[18,8,512]{2,1,0:T(8,128)S(1)}, f32[18,8,512]{2,1,0:T(8,128)S(1)}, u32[]{:S(2)}, u32[]{:S(2)}) collective-permute-start(f32[18,8,512]{2,1,0:T(8,128)S(1)} %get-tuple-element.50.after), channel_id=1, source_target_pairs={{0,31},{1,2},{2,1},{3,4},{4,3},{5,6},{6,5},{7,8},{8,7},{9,10},{10,... | collective-permute-start | bytes 884744 | tf_op jit(solution)/shard_map/ppermute | solution.py:820
  9.7 9.0 %collective-permute-start.1 = (f32[8,8,512]{2,1,0:T(8,128)S(1)}, f32[8,8,512]{2,1,0:T(8,128)S(1)}, u32[]{:S(2)}, u32[]{:S(2)}) collective-permute-start(f32[8,8,512]{2,1,0:T(8,128)S(1)} %get-tuple-element.55), channel_id=1, source_target_pairs={{0,1},{1,0},{2,3},{3,2},{4,5},{5,4},{6,7},{7,6},{8,9},{9,8},{10,11... | collective-permute-start | bytes 393224 | tf_op jit(solution)/shard_map/ppermute | solution.py:820
  19.0 4.8 %collective-permute-start.2 = (f32[5,8,512]{2,1,0:T(8,128)S(1)}, f32[5,8,512]{2,1,0:T(8,128)S(1)}, u32[]{:S(2)}, u32[]{:S(2)}) collective-permute-start(f32[5,8,512]{2,1,0:T(8,128)S(1)} %get-tuple-element.58.after), channel_id=1, source_target_pairs={{0,1},{1,0},{2,3},{3,2},{4,5},{5,4},{6,7},{7,6},{8,9},{9,8},{10,11... | collective-permute-start | bytes 245768 | tf_op jit(solution)/shard_map/ppermute | solution.py:820
  21.1 11.6 %collective-permute-start.3 = (f32[14,8,512]{2,1,0:T(8,128)S(1)}, f32[14,8,512]{2,1,0:T(8,128)S(1)}, u32[]{:S(2)}, u32[]{:S(2)}) collective-permute-start(f32[14,8,512]{2,1,0:T(8,128)S(1)} %get-tuple-element.61.after), channel_id=1, source_target_pairs={{0,31},{1,2},{2,1},{3,4},{4,3},{5,6},{6,5},{7,8},{8,7},{9,10},{10,... | collective-permute-start | bytes 688136 | tf_op jit(solution)/shard_map/ppermute | solution.py:820
  24.0 7.6 %collective-permute-start.4 = (f32[5,8,512]{2,1,0:T(8,128)S(1)}, f32[5,8,512]{2,1,0:T(8,128)S(1)}, u32[]{:S(2)}, u32[]{:S(2)}) collective-permute-start(f32[5,8,512]{2,1,0:T(8,128)S(1)} %get-tuple-element.64), channel_id=1, source_target_pairs={{0,1},{1,0},{2,3},{3,2},{4,5},{5,4},{6,7},{7,6},{8,9},{9,8},{10,11... | collective-permute-start | bytes 245768 | tf_op jit(solution)/shard_map/ppermute | solution.py:820
  31.8 4.5 %collective-permute-start.5 = (f32[5,8,512]{2,1,0:T(8,128)S(1)}, f32[5,8,512]{2,1,0:T(8,128)S(1)}, u32[]{:S(2)}, u32[]{:S(2)}) collective-permute-start(f32[5,8,512]{2,1,0:T(8,128)S(1)} %get-tuple-element.67), channel_id=1, source_target_pairs={{0,1},{1,0},{2,3},{3,2},{4,5},{5,4},{6,7},{7,6},{8,9},{9,8},{10,11... | collective-permute-start | bytes 245768 | tf_op jit(solution)/shard_map/ppermute | solution.py:820
  36.6 4.2 %collective-permute-start.6 = (f32[3,8,512]{2,1,0:T(8,128)S(1)}, f32[3,8,512]{2,1,0:T(8,128)S(1)}, u32[]{:S(2)}, u32[]{:S(2)}) collective-permute-start(f32[3,8,512]{2,1,0:T(8,128)S(1)} %get-tuple-element.75), channel_id=1, source_target_pairs={{0,1},{1,0},{2,3},{3,2},{4,5},{5,4},{6,7},{7,6},{8,9},{9,8},{10,11... | collective-permute-start | bytes 147464 | tf_op jit(solution)/shard_map/ppermute | solution.py:820
  36.9 7.7 %collective-permute-start.7 = (f32[3,8,512]{2,1,0:T(8,128)S(1)}, f32[3,8,512]{2,1,0:T(8,128)S(1)}, u32[]{:S(2)}, u32[]{:S(2)}) collective-permute-start(f32[3,8,512]{2,1,0:T(8,128)S(1)} %get-tuple-element.71.after), channel_id=1, source_target_pairs={{0,31},{1,2},{2,1},{3,4},{4,3},{5,6},{6,5},{7,8},{8,7},{9,10},{10,... | collective-permute-start | bytes 147464 | tf_op jit(solution)/shard_map/ppermute | solution.py:820
  45.0 6.4 %collective-permute-start.8 = (f32[2,4,16,128]{3,2,1,0:T(8,128)S(1)}, f32[2,4,16,128]{3,2,1,0:T(8,128)S(1)}, u32[]{:S(2)}, u32[]{:S(2)}) collective-permute-start(f32[2,4,16,128]{3,2,1,0:T(8,128)S(1)} %get-tuple-element.80), channel_id=1, source_target_pairs={{0,2},{1,3},{2,0},{3,1},{4,6},{5,7},{6,4},{7,5},{8,10},{9,11},{10,... | collective-permute-start | bytes 196616 | tf_op jit(solution)/shard_map/ppermute | solution.py:931
  45.0 6.3 %collective-permute-start.9 = (f32[2,4,16,128]{3,2,1,0:T(8,128)S(1)}, f32[2,4,16,128]{3,2,1,0:T(8,128)S(1)}, u32[]{:S(2)}, u32[]{:S(2)}) collective-permute-start(f32[2,4,16,128]{3,2,1,0:T(8,128)S(1)} %get-tuple-element.81), channel_id=1, source_target_pairs={{0,3},{1,2},{2,1},{3,0},{4,7},{5,6},{6,5},{7,4},{8,11},{9,10},{10,... | collective-permute-start | bytes 196616 | tf_op jit(solution)/shard_map/ppermute | solution.py:931
  46.1 5.8 %collective-permute-start.10 = (f32[2,4,16,128]{3,2,1,0:T(8,128)S(1)}, f32[2,4,16,128]{3,2,1,0:T(8,128)S(1)}, u32[]{:S(2)}, u32[]{:S(2)}) collective-permute-start(f32[2,4,16,128]{3,2,1,0:T(8,128)S(1)} %get-tuple-element.82), channel_id=1, source_target_pairs={{0,1},{1,0},{2,3},{3,2},{4,5},{5,4},{6,7},{7,6},{8,9},{9,8},{10,11... | collective-permute-start | bytes 196616 | tf_op jit(solution)/shard_map/ppermute | solution.py:931

commit v4 on v3

--- a/solution.py
+++ b/solution.py
@@ -154,22 +154,14 @@
     post = collide([pop[q, at, :] for q in range(19)], fc)
     for q in range(19):
         row[q, :, cut(c)] = post[q]
-    return post, fc
-
-
-def start_static(tiles, up, conc, poro, send, n):
-    x, beside = jnp.where(up, SUBS - 1, 0), jnp.where(up, SUBS - 2, 1)
-    for c in range(tiles):
-        send[n, :, cut(c)] = conc[strided(tiles, c, x), :]
-        send[n + 1, :, cut(c)] = conc[strided(tiles, c, beside), :]
-        send[n + 2, :, cut(c)] = poro[strided(tiles, c, x), :]
+    return fc
 
 
 def look_ahead(tiles, halves, up, edge, beside, send):
     lane, sub = iotas()
     toward, back = (UP, DOWN) if up else (DOWN, UP)
     for c in range(tiles):
-        sums = [None] * 4
+        sums = [None] * 3
         for q in range(19):
             if q in back:
                 continue
@@ -178,16 +170,34 @@
             else:
                 f = pull(beside if q in toward else edge, q, c, tiles, halves, lane, sub)
                 f = jnp.where(f != f, edge(OPP[q], c), f)
-            for k, e in enumerate((1, *DIRS[q])):
-                if e:
-                    t = f if e > 0 else -f
-                    sums[k] = t if sums[k] is None else sums[k] + t
             if q in toward:
                 i = toward.index(q)
                 send[i, :, cut(c)] = edge(q, c)
                 send[5 + i, :, cut(c)] = f
-        for k in range(4):
+            else:
+                for k, e in enumerate((1, *DIRS[q][1:])):
+                    if e:
+                        t = f if e > 0 else -f
+                        sums[k] = t if sums[k] is None else sums[k] + t
+        for k in range(3):
             send[10 + k, :, cut(c)] = sums[k]
+
+
+def start_rows(tiles, halves, chain, pop, phase, row, send, beside, ready=None):
+    up = upper(chain)
+    x, inwards = jnp.where(up, SUBS - 1, 0), jnp.where(up, SUBS - 2, 1)
+    for c in range(tiles):
+        if ready is not None:
+            ready(c)
+        send[13, :, cut(c)] = start_row(tiles, pop, phase, x, row, c)
+        start_row(tiles, pop, phase, inwards, beside, c)
+
+    def side(up):
+        look_ahead(
+            tiles, halves, up, lambda q, c: row[q, :, cut(c)], lambda q, c: beside[q, :, cut(c)], send
+        )
+
+    by_side(chain, side)
 
 
 def first_kernel(
@@ -204,35 +214,15 @@
     small[0].start()
     for copy in large + small[1:]:
         copy.start()
+    small[0].wait()
     flat = pop.reshape(pop.shape[0], SUBS * tiles * SUBS, LANES)
-    up = upper(1)
-    x, inwards = jnp.where(up, SUBS - 1, 0), jnp.where(up, SUBS - 2, 1)
-    small[0].wait()
-    for c in range(tiles):
-        large[c].wait()
-        _, fc = start_row(tiles, flat, phase, x, row, c)
-        send[14, :, cut(c)] = fc
-        start_row(tiles, flat, phase, inwards, beside, c)
-
-    def side(up):
-        look_ahead(
-            tiles, halves, up, lambda q, c: row[q, :, cut(c)], lambda q, c: beside[q, :, cut(c)], send
-        )
-
-    by_side(1, side)
+    start_rows(tiles, halves, 1, flat, phase, row, send, beside, ready=lambda c: large[c].wait())
     for copy in small[1:]:
         copy.wait()
-    start_static(tiles, up, conc, poro, send, 15)
-
-
-def second_kernel(tiles, pop, phase, conc, poro, after, row, send):
-    up = upper(0)
-    x = jnp.where(up, SUBS - 1, 0)
-    for c in range(tiles):
-        post, _ = start_row(tiles, pop, phase, x, row, c)
-        for i in range(5):
-            send[i, :, cut(c)] = jnp.where(up, post[UP[i]], post[DOWN[i]])
-    start_static(tiles, up, conc, poro, send, 5)
+
+
+def second_kernel(tiles, halves, pop, phase, after, row, send, beside):
+    start_rows(tiles, halves, 0, pop, phase, row, send, beside)
 
 
 def merge_rows(out, row0, row1, count):
@@ -294,23 +284,6 @@
                 open_ends[k, z * halves + h : z * halves + h + 1, :] = line.astype(F32)
 
 
-def edge_kernel(tiles, halves, chain, g, fac, halo, after, row, send):
-    rows = g.shape[1]
-    lane, sub = iotas()
-
-    def side(up):
-        x = rows - 1 if up else 0
-        lo, hi, place = (None, halo, "last") if up else (halo, None, "first")
-        for c in range(tiles):
-            post = collide(stream(g, lo, hi, x, c, tiles, halves, lane, sub, place), fac[x, :, cut(c)])
-            for q in range(19):
-                row[q, :, cut(c)] = post[q]
-            for i, q in enumerate(UP if up else DOWN):
-                send[i, :, cut(c)] = post[q]
-
-    by_side(chain, side)
-
-
 def inner_kernel(tiles, halves, g, fac, after, out):
     rows = g.shape[1]
     lane, sub = iotas()
@@ -330,7 +303,7 @@
     merge_rows(out, row0, row1, 19)
 
 
-def arrive_kernel(tiles, halves, g, fac, halo, still, row0, after, inner, out, ghost):
+def arrive_kernel(tiles, halves, chain, g, fac, halo, first_halo, after, inner, out, ghost):
     rows = g.shape[1]
     lane, sub = iotas()
 
@@ -338,21 +311,23 @@
         x = rows - 1 if up else 0
         lo, hi, place = (None, halo, "last") if up else (halo, None, "first")
         toward, back = (DOWN, UP) if up else (UP, DOWN)
-        for q in range(19):
-            out[q, rows - 1 - x] = row0[q]
         for c in range(tiles):
             post = collide(stream(g, lo, hi, x, c, tiles, halves, lane, sub, place), fac[x, :, cut(c)])
             for q in range(19):
                 out[q, x, :, cut(c)] = post[q]
-            sums = [halo[10 + k, :, cut(c)] for k in range(4)]
+            near = [halo[5 + i, :, cut(c)] for i in range(5)]
+            sums = [halo[10, :, cut(c)], None, halo[11, :, cut(c)], halo[12, :, cut(c)]]
+            known = list(zip(toward, near))
             for i, q in enumerate(back):
                 f = pull(lambda q, cc: g[q, x, :, cut(cc)], q, c, tiles, halves, lane, sub)
-                f = jnp.where(f != f, halo[i, :, cut(c)], f)
+                known.append((q, jnp.where(f != f, halo[i, :, cut(c)], f)))
+            for q, f in known:
                 for k, e in enumerate((1, *DIRS[q])):
                     if e:
-                        sums[k] = sums[k] + f if e > 0 else sums[k] - f
+                        t = f if e > 0 else -f
+                        sums[k] = t if sums[k] is None else sums[k] + t
             rho = sums[0]
-            inv = still[14, :, cut(c)] / rho
+            inv = first_halo[13, :, cut(c)] / rho
             v = [j * inv for j in sums[1:]]
             base = np.float32(1.0) - (v[0] * v[0] + v[1] * v[1] + v[2] * v[2]) * np.float32(1.0 / 6)
             for i, q in enumerate(toward):
@@ -363,12 +338,12 @@
                         along = t if along is None else along + t
                 weight = np.float32(1.25 / 18 if sum(map(abs, DIRS[q])) == 1 else 1.25 / 36)
                 feq = (rho * weight) * (base + along * (along * np.float32(0.5) + np.float32(1.0)))
-                ghost[i, :, cut(c)] = feq - halo[5 + i, :, cut(c)] * np.float32(0.25)
-
-    by_side(1, side)
-
-
-def far_kernel(tiles, halves, g, fac, halo, row, send, beside):
+                ghost[i, :, cut(c)] = feq - near[i] * np.float32(0.25)
+
+    by_side(chain, side)
+
+
+def far_kernel(tiles, halves, chain, g, fac, halo, slabs, after, row, send, beside):
     rows = g.shape[1]
     lane, sub = iotas()
 
@@ -384,8 +359,9 @@
         look_ahead(
             tiles, halves, up, lambda q, c: row[q, :, cut(c)], lambda q, c: beside[q, :, cut(c)], send
         )
-
-    by_side(1, side)
+        send[13] = slabs[0, x]
+
+    by_side(chain, side)
 
 
 def speed(f, fc):
@@ -601,38 +577,37 @@
             write(cs.at[k, r - 2], v)
 
 
-def static_readers(ends, up, slabs, still, base, flags):
+def static_readers(ends, up, slabs, halo, there, flags):
     rows = slabs.shape[1]
     first, last = ends_of(*ends)
 
     def conc(r):
-        if r < 0:
-            return [jnp.where(first, ZERO, t) for t in read(still.at[base - 1 - r])]
-        if r >= rows:
-            return pick(last, read(slabs.at[0, rows - 1]), read(still.at[base + r - rows]))
-        return read(slabs.at[0, r])
+        if 0 <= r < rows:
+            return read(slabs.at[0, r])
+        beyond = read(halo.at[13] if r in (-1, rows) else there.at[3])
+        return pick(last, read(slabs.at[0, rows - 1]), beyond) if up else [jnp.where(first, ZERO, t) for t in beyond]
 
     def poro(r):
         if 0 <= r < rows:
             return read(slabs.at[2, r])
-        return pick(last if up else first, read(flags.at[1 if up else 0]), read(still.at[base + 2]))
+        return pick(last if up else first, read(flags.at[1 if up else 0]), read(there.at[4]))
 
     return conc, poro
 
 
-def rim_kernel(tiles, halves, ends, chain, base, g, fac, halo, u, slabs, still, flags, after, ue, cs, send):
+def rim_kernel(tiles, halves, ends, chain, g, fac, ghost, u, slabs, halo, after, ue, cs, send):
     rows = g.shape[1]
     lane, sub = iotas()
 
     def side(up):
         x, beside = (rows - 1, rows - 2) if up else (0, 1)
-        lo, hi, place = (None, halo, "last") if up else (halo, None, "first")
+        lo, hi, place = (None, ghost, "last") if up else (ghost, None, "first")
         for n, (at, where) in enumerate(((x, place), (beside, "mid"))):
             for c in range(tiles):
                 f = stream(g, lo, hi, at, c, tiles, halves, lane, sub, where)
                 for i, v in enumerate(speed(f, fac[at, :, cut(c)])):
                     ue[n, i, :, cut(c)] = v
-        conc, poro = static_readers(ends, up, slabs, still, base, flags)
+        conc, poro = static_readers(ends, up, slabs, halo, None, None)
 
         def vel(k, r):
             return read(ue.at[0 if r == x else 1, k] if r in (x, beside) else u.at[k, r - 2])
@@ -648,6 +623,8 @@
                 write(cs.at[i, k], new[k])
             write(send.at[1 + i], new[0])
         send[0] = ue[0, 1]
+        send[3] = slabs[0, beside]
+        send[4] = slabs[2, x]
 
     by_side(chain, side)
 
@@ -681,7 +658,7 @@
 
 
 def late_kernel(
-    tiles, halves, ends, chain, base, slabs, u, ue, inner, rim, still, flags, there, after, out
+    tiles, halves, ends, chain, slabs, u, ue, inner, rim, halo, flags, there, after, out
 ):
     rows = slabs.shape[1]
     first, last = ends_of(*ends)
@@ -690,7 +667,7 @@
         x = rows - 1 if up else 0
         beyond = rows if up else -1
         ghost = last if up else first
-        conc, poro = static_readers(ends, up, slabs, still, base, flags)
+        conc, poro = static_readers(ends, up, slabs, halo, there, flags)
 
         def vel(k, r):
             if r == beyond:
@@ -776,7 +753,7 @@
         copy.wait()
 
 
-def call(kernel, out_shape, args, scratch=(), hbm=(), free=(), hbm_out=(), name=None, flops=0, aliases=None):
+def call(kernel, out_shape, args, scratch=(), hbm=(), free=(), hbm_out=(), name=None, aliases=None):
     def spec(i, hbm, free=()):
         return pl.BlockSpec(memory_space=pltpu.HBM if i in hbm else pl.ANY if i in free else pltpu.VMEM)
 
@@ -791,7 +768,7 @@
         name=name,
         input_output_aliases=aliases or {},
         compiler_params=pltpu.CompilerParams(vmem_limit_bytes=VMEM_LIMIT),
-        cost_estimate=pl.CostEstimate(flops=flops, bytes_accessed=flops // 10, transcendentals=0),
+        cost_estimate=pl.CostEstimate(flops=1024, bytes_accessed=1024, transcendentals=0),
     )(*args)
     return out[0] if single else out
 
@@ -808,7 +785,6 @@
         [(i, i ^ 1) for i in range(strips)],
         [(i, (i + 1 if i % 2 else i - 1) % strips) for i in range(strips)],
     )
-    cells = rows * SUBS * length
     slab = (SUBS, length)
     ends = (parts, strips)
     run = width // LANES * SUBS // parts
@@ -828,102 +804,105 @@
         functools.partial(first_kernel, tiles, halves),
         (
             hold(*chunks.shape), hold(*flat, dtype=jnp.int32), hold(*flat), hold(*flat), hold(*flat),
-            hold(*flags.shape, dtype=jnp.int32), hold(19, *slab), hold(18, *slab),
+            hold(*flags.shape, dtype=jnp.int32), hold(19, *slab), hold(14, *slab),
         ),
         given, scratch=(pltpu.VMEM((19, *slab), F32), pltpu.SemaphoreType.DMA((tiles + 5,))),
-        hbm=range(6), name="first", flops=50 * cells,
+        hbm=range(6), name="first",
     )
     popv = popv.reshape(pop.shape)
-    halo1 = still1 = swap(1, send)
+    halo1 = head1 = swap(1, send)
     row0, send = call(
-        functools.partial(second_kernel, tiles), (hold(19, *slab), hold(8, *slab)),
-        (popv, phv, cov, pov, send), free=(4,), name="second", flops=30 * cells,
-    )
-    halo0 = still0 = swap(0, send)
+        functools.partial(second_kernel, tiles, halves), (hold(19, *slab), hold(14, *slab)), (popv, phv, send),
+        scratch=(pltpu.VMEM((19, *slab), F32),), free=(2,), name="second",
+    )
+    halo0 = head0 = swap(0, send)
     g, fac, start, slabs, open_ends = call(
         functools.partial(first_inner_kernel, tiles, halves),
         (
             hold(19, rows, *slab), hold(rows, *slab), hold(19, rows, *slab), hold(3, rows, *slab),
             hold(2, *slab),
         ),
-        (popv, phv, cov, nav, pov, flv, row0, row1), name="first_inner", flops=300 * cells,
-    )
+        (popv, phv, cov, nav, pov, flv, row0, row1), name="first_inner",
+    )
+
+    def inner_rows(g, after):
+        return call(
+            functools.partial(inner_kernel, tiles, halves), hold(19, rows, *slab), (g, fac, after), free=(2,),
+            name="inner",
+        )
+
+    def arrive(chain, g, halo, head, after, new):
+        return call(
+            functools.partial(arrive_kernel, tiles, halves, chain), (hold(19, rows, *slab), hold(5, *slab)),
+            (g, fac, halo, head, after, new), free=(4, 5), name=f"arrive{chain}", aliases={5: 0},
+        )
+
+    def far(chain, g, ghost, after):
+        return call(
+            functools.partial(far_kernel, tiles, halves, chain), (hold(19, *slab), hold(14, *slab)),
+            (g, fac, ghost, slabs, after), scratch=(pltpu.VMEM((19, *slab), F32),), free=(4,), name=f"far{chain}",
+        )
+
+    def rim(chain, g, ghost, halo, after):
+        return call(
+            functools.partial(rim_kernel, tiles, halves, ends, chain),
+            (hold(2, 3, *slab), hold(2, 2, *slab), hold(5, *slab)),
+            (g, fac, ghost, u, slabs, halo, after), free=(6,), name=f"rim{chain}",
+        )
+
     after = slabs
-    for step in range(1, LBM_STEPS):
-        if step % 2 == 0:
-            row1, send1 = call(
-                functools.partial(far_kernel, tiles, halves), (hold(19, *slab), hold(14, *slab)),
-                (g, fac, ghost), scratch=(pltpu.VMEM((19, *slab), F32),), name="far", flops=60 * cells,
-            )
+    for pair in range(LBM_STEPS // 2):
+        new = inner_rows(g, after)
+        if pair < LBM_STEPS // 2 - 1:
+            later, ghost1 = arrive(1, g, halo1, head1, g, new)
+            row1, send1 = far(1, later, ghost1, ghost1)
             halo1 = swap(1, send1)
-            after = send1
-        new = call(
-            functools.partial(inner_kernel, tiles, halves), hold(19, rows, *slab), (g, fac, after),
-            free=(2,), name="inner", flops=250 * cells,
-        )
-        if step == LBM_STEPS - 1:
-            u = call(
-                functools.partial(inner_speed_kernel, tiles, halves), hold(3, rows - 4, *slab), (new, fac, after),
-                free=(2,), name="inner_speed", flops=100 * cells,
-            )
-        row0, send = call(
-            functools.partial(edge_kernel, tiles, halves, 0), (hold(19, *slab), hold(5, *slab)),
-            (g, fac, halo0, new), free=(3,), name="edge0", flops=30 * cells,
-        )
-        halo0 = swap(0, send)
-        if step % 2 == 0:
+            later, ghost0 = arrive(0, g, halo0, head0, send1, later)
+            row0, send0 = far(0, later, ghost0, ghost0)
+            halo0 = swap(0, send0)
+            new = inner_rows(later, send0)
             g = call(
-                put_kernel, hold(19, rows, *slab), (new, row0, row1), name="put", flops=10 * cells,
-                aliases={0: 0},
+                put_kernel, hold(19, rows, *slab), (new, row0, row1), name="put", aliases={0: 0}, free=(0,)
             )
             after = g
-        else:
-            g, ghost = call(
-                functools.partial(arrive_kernel, tiles, halves), (hold(19, rows, *slab), hold(5, *slab)),
-                (g, fac, halo1, still1, row0, u if step == LBM_STEPS - 1 else send, new), free=(5,),
-                name="arrive", flops=60 * cells, aliases={6: 0},
-            )
-            after = ghost
-    ue1, rim1, send = call(
-        functools.partial(rim_kernel, tiles, halves, ends, 1, 15),
-        (hold(2, 3, *slab), hold(2, 2, *slab), hold(3, *slab)),
-        (g, fac, ghost, u, slabs, still1, open_ends, u), free=(7,), name="rim1", flops=50 * cells,
-    )
-    there1 = swap(1, send)
-    ue0, rim0, send = call(
-        functools.partial(rim_kernel, tiles, halves, ends, 0, 5),
-        (hold(2, 3, *slab), hold(2, 2, *slab), hold(3, *slab)),
-        (g, fac, halo0, u, slabs, still0, open_ends, send), free=(7,), name="rim0", flops=50 * cells,
-    )
-    there0 = swap(0, send)
+    u = call(
+        functools.partial(inner_speed_kernel, tiles, halves), hold(3, rows - 4, *slab), (new, fac, new),
+        free=(2,), name="inner_speed",
+    )
+    later, ghost1 = arrive(1, g, halo1, head1, u, new)
+    ue1, rim1, send1 = rim(1, later, ghost1, halo1, ghost1)
+    there1 = swap(1, send1)
+    g, ghost0 = arrive(0, g, halo0, head0, send1, later)
+    ue0, rim0, send0 = rim(0, g, ghost0, halo0, ghost0)
+    there0 = swap(0, send0)
     inner = call(
         functools.partial(early_kernel, tiles, halves), hold(2, rows - 4, *slab), (slabs, u, ue0, ue1),
-        name="early", flops=60 * cells,
+        name="early",
     )
     mid = call(
         functools.partial(middle_kernel, tiles, halves), hold(rows - 6, *slab), (slabs, u, inner, rim0, rim1),
-        name="middle", flops=40 * cells,
-    )
-    late0 = call(
-        functools.partial(late_kernel, tiles, halves, ends, 0, 5), hold(4, *slab),
-        (slabs, u, ue0, inner, rim0, still0, open_ends, there0, mid), free=(8,), name="late0", flops=30 * cells,
+        name="middle",
     )
     out, token = call(
         functools.partial(final_kernel, tiles, halves),
         (jax.ShapeDtypeStruct((19, *flat), F32), hold(SUBS, LANES)),
-        (g, fac, halo0, ghost, start, late0),
+        (g, fac, ghost0, ghost1, start, mid),
         scratch=(pltpu.VMEM((19, *flat), F32), pltpu.SemaphoreType.DMA((19,))),
-        free=(5,), hbm_out=(0,), name="final", flops=400 * cells,
+        free=(5,), hbm_out=(0,), name="final",
     )
     late1 = call(
-        functools.partial(late_kernel, tiles, halves, ends, 1, 15), hold(4, *slab),
-        (slabs, u, ue1, inner, rim1, still1, open_ends, there1, token), free=(8,), name="late1", flops=30 * cells,
+        functools.partial(late_kernel, tiles, halves, ends, 1), hold(4, *slab),
+        (slabs, u, ue1, inner, rim1, halo1, open_ends, there1, token), free=(8,), name="late1",
+    )
+    late0 = call(
+        functools.partial(late_kernel, tiles, halves, ends, 0), hold(4, *slab),
+        (slabs, u, ue0, inner, rim0, halo0, open_ends, there0, late1), free=(8,), name="late0",
     )
     block = (2, layers, run, LANES)
     blocks = call(
         functools.partial(deal_kernel, tiles, halves, parts), tuple(hold(*block) for _ in range(parts)),
         (inner, rim0, rim1, late0, late1, mid),
-        scratch=(pltpu.VMEM((parts, *block), F32),), name="deal", flops=20 * cells,
+        scratch=(pltpu.VMEM((parts, *block), F32),), name="deal",
     )
     order = [0, *range(2, parts), 1]
     came = [blocks[0]]
@@ -933,7 +912,7 @@
     conc_out, napl_out = call(
         functools.partial(gather_kernel, parts, order),
         (jax.ShapeDtypeStruct(tile, F32), jax.ShapeDtypeStruct(tile, F32)),
-        came, scratch=(pltpu.SemaphoreType.DMA((2, parts)),), hbm_out=(0, 1), name="gather", flops=10 * cells,
+        came, scratch=(pltpu.SemaphoreType.DMA((2, parts)),), hbm_out=(0, 1), name="gather",
     )
     shape = (layers, rows * parts, width // parts)
 

time: 52.8 us -> 46.9 us (0.89)
  waiting for transfers between devices: 19.9 us -> 10.8 us
  starting transfers between devices: 17.5 us -> 20 us
  Pallas kernels: 14.5 us -> 15.2 us
    ppermute x8 -> x6, waiting for transfers between devices: 16.5 us -> 6.02 us  [swap(): return lax.ppermute(array, both, pairs[chain])]
    ppermute x8 -> x6, starting transfers between devices: 13.9 us -> 16.4 us  [swap(): return lax.ppermute(array, both, pairs[chain])]
    ppermute x3, waiting for transfers between devices: 3.37 us -> 4.76 us  [local(): lax.ppermute(blocks[k], 'narrow', [(i, i ^ k) for i in range(parts)])]
    pallas_call x23, Pallas kernels: 14.5 us -> 15.2 us  [call(): pl.pallas_call(kernel, out_shape=shapes, in_specs=[spec(i, hbm, free) for...]
  transfers between devices with their start and end apart: 11 -> 9, of which waited for: 8 -> 7; matrix products, arithmetic and copies ran while one was open for 0% -> 0% of each run, Pallas kernels for 20% -> 25%
where the time goes in v4:
time: 46.9 us; the launch traced here: 46.7 us
  starting transfers between devices  20 us (43%)
  Pallas kernels  15.2 us (32%)
  waiting for transfers between devices  10.8 us (23%)
  between operations  0.81 us (2%)
    ppermute x6, starting transfers between devices, swap(): return lax.ppermute(array, both, pairs[chain])  16.4 us
    pallas_call x23, Pallas kernels, call(): pl.pallas_call(kernel, out_shape=shapes, in_specs=[spec(i, hbm, free) for...  15.2 us
    ppermute x6, waiting for transfers between devices, swap(): return lax.ppermute(array, both, pairs[chain])  6.02 us
    ppermute x3, waiting for transfers between devices, local(): lax.ppermute(blocks[k], 'narrow', [(i, i ^ k) for i in range(parts)])  4.76 us
    ppermute x3, starting transfers between devices, local(): lax.ppermute(blocks[k], 'narrow', [(i, i ^ k) for i in range(parts)])  3.55 us
  transfers between devices with their start and end apart: 9, of which 7 were waited for; matrix products, arithmetic and copies ran while one was open for 0% of the time, Pallas kernels for 25%

profile of v4, /device:TPU:0, one launch (start us, length us, event | category | flops | bytes accessed | tf_op | source)
XLA Modules:
  0.0 46.7 jit_solution(7054471575550781183)
XLA Ops:
  0.6 2.2 %first.1 = (f32[19,8,4,8,128]{4,3,2,1,0:T(8,128)S(1)}, s32[256,128]{1,0:T(8,128)S(1)}, f32[256,128]{1,0:T(8,128)S(1)}, f32[256,128]{1,0:T(8,128)S(1)}, f32[256,1...) custom-call(f32[19,8,4,8,128]{4,3,2,1,0:T(8,128)} %bitcast.43, ...), custom_call_target="tpu_custom_call" | custom-call | flops 1024 | bytes 1024 | tf_op jit(solution)/shard_map/first/pallas_call | solution.py:762
  2.8 6.4 %collective-permute-start.1 = (f32[14,8,512]{2,1,0:T(8,128)S(1)}, f32[14,8,512]{2,1,0:T(8,128)S(1)}, u32[]{:S(2)}, u32[]{:S(2)}) collective-permute-start(f32[14,8,512]{2,1,0:T(8,128)S(1)} %get-tuple-element.50.after), channel_id=1, source_target_pairs={{0,31},{1,2},{2,1},{3,4},{4,3},{5,6},{6,5},{7,8},{8,7},{9,10},{10,... | collective-permute-start | bytes 688136 | tf_op jit(solution)/shard_map/ppermute | solution.py:796
  9.3 0.9 %second.1 = (f32[19,8,512]{2,1,0:T(8,128)S(1)}, f32[14,8,512]{2,1,0:T(8,128)S(1)}) custom-call(f32[19,256,128]{2,1,0:T(8,128)S(1)} %bitcast.41, s32[256,128]{1,0:T(8,128)S(1)} %get-tuple-element.45.phase, f32[14,8,512]{2,1,0:T(8,128)S(1)} %get-tuple-element.50.after), custom_call_target="tpu_custom_call" | custom-call | flops 1024 | bytes 1024 | tf_op jit(solution)/shard_map/second/pallas_call | solution.py:762
  10.2 1.5 %first_inner.1 = (f32[19,8,8,512]{3,2,1,0:T(8,128)S(1)}, f32[8,8,512]{2,1,0:T(8,128)S(1)}, f32[19,8,8,512]{3,2,1,0:T(8,128)S(1)}, f32[3,8,8,512]{3,2,1,0:T(8,128)S(1)}, f32[2,8,512]{2,1,0:T(8,128)S(1)}) custom-call(f32[19,256,128]{2,1,0:T(8,128)S(1)} %bitcast.42, s32[256,128]{1,0:T(8,128)S(1)} %get-tuple-element.45.phase, ...), custom_call_target="tpu_custom_call" | custom-call | flops 1024 | bytes 1024 | tf_op jit(solution)/shard_map/first_inner/pallas_call | solution.py:762
  11.7 1.2 %inner.3 = f32[19,8,8,512]{3,2,1,0:T(8,128)S(1)} custom-call(f32[19,8,8,512]{3,2,1,0:T(8,128)S(1)} %get-tuple-element.53.g.after, f32[8,8,512]{2,1,0:T(8,128)S(1)} %get-tuple-element.54.fac, f32[3,8,8,512]{3,2,1,0:T(8,128)S(1)} %get-tuple-element.56.after.slabs), custom_call_target="tpu_custom_call" | custom-call | flops 1024 | bytes 1024 | tf_op jit(solution)/shard_map/inner/pallas_call | solution.py:762
  13.0 2.4 %collective-permute-done.1.halo.first_halo = f32[14,8,512]{2,1,0:T(8,128)S(1)} collective-permute-done((f32[14,8,512]{2,1,0:T(8,128)S(1)}, f32[14,8,512]{2,1,0:T(8,128)S(1)}, u32[]{:S(2)}, u32[]{:S(2)}) %collective-permute-start.1) | collective-permute-done | bytes 229408 | tf_op jit(solution)/shard_map/ppermute | solution.py:796
  15.6 0.4 far1.1
  16.0 5.6 %collective-permute-start.3 = (f32[14,8,512]{2,1,0:T(8,128)S(1)}, f32[14,8,512]{2,1,0:T(8,128)S(1)}, u32[]{:S(2)}, u32[]{:S(2)}) collective-permute-start(f32[14,8,512]{2,1,0:T(8,128)S(1)} %get-tuple-element.59.after), channel_id=1, source_target_pairs={{0,31},{1,2},{2,1},{3,4},{4,3},{5,6},{6,5},{7,8},{8,7},{9,10},{10,... | collective-permute-start | bytes 688136 | tf_op jit(solution)/shard_map/ppermute | solution.py:796
  21.8 0.4 far0.1
  22.2 0.5 %collective-permute-start.2 = (f32[14,8,512]{2,1,0:T(8,128)S(1)}, f32[14,8,512]{2,1,0:T(8,128)S(1)}, u32[]{:S(2)}, u32[]{:S(2)}) collective-permute-start(f32[14,8,512]{2,1,0:T(8,128)S(1)} %get-tuple-element.62.after), channel_id=1, source_target_pairs={{0,1},{1,0},{2,3},{3,2},{4,5},{5,4},{6,7},{7,6},{8,9},{9,8},{10,11... | collective-permute-start | bytes 688136 | tf_op jit(solution)/shard_map/ppermute | solution.py:796
  22.7 1.2 %inner.4 = f32[19,8,8,512]{3,2,1,0:T(8,128)S(1)} custom-call(f32[19,8,8,512]{3,2,1,0:T(8,128)S(1)} %get-tuple-element.60.g, f32[8,8,512]{2,1,0:T(8,128)S(1)} %get-tuple-element.54.fac, f32[14,8,512]{2,1,0:T(8,128)S(1)} %get-tuple-element.62.after), custom_call_target="tpu_custom_call" | custom-call | flops 1024 | bytes 1024 | tf_op jit(solution)/shard_map/inner/pallas_call | solution.py:762
  24.0 1.2 %inner.5.g.after = f32[19,8,8,512]{3,2,1,0:T(8,128)S(1)} custom-call(f32[19,8,8,512]{3,2,1,0:T(8,128)S(1)} %put.1.g.after, f32[8,8,512]{2,1,0:T(8,128)S(1)} %get-tuple-element.54.fac, f32[19,8,8,512]{3,2,1,0:T(8,128)S(1)} %put.1.g.after), custom_call_target="tpu_custom_call" | custom-call | flops 1024 | bytes 1024 | tf_op jit(solution)/shard_map/inner/pallas_call | solution.py:762
  25.2 0.5 %inner_speed.1.after.u = f32[3,4,8,512]{3,2,1,0:T(8,128)S(1)} custom-call(f32[19,8,8,512]{3,2,1,0:T(8,128)S(1)} %inner.5.g.after, f32[8,8,512]{2,1,0:T(8,128)S(1)} %get-tuple-element.54.fac, f32[19,8,8,512]{3,2,1,0:T(8,128)S(1)} %inner.5.g.after), custom_call_target="tpu_custom_call" | custom-call | flops 1024 | bytes 1024 | tf_op jit(solution)/shard_map/inner_speed/pallas_call | solution.py:762
  25.7 2.0 %collective-permute-done.3.halo = f32[14,8,512]{2,1,0:T(8,128)S(1)} collective-permute-done((f32[14,8,512]{2,1,0:T(8,128)S(1)}, f32[14,8,512]{2,1,0:T(8,128)S(1)}, u32[]{:S(2)}, u32[]{:S(2)}) %collective-permute-start.3) | collective-permute-done | bytes 229408 | tf_op jit(solution)/shard_map/ppermute | solution.py:796
  28.3 3.8 %collective-permute-start.5 = (f32[5,8,512]{2,1,0:T(8,128)S(1)}, f32[5,8,512]{2,1,0:T(8,128)S(1)}, u32[]{:S(2)}, u32[]{:S(2)}) collective-permute-start(f32[5,8,512]{2,1,0:T(8,128)S(1)} %get-tuple-element.67.after), channel_id=1, source_target_pairs={{0,31},{1,2},{2,1},{3,4},{4,3},{5,6},{6,5},{7,8},{8,7},{9,10},{10,... | collective-permute-start | bytes 245768 | tf_op jit(solution)/shard_map/ppermute | solution.py:796
  33.4 1.9 %final.1 = (f32[19,256,128]{2,1,0:T(8,128)}, f32[8,128]{1,0:T(8,128)S(1)}) custom-call(f32[19,8,8,512]{3,2,1,0:T(8,128)S(1)} %get-tuple-element.68.g, f32[8,8,512]{2,1,0:T(8,128)S(1)} %get-tuple-element.54.fac, f32[5,8,512]{2,1,0:T(8,128)S(1)} %get-tuple-element.69.ghost.after.halo0, f32[5,8,512]{2,1,0:T(8,128)S(1)} %get-tuple-element.66.ghost.after.halo1, ...), custom_call_target="tpu_custom_call" | custom-call | flops 1024 | bytes 1024 | tf_op jit(solution)/shard_map/final/pallas_call | solution.py:762
  35.3 0.7 %collective-permute-done.5.there = f32[5,8,512]{2,1,0:T(8,128)S(1)} collective-permute-done((f32[5,8,512]{2,1,0:T(8,128)S(1)}, f32[5,8,512]{2,1,0:T(8,128)S(1)}, u32[]{:S(2)}, u32[]{:S(2)}) %collective-permute-start.5) | collective-permute-done | bytes 81952 | tf_op jit(solution)/shard_map/ppermute | solution.py:796
  36.3 0.9 %collective-permute-done.4.there = f32[5,8,512]{2,1,0:T(8,128)S(1)} collective-permute-done((f32[5,8,512]{2,1,0:T(8,128)S(1)}, f32[5,8,512]{2,1,0:T(8,128)S(1)}, u32[]{:S(2)}, u32[]{:S(2)}) %collective-permute-start.4) | collective-permute-done | bytes 81952 | tf_op jit(solution)/shard_map/ppermute | solution.py:796
  37.6 1.8 %collective-permute-start.6 = (f32[2,4,16,128]{3,2,1,0:T(8,128)S(1)}, f32[2,4,16,128]{3,2,1,0:T(8,128)S(1)}, u32[]{:S(2)}, u32[]{:S(2)}) collective-permute-start(f32[2,4,16,128]{3,2,1,0:T(8,128)S(1)} %get-tuple-element.80), channel_id=1, source_target_pairs={{0,2},{1,3},{2,0},{3,1},{4,6},{5,7},{6,4},{7,5},{8,10},{9,11},{10,... | collective-permute-start | bytes 196616 | tf_op jit(solution)/shard_map/ppermute | solution.py:910
  39.5 1.2 %collective-permute-start.7 = (f32[2,4,16,128]{3,2,1,0:T(8,128)S(1)}, f32[2,4,16,128]{3,2,1,0:T(8,128)S(1)}, u32[]{:S(2)}, u32[]{:S(2)}) collective-permute-start(f32[2,4,16,128]{3,2,1,0:T(8,128)S(1)} %get-tuple-element.81), channel_id=1, source_target_pairs={{0,3},{1,2},{2,1},{3,0},{4,7},{5,6},{6,5},{7,4},{8,11},{9,10},{10,... | collective-permute-start | bytes 196616 | tf_op jit(solution)/shard_map/ppermute | solution.py:910
  40.6 0.6 %collective-permute-start.8 = (f32[2,4,16,128]{3,2,1,0:T(8,128)S(1)}, f32[2,4,16,128]{3,2,1,0:T(8,128)S(1)}, u32[]{:S(2)}, u32[]{:S(2)}) collective-permute-start(f32[2,4,16,128]{3,2,1,0:T(8,128)S(1)} %get-tuple-element.82), channel_id=1, source_target_pairs={{0,1},{1,0},{2,3},{3,2},{4,5},{5,4},{6,7},{7,6},{8,9},{9,8},{10,11... | collective-permute-start | bytes 196616 | tf_op jit(solution)/shard_map/ppermute | solution.py:910
  41.2 3.7 %collective-permute-done.6.refs_1_ = f32[2,4,16,128]{3,2,1,0:T(8,128)S(1)} collective-permute-done((f32[2,4,16,128]{3,2,1,0:T(8,128)S(1)}, f32[2,4,16,128]{3,2,1,0:T(8,128)S(1)}, u32[]{:S(2)}, u32[]{:S(2)}) %collective-permute-start.6) | collective-permute-done | bytes 65568 | tf_op jit(solution)/shard_map/ppermute | solution.py:910
  44.9 0.8 %collective-permute-done.7.refs_2_ = f32[2,4,16,128]{3,2,1,0:T(8,128)S(1)} collective-permute-done((f32[2,4,16,128]{3,2,1,0:T(8,128)S(1)}, f32[2,4,16,128]{3,2,1,0:T(8,128)S(1)}, u32[]{:S(2)}, u32[]{:S(2)}) %collective-permute-start.7) | collective-permute-done | bytes 65568 | tf_op jit(solution)/shard_map/ppermute | solution.py:910
  46.0 0.8 %gather.1 = (f32[4,4,16,128]{3,2,1,0:T(8,128)}, f32[4,4,16,128]{3,2,1,0:T(8,128)}) custom-call(f32[2,4,16,128]{3,2,1,0:T(8,128)S(1)} %get-tuple-element.79.refs_0_, f32[2,4,16,128]{3,2,1,0:T(8,128)S(1)} %collective-permute-done.6.refs_1_, f32[2,4,16,128]{3,2,1,0:T(8,128)S(1)} %collective-permute-done.7.refs_2_, ...), custom_call_target="tpu_custom_call" | custom-call | flops 1024 | bytes 1024 | tf_op jit(solution)/shard_map/gather/pallas_call | solution.py:762
  (17 shorter events, 3.5 us)
Async XLA Ops:
  2.8 12.5 %collective-permute-start.1 = (f32[14,8,512]{2,1,0:T(8,128)S(1)}, f32[14,8,512]{2,1,0:T(8,128)S(1)}, u32[]{:S(2)}, u32[]{:S(2)}) collective-permute-start(f32[14,8,512]{2,1,0:T(8,128)S(1)} %get-tuple-element.50.after), channel_id=1, source_target_pairs={{0,31},{1,2},{2,1},{3,4},{4,3},{5,6},{6,5},{7,8},{8,7},{9,10},{10,... | collective-permute-start | bytes 688136 | tf_op jit(solution)/shard_map/ppermute | solution.py:796
  10.2 11.4 %collective-permute-start = (f32[14,8,512]{2,1,0:T(8,128)S(1)}, f32[14,8,512]{2,1,0:T(8,128)S(1)}, u32[]{:S(2)}, u32[]{:S(2)}) collective-permute-start(f32[14,8,512]{2,1,0:T(8,128)S(1)} %get-tuple-element.55), channel_id=1, source_target_pairs={{0,1},{1,0},{2,3},{3,2},{4,5},{5,4},{6,7},{7,6},{8,9},{9,8},{10,11... | collective-permute-start | bytes 688136 | tf_op jit(solution)/shard_map/ppermute | solution.py:796
  16.0 11.7 %collective-permute-start.3 = (f32[14,8,512]{2,1,0:T(8,128)S(1)}, f32[14,8,512]{2,1,0:T(8,128)S(1)}, u32[]{:S(2)}, u32[]{:S(2)}) collective-permute-start(f32[14,8,512]{2,1,0:T(8,128)S(1)} %get-tuple-element.59.after), channel_id=1, source_target_pairs={{0,31},{1,2},{2,1},{3,4},{4,3},{5,6},{6,5},{7,8},{8,7},{9,10},{10,... | collective-permute-start | bytes 688136 | tf_op jit(solution)/shard_map/ppermute | solution.py:796
  22.2 9.9 %collective-permute-start.2 = (f32[14,8,512]{2,1,0:T(8,128)S(1)}, f32[14,8,512]{2,1,0:T(8,128)S(1)}, u32[]{:S(2)}, u32[]{:S(2)}) collective-permute-start(f32[14,8,512]{2,1,0:T(8,128)S(1)} %get-tuple-element.62.after), channel_id=1, source_target_pairs={{0,1},{1,0},{2,3},{3,2},{4,5},{5,4},{6,7},{7,6},{8,9},{9,8},{10,11... | collective-permute-start | bytes 688136 | tf_op jit(solution)/shard_map/ppermute | solution.py:796
  28.3 7.7 %collective-permute-start.5 = (f32[5,8,512]{2,1,0:T(8,128)S(1)}, f32[5,8,512]{2,1,0:T(8,128)S(1)}, u32[]{:S(2)}, u32[]{:S(2)}) collective-permute-start(f32[5,8,512]{2,1,0:T(8,128)S(1)} %get-tuple-element.67.after), channel_id=1, source_target_pairs={{0,31},{1,2},{2,1},{3,4},{4,3},{5,6},{6,5},{7,8},{8,7},{9,10},{10,... | collective-permute-start | bytes 245768 | tf_op jit(solution)/shard_map/ppermute | solution.py:796
  32.7 4.5 %collective-permute-start.4 = (f32[5,8,512]{2,1,0:T(8,128)S(1)}, f32[5,8,512]{2,1,0:T(8,128)S(1)}, u32[]{:S(2)}, u32[]{:S(2)}) collective-permute-start(f32[5,8,512]{2,1,0:T(8,128)S(1)} %get-tuple-element.77), channel_id=1, source_target_pairs={{0,1},{1,0},{2,3},{3,2},{4,5},{5,4},{6,7},{7,6},{8,9},{9,8},{10,11... | collective-permute-start | bytes 245768 | tf_op jit(solution)/shard_map/ppermute | solution.py:796
  37.6 7.3 %collective-permute-start.6 = (f32[2,4,16,128]{3,2,1,0:T(8,128)S(1)}, f32[2,4,16,128]{3,2,1,0:T(8,128)S(1)}, u32[]{:S(2)}, u32[]{:S(2)}) collective-permute-start(f32[2,4,16,128]{3,2,1,0:T(8,128)S(1)} %get-tuple-element.80), channel_id=1, source_target_pairs={{0,2},{1,3},{2,0},{3,1},{4,6},{5,7},{6,4},{7,5},{8,10},{9,11},{10,... | collective-permute-start | bytes 196616 | tf_op jit(solution)/shard_map/ppermute | solution.py:910
  39.5 6.2 %collective-permute-start.7 = (f32[2,4,16,128]{3,2,1,0:T(8,128)S(1)}, f32[2,4,16,128]{3,2,1,0:T(8,128)S(1)}, u32[]{:S(2)}, u32[]{:S(2)}) collective-permute-start(f32[2,4,16,128]{3,2,1,0:T(8,128)S(1)} %get-tuple-element.81), channel_id=1, source_target_pairs={{0,3},{1,2},{2,1},{3,0},{4,7},{5,6},{6,5},{7,4},{8,11},{9,10},{10,... | collective-permute-start | bytes 196616 | tf_op jit(solution)/shard_map/ppermute | solution.py:910
  40.6 5.3 %collective-permute-start.8 = (f32[2,4,16,128]{3,2,1,0:T(8,128)S(1)}, f32[2,4,16,128]{3,2,1,0:T(8,128)S(1)}, u32[]{:S(2)}, u32[]{:S(2)}) collective-permute-start(f32[2,4,16,128]{3,2,1,0:T(8,128)S(1)} %get-tuple-element.82), channel_id=1, source_target_pairs={{0,1},{1,0},{2,3},{3,2},{4,5},{5,4},{6,7},{7,6},{8,9},{9,8},{10,11... | collective-permute-start | bytes 196616 | tf_op jit(solution)/shard_map/ppermute | solution.py:910

commit v5 on v4

--- a/solution.py
+++ b/solution.py
@@ -389,11 +389,10 @@
     lax.fori_loop(2, rows - 2, row, 0)
 
 
-def final_kernel(tiles, halves, g, fac, halo0, halo1, start, after, out, token, buf, sems):
+def final_kernel(tiles, halves, g, fac, halo0, halo1, start, after, out, buf, sems):
     rows = g.shape[1]
     lane, sub = iotas()
     odd = upper(1)
-    token[...] = jnp.zeros(token.shape, F32)
 
     def row_of(q, x):
         at = x - DIRS[q][0]
@@ -883,16 +882,9 @@
         functools.partial(middle_kernel, tiles, halves), hold(rows - 6, *slab), (slabs, u, inner, rim0, rim1),
         name="middle",
     )
-    out, token = call(
-        functools.partial(final_kernel, tiles, halves),
-        (jax.ShapeDtypeStruct((19, *flat), F32), hold(SUBS, LANES)),
-        (g, fac, ghost0, ghost1, start, mid),
-        scratch=(pltpu.VMEM((19, *flat), F32), pltpu.SemaphoreType.DMA((19,))),
-        free=(5,), hbm_out=(0,), name="final",
-    )
     late1 = call(
         functools.partial(late_kernel, tiles, halves, ends, 1), hold(4, *slab),
-        (slabs, u, ue1, inner, rim1, halo1, open_ends, there1, token), free=(8,), name="late1",
+        (slabs, u, ue1, inner, rim1, halo1, open_ends, there1, mid), free=(8,), name="late1",
     )
     late0 = call(
         functools.partial(late_kernel, tiles, halves, ends, 0), hold(4, *slab),
@@ -904,10 +896,17 @@
         (inner, rim0, rim1, late0, late1, mid),
         scratch=(pltpu.VMEM((parts, *block), F32),), name="deal",
     )
-    order = [0, *range(2, parts), 1]
+    order = [0, *range(parts - 1, 0, -1)]
     came = [blocks[0]]
     for k in order[1:]:
         came.append(lax.ppermute(blocks[k], "narrow", [(i, i ^ k) for i in range(parts)]))
+    out = call(
+        functools.partial(final_kernel, tiles, halves),
+        jax.ShapeDtypeStruct((19, *flat), F32),
+        (g, fac, ghost0, ghost1, start, blocks[0]),
+        scratch=(pltpu.VMEM((19, *flat), F32), pltpu.SemaphoreType.DMA((19,))),
+        free=(5,), hbm_out=(0,), name="final",
+    )
     tile = (layers, parts, run, LANES)
     conc_out, napl_out = call(
         functools.partial(gather_kernel, parts, order),

time: 46.9 us -> 47.1 us (level)
  starting transfers between devices: 20 us -> 20.9 us
  waiting for transfers between devices: 10.8 us -> 10.1 us
    ppermute x3, waiting for transfers between devices: 4.76 us -> 2.12 us  [local(): lax.ppermute(blocks[k], 'narrow', [(i, i ^ k) for i in range(parts)])]
    ppermute x6, waiting for transfers between devices: 6.02 us -> 7.94 us  [swap(): return lax.ppermute(array, both, pairs[chain])]
    ppermute x3, starting transfers between devices: 3.55 us -> 4.45 us  [local(): lax.ppermute(blocks[k], 'narrow', [(i, i ^ k) for i in range(parts)])]
  transfers between devices with their start and end apart: 9 -> 9, of which waited for: 7 -> 6; matrix products, arithmetic and copies ran while one was open for 0% -> 0% of each run, Pallas kernels for 25% -> 25%
where the time goes in v5:
time: 47.1 us; the launch traced here: 46.9 us
  starting transfers between devices  20.9 us (44%)
  Pallas kernels  15.2 us (32%)
  waiting for transfers between devices  10.1 us (21%)
  between operations  0.82 us (2%)
    ppermute x6, starting transfers between devices, swap(): return lax.ppermute(array, both, pairs[chain])  16.4 us
    pallas_call x23, Pallas kernels, call(): pl.pallas_call(kernel, out_shape=shapes, in_specs=[spec(i, hbm, free) for...  15.2 us
    ppermute x6, waiting for transfers between devices, swap(): return lax.ppermute(array, both, pairs[chain])  7.94 us
    ppermute x3, starting transfers between devices, local(): lax.ppermute(blocks[k], 'narrow', [(i, i ^ k) for i in range(parts)])  4.45 us
    ppermute x3, waiting for transfers between devices, local(): lax.ppermute(blocks[k], 'narrow', [(i, i ^ k) for i in range(parts)])  2.12 us
  transfers between devices with their start and end apart: 9, of which 6 were waited for; matrix products, arithmetic and copies ran while one was open for 0% of the time, Pallas kernels for 25%

profile of v5, /device:TPU:0, one launch (start us, length us, event | category | flops | bytes accessed | tf_op | source)
XLA Modules:
  0.0 46.9 jit_solution(12193597198014108629)
XLA Ops:
  0.6 2.2 %first.1 = (f32[19,8,4,8,128]{4,3,2,1,0:T(8,128)S(1)}, s32[256,128]{1,0:T(8,128)S(1)}, f32[256,128]{1,0:T(8,128)S(1)}, f32[256,128]{1,0:T(8,128)S(1)}, f32[256,1...) custom-call(f32[19,8,4,8,128]{4,3,2,1,0:T(8,128)} %bitcast.43, ...), custom_call_target="tpu_custom_call" | custom-call | flops 1024 | bytes 1024 | tf_op jit(solution)/shard_map/first/pallas_call | solution.py:761
  2.8 6.4 %collective-permute-start.1 = (f32[14,8,512]{2,1,0:T(8,128)S(1)}, f32[14,8,512]{2,1,0:T(8,128)S(1)}, u32[]{:S(2)}, u32[]{:S(2)}) collective-permute-start(f32[14,8,512]{2,1,0:T(8,128)S(1)} %get-tuple-element.48.after), channel_id=1, source_target_pairs={{0,31},{1,2},{2,1},{3,4},{4,3},{5,6},{6,5},{7,8},{8,7},{9,10},{10,... | collective-permute-start | bytes 688136 | tf_op jit(solution)/shard_map/ppermute | solution.py:795
  9.3 0.9 %second.1 = (f32[19,8,512]{2,1,0:T(8,128)S(1)}, f32[14,8,512]{2,1,0:T(8,128)S(1)}) custom-call(f32[19,256,128]{2,1,0:T(8,128)S(1)} %bitcast.41, s32[256,128]{1,0:T(8,128)S(1)} %get-tuple-element.43.phase, f32[14,8,512]{2,1,0:T(8,128)S(1)} %get-tuple-element.48.after), custom_call_target="tpu_custom_call" | custom-call | flops 1024 | bytes 1024 | tf_op jit(solution)/shard_map/second/pallas_call | solution.py:761
  10.2 1.5 %first_inner.1 = (f32[19,8,8,512]{3,2,1,0:T(8,128)S(1)}, f32[8,8,512]{2,1,0:T(8,128)S(1)}, f32[19,8,8,512]{3,2,1,0:T(8,128)S(1)}, f32[3,8,8,512]{3,2,1,0:T(8,128)S(1)}, f32[2,8,512]{2,1,0:T(8,128)S(1)}) custom-call(f32[19,256,128]{2,1,0:T(8,128)S(1)} %bitcast.42, s32[256,128]{1,0:T(8,128)S(1)} %get-tuple-element.43.phase, ...), custom_call_target="tpu_custom_call" | custom-call | flops 1024 | bytes 1024 | tf_op jit(solution)/shard_map/first_inner/pallas_call | solution.py:761
  11.7 1.2 %inner.3 = f32[19,8,8,512]{3,2,1,0:T(8,128)S(1)} custom-call(f32[19,8,8,512]{3,2,1,0:T(8,128)S(1)} %get-tuple-element.51.g.after, f32[8,8,512]{2,1,0:T(8,128)S(1)} %get-tuple-element.52.fac, f32[3,8,8,512]{3,2,1,0:T(8,128)S(1)} %get-tuple-element.54.after.slabs), custom_call_target="tpu_custom_call" | custom-call | flops 1024 | bytes 1024 | tf_op jit(solution)/shard_map/inner/pallas_call | solution.py:761
  13.0 2.4 %collective-permute-done.1.halo.first_halo = f32[14,8,512]{2,1,0:T(8,128)S(1)} collective-permute-done((f32[14,8,512]{2,1,0:T(8,128)S(1)}, f32[14,8,512]{2,1,0:T(8,128)S(1)}, u32[]{:S(2)}, u32[]{:S(2)}) %collective-permute-start.1) | collective-permute-done | bytes 229408 | tf_op jit(solution)/shard_map/ppermute | solution.py:795
  15.6 0.4 far1.1
  16.0 5.6 %collective-permute-start.3 = (f32[14,8,512]{2,1,0:T(8,128)S(1)}, f32[14,8,512]{2,1,0:T(8,128)S(1)}, u32[]{:S(2)}, u32[]{:S(2)}) collective-permute-start(f32[14,8,512]{2,1,0:T(8,128)S(1)} %get-tuple-element.57.after), channel_id=1, source_target_pairs={{0,31},{1,2},{2,1},{3,4},{4,3},{5,6},{6,5},{7,8},{8,7},{9,10},{10,... | collective-permute-start | bytes 688136 | tf_op jit(solution)/shard_map/ppermute | solution.py:795
  21.8 0.4 far0.1
  22.2 0.5 %collective-permute-start.2 = (f32[14,8,512]{2,1,0:T(8,128)S(1)}, f32[14,8,512]{2,1,0:T(8,128)S(1)}, u32[]{:S(2)}, u32[]{:S(2)}) collective-permute-start(f32[14,8,512]{2,1,0:T(8,128)S(1)} %get-tuple-element.60.after), channel_id=1, source_target_pairs={{0,1},{1,0},{2,3},{3,2},{4,5},{5,4},{6,7},{7,6},{8,9},{9,8},{10,11... | collective-permute-start | bytes 688136 | tf_op jit(solution)/shard_map/ppermute | solution.py:795
  22.7 1.2 %inner.4 = f32[19,8,8,512]{3,2,1,0:T(8,128)S(1)} custom-call(f32[19,8,8,512]{3,2,1,0:T(8,128)S(1)} %get-tuple-element.58.g, f32[8,8,512]{2,1,0:T(8,128)S(1)} %get-tuple-element.52.fac, f32[14,8,512]{2,1,0:T(8,128)S(1)} %get-tuple-element.60.after), custom_call_target="tpu_custom_call" | custom-call | flops 1024 | bytes 1024 | tf_op jit(solution)/shard_map/inner/pallas_call | solution.py:761
  24.0 1.2 %inner.5.g.after = f32[19,8,8,512]{3,2,1,0:T(8,128)S(1)} custom-call(f32[19,8,8,512]{3,2,1,0:T(8,128)S(1)} %put.1.g.after, f32[8,8,512]{2,1,0:T(8,128)S(1)} %get-tuple-element.52.fac, f32[19,8,8,512]{3,2,1,0:T(8,128)S(1)} %put.1.g.after), custom_call_target="tpu_custom_call" | custom-call | flops 1024 | bytes 1024 | tf_op jit(solution)/shard_map/inner/pallas_call | solution.py:761
  25.2 0.5 %inner_speed.1.after.u = f32[3,4,8,512]{3,2,1,0:T(8,128)S(1)} custom-call(f32[19,8,8,512]{3,2,1,0:T(8,128)S(1)} %inner.5.g.after, f32[8,8,512]{2,1,0:T(8,128)S(1)} %get-tuple-element.52.fac, f32[19,8,8,512]{3,2,1,0:T(8,128)S(1)} %inner.5.g.after), custom_call_target="tpu_custom_call" | custom-call | flops 1024 | bytes 1024 | tf_op jit(solution)/shard_map/inner_speed/pallas_call | solution.py:761
  25.7 2.0 %collective-permute-done.3.halo = f32[14,8,512]{2,1,0:T(8,128)S(1)} collective-permute-done((f32[14,8,512]{2,1,0:T(8,128)S(1)}, f32[14,8,512]{2,1,0:T(8,128)S(1)}, u32[]{:S(2)}, u32[]{:S(2)}) %collective-permute-start.3) | collective-permute-done | bytes 229408 | tf_op jit(solution)/shard_map/ppermute | solution.py:795
  28.0 0.4 rim1.1
  28.3 3.8 %collective-permute-start.5 = (f32[5,8,512]{2,1,0:T(8,128)S(1)}, f32[5,8,512]{2,1,0:T(8,128)S(1)}, u32[]{:S(2)}, u32[]{:S(2)}) collective-permute-start(f32[5,8,512]{2,1,0:T(8,128)S(1)} %get-tuple-element.65.after), channel_id=1, source_target_pairs={{0,31},{1,2},{2,1},{3,4},{4,3},{5,6},{6,5},{7,8},{8,7},{9,10},{10,... | collective-permute-start | bytes 245768 | tf_op jit(solution)/shard_map/ppermute | solution.py:795
  32.4 0.4 rim0.1
  33.4 2.6 %collective-permute-done.5.there = f32[5,8,512]{2,1,0:T(8,128)S(1)} collective-permute-done((f32[5,8,512]{2,1,0:T(8,128)S(1)}, f32[5,8,512]{2,1,0:T(8,128)S(1)}, u32[]{:S(2)}, u32[]{:S(2)}) %collective-permute-start.5) | collective-permute-done | bytes 81952 | tf_op jit(solution)/shard_map/ppermute | solution.py:795
  36.3 0.9 %collective-permute-done.4.there = f32[5,8,512]{2,1,0:T(8,128)S(1)} collective-permute-done((f32[5,8,512]{2,1,0:T(8,128)S(1)}, f32[5,8,512]{2,1,0:T(8,128)S(1)}, u32[]{:S(2)}, u32[]{:S(2)}) %collective-permute-start.4) | collective-permute-done | bytes 81952 | tf_op jit(solution)/shard_map/ppermute | solution.py:795
  37.6 2.9 %collective-permute-start.6 = (f32[2,4,16,128]{3,2,1,0:T(8,128)S(1)}, f32[2,4,16,128]{3,2,1,0:T(8,128)S(1)}, u32[]{:S(2)}, u32[]{:S(2)}) collective-permute-start(f32[2,4,16,128]{3,2,1,0:T(8,128)S(1)} %get-tuple-element.76), channel_id=1, source_target_pairs={{0,3},{1,2},{2,1},{3,0},{4,7},{5,6},{6,5},{7,4},{8,11},{9,10},{10,... | collective-permute-start | bytes 196616 | tf_op jit(solution)/shard_map/ppermute | solution.py:902
  40.6 1.5 %collective-permute-start.8 = (f32[2,4,16,128]{3,2,1,0:T(8,128)S(1)}, f32[2,4,16,128]{3,2,1,0:T(8,128)S(1)}, u32[]{:S(2)}, u32[]{:S(2)}) collective-permute-start(f32[2,4,16,128]{3,2,1,0:T(8,128)S(1)} %get-tuple-element.78), channel_id=1, source_target_pairs={{0,1},{1,0},{2,3},{3,2},{4,5},{5,4},{6,7},{7,6},{8,9},{9,8},{10,11... | collective-permute-start | bytes 196616 | tf_op jit(solution)/shard_map/ppermute | solution.py:902
  42.1 1.9 %final.1 = f32[19,256,128]{2,1,0:T(8,128)} custom-call(f32[19,8,8,512]{3,2,1,0:T(8,128)S(1)} %get-tuple-element.66.g, f32[8,8,512]{2,1,0:T(8,128)S(1)} %get-tuple-element.52.fac, f32[5,8,512]{2,1,0:T(8,128)S(1)} %get-tuple-element.67.ghost.after.halo0, f32[5,8,512]{2,1,0:T(8,128)S(1)} %get-tuple-element.64.ghost.after.halo1, ...), custom_call_target="tpu_custom_call" | custom-call | flops 1024 | bytes 1024 | tf_op jit(solution)/shard_map/final/pallas_call | solution.py:761
  44.0 2.0 %collective-permute-done.7.refs_2_ = f32[2,4,16,128]{3,2,1,0:T(8,128)S(1)} collective-permute-done((f32[2,4,16,128]{3,2,1,0:T(8,128)S(1)}, f32[2,4,16,128]{3,2,1,0:T(8,128)S(1)}, u32[]{:S(2)}, u32[]{:S(2)}) %collective-permute-start.7) | collective-permute-done | bytes 65568 | tf_op jit(solution)/shard_map/ppermute | solution.py:902
  46.1 0.8 %gather.1 = (f32[4,4,16,128]{3,2,1,0:T(8,128)}, f32[4,4,16,128]{3,2,1,0:T(8,128)}) custom-call(f32[2,4,16,128]{3,2,1,0:T(8,128)S(1)} %get-tuple-element.75.after.refs_0_, f32[2,4,16,128]{3,2,1,0:T(8,128)S(1)} %collective-permute-done.6.refs_1_, f32[2,4,16,128]{3,2,1,0:T(8,128)S(1)} %collective-permute-done.7.refs_2_, ...), custom_call_target="tpu_custom_call" | custom-call | flops 1024 | bytes 1024 | tf_op jit(solution)/shard_map/gather/pallas_call | solution.py:761
  (17 shorter events, 2.6 us)
Async XLA Ops:
  2.8 12.5 %collective-permute-start.1 = (f32[14,8,512]{2,1,0:T(8,128)S(1)}, f32[14,8,512]{2,1,0:T(8,128)S(1)}, u32[]{:S(2)}, u32[]{:S(2)}) collective-permute-start(f32[14,8,512]{2,1,0:T(8,128)S(1)} %get-tuple-element.48.after), channel_id=1, source_target_pairs={{0,31},{1,2},{2,1},{3,4},{4,3},{5,6},{6,5},{7,8},{8,7},{9,10},{10,... | collective-permute-start | bytes 688136 | tf_op jit(solution)/shard_map/ppermute | solution.py:795
  10.2 11.4 %collective-permute-start = (f32[14,8,512]{2,1,0:T(8,128)S(1)}, f32[14,8,512]{2,1,0:T(8,128)S(1)}, u32[]{:S(2)}, u32[]{:S(2)}) collective-permute-start(f32[14,8,512]{2,1,0:T(8,128)S(1)} %get-tuple-element.53), channel_id=1, source_target_pairs={{0,1},{1,0},{2,3},{3,2},{4,5},{5,4},{6,7},{7,6},{8,9},{9,8},{10,11... | collective-permute-start | bytes 688136 | tf_op jit(solution)/shard_map/ppermute | solution.py:795
  16.0 11.7 %collective-permute-start.3 = (f32[14,8,512]{2,1,0:T(8,128)S(1)}, f32[14,8,512]{2,1,0:T(8,128)S(1)}, u32[]{:S(2)}, u32[]{:S(2)}) collective-permute-start(f32[14,8,512]{2,1,0:T(8,128)S(1)} %get-tuple-element.57.after), channel_id=1, source_target_pairs={{0,31},{1,2},{2,1},{3,4},{4,3},{5,6},{6,5},{7,8},{8,7},{9,10},{10,... | collective-permute-start | bytes 688136 | tf_op jit(solution)/shard_map/ppermute | solution.py:795
  22.2 9.9 %collective-permute-start.2 = (f32[14,8,512]{2,1,0:T(8,128)S(1)}, f32[14,8,512]{2,1,0:T(8,128)S(1)}, u32[]{:S(2)}, u32[]{:S(2)}) collective-permute-start(f32[14,8,512]{2,1,0:T(8,128)S(1)} %get-tuple-element.60.after), channel_id=1, source_target_pairs={{0,1},{1,0},{2,3},{3,2},{4,5},{5,4},{6,7},{7,6},{8,9},{9,8},{10,11... | collective-permute-start | bytes 688136 | tf_op jit(solution)/shard_map/ppermute | solution.py:795
  28.3 7.7 %collective-permute-start.5 = (f32[5,8,512]{2,1,0:T(8,128)S(1)}, f32[5,8,512]{2,1,0:T(8,128)S(1)}, u32[]{:S(2)}, u32[]{:S(2)}) collective-permute-start(f32[5,8,512]{2,1,0:T(8,128)S(1)} %get-tuple-element.65.after), channel_id=1, source_target_pairs={{0,31},{1,2},{2,1},{3,4},{4,3},{5,6},{6,5},{7,8},{8,7},{9,10},{10,... | collective-permute-start | bytes 245768 | tf_op jit(solution)/shard_map/ppermute | solution.py:795
  32.7 4.5 %collective-permute-start.4 = (f32[5,8,512]{2,1,0:T(8,128)S(1)}, f32[5,8,512]{2,1,0:T(8,128)S(1)}, u32[]{:S(2)}, u32[]{:S(2)}) collective-permute-start(f32[5,8,512]{2,1,0:T(8,128)S(1)} %get-tuple-element.74), channel_id=1, source_target_pairs={{0,1},{1,0},{2,3},{3,2},{4,5},{5,4},{6,7},{7,6},{8,9},{9,8},{10,11... | collective-permute-start | bytes 245768 | tf_op jit(solution)/shard_map/ppermute | solution.py:795
  37.6 6.4 %collective-permute-start.6 = (f32[2,4,16,128]{3,2,1,0:T(8,128)S(1)}, f32[2,4,16,128]{3,2,1,0:T(8,128)S(1)}, u32[]{:S(2)}, u32[]{:S(2)}) collective-permute-start(f32[2,4,16,128]{3,2,1,0:T(8,128)S(1)} %get-tuple-element.76), channel_id=1, source_target_pairs={{0,3},{1,2},{2,1},{3,0},{4,7},{5,6},{6,5},{7,4},{8,11},{9,10},{10,... | collective-permute-start | bytes 196616 | tf_op jit(solution)/shard_map/ppermute | solution.py:902
  40.6 5.4 %collective-permute-start.7 = (f32[2,4,16,128]{3,2,1,0:T(8,128)S(1)}, f32[2,4,16,128]{3,2,1,0:T(8,128)S(1)}, u32[]{:S(2)}, u32[]{:S(2)}) collective-permute-start(f32[2,4,16,128]{3,2,1,0:T(8,128)S(1)} %get-tuple-element.77), channel_id=1, source_target_pairs={{0,2},{1,3},{2,0},{3,1},{4,6},{5,7},{6,4},{7,5},{8,10},{9,11},{10,... | collective-permute-start | bytes 196616 | tf_op jit(solution)/shard_map/ppermute | solution.py:902
  40.6 5.6 %collective-permute-start.8 = (f32[2,4,16,128]{3,2,1,0:T(8,128)S(1)}, f32[2,4,16,128]{3,2,1,0:T(8,128)S(1)}, u32[]{:S(2)}, u32[]{:S(2)}) collective-permute-start(f32[2,4,16,128]{3,2,1,0:T(8,128)S(1)} %get-tuple-element.78), channel_id=1, source_target_pairs={{0,1},{1,0},{2,3},{3,2},{4,5},{5,4},{6,7},{7,6},{8,9},{9,8},{10,11... | collective-permute-start | bytes 196616 | tf_op jit(solution)/shard_map/ppermute | solution.py:902

commit v6 on v4

--- a/solution.py
+++ b/solution.py
@@ -237,8 +237,9 @@
 
 
 def first_inner_kernel(
-    tiles, halves, pop, phase, conc, napl, poro, flags, row0, row1, g, fac, start, slabs, open_ends
+    tiles, halves, pop, phase, conc, napl, poro, flags, row0, row1, planes, g, fac, start, slabs, open_ends, passed
 ):
+    passed[...] = planes[...]
     rows = g.shape[1]
     length = tiles * LANES
     _, sub = iotas()
@@ -299,7 +300,8 @@
     lax.fori_loop(1, rows - 1, row, 0)
 
 
-def put_kernel(inner, row0, row1, out):
+def put_kernel(inner, row0, row1, planes, out, passed):
+    passed[...] = planes[...]
     merge_rows(out, row0, row1, 19)
 
 
@@ -811,19 +813,19 @@
     )
     popv = popv.reshape(pop.shape)
     halo1 = head1 = swap(1, send)
-    row0, send = call(
+    row0, planes = call(
         functools.partial(second_kernel, tiles, halves), (hold(19, *slab), hold(14, *slab)), (popv, phv, send),
         scratch=(pltpu.VMEM((19, *slab), F32),), free=(2,), name="second",
     )
-    halo0 = head0 = swap(0, send)
-    g, fac, start, slabs, open_ends = call(
+    g, fac, start, slabs, open_ends, send = call(
         functools.partial(first_inner_kernel, tiles, halves),
         (
             hold(19, rows, *slab), hold(rows, *slab), hold(19, rows, *slab), hold(3, rows, *slab),
-            hold(2, *slab),
+            hold(2, *slab), hold(14, *slab),
         ),
-        (popv, phv, cov, nav, pov, flv, row0, row1), name="first_inner",
-    )
+        (popv, phv, cov, nav, pov, flv, row0, row1, planes), name="first_inner",
+    )
+    halo0 = head0 = swap(0, send)
 
     def inner_rows(g, after):
         return call(
@@ -858,12 +860,13 @@
             row1, send1 = far(1, later, ghost1, ghost1)
             halo1 = swap(1, send1)
             later, ghost0 = arrive(0, g, halo0, head0, send1, later)
-            row0, send0 = far(0, later, ghost0, ghost0)
+            row0, planes = far(0, later, ghost0, ghost0)
+            new = inner_rows(later, planes)
+            g, send0 = call(
+                put_kernel, (hold(19, rows, *slab), hold(14, *slab)), (new, row0, row1, planes), name="put",
+                aliases={0: 0}, free=(0,),
+            )
             halo0 = swap(0, send0)
-            new = inner_rows(later, send0)
-            g = call(
-                put_kernel, hold(19, rows, *slab), (new, row0, row1), name="put", aliases={0: 0}, free=(0,)
-            )
             after = g
     u = call(
         functools.partial(inner_speed_kernel, tiles, halves), hold(3, rows - 4, *slab), (new, fac, new),

time: 46.9 us -> 47.6 us (1.015)
  starting transfers between devices: 20 us -> 21.4 us
  waiting for transfers between devices: 10.8 us -> 10 us
    ppermute x6, starting transfers between devices: 16.4 us -> 17.1 us  [swap(): return lax.ppermute(array, both, pairs[chain])]
    ppermute x3, starting transfers between devices: 3.55 us -> 4.23 us  [local(): lax.ppermute(blocks[k], 'narrow', [(i, i ^ k) for i in range(parts)])]
    ppermute x6, waiting for transfers between devices: 6.02 us -> 5.52 us  [swap(): return lax.ppermute(array, both, pairs[chain])]
  transfers between devices with their start and end apart: 9 -> 9, of which waited for: 7 -> 5; matrix products, arithmetic and copies ran while one was open for 0% -> 0% of each run, Pallas kernels for 25% -> 25%
where the time goes in v6:
time: 47.6 us; the launch traced here: 47.4 us
  starting transfers between devices  21.4 us (45%)
  Pallas kernels  15.2 us (32%)
  waiting for transfers between devices  10 us (21%)
  between operations  0.82 us (2%)
    ppermute x6, starting transfers between devices, swap(): return lax.ppermute(array, both, pairs[chain])  17.1 us
    pallas_call x23, Pallas kernels, call(): pl.pallas_call(kernel, out_shape=shapes, in_specs=[spec(i, hbm, free) for...  15.2 us
    ppermute x6, waiting for transfers between devices, swap(): return lax.ppermute(array, both, pairs[chain])  5.52 us
    ppermute x3, waiting for transfers between devices, local(): lax.ppermute(blocks[k], 'narrow', [(i, i ^ k) for i in range(parts)])  4.51 us
    ppermute x3, starting transfers between devices, local(): lax.ppermute(blocks[k], 'narrow', [(i, i ^ k) for i in range(parts)])  4.23 us
  transfers between devices with their start and end apart: 9, of which 5 were waited for; matrix products, arithmetic and copies ran while one was open for 0% of the time, Pallas kernels for 25%

profile of v6, /device:TPU:0, one launch (start us, length us, event | category | flops | bytes accessed | tf_op | source)
XLA Modules:
  0.0 47.4 jit_solution(3130301396138598768)
XLA Ops:
  0.6 2.2 %first.1 = (f32[19,8,4,8,128]{4,3,2,1,0:T(8,128)S(1)}, s32[256,128]{1,0:T(8,128)S(1)}, f32[256,128]{1,0:T(8,128)S(1)}, f32[256,128]{1,0:T(8,128)S(1)}, f32[256,1...) custom-call(f32[19,8,4,8,128]{4,3,2,1,0:T(8,128)} %bitcast.43, ...), custom_call_target="tpu_custom_call" | custom-call | flops 1024 | bytes 1024 | tf_op jit(solution)/shard_map/first/pallas_call | solution.py:764
  2.8 6.4 %collective-permute-start.1 = (f32[14,8,512]{2,1,0:T(8,128)S(1)}, f32[14,8,512]{2,1,0:T(8,128)S(1)}, u32[]{:S(2)}, u32[]{:S(2)}) collective-permute-start(f32[14,8,512]{2,1,0:T(8,128)S(1)} %get-tuple-element.53.after), channel_id=1, source_target_pairs={{0,31},{1,2},{2,1},{3,4},{4,3},{5,6},{6,5},{7,8},{8,7},{9,10},{10,... | collective-permute-start | bytes 688136 | tf_op jit(solution)/shard_map/ppermute | solution.py:798
  9.3 0.9 %second.1 = (f32[19,8,512]{2,1,0:T(8,128)S(1)}, f32[14,8,512]{2,1,0:T(8,128)S(1)}) custom-call(f32[19,256,128]{2,1,0:T(8,128)S(1)} %bitcast.41, s32[256,128]{1,0:T(8,128)S(1)} %get-tuple-element.48.phase, f32[14,8,512]{2,1,0:T(8,128)S(1)} %get-tuple-element.53.after), custom_call_target="tpu_custom_call" | custom-call | flops 1024 | bytes 1024 | tf_op jit(solution)/shard_map/second/pallas_call | solution.py:764
  10.2 1.5 %first_inner.1 = (f32[19,8,8,512]{3,2,1,0:T(8,128)S(1)}, f32[8,8,512]{2,1,0:T(8,128)S(1)}, f32[19,8,8,512]{3,2,1,0:T(8,128)S(1)}, f32[3,8,8,512]{3,2,1,0:T(8,128...) custom-call(f32[19,256,128]{2,1,0:T(8,128)S(1)} %bitcast.42, s32[256,128]{1,0:T(8,128)S(1)} %get-tuple-element.48.phase, ...), custom_call_target="tpu_custom_call" | custom-call | flops 1024 | bytes 1024 | tf_op jit(solution)/shard_map/first_inner/pallas_call | solution.py:764
  11.8 1.2 %inner.3 = f32[19,8,8,512]{3,2,1,0:T(8,128)S(1)} custom-call(f32[19,8,8,512]{3,2,1,0:T(8,128)S(1)} %get-tuple-element.57.g.after, f32[8,8,512]{2,1,0:T(8,128)S(1)} %get-tuple-element.58.fac, f32[3,8,8,512]{3,2,1,0:T(8,128)S(1)} %get-tuple-element.60.after.slabs), custom_call_target="tpu_custom_call" | custom-call | flops 1024 | bytes 1024 | tf_op jit(solution)/shard_map/inner/pallas_call | solution.py:764
  13.0 2.3 %collective-permute-done.1.halo.first_halo = f32[14,8,512]{2,1,0:T(8,128)S(1)} collective-permute-done((f32[14,8,512]{2,1,0:T(8,128)S(1)}, f32[14,8,512]{2,1,0:T(8,128)S(1)}, u32[]{:S(2)}, u32[]{:S(2)}) %collective-permute-start.1) | collective-permute-done | bytes 229408 | tf_op jit(solution)/shard_map/ppermute | solution.py:798
  15.6 0.4 far1.1
  16.0 5.6 %collective-permute-start.3 = (f32[14,8,512]{2,1,0:T(8,128)S(1)}, f32[14,8,512]{2,1,0:T(8,128)S(1)}, u32[]{:S(2)}, u32[]{:S(2)}) collective-permute-start(f32[14,8,512]{2,1,0:T(8,128)S(1)} %get-tuple-element.63.after), channel_id=1, source_target_pairs={{0,31},{1,2},{2,1},{3,4},{4,3},{5,6},{6,5},{7,8},{8,7},{9,10},{10,... | collective-permute-start | bytes 688136 | tf_op jit(solution)/shard_map/ppermute | solution.py:798
  21.8 0.4 far0.1
  22.2 1.2 %inner.4 = f32[19,8,8,512]{3,2,1,0:T(8,128)S(1)} custom-call(f32[19,8,8,512]{3,2,1,0:T(8,128)S(1)} %get-tuple-element.64.g, f32[8,8,512]{2,1,0:T(8,128)S(1)} %get-tuple-element.58.fac, f32[14,8,512]{2,1,0:T(8,128)S(1)} %get-tuple-element.66.after.planes), custom_call_target="tpu_custom_call" | custom-call | flops 1024 | bytes 1024 | tf_op jit(solution)/shard_map/inner/pallas_call | solution.py:764
  23.5 0.5 collective-permute-start.2
  23.9 1.2 %inner.5.g.after = f32[19,8,8,512]{3,2,1,0:T(8,128)S(1)} custom-call(f32[19,8,8,512]{3,2,1,0:T(8,128)S(1)} %get-tuple-element.69.g.after, f32[8,8,512]{2,1,0:T(8,128)S(1)} %get-tuple-element.58.fac, f32[19,8,8,512]{3,2,1,0:T(8,128)S(1)} %get-tuple-element.69.g.after), custom_call_target="tpu_custom_call" | custom-call | flops 1024 | bytes 1024 | tf_op jit(solution)/shard_map/inner/pallas_call | solution.py:764
  25.1 0.5 %inner_speed.1.after.u = f32[3,4,8,512]{3,2,1,0:T(8,128)S(1)} custom-call(f32[19,8,8,512]{3,2,1,0:T(8,128)S(1)} %inner.5.g.after, f32[8,8,512]{2,1,0:T(8,128)S(1)} %get-tuple-element.58.fac, f32[19,8,8,512]{3,2,1,0:T(8,128)S(1)} %inner.5.g.after), custom_call_target="tpu_custom_call" | custom-call | flops 1024 | bytes 1024 | tf_op jit(solution)/shard_map/inner_speed/pallas_call | solution.py:764
  25.7 1.6 %collective-permute-done.3.halo = f32[14,8,512]{2,1,0:T(8,128)S(1)} collective-permute-done((f32[14,8,512]{2,1,0:T(8,128)S(1)}, f32[14,8,512]{2,1,0:T(8,128)S(1)}, u32[]{:S(2)}, u32[]{:S(2)}) %collective-permute-start.3) | collective-permute-done | bytes 229408 | tf_op jit(solution)/shard_map/ppermute | solution.py:798
  27.5 0.4 rim1.1
  27.8 4.5 %collective-permute-start.5 = (f32[5,8,512]{2,1,0:T(8,128)S(1)}, f32[5,8,512]{2,1,0:T(8,128)S(1)}, u32[]{:S(2)}, u32[]{:S(2)}) collective-permute-start(f32[5,8,512]{2,1,0:T(8,128)S(1)} %get-tuple-element.73.after), channel_id=1, source_target_pairs={{0,31},{1,2},{2,1},{3,4},{4,3},{5,6},{6,5},{7,8},{8,7},{9,10},{10,... | collective-permute-start | bytes 245768 | tf_op jit(solution)/shard_map/ppermute | solution.py:798
  33.7 1.9 %final.1 = (f32[19,256,128]{2,1,0:T(8,128)}, f32[8,128]{1,0:T(8,128)S(1)}) custom-call(f32[19,8,8,512]{3,2,1,0:T(8,128)S(1)} %get-tuple-element.74.g, f32[8,8,512]{2,1,0:T(8,128)S(1)} %get-tuple-element.58.fac, f32[5,8,512]{2,1,0:T(8,128)S(1)} %get-tuple-element.75.ghost.after.halo0, f32[5,8,512]{2,1,0:T(8,128)S(1)} %get-tuple-element.72.ghost.after.halo1, ...), custom_call_target="tpu_custom_call" | custom-call | flops 1024 | bytes 1024 | tf_op jit(solution)/shard_map/final/pallas_call | solution.py:764
  35.9 1.6 %collective-permute-done.4.there = f32[5,8,512]{2,1,0:T(8,128)S(1)} collective-permute-done((f32[5,8,512]{2,1,0:T(8,128)S(1)}, f32[5,8,512]{2,1,0:T(8,128)S(1)}, u32[]{:S(2)}, u32[]{:S(2)}) %collective-permute-start.4) | collective-permute-done | bytes 81952 | tf_op jit(solution)/shard_map/ppermute | solution.py:798
  37.9 2.6 %collective-permute-start.6 = (f32[2,4,16,128]{3,2,1,0:T(8,128)S(1)}, f32[2,4,16,128]{3,2,1,0:T(8,128)S(1)}, u32[]{:S(2)}, u32[]{:S(2)}) collective-permute-start(f32[2,4,16,128]{3,2,1,0:T(8,128)S(1)} %get-tuple-element.86), channel_id=1, source_target_pairs={{0,2},{1,3},{2,0},{3,1},{4,6},{5,7},{6,4},{7,5},{8,10},{9,11},{10,... | collective-permute-start | bytes 196616 | tf_op jit(solution)/shard_map/ppermute | solution.py:913
  40.6 1.1 %collective-permute-start.7 = (f32[2,4,16,128]{3,2,1,0:T(8,128)S(1)}, f32[2,4,16,128]{3,2,1,0:T(8,128)S(1)}, u32[]{:S(2)}, u32[]{:S(2)}) collective-permute-start(f32[2,4,16,128]{3,2,1,0:T(8,128)S(1)} %get-tuple-element.87), channel_id=1, source_target_pairs={{0,3},{1,2},{2,1},{3,0},{4,7},{5,6},{6,5},{7,4},{8,11},{9,10},{10,... | collective-permute-start | bytes 196616 | tf_op jit(solution)/shard_map/ppermute | solution.py:913
  41.7 0.5 %collective-permute-start.8 = (f32[2,4,16,128]{3,2,1,0:T(8,128)S(1)}, f32[2,4,16,128]{3,2,1,0:T(8,128)S(1)}, u32[]{:S(2)}, u32[]{:S(2)}) collective-permute-start(f32[2,4,16,128]{3,2,1,0:T(8,128)S(1)} %get-tuple-element.88), channel_id=1, source_target_pairs={{0,1},{1,0},{2,3},{3,2},{4,5},{5,4},{6,7},{7,6},{8,9},{9,8},{10,11... | collective-permute-start | bytes 196616 | tf_op jit(solution)/shard_map/ppermute | solution.py:913
  42.2 3.0 %collective-permute-done.6.refs_1_ = f32[2,4,16,128]{3,2,1,0:T(8,128)S(1)} collective-permute-done((f32[2,4,16,128]{3,2,1,0:T(8,128)S(1)}, f32[2,4,16,128]{3,2,1,0:T(8,128)S(1)}, u32[]{:S(2)}, u32[]{:S(2)}) %collective-permute-start.6) | collective-permute-done | bytes 65568 | tf_op jit(solution)/shard_map/ppermute | solution.py:913
  45.1 1.6 %collective-permute-done.7.refs_2_ = f32[2,4,16,128]{3,2,1,0:T(8,128)S(1)} collective-permute-done((f32[2,4,16,128]{3,2,1,0:T(8,128)S(1)}, f32[2,4,16,128]{3,2,1,0:T(8,128)S(1)}, u32[]{:S(2)}, u32[]{:S(2)}) %collective-permute-start.7) | collective-permute-done | bytes 65568 | tf_op jit(solution)/shard_map/ppermute | solution.py:913
  46.7 0.8 %gather.1 = (f32[4,4,16,128]{3,2,1,0:T(8,128)}, f32[4,4,16,128]{3,2,1,0:T(8,128)}) custom-call(f32[2,4,16,128]{3,2,1,0:T(8,128)S(1)} %get-tuple-element.85.refs_0_, f32[2,4,16,128]{3,2,1,0:T(8,128)S(1)} %collective-permute-done.6.refs_1_, f32[2,4,16,128]{3,2,1,0:T(8,128)S(1)} %collective-permute-done.7.refs_2_, ...), custom_call_target="tpu_custom_call" | custom-call | flops 1024 | bytes 1024 | tf_op jit(solution)/shard_map/gather/pallas_call | solution.py:764
  (17 shorter events, 2.9 us)
Async XLA Ops:
  2.8 12.5 %collective-permute-start.1 = (f32[14,8,512]{2,1,0:T(8,128)S(1)}, f32[14,8,512]{2,1,0:T(8,128)S(1)}, u32[]{:S(2)}, u32[]{:S(2)}) collective-permute-start(f32[14,8,512]{2,1,0:T(8,128)S(1)} %get-tuple-element.53.after), channel_id=1, source_target_pairs={{0,31},{1,2},{2,1},{3,4},{4,3},{5,6},{6,5},{7,8},{8,7},{9,10},{10,... | collective-permute-start | bytes 688136 | tf_op jit(solution)/shard_map/ppermute | solution.py:798
  11.7 9.9 %collective-permute-start = (f32[14,8,512]{2,1,0:T(8,128)S(1)}, f32[14,8,512]{2,1,0:T(8,128)S(1)}, u32[]{:S(2)}, u32[]{:S(2)}) collective-permute-start(f32[14,8,512]{2,1,0:T(8,128)S(1)} %get-tuple-element.59), channel_id=1, source_target_pairs={{0,1},{1,0},{2,3},{3,2},{4,5},{5,4},{6,7},{7,6},{8,9},{9,8},{10,11... | collective-permute-start | bytes 688136 | tf_op jit(solution)/shard_map/ppermute | solution.py:798
  16.0 11.2 %collective-permute-start.3 = (f32[14,8,512]{2,1,0:T(8,128)S(1)}, f32[14,8,512]{2,1,0:T(8,128)S(1)}, u32[]{:S(2)}, u32[]{:S(2)}) collective-permute-start(f32[14,8,512]{2,1,0:T(8,128)S(1)} %get-tuple-element.63.after), channel_id=1, source_target_pairs={{0,31},{1,2},{2,1},{3,4},{4,3},{5,6},{6,5},{7,8},{8,7},{9,10},{10,... | collective-permute-start | bytes 688136 | tf_op jit(solution)/shard_map/ppermute | solution.py:798
  23.5 8.9 %collective-permute-start.2 = (f32[14,8,512]{2,1,0:T(8,128)S(1)}, f32[14,8,512]{2,1,0:T(8,128)S(1)}, u32[]{:S(2)}, u32[]{:S(2)}) collective-permute-start(f32[14,8,512]{2,1,0:T(8,128)S(1)} %get-tuple-element.70), channel_id=1, source_target_pairs={{0,1},{1,0},{2,3},{3,2},{4,5},{5,4},{6,7},{7,6},{8,9},{9,8},{10,11... | collective-permute-start | bytes 688136 | tf_op jit(solution)/shard_map/ppermute | solution.py:798
  27.8 7.7 %collective-permute-start.5 = (f32[5,8,512]{2,1,0:T(8,128)S(1)}, f32[5,8,512]{2,1,0:T(8,128)S(1)}, u32[]{:S(2)}, u32[]{:S(2)}) collective-permute-start(f32[5,8,512]{2,1,0:T(8,128)S(1)} %get-tuple-element.73.after), channel_id=1, source_target_pairs={{0,31},{1,2},{2,1},{3,4},{4,3},{5,6},{6,5},{7,8},{8,7},{9,10},{10,... | collective-permute-start | bytes 245768 | tf_op jit(solution)/shard_map/ppermute | solution.py:798
  33.0 4.5 %collective-permute-start.4 = (f32[5,8,512]{2,1,0:T(8,128)S(1)}, f32[5,8,512]{2,1,0:T(8,128)S(1)}, u32[]{:S(2)}, u32[]{:S(2)}) collective-permute-start(f32[5,8,512]{2,1,0:T(8,128)S(1)} %get-tuple-element.83), channel_id=1, source_target_pairs={{0,1},{1,0},{2,3},{3,2},{4,5},{5,4},{6,7},{7,6},{8,9},{9,8},{10,11... | collective-permute-start | bytes 245768 | tf_op jit(solution)/shard_map/ppermute | solution.py:798
  37.9 7.2 %collective-permute-start.6 = (f32[2,4,16,128]{3,2,1,0:T(8,128)S(1)}, f32[2,4,16,128]{3,2,1,0:T(8,128)S(1)}, u32[]{:S(2)}, u32[]{:S(2)}) collective-permute-start(f32[2,4,16,128]{3,2,1,0:T(8,128)S(1)} %get-tuple-element.86), channel_id=1, source_target_pairs={{0,2},{1,3},{2,0},{3,1},{4,6},{5,7},{6,4},{7,5},{8,10},{9,11},{10,... | collective-permute-start | bytes 196616 | tf_op jit(solution)/shard_map/ppermute | solution.py:913
  40.6 6.1 %collective-permute-start.7 = (f32[2,4,16,128]{3,2,1,0:T(8,128)S(1)}, f32[2,4,16,128]{3,2,1,0:T(8,128)S(1)}, u32[]{:S(2)}, u32[]{:S(2)}) collective-permute-start(f32[2,4,16,128]{3,2,1,0:T(8,128)S(1)} %get-tuple-element.87), channel_id=1, source_target_pairs={{0,3},{1,2},{2,1},{3,0},{4,7},{5,6},{6,5},{7,4},{8,11},{9,10},{10,... | collective-permute-start | bytes 196616 | tf_op jit(solution)/shard_map/ppermute | solution.py:913
  41.7 5.0 %collective-permute-start.8 = (f32[2,4,16,128]{3,2,1,0:T(8,128)S(1)}, f32[2,4,16,128]{3,2,1,0:T(8,128)S(1)}, u32[]{:S(2)}, u32[]{:S(2)}) collective-permute-start(f32[2,4,16,128]{3,2,1,0:T(8,128)S(1)} %get-tuple-element.88), channel_id=1, source_target_pairs={{0,1},{1,0},{2,3},{3,2},{4,5},{5,4},{6,7},{7,6},{8,9},{9,8},{10,11... | collective-permute-start | bytes 196616 | tf_op jit(solution)/shard_map/ppermute | solution.py:913

commit v7 on v5

--- a/solution.py
+++ b/solution.py
@@ -146,15 +146,6 @@
 
 def pick(flag, a, b):
     return [jnp.where(flag, x, y) for x, y in zip(a, b)]
-
-
-def start_row(tiles, pop, phase, x, row, c):
-    at = strided(tiles, c, x)
-    fc = drag(phase[at, :])
-    post = collide([pop[q, at, :] for q in range(19)], fc)
-    for q in range(19):
-        row[q, :, cut(c)] = post[q]
-    return fc
 
 
 def look_ahead(tiles, halves, up, edge, beside, send):
@@ -183,14 +174,19 @@
             send[10 + k, :, cut(c)] = sums[k]
 
 
-def start_rows(tiles, halves, chain, pop, phase, row, send, beside, ready=None):
-    up = upper(chain)
-    x, inwards = jnp.where(up, SUBS - 1, 0), jnp.where(up, SUBS - 2, 1)
+def start_rows(tiles, halves, chain, pairs, phase, row, send, beside, ready):
+    def tile(c, up):
+        for at, k, ref in ((SUBS - 1, 1, row), (SUBS - 2, 0, beside)) if up else ((0, 0, row), (1, 1, beside)):
+            fc = drag(phase[strided(tiles, c, at), :])
+            post = collide([pairs[c, q, :, k, :] for q in range(19)], fc)
+            for q in range(19):
+                ref[q, :, cut(c)] = post[q]
+            if ref is row:
+                send[13, :, cut(c)] = fc
+
     for c in range(tiles):
-        if ready is not None:
-            ready(c)
-        send[13, :, cut(c)] = start_row(tiles, pop, phase, x, row, c)
-        start_row(tiles, pop, phase, inwards, beside, c)
+        ready(c)
+        by_side(chain, functools.partial(tile, c))
 
     def side(up):
         look_ahead(
@@ -200,29 +196,26 @@
     by_side(chain, side)
 
 
-def first_kernel(
-    tiles, halves, pop_h, phase_h, conc_h, napl_h, poro_h, flags_h,
-    pop, phase, conc, napl, poro, flags, row, send, beside, sems,
-):
-    small = [
-        pltpu.make_async_copy(a, b, sems.at[tiles + i])
-        for i, (a, b) in enumerate(
-            ((phase_h, phase), (conc_h, conc), (poro_h, poro), (napl_h, napl), (flags_h, flags))
-        )
-    ]
-    large = [pltpu.make_async_copy(pop_h.at[:, :, c], pop.at[:, :, c], sems.at[c]) for c in range(tiles)]
-    small[0].start()
-    for copy in large + small[1:]:
-        copy.start()
-    small[0].wait()
-    flat = pop.reshape(pop.shape[0], SUBS * tiles * SUBS, LANES)
-    start_rows(tiles, halves, 1, flat, phase, row, send, beside, ready=lambda c: large[c].wait())
-    for copy in small[1:]:
+def first_kernel(tiles, halves, pairs_h, phase_h, phase, row, send, mate, beside, mine, sems):
+    labels = pltpu.make_async_copy(phase_h, phase, sems.at[2 * tiles])
+    labels.start()
+    up = upper(1)
+    copies = []
+    for chain, into in ((1, mine), (0, mate)):
+        pair = jnp.where(up, 3, 0) if chain else jnp.where(up, 0, 3)
+        for c in range(tiles):
+            copies.append(
+                pltpu.make_async_copy(pairs_h.at[:, :, c, pair], into.at[c], sems.at[(1 - chain) * tiles + c])
+            )
+            copies[-1].start()
+    labels.wait()
+    start_rows(tiles, halves, 1, mine, phase, row, send, beside, lambda c: copies[c].wait())
+    for copy in copies[tiles:]:
         copy.wait()
 
 
-def second_kernel(tiles, halves, pop, phase, after, row, send, beside):
-    start_rows(tiles, halves, 0, pop, phase, row, send, beside)
+def second_kernel(tiles, halves, mate, phase, after, row, send, beside):
+    start_rows(tiles, halves, 0, mate, phase, row, send, beside, lambda c: None)
 
 
 def merge_rows(out, row0, row1, count):
@@ -237,11 +230,24 @@
 
 
 def first_inner_kernel(
-    tiles, halves, pop, phase, conc, napl, poro, flags, row0, row1, g, fac, start, slabs, open_ends
+    tiles, halves, pop_h, conc_h, napl_h, poro_h, flags_h, phase, row0, row1, g, fac, start, slabs, open_ends,
+    pop, conc, napl, poro, flags, sems,
 ):
     rows = g.shape[1]
     length = tiles * LANES
     _, sub = iotas()
+
+    def load(q):
+        return pltpu.make_async_copy(pop_h.at[q], pop.at[q], sems.at[q])
+
+    for q in range(19):
+        load(q).start()
+    small = [
+        pltpu.make_async_copy(a, b, sems.at[19 + i])
+        for i, (a, b) in enumerate(((conc_h, conc), (napl_h, napl), (poro_h, poro), (flags_h, flags)))
+    ]
+    for copy in small:
+        copy.start()
 
     def to_slabs(read, write):
         for c in range(tiles):
@@ -261,6 +267,7 @@
     to_slabs(lambda at: drag(phase[at, :]), store_fac)
 
     def direction(q, _):
+        load(q).wait()
         to_slabs(lambda at: pop[q, at, :], store(start, q))
         return 0
 
@@ -275,6 +282,8 @@
 
     lax.fori_loop(1, rows - 1, row, 0)
     merge_rows(g, row0, row1, 19)
+    for copy in small:
+        copy.wait()
     for k, ref in enumerate((conc, napl, poro)):
         to_slabs(lambda at, ref=ref: ref[at, :], store(slabs, k))
     for k in range(2):
@@ -797,21 +806,23 @@
     pop = to_view(populations)
     views = [to_view(a) for a in (phase, concentration, napl, porosity)]
     flat = views[0].shape
-    chunks = pop.reshape(19, SUBS, tiles, SUBS, LANES)
-    given = [pltpu.with_memory_space_constraint(a, pltpu.HBM) for a in (chunks, *views, flags)]
-    popv, phv, cov, nav, pov, flv, row1, send = call(
+    pairs_of = pop.reshape(19, SUBS, tiles, SUBS // 2, 2, LANES)
+    given = [pltpu.with_memory_space_constraint(a, pltpu.HBM) for a in (pairs_of, *views, pop, flags)]
+    phv, row1, send, mate = call(
         functools.partial(first_kernel, tiles, halves),
         (
-            hold(*chunks.shape), hold(*flat, dtype=jnp.int32), hold(*flat), hold(*flat), hold(*flat),
-            hold(*flags.shape, dtype=jnp.int32), hold(19, *slab), hold(14, *slab),
+            hold(*flat, dtype=jnp.int32), hold(19, *slab), hold(14, *slab), hold(tiles, 19, SUBS, 2, LANES),
         ),
-        given, scratch=(pltpu.VMEM((19, *slab), F32), pltpu.SemaphoreType.DMA((tiles + 5,))),
-        hbm=range(6), name="first",
-    )
-    popv = popv.reshape(pop.shape)
+        given[:2],
+        scratch=(
+            pltpu.VMEM((19, *slab), F32), pltpu.VMEM((tiles, 19, SUBS, 2, LANES), F32),
+            pltpu.SemaphoreType.DMA((2 * tiles + 1,)),
+        ),
+        hbm=range(2), name="first",
+    )
     halo1 = head1 = swap(1, send)
     row0, send = call(
-        functools.partial(second_kernel, tiles, halves), (hold(19, *slab), hold(14, *slab)), (popv, phv, send),
+        functools.partial(second_kernel, tiles, halves), (hold(19, *slab), hold(14, *slab)), (mate, phv, send),
         scratch=(pltpu.VMEM((19, *slab), F32),), free=(2,), name="second",
     )
     halo0 = head0 = swap(0, send)
@@ -821,7 +832,12 @@
             hold(19, rows, *slab), hold(rows, *slab), hold(19, rows, *slab), hold(3, rows, *slab),
             hold(2, *slab),
         ),
-        (popv, phv, cov, nav, pov, flv, row0, row1), name="first_inner",
+        (given[5], *given[2:5], given[6], phv, row0, row1),
+        scratch=(
+            pltpu.VMEM((19, *flat), F32), pltpu.VMEM(flat, F32), pltpu.VMEM(flat, F32), pltpu.VMEM(flat, F32),
+            pltpu.VMEM(flags.shape, jnp.int32), pltpu.SemaphoreType.DMA((23,)),
+        ),
+        hbm=range(5), name="first_inner",
     )
 
     def inner_rows(g, after):
@@ -896,7 +912,7 @@
         (inner, rim0, rim1, late0, late1, mid),
         scratch=(pltpu.VMEM((parts, *block), F32),), name="deal",
     )
-    order = [0, *range(parts - 1, 0, -1)]
+    order = [0, *range(2, parts), 1]
     came = [blocks[0]]
     for k in order[1:]:
         came.append(lax.ppermute(blocks[k], "narrow", [(i, i ^ k) for i in range(parts)]))

time: 47.1 us -> 47.3 us (level)
  Pallas kernels: 15.2 us -> 17 us
  waiting for transfers between devices: 10.1 us -> 8.93 us
  starting transfers between devices: 20.9 us -> 20.3 us
    pallas_call x23, Pallas kernels: 15.2 us -> 17 us  [call(): pl.pallas_call(kernel, out_shape=shapes, in_specs=[spec(i, hbm, free) for...]
    ppermute x6, waiting for transfers between devices: 7.94 us -> 6.3 us  [swap(): return lax.ppermute(array, both, pairs[chain])]
    ppermute x3, starting transfers between devices: 4.45 us -> 3.87 us  [local(): lax.ppermute(blocks[k], 'narrow', [(i, i ^ k) for i in range(parts)])]
    ppermute x3, waiting for transfers between devices: 2.12 us -> 2.63 us  [local(): lax.ppermute(blocks[k], 'narrow', [(i, i ^ k) for i in range(parts)])]
  transfers between devices with their start and end apart: 9 -> 9, of which waited for: 6 -> 7; matrix products, arithmetic and copies ran while one was open for 0% -> 0% of each run, Pallas kernels for 25% -> 29%
where the time goes in v7:
time: 47.3 us; the launch traced here: 47.1 us
  starting transfers between devices  20.3 us (43%)
  Pallas kernels  17 us (36%)
  waiting for transfers between devices  8.93 us (19%)
  between operations  0.97 us (2%)
    pallas_call x23, Pallas kernels, call(): pl.pallas_call(kernel, out_shape=shapes, in_specs=[spec(i, hbm, free) for...  17 us
    ppermute x6, starting transfers between devices, swap(): return lax.ppermute(array, both, pairs[chain])  16.4 us
    ppermute x6, waiting for transfers between devices, swap(): return lax.ppermute(array, both, pairs[chain])  6.3 us
    ppermute x3, starting transfers between devices, local(): lax.ppermute(blocks[k], 'narrow', [(i, i ^ k) for i in range(parts)])  3.87 us
    ppermute x3, waiting for transfers between devices, local(): lax.ppermute(blocks[k], 'narrow', [(i, i ^ k) for i in range(parts)])  2.63 us
  transfers between devices with their start and end apart: 9, of which 7 were waited for; matrix products, arithmetic and copies ran while one was open for 0% of the time, Pallas kernels for 29%

profile of v7, /device:TPU:0, one launch (start us, length us, event | category | flops | bytes accessed | tf_op | source)
XLA Modules:
  0.0 47.1 jit_solution(740010051747108669)
XLA Ops:
  0.6 2.3 %first.1 = (s32[256,128]{1,0:T(8,128)S(1)}, f32[19,8,512]{2,1,0:T(8,128)S(1)}, f32[14,8,512]{2,1,0:T(8,128)S(1)}, f32[4,19,8,2,128]{4,3,2,1,0:T(2,128)S(1)}) custom-call(f32[19,8,4,4,2,128]{5,4,3,2,1,0:T(2,128)} %bitcast.42, s32[256,128]{1,0:T(8,128)} %bitcast.45), custom_call_target="tpu_custom_call" | custom-call | flops 1024 | bytes 1024 | tf_op jit(solution)/shard_map/first/pallas_call | solution.py:770
  2.9 6.4 %collective-permute-start.1 = (f32[14,8,512]{2,1,0:T(8,128)S(1)}, f32[14,8,512]{2,1,0:T(8,128)S(1)}, u32[]{:S(2)}, u32[]{:S(2)}) collective-permute-start(f32[14,8,512]{2,1,0:T(8,128)S(1)} %get-tuple-element.40.after), channel_id=1, source_target_pairs={{0,31},{1,2},{2,1},{3,4},{4,3},{5,6},{6,5},{7,8},{8,7},{9,10},{10,... | collective-permute-start | bytes 688136 | tf_op jit(solution)/shard_map/ppermute | solution.py:804
  9.4 1.3 %second.1 = (f32[19,8,512]{2,1,0:T(8,128)S(1)}, f32[14,8,512]{2,1,0:T(8,128)S(1)}) custom-call(f32[4,19,8,2,128]{4,3,2,1,0:T(2,128)S(1)} %get-tuple-element.39.mate, s32[256,128]{1,0:T(8,128)S(1)} %get-tuple-element.38.phase, f32[14,8,512]{2,1,0:T(8,128)S(1)} %get-tuple-element.40.after), custom_call_target="tpu_custom_call" | custom-call | flops 1024 | bytes 1024 | tf_op jit(solution)/shard_map/second/pallas_call | solution.py:770
  10.7 2.8 %first_inner.1 = (f32[19,8,8,512]{3,2,1,0:T(8,128)S(1)}, f32[8,8,512]{2,1,0:T(8,128)S(1)}, f32[19,8,8,512]{3,2,1,0:T(8,128)S(1)}, f32[3,8,8,512]{3,2,1,0:T(8,128)S(1)}, f32[2,8,512]{2,1,0:T(8,128)S(1)}) custom-call(f32[19,256,128]{2,1,0:T(8,128)} %bitcast.43, f32[256,128]{1,0:T(8,128)} %bitcast.46, f32[256,128]{1,0:T(8,128)} %bitcast.47, ...), custom_call_target="tpu_custom_call" | custom-call | flops 1024 | bytes 1024 | tf_op jit(solution)/shard_map/first_inner/pallas_call | solution.py:770
  13.5 1.2 %inner.3 = f32[19,8,8,512]{3,2,1,0:T(8,128)S(1)} custom-call(f32[19,8,8,512]{3,2,1,0:T(8,128)S(1)} %get-tuple-element.43.g.after, f32[8,8,512]{2,1,0:T(8,128)S(1)} %get-tuple-element.44.fac, f32[3,8,8,512]{3,2,1,0:T(8,128)S(1)} %get-tuple-element.46.after.slabs), custom_call_target="tpu_custom_call" | custom-call | flops 1024 | bytes 1024 | tf_op jit(solution)/shard_map/inner/pallas_call | solution.py:770
  14.8 0.7 %collective-permute-done.1.halo.first_halo = f32[14,8,512]{2,1,0:T(8,128)S(1)} collective-permute-done((f32[14,8,512]{2,1,0:T(8,128)S(1)}, f32[14,8,512]{2,1,0:T(8,128)S(1)}, u32[]{:S(2)}, u32[]{:S(2)}) %collective-permute-start.1) | collective-permute-done | bytes 229408 | tf_op jit(solution)/shard_map/ppermute | solution.py:804
  15.8 0.4 far1.1
  16.1 5.6 %collective-permute-start.3 = (f32[14,8,512]{2,1,0:T(8,128)S(1)}, f32[14,8,512]{2,1,0:T(8,128)S(1)}, u32[]{:S(2)}, u32[]{:S(2)}) collective-permute-start(f32[14,8,512]{2,1,0:T(8,128)S(1)} %get-tuple-element.49.after), channel_id=1, source_target_pairs={{0,31},{1,2},{2,1},{3,4},{4,3},{5,6},{6,5},{7,8},{8,7},{9,10},{10,... | collective-permute-start | bytes 688136 | tf_op jit(solution)/shard_map/ppermute | solution.py:804
  22.0 0.4 far0.1
  22.3 0.5 %collective-permute-start.2 = (f32[14,8,512]{2,1,0:T(8,128)S(1)}, f32[14,8,512]{2,1,0:T(8,128)S(1)}, u32[]{:S(2)}, u32[]{:S(2)}) collective-permute-start(f32[14,8,512]{2,1,0:T(8,128)S(1)} %get-tuple-element.52.after), channel_id=1, source_target_pairs={{0,1},{1,0},{2,3},{3,2},{4,5},{5,4},{6,7},{7,6},{8,9},{9,8},{10,11... | collective-permute-start | bytes 688136 | tf_op jit(solution)/shard_map/ppermute | solution.py:804
  22.8 1.2 %inner.4 = f32[19,8,8,512]{3,2,1,0:T(8,128)S(1)} custom-call(f32[19,8,8,512]{3,2,1,0:T(8,128)S(1)} %get-tuple-element.50.g, f32[8,8,512]{2,1,0:T(8,128)S(1)} %get-tuple-element.44.fac, f32[14,8,512]{2,1,0:T(8,128)S(1)} %get-tuple-element.52.after), custom_call_target="tpu_custom_call" | custom-call | flops 1024 | bytes 1024 | tf_op jit(solution)/shard_map/inner/pallas_call | solution.py:770
  24.1 1.2 %inner.5.g.after = f32[19,8,8,512]{3,2,1,0:T(8,128)S(1)} custom-call(f32[19,8,8,512]{3,2,1,0:T(8,128)S(1)} %put.1.g.after, f32[8,8,512]{2,1,0:T(8,128)S(1)} %get-tuple-element.44.fac, f32[19,8,8,512]{3,2,1,0:T(8,128)S(1)} %put.1.g.after), custom_call_target="tpu_custom_call" | custom-call | flops 1024 | bytes 1024 | tf_op jit(solution)/shard_map/inner/pallas_call | solution.py:770
  25.3 0.5 %inner_speed.1.after.u = f32[3,4,8,512]{3,2,1,0:T(8,128)S(1)} custom-call(f32[19,8,8,512]{3,2,1,0:T(8,128)S(1)} %inner.5.g.after, f32[8,8,512]{2,1,0:T(8,128)S(1)} %get-tuple-element.44.fac, f32[19,8,8,512]{3,2,1,0:T(8,128)S(1)} %inner.5.g.after), custom_call_target="tpu_custom_call" | custom-call | flops 1024 | bytes 1024 | tf_op jit(solution)/shard_map/inner_speed/pallas_call | solution.py:770
  25.9 2.0 %collective-permute-done.3.halo = f32[14,8,512]{2,1,0:T(8,128)S(1)} collective-permute-done((f32[14,8,512]{2,1,0:T(8,128)S(1)}, f32[14,8,512]{2,1,0:T(8,128)S(1)}, u32[]{:S(2)}, u32[]{:S(2)}) %collective-permute-start.3) | collective-permute-done | bytes 229408 | tf_op jit(solution)/shard_map/ppermute | solution.py:804
  28.5 3.8 %collective-permute-start.5 = (f32[5,8,512]{2,1,0:T(8,128)S(1)}, f32[5,8,512]{2,1,0:T(8,128)S(1)}, u32[]{:S(2)}, u32[]{:S(2)}) collective-permute-start(f32[5,8,512]{2,1,0:T(8,128)S(1)} %get-tuple-element.57.after), channel_id=1, source_target_pairs={{0,31},{1,2},{2,1},{3,4},{4,3},{5,6},{6,5},{7,8},{8,7},{9,10},{10,... | collective-permute-start | bytes 245768 | tf_op jit(solution)/shard_map/ppermute | solution.py:804
  33.5 2.7 %collective-permute-done.5.there = f32[5,8,512]{2,1,0:T(8,128)S(1)} collective-permute-done((f32[5,8,512]{2,1,0:T(8,128)S(1)}, f32[5,8,512]{2,1,0:T(8,128)S(1)}, u32[]{:S(2)}, u32[]{:S(2)}) %collective-permute-start.5) | collective-permute-done | bytes 81952 | tf_op jit(solution)/shard_map/ppermute | solution.py:804
  36.5 0.9 %collective-permute-done.4.there = f32[5,8,512]{2,1,0:T(8,128)S(1)} collective-permute-done((f32[5,8,512]{2,1,0:T(8,128)S(1)}, f32[5,8,512]{2,1,0:T(8,128)S(1)}, u32[]{:S(2)}, u32[]{:S(2)}) %collective-permute-start.4) | collective-permute-done | bytes 81952 | tf_op jit(solution)/shard_map/ppermute | solution.py:804
  37.8 1.8 %collective-permute-start.6 = (f32[2,4,16,128]{3,2,1,0:T(8,128)S(1)}, f32[2,4,16,128]{3,2,1,0:T(8,128)S(1)}, u32[]{:S(2)}, u32[]{:S(2)}) collective-permute-start(f32[2,4,16,128]{3,2,1,0:T(8,128)S(1)} %get-tuple-element.68), channel_id=1, source_target_pairs={{0,2},{1,3},{2,0},{3,1},{4,6},{5,7},{6,4},{7,5},{8,10},{9,11},{10,... | collective-permute-start | bytes 196616 | tf_op jit(solution)/shard_map/ppermute | solution.py:918
  39.6 1.5 %collective-permute-start.7 = (f32[2,4,16,128]{3,2,1,0:T(8,128)S(1)}, f32[2,4,16,128]{3,2,1,0:T(8,128)S(1)}, u32[]{:S(2)}, u32[]{:S(2)}) collective-permute-start(f32[2,4,16,128]{3,2,1,0:T(8,128)S(1)} %get-tuple-element.69), channel_id=1, source_target_pairs={{0,3},{1,2},{2,1},{3,0},{4,7},{5,6},{6,5},{7,4},{8,11},{9,10},{10,... | collective-permute-start | bytes 196616 | tf_op jit(solution)/shard_map/ppermute | solution.py:918
  41.2 0.5 %collective-permute-start.8 = (f32[2,4,16,128]{3,2,1,0:T(8,128)S(1)}, f32[2,4,16,128]{3,2,1,0:T(8,128)S(1)}, u32[]{:S(2)}, u32[]{:S(2)}) collective-permute-start(f32[2,4,16,128]{3,2,1,0:T(8,128)S(1)} %get-tuple-element.70), channel_id=1, source_target_pairs={{0,1},{1,0},{2,3},{3,2},{4,5},{5,4},{6,7},{7,6},{8,9},{9,8},{10,11... | collective-permute-start | bytes 196616 | tf_op jit(solution)/shard_map/ppermute | solution.py:918
  41.7 1.9 %final.1 = f32[19,256,128]{2,1,0:T(8,128)} custom-call(f32[19,8,8,512]{3,2,1,0:T(8,128)S(1)} %get-tuple-element.58.g, f32[8,8,512]{2,1,0:T(8,128)S(1)} %get-tuple-element.44.fac, f32[5,8,512]{2,1,0:T(8,128)S(1)} %get-tuple-element.59.ghost.after.halo0, f32[5,8,512]{2,1,0:T(8,128)S(1)} %get-tuple-element.56.ghost.after.halo1, ...), custom_call_target="tpu_custom_call" | custom-call | flops 1024 | bytes 1024 | tf_op jit(solution)/shard_map/final/pallas_call | solution.py:770
  43.6 1.2 %collective-permute-done.6.refs_1_ = f32[2,4,16,128]{3,2,1,0:T(8,128)S(1)} collective-permute-done((f32[2,4,16,128]{3,2,1,0:T(8,128)S(1)}, f32[2,4,16,128]{3,2,1,0:T(8,128)S(1)}, u32[]{:S(2)}, u32[]{:S(2)}) %collective-permute-start.6) | collective-permute-done | bytes 65568 | tf_op jit(solution)/shard_map/ppermute | solution.py:918
  44.8 1.1 %collective-permute-done.7.refs_2_ = f32[2,4,16,128]{3,2,1,0:T(8,128)S(1)} collective-permute-done((f32[2,4,16,128]{3,2,1,0:T(8,128)S(1)}, f32[2,4,16,128]{3,2,1,0:T(8,128)S(1)}, u32[]{:S(2)}, u32[]{:S(2)}) %collective-permute-start.7) | collective-permute-done | bytes 65568 | tf_op jit(solution)/shard_map/ppermute | solution.py:918
  46.2 0.8 %gather.1 = (f32[4,4,16,128]{3,2,1,0:T(8,128)}, f32[4,4,16,128]{3,2,1,0:T(8,128)}) custom-call(f32[2,4,16,128]{3,2,1,0:T(8,128)S(1)} %get-tuple-element.67.after.refs_0_, f32[2,4,16,128]{3,2,1,0:T(8,128)S(1)} %collective-permute-done.6.refs_1_, f32[2,4,16,128]{3,2,1,0:T(8,128)S(1)} %collective-permute-done.7.refs_2_, ...), custom_call_target="tpu_custom_call" | custom-call | flops 1024 | bytes 1024 | tf_op jit(solution)/shard_map/gather/pallas_call | solution.py:770
  (17 shorter events, 3.5 us)
Async XLA Ops:
  2.9 12.5 %collective-permute-start.1 = (f32[14,8,512]{2,1,0:T(8,128)S(1)}, f32[14,8,512]{2,1,0:T(8,128)S(1)}, u32[]{:S(2)}, u32[]{:S(2)}) collective-permute-start(f32[14,8,512]{2,1,0:T(8,128)S(1)} %get-tuple-element.40.after), channel_id=1, source_target_pairs={{0,31},{1,2},{2,1},{3,4},{4,3},{5,6},{6,5},{7,8},{8,7},{9,10},{10,... | collective-permute-start | bytes 688136 | tf_op jit(solution)/shard_map/ppermute | solution.py:804
  10.7 11.0 %collective-permute-start = (f32[14,8,512]{2,1,0:T(8,128)S(1)}, f32[14,8,512]{2,1,0:T(8,128)S(1)}, u32[]{:S(2)}, u32[]{:S(2)}) collective-permute-start(f32[14,8,512]{2,1,0:T(8,128)S(1)} %get-tuple-element.45), channel_id=1, source_target_pairs={{0,1},{1,0},{2,3},{3,2},{4,5},{5,4},{6,7},{7,6},{8,9},{9,8},{10,11... | collective-permute-start | bytes 688136 | tf_op jit(solution)/shard_map/ppermute | solution.py:804
  16.1 11.7 %collective-permute-start.3 = (f32[14,8,512]{2,1,0:T(8,128)S(1)}, f32[14,8,512]{2,1,0:T(8,128)S(1)}, u32[]{:S(2)}, u32[]{:S(2)}) collective-permute-start(f32[14,8,512]{2,1,0:T(8,128)S(1)} %get-tuple-element.49.after), channel_id=1, source_target_pairs={{0,31},{1,2},{2,1},{3,4},{4,3},{5,6},{6,5},{7,8},{8,7},{9,10},{10,... | collective-permute-start | bytes 688136 | tf_op jit(solution)/shard_map/ppermute | solution.py:804
  22.3 9.9 %collective-permute-start.2 = (f32[14,8,512]{2,1,0:T(8,128)S(1)}, f32[14,8,512]{2,1,0:T(8,128)S(1)}, u32[]{:S(2)}, u32[]{:S(2)}) collective-permute-start(f32[14,8,512]{2,1,0:T(8,128)S(1)} %get-tuple-element.52.after), channel_id=1, source_target_pairs={{0,1},{1,0},{2,3},{3,2},{4,5},{5,4},{6,7},{7,6},{8,9},{9,8},{10,11... | collective-permute-start | bytes 688136 | tf_op jit(solution)/shard_map/ppermute | solution.py:804
  28.5 7.7 %collective-permute-start.5 = (f32[5,8,512]{2,1,0:T(8,128)S(1)}, f32[5,8,512]{2,1,0:T(8,128)S(1)}, u32[]{:S(2)}, u32[]{:S(2)}) collective-permute-start(f32[5,8,512]{2,1,0:T(8,128)S(1)} %get-tuple-element.57.after), channel_id=1, source_target_pairs={{0,31},{1,2},{2,1},{3,4},{4,3},{5,6},{6,5},{7,8},{8,7},{9,10},{10,... | collective-permute-start | bytes 245768 | tf_op jit(solution)/shard_map/ppermute | solution.py:804
  32.9 4.5 %collective-permute-start.4 = (f32[5,8,512]{2,1,0:T(8,128)S(1)}, f32[5,8,512]{2,1,0:T(8,128)S(1)}, u32[]{:S(2)}, u32[]{:S(2)}) collective-permute-start(f32[5,8,512]{2,1,0:T(8,128)S(1)} %get-tuple-element.66), channel_id=1, source_target_pairs={{0,1},{1,0},{2,3},{3,2},{4,5},{5,4},{6,7},{7,6},{8,9},{9,8},{10,11... | collective-permute-start | bytes 245768 | tf_op jit(solution)/shard_map/ppermute | solution.py:804
  37.8 7.0 %collective-permute-start.6 = (f32[2,4,16,128]{3,2,1,0:T(8,128)S(1)}, f32[2,4,16,128]{3,2,1,0:T(8,128)S(1)}, u32[]{:S(2)}, u32[]{:S(2)}) collective-permute-start(f32[2,4,16,128]{3,2,1,0:T(8,128)S(1)} %get-tuple-element.68), channel_id=1, source_target_pairs={{0,2},{1,3},{2,0},{3,1},{4,6},{5,7},{6,4},{7,5},{8,10},{9,11},{10,... | collective-permute-start | bytes 196616 | tf_op jit(solution)/shard_map/ppermute | solution.py:918
  39.6 6.2 %collective-permute-start.7 = (f32[2,4,16,128]{3,2,1,0:T(8,128)S(1)}, f32[2,4,16,128]{3,2,1,0:T(8,128)S(1)}, u32[]{:S(2)}, u32[]{:S(2)}) collective-permute-start(f32[2,4,16,128]{3,2,1,0:T(8,128)S(1)} %get-tuple-element.69), channel_id=1, source_target_pairs={{0,3},{1,2},{2,1},{3,0},{4,7},{5,6},{6,5},{7,4},{8,11},{9,10},{10,... | collective-permute-start | bytes 196616 | tf_op jit(solution)/shard_map/ppermute | solution.py:918
  41.2 5.0 %collective-permute-start.8 = (f32[2,4,16,128]{3,2,1,0:T(8,128)S(1)}, f32[2,4,16,128]{3,2,1,0:T(8,128)S(1)}, u32[]{:S(2)}, u32[]{:S(2)}) collective-permute-start(f32[2,4,16,128]{3,2,1,0:T(8,128)S(1)} %get-tuple-element.70), channel_id=1, source_target_pairs={{0,1},{1,0},{2,3},{3,2},{4,5},{5,4},{6,7},{7,6},{8,9},{9,8},{10,11... | collective-permute-start | bytes 196616 | tf_op jit(solution)/shard_map/ppermute | solution.py:918

commit v8 on v4

--- a/solution.py
+++ b/solution.py
@@ -221,8 +221,16 @@
         copy.wait()
 
 
-def second_kernel(tiles, halves, pop, phase, after, row, send, beside):
-    start_rows(tiles, halves, 0, pop, phase, row, send, beside)
+def second_kernel(tiles, pop, phase, after, row, send):
+    x = jnp.where(upper(0), SUBS - 1, 0)
+    for c in range(tiles):
+        start_row(tiles, pop, phase, x, row, c)
+
+    def side(up):
+        for i, q in enumerate(UP if up else DOWN):
+            send[i] = row[q]
+
+    by_side(0, side)
 
 
 def merge_rows(out, row0, row1, count):
@@ -299,11 +307,35 @@
     lax.fori_loop(1, rows - 1, row, 0)
 
 
-def put_kernel(inner, row0, row1, out):
-    merge_rows(out, row0, row1, 19)
-
-
-def arrive_kernel(tiles, halves, chain, g, fac, halo, first_halo, after, inner, out, ghost):
+def put_kernel(chain, inner, row, out):
+    rows = out.shape[1]
+
+    def side(up):
+        for q in range(19):
+            out[q, rows - 1 if up else 0] = row[q]
+
+    by_side(chain, side)
+
+
+def edge_kernel(tiles, halves, chain, g, fac, halo, slabs, after, row, send):
+    rows = g.shape[1]
+    lane, sub = iotas()
+
+    def side(up):
+        x = rows - 1 if up else 0
+        lo, hi, place = (None, halo, "last") if up else (halo, None, "first")
+        for c in range(tiles):
+            post = collide(stream(g, lo, hi, x, c, tiles, halves, lane, sub, place), fac[x, :, cut(c)])
+            for q in range(19):
+                row[q, :, cut(c)] = post[q]
+            for i, q in enumerate(UP if up else DOWN):
+                send[i, :, cut(c)] = post[q]
+        send[5] = slabs[0, x]
+
+    by_side(chain, side)
+
+
+def arrive_kernel(tiles, halves, chain, g, fac, halo, first_halo, other, after, inner, out, ghost):
     rows = g.shape[1]
     lane, sub = iotas()
 
@@ -311,6 +343,8 @@
         x = rows - 1 if up else 0
         lo, hi, place = (None, halo, "last") if up else (halo, None, "first")
         toward, back = (DOWN, UP) if up else (UP, DOWN)
+        for q in range(19):
+            out[q, rows - 1 - x] = other[q]
         for c in range(tiles):
             post = collide(stream(g, lo, hi, x, c, tiles, halves, lane, sub, place), fac[x, :, cut(c)])
             for q in range(19):
@@ -359,7 +393,7 @@
         look_ahead(
             tiles, halves, up, lambda q, c: row[q, :, cut(c)], lambda q, c: beside[q, :, cut(c)], send
         )
-        send[13] = slabs[0, x]
+        send[13] = slabs[0, x] if chain else fac[x]
 
     by_side(chain, side)
 
@@ -577,14 +611,14 @@
             write(cs.at[k, r - 2], v)
 
 
-def static_readers(ends, up, slabs, halo, there, flags):
+def static_readers(ends, up, slabs, halo, k, there, flags):
     rows = slabs.shape[1]
     first, last = ends_of(*ends)
 
     def conc(r):
         if 0 <= r < rows:
             return read(slabs.at[0, r])
-        beyond = read(halo.at[13] if r in (-1, rows) else there.at[3])
+        beyond = read(halo.at[k] if r in (-1, rows) else there.at[3])
         return pick(last, read(slabs.at[0, rows - 1]), beyond) if up else [jnp.where(first, ZERO, t) for t in beyond]
 
     def poro(r):
@@ -607,7 +641,7 @@
                 f = stream(g, lo, hi, at, c, tiles, halves, lane, sub, where)
                 for i, v in enumerate(speed(f, fac[at, :, cut(c)])):
                     ue[n, i, :, cut(c)] = v
-        conc, poro = static_readers(ends, up, slabs, halo, None, None)
+        conc, poro = static_readers(ends, up, slabs, halo, 13 if chain else 5, None, None)
 
         def vel(k, r):
             return read(ue.at[0 if r == x else 1, k] if r in (x, beside) else u.at[k, r - 2])
@@ -667,7 +701,7 @@
         x = rows - 1 if up else 0
         beyond = rows if up else -1
         ghost = last if up else first
-        conc, poro = static_readers(ends, up, slabs, halo, there, flags)
+        conc, poro = static_readers(ends, up, slabs, halo, 13 if chain else 5, there, flags)
 
         def vel(k, r):
             if r == beyond:
@@ -812,10 +846,10 @@
     popv = popv.reshape(pop.shape)
     halo1 = head1 = swap(1, send)
     row0, send = call(
-        functools.partial(second_kernel, tiles, halves), (hold(19, *slab), hold(14, *slab)), (popv, phv, send),
-        scratch=(pltpu.VMEM((19, *slab), F32),), free=(2,), name="second",
-    )
-    halo0 = head0 = swap(0, send)
+        functools.partial(second_kernel, tiles), (hold(19, *slab), hold(5, *slab)), (popv, phv, send),
+        free=(2,), name="second",
+    )
+    halo0 = swap(0, send)
     g, fac, start, slabs, open_ends = call(
         functools.partial(first_inner_kernel, tiles, halves),
         (
@@ -831,10 +865,10 @@
             name="inner",
         )
 
-    def arrive(chain, g, halo, head, after, new):
+    def arrive(chain, g, halo, head, other, after, new):
         return call(
             functools.partial(arrive_kernel, tiles, halves, chain), (hold(19, rows, *slab), hold(5, *slab)),
-            (g, fac, halo, head, after, new), free=(4, 5), name=f"arrive{chain}", aliases={5: 0},
+            (g, fac, halo, head, other, after, new), free=(5, 6), name=f"arrive{chain}", aliases={6: 0},
         )
 
     def far(chain, g, ghost, after):
@@ -850,31 +884,32 @@
             (g, fac, ghost, u, slabs, halo, after), free=(6,), name=f"rim{chain}",
         )
 
-    after = slabs
-    for pair in range(LBM_STEPS // 2):
-        new = inner_rows(g, after)
-        if pair < LBM_STEPS // 2 - 1:
-            later, ghost1 = arrive(1, g, halo1, head1, g, new)
-            row1, send1 = far(1, later, ghost1, ghost1)
-            halo1 = swap(1, send1)
-            later, ghost0 = arrive(0, g, halo0, head0, send1, later)
-            row0, send0 = far(0, later, ghost0, ghost0)
-            halo0 = swap(0, send0)
-            new = inner_rows(later, send0)
-            g = call(
-                put_kernel, hold(19, rows, *slab), (new, row0, row1), name="put", aliases={0: 0}, free=(0,)
-            )
-            after = g
+    new = inner_rows(g, slabs)
+    row0, send0 = far(0, g, halo0, new)
+    halo0 = swap(0, send0)
+    g, ghost1 = arrive(1, g, halo1, head1, row0, send0, new)
+    row1, send1 = far(1, g, ghost1, ghost1)
+    halo1 = swap(1, send1)
+    new = inner_rows(g, send1)
+    g, ghost0 = arrive(0, g, halo0, halo0, row1, row1, new)
+    row0, send0 = call(
+        functools.partial(edge_kernel, tiles, halves, 0), (hold(19, *slab), hold(6, *slab)),
+        (g, fac, ghost0, slabs, ghost0), free=(4,), name="edge0",
+    )
+    halo0 = swap(0, send0)
+    new = inner_rows(g, send0)
     u = call(
         functools.partial(inner_speed_kernel, tiles, halves), hold(3, rows - 4, *slab), (new, fac, new),
         free=(2,), name="inner_speed",
     )
-    later, ghost1 = arrive(1, g, halo1, head1, u, new)
-    ue1, rim1, send1 = rim(1, later, ghost1, halo1, ghost1)
+    part = call(
+        functools.partial(put_kernel, 0), hold(19, rows, *slab), (new, row0), name="put", aliases={0: 0}, free=(0,)
+    )
+    ue0, rim0, send0 = rim(0, part, halo0, halo0, u)
+    there0 = swap(0, send0)
+    g, ghost1 = arrive(1, g, halo1, head1, row0, send0, part)
+    ue1, rim1, send1 = rim(1, g, ghost1, halo1, ghost1)
     there1 = swap(1, send1)
-    g, ghost0 = arrive(0, g, halo0, head0, send1, later)
-    ue0, rim0, send0 = rim(0, g, ghost0, halo0, ghost0)
-    there0 = swap(0, send0)
     inner = call(
         functools.partial(early_kernel, tiles, halves), hold(2, rows - 4, *slab), (slabs, u, ue0, ue1),
         name="early",
@@ -883,20 +918,20 @@
         functools.partial(middle_kernel, tiles, halves), hold(rows - 6, *slab), (slabs, u, inner, rim0, rim1),
         name="middle",
     )
+    late0 = call(
+        functools.partial(late_kernel, tiles, halves, ends, 0), hold(4, *slab),
+        (slabs, u, ue0, inner, rim0, halo0, open_ends, there0, mid), free=(8,), name="late0",
+    )
     out, token = call(
         functools.partial(final_kernel, tiles, halves),
         (jax.ShapeDtypeStruct((19, *flat), F32), hold(SUBS, LANES)),
-        (g, fac, ghost0, ghost1, start, mid),
+        (g, fac, halo0, ghost1, start, late0),
         scratch=(pltpu.VMEM((19, *flat), F32), pltpu.SemaphoreType.DMA((19,))),
         free=(5,), hbm_out=(0,), name="final",
     )
     late1 = call(
         functools.partial(late_kernel, tiles, halves, ends, 1), hold(4, *slab),
         (slabs, u, ue1, inner, rim1, halo1, open_ends, there1, token), free=(8,), name="late1",
-    )
-    late0 = call(
-        functools.partial(late_kernel, tiles, halves, ends, 0), hold(4, *slab),
-        (slabs, u, ue0, inner, rim0, halo0, open_ends, there0, late1), free=(8,), name="late0",
     )
     block = (2, layers, run, LANES)
     blocks = call(

time: 46.9 us -> 50.1 us (1.068)
  waiting for transfers between devices: 10.8 us -> 15.7 us
  starting transfers between devices: 20 us -> 18.9 us
  Pallas kernels: 15.2 us -> 14.6 us
    ppermute x6 -> x7, waiting for transfers between devices: 6.02 us -> 11.4 us  [swap(): return lax.ppermute(array, both, pairs[chain])]
    ppermute x6 -> x7, starting transfers between devices: 16.4 us -> 15.3 us  [swap(): return lax.ppermute(array, both, pairs[chain])]
    pallas_call x23, Pallas kernels: 15.2 us -> 14.6 us  [call(): pl.pallas_call(kernel, out_shape=shapes, in_specs=[spec(i, hbm, free) for...]
  transfers between devices with their start and end apart: 9 -> 10, of which waited for: 7 -> 8; matrix products, arithmetic and copies ran while one was open for 0% -> 0% of each run, Pallas kernels for 25% -> 23%
where the time goes in v8:
time: 50.1 us; the launch traced here: 50 us
  starting transfers between devices  18.9 us (38%)
  waiting for transfers between devices  15.7 us (31%)
  Pallas kernels  14.6 us (29%)
  between operations  0.81 us (2%)
    ppermute x7, starting transfers between devices, swap(): return lax.ppermute(array, both, pairs[chain])  15.3 us
    pallas_call x23, Pallas kernels, call(): pl.pallas_call(kernel, out_shape=shapes, in_specs=[spec(i, hbm, free) for...  14.6 us
    ppermute x7, waiting for transfers between devices, swap(): return lax.ppermute(array, both, pairs[chain])  11.4 us
    ppermute x3, waiting for transfers between devices, local(): lax.ppermute(blocks[k], 'narrow', [(i, i ^ k) for i in range(parts)])  4.31 us
    ppermute x3, starting transfers between devices, local(): lax.ppermute(blocks[k], 'narrow', [(i, i ^ k) for i in range(parts)])  3.55 us
  transfers between devices with their start and end apart: 10, of which 8 were waited for; matrix products, arithmetic and copies ran while one was open for 0% of the time, Pallas kernels for 23%

profile of v8, /device:TPU:0, one launch (start us, length us, event | category | flops | bytes accessed | tf_op | source)
XLA Modules:
  0.0 50.0 jit_solution(10907698004566782223)
XLA Ops:
  0.6 2.2 %first.1 = (f32[19,8,4,8,128]{4,3,2,1,0:T(8,128)S(1)}, s32[256,128]{1,0:T(8,128)S(1)}, f32[256,128]{1,0:T(8,128)S(1)}, f32[256,128]{1,0:T(8,128)S(1)}, f32[256,1...) custom-call(f32[19,8,4,8,128]{4,3,2,1,0:T(8,128)} %bitcast.43, ...), custom_call_target="tpu_custom_call" | custom-call | flops 1024 | bytes 1024 | tf_op jit(solution)/shard_map/first/pallas_call | solution.py:796
  2.8 6.4 %collective-permute-start = (f32[14,8,512]{2,1,0:T(8,128)S(1)}, f32[14,8,512]{2,1,0:T(8,128)S(1)}, u32[]{:S(2)}, u32[]{:S(2)}) collective-permute-start(f32[14,8,512]{2,1,0:T(8,128)S(1)} %get-tuple-element.50.after), channel_id=1, source_target_pairs={{0,31},{1,2},{2,1},{3,4},{4,3},{5,6},{6,5},{7,8},{8,7},{9,10},{10,... | collective-permute-start | bytes 688136 | tf_op jit(solution)/shard_map/ppermute | solution.py:830
  9.3 0.4 second.1
  9.8 1.5 %first_inner.1 = (f32[19,8,8,512]{3,2,1,0:T(8,128)S(1)}, f32[8,8,512]{2,1,0:T(8,128)S(1)}, f32[19,8,8,512]{3,2,1,0:T(8,128)S(1)}, f32[3,8,8,512]{3,2,1,0:T(8,128)S(1)}, f32[2,8,512]{2,1,0:T(8,128)S(1)}) custom-call(f32[19,256,128]{2,1,0:T(8,128)S(1)} %bitcast.42, s32[256,128]{1,0:T(8,128)S(1)} %get-tuple-element.45.phase, ...), custom_call_target="tpu_custom_call" | custom-call | flops 1024 | bytes 1024 | tf_op jit(solution)/shard_map/first_inner/pallas_call | solution.py:796
  11.3 1.2 %inner.3.after = f32[19,8,8,512]{3,2,1,0:T(8,128)S(1)} custom-call(f32[19,8,8,512]{3,2,1,0:T(8,128)S(1)} %get-tuple-element.53.g, f32[8,8,512]{2,1,0:T(8,128)S(1)} %get-tuple-element.54.fac, f32[3,8,8,512]{3,2,1,0:T(8,128)S(1)} %get-tuple-element.56.after.slabs), custom_call_target="tpu_custom_call" | custom-call | flops 1024 | bytes 1024 | tf_op jit(solution)/shard_map/inner/pallas_call | solution.py:796
  12.5 3.8 %collective-permute-done.1.halo = f32[5,8,512]{2,1,0:T(8,128)S(1)} collective-permute-done((f32[5,8,512]{2,1,0:T(8,128)S(1)}, f32[5,8,512]{2,1,0:T(8,128)S(1)}, u32[]{:S(2)}, u32[]{:S(2)}) %collective-permute-start.1) | collective-permute-done | bytes 81952 | tf_op jit(solution)/shard_map/ppermute | solution.py:830
  16.6 1.5 %collective-permute-start.2 = (f32[14,8,512]{2,1,0:T(8,128)S(1)}, f32[14,8,512]{2,1,0:T(8,128)S(1)}, u32[]{:S(2)}, u32[]{:S(2)}) collective-permute-start(f32[14,8,512]{2,1,0:T(8,128)S(1)} %get-tuple-element.58.after), channel_id=1, source_target_pairs={{0,1},{1,0},{2,3},{3,2},{4,5},{5,4},{6,7},{7,6},{8,9},{9,8},{10,11... | collective-permute-start | bytes 688136 | tf_op jit(solution)/shard_map/ppermute | solution.py:830
  18.7 1.9 %collective-permute-start.3 = (f32[14,8,512]{2,1,0:T(8,128)S(1)}, f32[14,8,512]{2,1,0:T(8,128)S(1)}, u32[]{:S(2)}, u32[]{:S(2)}) collective-permute-start(f32[14,8,512]{2,1,0:T(8,128)S(1)} %get-tuple-element.62.after), channel_id=1, source_target_pairs={{0,31},{1,2},{2,1},{3,4},{4,3},{5,6},{6,5},{7,8},{8,7},{9,10},{10,... | collective-permute-start | bytes 688136 | tf_op jit(solution)/shard_map/ppermute | solution.py:830
  20.6 1.2 %inner.4 = f32[19,8,8,512]{3,2,1,0:T(8,128)S(1)} custom-call(f32[19,8,8,512]{3,2,1,0:T(8,128)S(1)} %get-tuple-element.59.g, f32[8,8,512]{2,1,0:T(8,128)S(1)} %get-tuple-element.54.fac, f32[14,8,512]{2,1,0:T(8,128)S(1)} %get-tuple-element.62.after), custom_call_target="tpu_custom_call" | custom-call | flops 1024 | bytes 1024 | tf_op jit(solution)/shard_map/inner/pallas_call | solution.py:796
  21.8 2.4 %collective-permute-done.2.halo.first_halo = f32[14,8,512]{2,1,0:T(8,128)S(1)} collective-permute-done((f32[14,8,512]{2,1,0:T(8,128)S(1)}, f32[14,8,512]{2,1,0:T(8,128)S(1)}, u32[]{:S(2)}, u32[]{:S(2)}) %collective-permute-start.2) | collective-permute-done | bytes 229408 | tf_op jit(solution)/shard_map/ppermute | solution.py:830
  24.7 2.5 %collective-permute-start.4 = (f32[6,8,512]{2,1,0:T(8,128)S(1)}, f32[6,8,512]{2,1,0:T(8,128)S(1)}, u32[]{:S(2)}, u32[]{:S(2)}) collective-permute-start(f32[6,8,512]{2,1,0:T(8,128)S(1)} %get-tuple-element.66.after), channel_id=1, source_target_pairs={{0,1},{1,0},{2,3},{3,2},{4,5},{5,4},{6,7},{7,6},{8,9},{9,8},{10,11... | collective-permute-start | bytes 294920 | tf_op jit(solution)/shard_map/ppermute | solution.py:830
  27.2 1.2 %inner.5.g.after = f32[19,8,8,512]{3,2,1,0:T(8,128)S(1)} custom-call(f32[19,8,8,512]{3,2,1,0:T(8,128)S(1)} %get-tuple-element.63.g, f32[8,8,512]{2,1,0:T(8,128)S(1)} %get-tuple-element.54.fac, f32[6,8,512]{2,1,0:T(8,128)S(1)} %get-tuple-element.66.after), custom_call_target="tpu_custom_call" | custom-call | flops 1024 | bytes 1024 | tf_op jit(solution)/shard_map/inner/pallas_call | solution.py:796
  28.4 0.5 %inner_speed.1.u.after = f32[3,4,8,512]{3,2,1,0:T(8,128)S(1)} custom-call(f32[19,8,8,512]{3,2,1,0:T(8,128)S(1)} %inner.5.g.after, f32[8,8,512]{2,1,0:T(8,128)S(1)} %get-tuple-element.54.fac, f32[19,8,8,512]{3,2,1,0:T(8,128)S(1)} %inner.5.g.after), custom_call_target="tpu_custom_call" | custom-call | flops 1024 | bytes 1024 | tf_op jit(solution)/shard_map/inner_speed/pallas_call | solution.py:796
  29.0 2.8 %collective-permute-done.4.ghost.halo.halo0 = f32[6,8,512]{2,1,0:T(8,128)S(1)} collective-permute-done((f32[6,8,512]{2,1,0:T(8,128)S(1)}, f32[6,8,512]{2,1,0:T(8,128)S(1)}, u32[]{:S(2)}, u32[]{:S(2)}) %collective-permute-start.4) | collective-permute-done | bytes 98336 | tf_op jit(solution)/shard_map/ppermute | solution.py:830
  32.9 2.9 %collective-permute-start.6 = (f32[5,8,512]{2,1,0:T(8,128)S(1)}, f32[5,8,512]{2,1,0:T(8,128)S(1)}, u32[]{:S(2)}, u32[]{:S(2)}) collective-permute-start(f32[5,8,512]{2,1,0:T(8,128)S(1)} %get-tuple-element.77), channel_id=1, source_target_pairs={{0,31},{1,2},{2,1},{3,4},{4,3},{5,6},{6,5},{7,8},{8,7},{9,10},{10,... | collective-permute-start | bytes 245768 | tf_op jit(solution)/shard_map/ppermute | solution.py:830
  36.9 1.9 %final.1 = (f32[19,256,128]{2,1,0:T(8,128)}, f32[8,128]{1,0:T(8,128)S(1)}) custom-call(f32[19,8,8,512]{3,2,1,0:T(8,128)S(1)} %get-tuple-element.68.g, f32[8,8,512]{2,1,0:T(8,128)S(1)} %get-tuple-element.54.fac, f32[6,8,512]{2,1,0:T(8,128)S(1)} %collective-permute-done.4.ghost.halo.halo0, f32[5,8,512]{2,1,0:T(8,128)S(1)} %get-tuple-element.69.ghost.after.halo1, ...), custom_call_target="tpu_custom_call" | custom-call | flops 1024 | bytes 1024 | tf_op jit(solution)/shard_map/final/pallas_call | solution.py:796
  38.8 2.1 %collective-permute-done.6.there = f32[5,8,512]{2,1,0:T(8,128)S(1)} collective-permute-done((f32[5,8,512]{2,1,0:T(8,128)S(1)}, f32[5,8,512]{2,1,0:T(8,128)S(1)}, u32[]{:S(2)}, u32[]{:S(2)}) %collective-permute-start.6) | collective-permute-done | bytes 81952 | tf_op jit(solution)/shard_map/ppermute | solution.py:830
  41.4 1.2 %collective-permute-start.7 = (f32[2,4,16,128]{3,2,1,0:T(8,128)S(1)}, f32[2,4,16,128]{3,2,1,0:T(8,128)S(1)}, u32[]{:S(2)}, u32[]{:S(2)}) collective-permute-start(f32[2,4,16,128]{3,2,1,0:T(8,128)S(1)} %get-tuple-element.80), channel_id=1, source_target_pairs={{0,2},{1,3},{2,0},{3,1},{4,6},{5,7},{6,4},{7,5},{8,10},{9,11},{10,... | collective-permute-start | bytes 196616 | tf_op jit(solution)/shard_map/ppermute | solution.py:945
  42.5 0.5 %collective-permute-start.8 = (f32[2,4,16,128]{3,2,1,0:T(8,128)S(1)}, f32[2,4,16,128]{3,2,1,0:T(8,128)S(1)}, u32[]{:S(2)}, u32[]{:S(2)}) collective-permute-start(f32[2,4,16,128]{3,2,1,0:T(8,128)S(1)} %get-tuple-element.81), channel_id=1, source_target_pairs={{0,3},{1,2},{2,1},{3,0},{4,7},{5,6},{6,5},{7,4},{8,11},{9,10},{10,... | collective-permute-start | bytes 196616 | tf_op jit(solution)/shard_map/ppermute | solution.py:945
  43.1 1.9 %collective-permute-start.9 = (f32[2,4,16,128]{3,2,1,0:T(8,128)S(1)}, f32[2,4,16,128]{3,2,1,0:T(8,128)S(1)}, u32[]{:S(2)}, u32[]{:S(2)}) collective-permute-start(f32[2,4,16,128]{3,2,1,0:T(8,128)S(1)} %get-tuple-element.82), channel_id=1, source_target_pairs={{0,1},{1,0},{2,3},{3,2},{4,5},{5,4},{6,7},{7,6},{8,9},{9,8},{10,11... | collective-permute-start | bytes 196616 | tf_op jit(solution)/shard_map/ppermute | solution.py:945
  44.9 3.0 %collective-permute-done.7.refs_1_ = f32[2,4,16,128]{3,2,1,0:T(8,128)S(1)} collective-permute-done((f32[2,4,16,128]{3,2,1,0:T(8,128)S(1)}, f32[2,4,16,128]{3,2,1,0:T(8,128)S(1)}, u32[]{:S(2)}, u32[]{:S(2)}) %collective-permute-start.7) | collective-permute-done | bytes 65568 | tf_op jit(solution)/shard_map/ppermute | solution.py:945
  47.9 0.9 %collective-permute-done.8.refs_2_ = f32[2,4,16,128]{3,2,1,0:T(8,128)S(1)} collective-permute-done((f32[2,4,16,128]{3,2,1,0:T(8,128)S(1)}, f32[2,4,16,128]{3,2,1,0:T(8,128)S(1)}, u32[]{:S(2)}, u32[]{:S(2)}) %collective-permute-start.8) | collective-permute-done | bytes 65568 | tf_op jit(solution)/shard_map/ppermute | solution.py:945
  48.8 0.5 collective-permute-done.9.refs_3_
  49.2 0.8 %gather.1 = (f32[4,4,16,128]{3,2,1,0:T(8,128)}, f32[4,4,16,128]{3,2,1,0:T(8,128)}) custom-call(f32[2,4,16,128]{3,2,1,0:T(8,128)S(1)} %get-tuple-element.79.refs_0_, f32[2,4,16,128]{3,2,1,0:T(8,128)S(1)} %collective-permute-done.7.refs_1_, f32[2,4,16,128]{3,2,1,0:T(8,128)S(1)} %collective-permute-done.8.refs_2_, ...), custom_call_target="tpu_custom_call" | custom-call | flops 1024 | bytes 1024 | tf_op jit(solution)/shard_map/gather/pallas_call | solution.py:796
  (19 shorter events, 4.2 us)
Async XLA Ops:
  2.8 15.2 %collective-permute-start = (f32[14,8,512]{2,1,0:T(8,128)S(1)}, f32[14,8,512]{2,1,0:T(8,128)S(1)}, u32[]{:S(2)}, u32[]{:S(2)}) collective-permute-start(f32[14,8,512]{2,1,0:T(8,128)S(1)} %get-tuple-element.50.after), channel_id=1, source_target_pairs={{0,31},{1,2},{2,1},{3,4},{4,3},{5,6},{6,5},{7,8},{8,7},{9,10},{10,... | collective-permute-start | bytes 688136 | tf_op jit(solution)/shard_map/ppermute | solution.py:830
  9.7 6.6 %collective-permute-start.1 = (f32[5,8,512]{2,1,0:T(8,128)S(1)}, f32[5,8,512]{2,1,0:T(8,128)S(1)}, u32[]{:S(2)}, u32[]{:S(2)}) collective-permute-start(f32[5,8,512]{2,1,0:T(8,128)S(1)} %get-tuple-element.55), channel_id=1, source_target_pairs={{0,1},{1,0},{2,3},{3,2},{4,5},{5,4},{6,7},{7,6},{8,9},{9,8},{10,11... | collective-permute-start | bytes 245768 | tf_op jit(solution)/shard_map/ppermute | solution.py:830
  16.6 7.6 %collective-permute-start.2 = (f32[14,8,512]{2,1,0:T(8,128)S(1)}, f32[14,8,512]{2,1,0:T(8,128)S(1)}, u32[]{:S(2)}, u32[]{:S(2)}) collective-permute-start(f32[14,8,512]{2,1,0:T(8,128)S(1)} %get-tuple-element.58.after), channel_id=1, source_target_pairs={{0,1},{1,0},{2,3},{3,2},{4,5},{5,4},{6,7},{7,6},{8,9},{9,8},{10,11... | collective-permute-start | bytes 688136 | tf_op jit(solution)/shard_map/ppermute | solution.py:830
  18.7 13.5 %collective-permute-start.3 = (f32[14,8,512]{2,1,0:T(8,128)S(1)}, f32[14,8,512]{2,1,0:T(8,128)S(1)}, u32[]{:S(2)}, u32[]{:S(2)}) collective-permute-start(f32[14,8,512]{2,1,0:T(8,128)S(1)} %get-tuple-element.62.after), channel_id=1, source_target_pairs={{0,31},{1,2},{2,1},{3,4},{4,3},{5,6},{6,5},{7,8},{8,7},{9,10},{10,... | collective-permute-start | bytes 688136 | tf_op jit(solution)/shard_map/ppermute | solution.py:830
  24.7 7.0 %collective-permute-start.4 = (f32[6,8,512]{2,1,0:T(8,128)S(1)}, f32[6,8,512]{2,1,0:T(8,128)S(1)}, u32[]{:S(2)}, u32[]{:S(2)}) collective-permute-start(f32[6,8,512]{2,1,0:T(8,128)S(1)} %get-tuple-element.66.after), channel_id=1, source_target_pairs={{0,1},{1,0},{2,3},{3,2},{4,5},{5,4},{6,7},{7,6},{8,9},{9,8},{10,11... | collective-permute-start | bytes 294920 | tf_op jit(solution)/shard_map/ppermute | solution.py:830
  32.1 4.5 %collective-permute-start.5 = (f32[5,8,512]{2,1,0:T(8,128)S(1)}, f32[5,8,512]{2,1,0:T(8,128)S(1)}, u32[]{:S(2)}, u32[]{:S(2)}) collective-permute-start(f32[5,8,512]{2,1,0:T(8,128)S(1)} %get-tuple-element.67.after), channel_id=1, source_target_pairs={{0,1},{1,0},{2,3},{3,2},{4,5},{5,4},{6,7},{7,6},{8,9},{9,8},{10,11... | collective-permute-start | bytes 245768 | tf_op jit(solution)/shard_map/ppermute | solution.py:830
  32.9 8.1 %collective-permute-start.6 = (f32[5,8,512]{2,1,0:T(8,128)S(1)}, f32[5,8,512]{2,1,0:T(8,128)S(1)}, u32[]{:S(2)}, u32[]{:S(2)}) collective-permute-start(f32[5,8,512]{2,1,0:T(8,128)S(1)} %get-tuple-element.77), channel_id=1, source_target_pairs={{0,31},{1,2},{2,1},{3,4},{4,3},{5,6},{6,5},{7,8},{8,7},{9,10},{10,... | collective-permute-start | bytes 245768 | tf_op jit(solution)/shard_map/ppermute | solution.py:830
  41.4 6.5 %collective-permute-start.7 = (f32[2,4,16,128]{3,2,1,0:T(8,128)S(1)}, f32[2,4,16,128]{3,2,1,0:T(8,128)S(1)}, u32[]{:S(2)}, u32[]{:S(2)}) collective-permute-start(f32[2,4,16,128]{3,2,1,0:T(8,128)S(1)} %get-tuple-element.80), channel_id=1, source_target_pairs={{0,2},{1,3},{2,0},{3,1},{4,6},{5,7},{6,4},{7,5},{8,10},{9,11},{10,... | collective-permute-start | bytes 196616 | tf_op jit(solution)/shard_map/ppermute | solution.py:945
  42.5 6.2 %collective-permute-start.8 = (f32[2,4,16,128]{3,2,1,0:T(8,128)S(1)}, f32[2,4,16,128]{3,2,1,0:T(8,128)S(1)}, u32[]{:S(2)}, u32[]{:S(2)}) collective-permute-start(f32[2,4,16,128]{3,2,1,0:T(8,128)S(1)} %get-tuple-element.81), channel_id=1, source_target_pairs={{0,3},{1,2},{2,1},{3,0},{4,7},{5,6},{6,5},{7,4},{8,11},{9,10},{10,... | collective-permute-start | bytes 196616 | tf_op jit(solution)/shard_map/ppermute | solution.py:945
  43.1 6.2 %collective-permute-start.9 = (f32[2,4,16,128]{3,2,1,0:T(8,128)S(1)}, f32[2,4,16,128]{3,2,1,0:T(8,128)S(1)}, u32[]{:S(2)}, u32[]{:S(2)}) collective-permute-start(f32[2,4,16,128]{3,2,1,0:T(8,128)S(1)} %get-tuple-element.82), channel_id=1, source_target_pairs={{0,1},{1,0},{2,3},{3,2},{4,5},{5,4},{6,7},{7,6},{8,9},{9,8},{10,11... | collective-permute-start | bytes 196616 | tf_op jit(solution)/shard_map/ppermute | solution.py:945

commit v9 on v4

--- a/solution.py
+++ b/solution.py
@@ -184,13 +184,15 @@
 
 
 def start_rows(tiles, halves, chain, pop, phase, row, send, beside, ready=None):
-    up = upper(chain)
-    x, inwards = jnp.where(up, SUBS - 1, 0), jnp.where(up, SUBS - 2, 1)
+    def tile(c, up):
+        x, inwards = (SUBS - 1, SUBS - 2) if up else (0, 1)
+        send[13, :, cut(c)] = start_row(tiles, pop, phase, x, row, c)
+        start_row(tiles, pop, phase, inwards, beside, c)
+
     for c in range(tiles):
         if ready is not None:
             ready(c)
-        send[13, :, cut(c)] = start_row(tiles, pop, phase, x, row, c)
-        start_row(tiles, pop, phase, inwards, beside, c)
+        by_side(chain, functools.partial(tile, c))
 
     def side(up):
         look_ahead(

time: 46.9 us -> 46.9 us (level)
  no operation moved by 1% of the time
where the time goes in v9:
time: 46.9 us; the launch traced here: 46.8 us
  starting transfers between devices  20 us (43%)
  Pallas kernels  15.2 us (32%)
  waiting for transfers between devices  10.8 us (23%)
  between operations  0.81 us (2%)
    ppermute x6, starting transfers between devices, swap(): return lax.ppermute(array, both, pairs[chain])  16.4 us
    pallas_call x23, Pallas kernels, call(): pl.pallas_call(kernel, out_shape=shapes, in_specs=[spec(i, hbm, free) for...  15.2 us
    ppermute x6, waiting for transfers between devices, swap(): return lax.ppermute(array, both, pairs[chain])  5.96 us
    ppermute x3, waiting for transfers between devices, local(): lax.ppermute(blocks[k], 'narrow', [(i, i ^ k) for i in range(parts)])  4.82 us
    ppermute x3, starting transfers between devices, local(): lax.ppermute(blocks[k], 'narrow', [(i, i ^ k) for i in range(parts)])  3.55 us
  transfers between devices with their start and end apart: 9, of which 7 were waited for; matrix products, arithmetic and copies ran while one was open for 0% of the time, Pallas kernels for 25%

profile of v9, /device:TPU:0, one launch (start us, length us, event | category | flops | bytes accessed | tf_op | source)
XLA Modules:
  0.0 46.8 jit_solution(13310340984400764614)
XLA Ops:
  0.6 2.2 %first.1 = (f32[19,8,4,8,128]{4,3,2,1,0:T(8,128)S(1)}, s32[256,128]{1,0:T(8,128)S(1)}, f32[256,128]{1,0:T(8,128)S(1)}, f32[256,128]{1,0:T(8,128)S(1)}, f32[256,1...) custom-call(f32[19,8,4,8,128]{4,3,2,1,0:T(8,128)} %bitcast.43, ...), custom_call_target="tpu_custom_call" | custom-call | flops 1024 | bytes 1024 | tf_op jit(solution)/shard_map/first/pallas_call | solution.py:764
  2.8 6.4 %collective-permute-start.1 = (f32[14,8,512]{2,1,0:T(8,128)S(1)}, f32[14,8,512]{2,1,0:T(8,128)S(1)}, u32[]{:S(2)}, u32[]{:S(2)}) collective-permute-start(f32[14,8,512]{2,1,0:T(8,128)S(1)} %get-tuple-element.50.after), channel_id=1, source_target_pairs={{0,31},{1,2},{2,1},{3,4},{4,3},{5,6},{6,5},{7,8},{8,7},{9,10},{10,... | collective-permute-start | bytes 688136 | tf_op jit(solution)/shard_map/ppermute | solution.py:798
  9.3 0.9 %second.1 = (f32[19,8,512]{2,1,0:T(8,128)S(1)}, f32[14,8,512]{2,1,0:T(8,128)S(1)}) custom-call(f32[19,256,128]{2,1,0:T(8,128)S(1)} %bitcast.41, s32[256,128]{1,0:T(8,128)S(1)} %get-tuple-element.45.phase, f32[14,8,512]{2,1,0:T(8,128)S(1)} %get-tuple-element.50.after), custom_call_target="tpu_custom_call" | custom-call | flops 1024 | bytes 1024 | tf_op jit(solution)/shard_map/second/pallas_call | solution.py:764
  10.3 1.5 %first_inner.1 = (f32[19,8,8,512]{3,2,1,0:T(8,128)S(1)}, f32[8,8,512]{2,1,0:T(8,128)S(1)}, f32[19,8,8,512]{3,2,1,0:T(8,128)S(1)}, f32[3,8,8,512]{3,2,1,0:T(8,128)S(1)}, f32[2,8,512]{2,1,0:T(8,128)S(1)}) custom-call(f32[19,256,128]{2,1,0:T(8,128)S(1)} %bitcast.42, s32[256,128]{1,0:T(8,128)S(1)} %get-tuple-element.45.phase, ...), custom_call_target="tpu_custom_call" | custom-call | flops 1024 | bytes 1024 | tf_op jit(solution)/shard_map/first_inner/pallas_call | solution.py:764
  11.8 1.2 %inner.3 = f32[19,8,8,512]{3,2,1,0:T(8,128)S(1)} custom-call(f32[19,8,8,512]{3,2,1,0:T(8,128)S(1)} %get-tuple-element.53.g.after, f32[8,8,512]{2,1,0:T(8,128)S(1)} %get-tuple-element.54.fac, f32[3,8,8,512]{3,2,1,0:T(8,128)S(1)} %get-tuple-element.56.after.slabs), custom_call_target="tpu_custom_call" | custom-call | flops 1024 | bytes 1024 | tf_op jit(solution)/shard_map/inner/pallas_call | solution.py:764
  13.0 2.3 %collective-permute-done.1.halo.first_halo = f32[14,8,512]{2,1,0:T(8,128)S(1)} collective-permute-done((f32[14,8,512]{2,1,0:T(8,128)S(1)}, f32[14,8,512]{2,1,0:T(8,128)S(1)}, u32[]{:S(2)}, u32[]{:S(2)}) %collective-permute-start.1) | collective-permute-done | bytes 229408 | tf_op jit(solution)/shard_map/ppermute | solution.py:798
  15.6 0.4 far1.1
  16.0 5.6 %collective-permute-start.3 = (f32[14,8,512]{2,1,0:T(8,128)S(1)}, f32[14,8,512]{2,1,0:T(8,128)S(1)}, u32[]{:S(2)}, u32[]{:S(2)}) collective-permute-start(f32[14,8,512]{2,1,0:T(8,128)S(1)} %get-tuple-element.59.after), channel_id=1, source_target_pairs={{0,31},{1,2},{2,1},{3,4},{4,3},{5,6},{6,5},{7,8},{8,7},{9,10},{10,... | collective-permute-start | bytes 688136 | tf_op jit(solution)/shard_map/ppermute | solution.py:798
  21.8 0.4 far0.1
  22.2 0.5 %collective-permute-start.2 = (f32[14,8,512]{2,1,0:T(8,128)S(1)}, f32[14,8,512]{2,1,0:T(8,128)S(1)}, u32[]{:S(2)}, u32[]{:S(2)}) collective-permute-start(f32[14,8,512]{2,1,0:T(8,128)S(1)} %get-tuple-element.62.after), channel_id=1, source_target_pairs={{0,1},{1,0},{2,3},{3,2},{4,5},{5,4},{6,7},{7,6},{8,9},{9,8},{10,11... | collective-permute-start | bytes 688136 | tf_op jit(solution)/shard_map/ppermute | solution.py:798
  22.7 1.2 %inner.4 = f32[19,8,8,512]{3,2,1,0:T(8,128)S(1)} custom-call(f32[19,8,8,512]{3,2,1,0:T(8,128)S(1)} %get-tuple-element.60.g, f32[8,8,512]{2,1,0:T(8,128)S(1)} %get-tuple-element.54.fac, f32[14,8,512]{2,1,0:T(8,128)S(1)} %get-tuple-element.62.after), custom_call_target="tpu_custom_call" | custom-call | flops 1024 | bytes 1024 | tf_op jit(solution)/shard_map/inner/pallas_call | solution.py:764
  24.0 1.2 %inner.5.g.after = f32[19,8,8,512]{3,2,1,0:T(8,128)S(1)} custom-call(f32[19,8,8,512]{3,2,1,0:T(8,128)S(1)} %put.1.g.after, f32[8,8,512]{2,1,0:T(8,128)S(1)} %get-tuple-element.54.fac, f32[19,8,8,512]{3,2,1,0:T(8,128)S(1)} %put.1.g.after), custom_call_target="tpu_custom_call" | custom-call | flops 1024 | bytes 1024 | tf_op jit(solution)/shard_map/inner/pallas_call | solution.py:764
  25.2 0.5 %inner_speed.1.after.u = f32[3,4,8,512]{3,2,1,0:T(8,128)S(1)} custom-call(f32[19,8,8,512]{3,2,1,0:T(8,128)S(1)} %inner.5.g.after, f32[8,8,512]{2,1,0:T(8,128)S(1)} %get-tuple-element.54.fac, f32[19,8,8,512]{3,2,1,0:T(8,128)S(1)} %inner.5.g.after), custom_call_target="tpu_custom_call" | custom-call | flops 1024 | bytes 1024 | tf_op jit(solution)/shard_map/inner_speed/pallas_call | solution.py:764
  25.7 2.0 %collective-permute-done.3.halo = f32[14,8,512]{2,1,0:T(8,128)S(1)} collective-permute-done((f32[14,8,512]{2,1,0:T(8,128)S(1)}, f32[14,8,512]{2,1,0:T(8,128)S(1)}, u32[]{:S(2)}, u32[]{:S(2)}) %collective-permute-start.3) | collective-permute-done | bytes 229408 | tf_op jit(solution)/shard_map/ppermute | solution.py:798
  28.3 3.8 %collective-permute-start.5 = (f32[5,8,512]{2,1,0:T(8,128)S(1)}, f32[5,8,512]{2,1,0:T(8,128)S(1)}, u32[]{:S(2)}, u32[]{:S(2)}) collective-permute-start(f32[5,8,512]{2,1,0:T(8,128)S(1)} %get-tuple-element.67.after), channel_id=1, source_target_pairs={{0,31},{1,2},{2,1},{3,4},{4,3},{5,6},{6,5},{7,8},{8,7},{9,10},{10,... | collective-permute-start | bytes 245768 | tf_op jit(solution)/shard_map/ppermute | solution.py:798
  33.4 1.9 %final.1 = (f32[19,256,128]{2,1,0:T(8,128)}, f32[8,128]{1,0:T(8,128)S(1)}) custom-call(f32[19,8,8,512]{3,2,1,0:T(8,128)S(1)} %get-tuple-element.68.g, f32[8,8,512]{2,1,0:T(8,128)S(1)} %get-tuple-element.54.fac, f32[5,8,512]{2,1,0:T(8,128)S(1)} %get-tuple-element.69.ghost.after.halo0, f32[5,8,512]{2,1,0:T(8,128)S(1)} %get-tuple-element.66.ghost.after.halo1, ...), custom_call_target="tpu_custom_call" | custom-call | flops 1024 | bytes 1024 | tf_op jit(solution)/shard_map/final/pallas_call | solution.py:764
  35.3 0.7 %collective-permute-done.5.there = f32[5,8,512]{2,1,0:T(8,128)S(1)} collective-permute-done((f32[5,8,512]{2,1,0:T(8,128)S(1)}, f32[5,8,512]{2,1,0:T(8,128)S(1)}, u32[]{:S(2)}, u32[]{:S(2)}) %collective-permute-start.5) | collective-permute-done | bytes 81952 | tf_op jit(solution)/shard_map/ppermute | solution.py:798
  36.3 0.9 %collective-permute-done.4.there = f32[5,8,512]{2,1,0:T(8,128)S(1)} collective-permute-done((f32[5,8,512]{2,1,0:T(8,128)S(1)}, f32[5,8,512]{2,1,0:T(8,128)S(1)}, u32[]{:S(2)}, u32[]{:S(2)}) %collective-permute-start.4) | collective-permute-done | bytes 81952 | tf_op jit(solution)/shard_map/ppermute | solution.py:798
  37.7 1.9 %collective-permute-start.6 = (f32[2,4,16,128]{3,2,1,0:T(8,128)S(1)}, f32[2,4,16,128]{3,2,1,0:T(8,128)S(1)}, u32[]{:S(2)}, u32[]{:S(2)}) collective-permute-start(f32[2,4,16,128]{3,2,1,0:T(8,128)S(1)} %get-tuple-element.80), channel_id=1, source_target_pairs={{0,2},{1,3},{2,0},{3,1},{4,6},{5,7},{6,4},{7,5},{8,10},{9,11},{10,... | collective-permute-start | bytes 196616 | tf_op jit(solution)/shard_map/ppermute | solution.py:912
  39.6 1.1 %collective-permute-start.7 = (f32[2,4,16,128]{3,2,1,0:T(8,128)S(1)}, f32[2,4,16,128]{3,2,1,0:T(8,128)S(1)}, u32[]{:S(2)}, u32[]{:S(2)}) collective-permute-start(f32[2,4,16,128]{3,2,1,0:T(8,128)S(1)} %get-tuple-element.81), channel_id=1, source_target_pairs={{0,3},{1,2},{2,1},{3,0},{4,7},{5,6},{6,5},{7,4},{8,11},{9,10},{10,... | collective-permute-start | bytes 196616 | tf_op jit(solution)/shard_map/ppermute | solution.py:912
  40.7 0.5 %collective-permute-start.8 = (f32[2,4,16,128]{3,2,1,0:T(8,128)S(1)}, f32[2,4,16,128]{3,2,1,0:T(8,128)S(1)}, u32[]{:S(2)}, u32[]{:S(2)}) collective-permute-start(f32[2,4,16,128]{3,2,1,0:T(8,128)S(1)} %get-tuple-element.82), channel_id=1, source_target_pairs={{0,1},{1,0},{2,3},{3,2},{4,5},{5,4},{6,7},{7,6},{8,9},{9,8},{10,11... | collective-permute-start | bytes 196616 | tf_op jit(solution)/shard_map/ppermute | solution.py:912
  41.2 3.5 %collective-permute-done.6.refs_1_ = f32[2,4,16,128]{3,2,1,0:T(8,128)S(1)} collective-permute-done((f32[2,4,16,128]{3,2,1,0:T(8,128)S(1)}, f32[2,4,16,128]{3,2,1,0:T(8,128)S(1)}, u32[]{:S(2)}, u32[]{:S(2)}) %collective-permute-start.6) | collective-permute-done | bytes 65568 | tf_op jit(solution)/shard_map/ppermute | solution.py:912
  44.7 1.1 %collective-permute-done.7.refs_2_ = f32[2,4,16,128]{3,2,1,0:T(8,128)S(1)} collective-permute-done((f32[2,4,16,128]{3,2,1,0:T(8,128)S(1)}, f32[2,4,16,128]{3,2,1,0:T(8,128)S(1)}, u32[]{:S(2)}, u32[]{:S(2)}) %collective-permute-start.7) | collective-permute-done | bytes 65568 | tf_op jit(solution)/shard_map/ppermute | solution.py:912
  46.0 0.8 %gather.1 = (f32[4,4,16,128]{3,2,1,0:T(8,128)}, f32[4,4,16,128]{3,2,1,0:T(8,128)}) custom-call(f32[2,4,16,128]{3,2,1,0:T(8,128)S(1)} %get-tuple-element.79.refs_0_, f32[2,4,16,128]{3,2,1,0:T(8,128)S(1)} %collective-permute-done.6.refs_1_, f32[2,4,16,128]{3,2,1,0:T(8,128)S(1)} %collective-permute-done.7.refs_2_, ...), custom_call_target="tpu_custom_call" | custom-call | flops 1024 | bytes 1024 | tf_op jit(solution)/shard_map/gather/pallas_call | solution.py:764
  (17 shorter events, 3.4 us)
Async XLA Ops:
  2.8 12.5 %collective-permute-start.1 = (f32[14,8,512]{2,1,0:T(8,128)S(1)}, f32[14,8,512]{2,1,0:T(8,128)S(1)}, u32[]{:S(2)}, u32[]{:S(2)}) collective-permute-start(f32[14,8,512]{2,1,0:T(8,128)S(1)} %get-tuple-element.50.after), channel_id=1, source_target_pairs={{0,31},{1,2},{2,1},{3,4},{4,3},{5,6},{6,5},{7,8},{8,7},{9,10},{10,... | collective-permute-start | bytes 688136 | tf_op jit(solution)/shard_map/ppermute | solution.py:798
  10.2 11.3 %collective-permute-start = (f32[14,8,512]{2,1,0:T(8,128)S(1)}, f32[14,8,512]{2,1,0:T(8,128)S(1)}, u32[]{:S(2)}, u32[]{:S(2)}) collective-permute-start(f32[14,8,512]{2,1,0:T(8,128)S(1)} %get-tuple-element.55), channel_id=1, source_target_pairs={{0,1},{1,0},{2,3},{3,2},{4,5},{5,4},{6,7},{7,6},{8,9},{9,8},{10,11... | collective-permute-start | bytes 688136 | tf_op jit(solution)/shard_map/ppermute | solution.py:798
  16.0 11.7 %collective-permute-start.3 = (f32[14,8,512]{2,1,0:T(8,128)S(1)}, f32[14,8,512]{2,1,0:T(8,128)S(1)}, u32[]{:S(2)}, u32[]{:S(2)}) collective-permute-start(f32[14,8,512]{2,1,0:T(8,128)S(1)} %get-tuple-element.59.after), channel_id=1, source_target_pairs={{0,31},{1,2},{2,1},{3,4},{4,3},{5,6},{6,5},{7,8},{8,7},{9,10},{10,... | collective-permute-start | bytes 688136 | tf_op jit(solution)/shard_map/ppermute | solution.py:798
  22.2 9.9 %collective-permute-start.2 = (f32[14,8,512]{2,1,0:T(8,128)S(1)}, f32[14,8,512]{2,1,0:T(8,128)S(1)}, u32[]{:S(2)}, u32[]{:S(2)}) collective-permute-start(f32[14,8,512]{2,1,0:T(8,128)S(1)} %get-tuple-element.62.after), channel_id=1, source_target_pairs={{0,1},{1,0},{2,3},{3,2},{4,5},{5,4},{6,7},{7,6},{8,9},{9,8},{10,11... | collective-permute-start | bytes 688136 | tf_op jit(solution)/shard_map/ppermute | solution.py:798
  28.3 7.7 %collective-permute-start.5 = (f32[5,8,512]{2,1,0:T(8,128)S(1)}, f32[5,8,512]{2,1,0:T(8,128)S(1)}, u32[]{:S(2)}, u32[]{:S(2)}) collective-permute-start(f32[5,8,512]{2,1,0:T(8,128)S(1)} %get-tuple-element.67.after), channel_id=1, source_target_pairs={{0,31},{1,2},{2,1},{3,4},{4,3},{5,6},{6,5},{7,8},{8,7},{9,10},{10,... | collective-permute-start | bytes 245768 | tf_op jit(solution)/shard_map/ppermute | solution.py:798
  32.7 4.5 %collective-permute-start.4 = (f32[5,8,512]{2,1,0:T(8,128)S(1)}, f32[5,8,512]{2,1,0:T(8,128)S(1)}, u32[]{:S(2)}, u32[]{:S(2)}) collective-permute-start(f32[5,8,512]{2,1,0:T(8,128)S(1)} %get-tuple-element.77), channel_id=1, source_target_pairs={{0,1},{1,0},{2,3},{3,2},{4,5},{5,4},{6,7},{7,6},{8,9},{9,8},{10,11... | collective-permute-start | bytes 245768 | tf_op jit(solution)/shard_map/ppermute | solution.py:798
  37.7 7.1 %collective-permute-start.6 = (f32[2,4,16,128]{3,2,1,0:T(8,128)S(1)}, f32[2,4,16,128]{3,2,1,0:T(8,128)S(1)}, u32[]{:S(2)}, u32[]{:S(2)}) collective-permute-start(f32[2,4,16,128]{3,2,1,0:T(8,128)S(1)} %get-tuple-element.80), channel_id=1, source_target_pairs={{0,2},{1,3},{2,0},{3,1},{4,6},{5,7},{6,4},{7,5},{8,10},{9,11},{10,... | collective-permute-start | bytes 196616 | tf_op jit(solution)/shard_map/ppermute | solution.py:912
  39.6 6.2 %collective-permute-start.7 = (f32[2,4,16,128]{3,2,1,0:T(8,128)S(1)}, f32[2,4,16,128]{3,2,1,0:T(8,128)S(1)}, u32[]{:S(2)}, u32[]{:S(2)}) collective-permute-start(f32[2,4,16,128]{3,2,1,0:T(8,128)S(1)} %get-tuple-element.81), channel_id=1, source_target_pairs={{0,3},{1,2},{2,1},{3,0},{4,7},{5,6},{6,5},{7,4},{8,11},{9,10},{10,... | collective-permute-start | bytes 196616 | tf_op jit(solution)/shard_map/ppermute | solution.py:912
  40.7 5.3 %collective-permute-start.8 = (f32[2,4,16,128]{3,2,1,0:T(8,128)S(1)}, f32[2,4,16,128]{3,2,1,0:T(8,128)S(1)}, u32[]{:S(2)}, u32[]{:S(2)}) collective-permute-start(f32[2,4,16,128]{3,2,1,0:T(8,128)S(1)} %get-tuple-element.82), channel_id=1, source_target_pairs={{0,1},{1,0},{2,3},{3,2},{4,5},{5,4},{6,7},{7,6},{8,9},{9,8},{10,11... | collective-permute-start | bytes 196616 | tf_op jit(solution)/shard_map/ppermute | solution.py:912

commit v10 on v9

--- a/solution.py
+++ b/solution.py
@@ -207,18 +207,22 @@
     pop, phase, conc, napl, poro, flags, row, send, beside, sems,
 ):
     small = [
-        pltpu.make_async_copy(a, b, sems.at[tiles + i])
+        pltpu.make_async_copy(a, b, sems.at[4 * tiles + i])
         for i, (a, b) in enumerate(
             ((phase_h, phase), (conc_h, conc), (poro_h, poro), (napl_h, napl), (flags_h, flags))
         )
     ]
-    large = [pltpu.make_async_copy(pop_h.at[:, :, c], pop.at[:, :, c], sems.at[c]) for c in range(tiles)]
+    groups = [pl.ds(q, min(5, 19 - q)) for q in range(0, 19, 5)]
+    large = [
+        [pltpu.make_async_copy(pop_h.at[qs, :, c], pop.at[qs, :, c], sems.at[4 * c + i]) for i, qs in enumerate(groups)]
+        for c in range(tiles)
+    ]
     small[0].start()
-    for copy in large + small[1:]:
+    for copy in sum(large, []) + small[1:]:
         copy.start()
     small[0].wait()
     flat = pop.reshape(pop.shape[0], SUBS * tiles * SUBS, LANES)
-    start_rows(tiles, halves, 1, flat, phase, row, send, beside, ready=lambda c: large[c].wait())
+    start_rows(tiles, halves, 1, flat, phase, row, send, beside, ready=lambda c: [copy.wait() for copy in large[c]])
     for copy in small[1:]:
         copy.wait()
 
@@ -808,7 +812,7 @@
             hold(*chunks.shape), hold(*flat, dtype=jnp.int32), hold(*flat), hold(*flat), hold(*flat),
             hold(*flags.shape, dtype=jnp.int32), hold(19, *slab), hold(14, *slab),
         ),
-        given, scratch=(pltpu.VMEM((19, *slab), F32), pltpu.SemaphoreType.DMA((tiles + 5,))),
+        given, scratch=(pltpu.VMEM((19, *slab), F32), pltpu.SemaphoreType.DMA((4 * tiles + 5,))),
         hbm=range(6), name="first",
     )
     popv = popv.reshape(pop.shape)

time: 46.9 us -> 47.1 us (level)
  no operation moved by 1% of the time
where the time goes in v10:
time: 47.1 us; the launch traced here: 47 us
  starting transfers between devices  20 us (42%)
  Pallas kernels  15.4 us (33%)
  waiting for transfers between devices  10.8 us (23%)
  between operations  0.81 us (2%)
    ppermute x6, starting transfers between devices, swap(): return lax.ppermute(array, both, pairs[chain])  16.4 us
    pallas_call x23, Pallas kernels, call(): pl.pallas_call(kernel, out_shape=shapes, in_specs=[spec(i, hbm, free) for...  15.4 us
    ppermute x6, waiting for transfers between devices, swap(): return lax.ppermute(array, both, pairs[chain])  5.97 us
    ppermute x3, waiting for transfers between devices, local(): lax.ppermute(blocks[k], 'narrow', [(i, i ^ k) for i in range(parts)])  4.81 us
    ppermute x3, starting transfers between devices, local(): lax.ppermute(blocks[k], 'narrow', [(i, i ^ k) for i in range(parts)])  3.55 us
  transfers between devices with their start and end apart: 9, of which 7 were waited for; matrix products, arithmetic and copies ran while one was open for 0% of the time, Pallas kernels for 25%

profile of v10, /device:TPU:0, one launch (start us, length us, event | category | flops | bytes accessed | tf_op | source)
XLA Modules:
  0.0 47.0 jit_solution(15338089332430296067)
XLA Ops:
  0.6 2.4 %first.1 = (f32[19,8,4,8,128]{4,3,2,1,0:T(8,128)S(1)}, s32[256,128]{1,0:T(8,128)S(1)}, f32[256,128]{1,0:T(8,128)S(1)}, f32[256,128]{1,0:T(8,128)S(1)}, f32[256,1...) custom-call(f32[19,8,4,8,128]{4,3,2,1,0:T(8,128)} %bitcast.43, ...), custom_call_target="tpu_custom_call" | custom-call | flops 1024 | bytes 1024 | tf_op jit(solution)/shard_map/first/pallas_call | solution.py:768
  3.0 6.4 %collective-permute-start.1 = (f32[14,8,512]{2,1,0:T(8,128)S(1)}, f32[14,8,512]{2,1,0:T(8,128)S(1)}, u32[]{:S(2)}, u32[]{:S(2)}) collective-permute-start(f32[14,8,512]{2,1,0:T(8,128)S(1)} %get-tuple-element.50.after), channel_id=1, source_target_pairs={{0,31},{1,2},{2,1},{3,4},{4,3},{5,6},{6,5},{7,8},{8,7},{9,10},{10,... | collective-permute-start | bytes 688136 | tf_op jit(solution)/shard_map/ppermute | solution.py:802
  9.5 0.9 %second.1 = (f32[19,8,512]{2,1,0:T(8,128)S(1)}, f32[14,8,512]{2,1,0:T(8,128)S(1)}) custom-call(f32[19,256,128]{2,1,0:T(8,128)S(1)} %bitcast.41, s32[256,128]{1,0:T(8,128)S(1)} %get-tuple-element.45.phase, f32[14,8,512]{2,1,0:T(8,128)S(1)} %get-tuple-element.50.after), custom_call_target="tpu_custom_call" | custom-call | flops 1024 | bytes 1024 | tf_op jit(solution)/shard_map/second/pallas_call | solution.py:768
  10.5 1.5 %first_inner.1 = (f32[19,8,8,512]{3,2,1,0:T(8,128)S(1)}, f32[8,8,512]{2,1,0:T(8,128)S(1)}, f32[19,8,8,512]{3,2,1,0:T(8,128)S(1)}, f32[3,8,8,512]{3,2,1,0:T(8,128)S(1)}, f32[2,8,512]{2,1,0:T(8,128)S(1)}) custom-call(f32[19,256,128]{2,1,0:T(8,128)S(1)} %bitcast.42, s32[256,128]{1,0:T(8,128)S(1)} %get-tuple-element.45.phase, ...), custom_call_target="tpu_custom_call" | custom-call | flops 1024 | bytes 1024 | tf_op jit(solution)/shard_map/first_inner/pallas_call | solution.py:768
  12.0 1.2 %inner.3 = f32[19,8,8,512]{3,2,1,0:T(8,128)S(1)} custom-call(f32[19,8,8,512]{3,2,1,0:T(8,128)S(1)} %get-tuple-element.53.g.after, f32[8,8,512]{2,1,0:T(8,128)S(1)} %get-tuple-element.54.fac, f32[3,8,8,512]{3,2,1,0:T(8,128)S(1)} %get-tuple-element.56.after.slabs), custom_call_target="tpu_custom_call" | custom-call | flops 1024 | bytes 1024 | tf_op jit(solution)/shard_map/inner/pallas_call | solution.py:768
  13.2 2.3 %collective-permute-done.1.halo.first_halo = f32[14,8,512]{2,1,0:T(8,128)S(1)} collective-permute-done((f32[14,8,512]{2,1,0:T(8,128)S(1)}, f32[14,8,512]{2,1,0:T(8,128)S(1)}, u32[]{:S(2)}, u32[]{:S(2)}) %collective-permute-start.1) | collective-permute-done | bytes 229408 | tf_op jit(solution)/shard_map/ppermute | solution.py:802
  15.8 0.4 far1.1
  16.2 5.6 %collective-permute-start.3 = (f32[14,8,512]{2,1,0:T(8,128)S(1)}, f32[14,8,512]{2,1,0:T(8,128)S(1)}, u32[]{:S(2)}, u32[]{:S(2)}) collective-permute-start(f32[14,8,512]{2,1,0:T(8,128)S(1)} %get-tuple-element.59.after), channel_id=1, source_target_pairs={{0,31},{1,2},{2,1},{3,4},{4,3},{5,6},{6,5},{7,8},{8,7},{9,10},{10,... | collective-permute-start | bytes 688136 | tf_op jit(solution)/shard_map/ppermute | solution.py:802
  22.0 0.4 far0.1
  22.4 0.5 %collective-permute-start.2 = (f32[14,8,512]{2,1,0:T(8,128)S(1)}, f32[14,8,512]{2,1,0:T(8,128)S(1)}, u32[]{:S(2)}, u32[]{:S(2)}) collective-permute-start(f32[14,8,512]{2,1,0:T(8,128)S(1)} %get-tuple-element.62.after), channel_id=1, source_target_pairs={{0,1},{1,0},{2,3},{3,2},{4,5},{5,4},{6,7},{7,6},{8,9},{9,8},{10,11... | collective-permute-start | bytes 688136 | tf_op jit(solution)/shard_map/ppermute | solution.py:802
  22.9 1.2 %inner.4 = f32[19,8,8,512]{3,2,1,0:T(8,128)S(1)} custom-call(f32[19,8,8,512]{3,2,1,0:T(8,128)S(1)} %get-tuple-element.60.g, f32[8,8,512]{2,1,0:T(8,128)S(1)} %get-tuple-element.54.fac, f32[14,8,512]{2,1,0:T(8,128)S(1)} %get-tuple-element.62.after), custom_call_target="tpu_custom_call" | custom-call | flops 1024 | bytes 1024 | tf_op jit(solution)/shard_map/inner/pallas_call | solution.py:768
  24.2 1.2 %inner.5.g.after = f32[19,8,8,512]{3,2,1,0:T(8,128)S(1)} custom-call(f32[19,8,8,512]{3,2,1,0:T(8,128)S(1)} %put.1.g.after, f32[8,8,512]{2,1,0:T(8,128)S(1)} %get-tuple-element.54.fac, f32[19,8,8,512]{3,2,1,0:T(8,128)S(1)} %put.1.g.after), custom_call_target="tpu_custom_call" | custom-call | flops 1024 | bytes 1024 | tf_op jit(solution)/shard_map/inner/pallas_call | solution.py:768
  25.4 0.5 %inner_speed.1.after.u = f32[3,4,8,512]{3,2,1,0:T(8,128)S(1)} custom-call(f32[19,8,8,512]{3,2,1,0:T(8,128)S(1)} %inner.5.g.after, f32[8,8,512]{2,1,0:T(8,128)S(1)} %get-tuple-element.54.fac, f32[19,8,8,512]{3,2,1,0:T(8,128)S(1)} %inner.5.g.after), custom_call_target="tpu_custom_call" | custom-call | flops 1024 | bytes 1024 | tf_op jit(solution)/shard_map/inner_speed/pallas_call | solution.py:768
  25.9 2.0 %collective-permute-done.3.halo = f32[14,8,512]{2,1,0:T(8,128)S(1)} collective-permute-done((f32[14,8,512]{2,1,0:T(8,128)S(1)}, f32[14,8,512]{2,1,0:T(8,128)S(1)}, u32[]{:S(2)}, u32[]{:S(2)}) %collective-permute-start.3) | collective-permute-done | bytes 229408 | tf_op jit(solution)/shard_map/ppermute | solution.py:802
  28.5 3.8 %collective-permute-start.5 = (f32[5,8,512]{2,1,0:T(8,128)S(1)}, f32[5,8,512]{2,1,0:T(8,128)S(1)}, u32[]{:S(2)}, u32[]{:S(2)}) collective-permute-start(f32[5,8,512]{2,1,0:T(8,128)S(1)} %get-tuple-element.67.after), channel_id=1, source_target_pairs={{0,31},{1,2},{2,1},{3,4},{4,3},{5,6},{6,5},{7,8},{8,7},{9,10},{10,... | collective-permute-start | bytes 245768 | tf_op jit(solution)/shard_map/ppermute | solution.py:802
  33.6 1.9 %final.1 = (f32[19,256,128]{2,1,0:T(8,128)}, f32[8,128]{1,0:T(8,128)S(1)}) custom-call(f32[19,8,8,512]{3,2,1,0:T(8,128)S(1)} %get-tuple-element.68.g, f32[8,8,512]{2,1,0:T(8,128)S(1)} %get-tuple-element.54.fac, f32[5,8,512]{2,1,0:T(8,128)S(1)} %get-tuple-element.69.ghost.after.halo0, f32[5,8,512]{2,1,0:T(8,128)S(1)} %get-tuple-element.66.ghost.after.halo1, ...), custom_call_target="tpu_custom_call" | custom-call | flops 1024 | bytes 1024 | tf_op jit(solution)/shard_map/final/pallas_call | solution.py:768
  35.5 0.7 %collective-permute-done.5.there = f32[5,8,512]{2,1,0:T(8,128)S(1)} collective-permute-done((f32[5,8,512]{2,1,0:T(8,128)S(1)}, f32[5,8,512]{2,1,0:T(8,128)S(1)}, u32[]{:S(2)}, u32[]{:S(2)}) %collective-permute-start.5) | collective-permute-done | bytes 81952 | tf_op jit(solution)/shard_map/ppermute | solution.py:802
  36.5 0.9 %collective-permute-done.4.there = f32[5,8,512]{2,1,0:T(8,128)S(1)} collective-permute-done((f32[5,8,512]{2,1,0:T(8,128)S(1)}, f32[5,8,512]{2,1,0:T(8,128)S(1)}, u32[]{:S(2)}, u32[]{:S(2)}) %collective-permute-start.4) | collective-permute-done | bytes 81952 | tf_op jit(solution)/shard_map/ppermute | solution.py:802
  37.8 1.9 %collective-permute-start.6 = (f32[2,4,16,128]{3,2,1,0:T(8,128)S(1)}, f32[2,4,16,128]{3,2,1,0:T(8,128)S(1)}, u32[]{:S(2)}, u32[]{:S(2)}) collective-permute-start(f32[2,4,16,128]{3,2,1,0:T(8,128)S(1)} %get-tuple-element.80), channel_id=1, source_target_pairs={{0,2},{1,3},{2,0},{3,1},{4,6},{5,7},{6,4},{7,5},{8,10},{9,11},{10,... | collective-permute-start | bytes 196616 | tf_op jit(solution)/shard_map/ppermute | solution.py:916
  39.8 1.1 %collective-permute-start.7 = (f32[2,4,16,128]{3,2,1,0:T(8,128)S(1)}, f32[2,4,16,128]{3,2,1,0:T(8,128)S(1)}, u32[]{:S(2)}, u32[]{:S(2)}) collective-permute-start(f32[2,4,16,128]{3,2,1,0:T(8,128)S(1)} %get-tuple-element.81), channel_id=1, source_target_pairs={{0,3},{1,2},{2,1},{3,0},{4,7},{5,6},{6,5},{7,4},{8,11},{9,10},{10,... | collective-permute-start | bytes 196616 | tf_op jit(solution)/shard_map/ppermute | solution.py:916
  40.9 0.5 %collective-permute-start.8 = (f32[2,4,16,128]{3,2,1,0:T(8,128)S(1)}, f32[2,4,16,128]{3,2,1,0:T(8,128)S(1)}, u32[]{:S(2)}, u32[]{:S(2)}) collective-permute-start(f32[2,4,16,128]{3,2,1,0:T(8,128)S(1)} %get-tuple-element.82), channel_id=1, source_target_pairs={{0,1},{1,0},{2,3},{3,2},{4,5},{5,4},{6,7},{7,6},{8,9},{9,8},{10,11... | collective-permute-start | bytes 196616 | tf_op jit(solution)/shard_map/ppermute | solution.py:916
  41.4 3.5 %collective-permute-done.6.refs_1_ = f32[2,4,16,128]{3,2,1,0:T(8,128)S(1)} collective-permute-done((f32[2,4,16,128]{3,2,1,0:T(8,128)S(1)}, f32[2,4,16,128]{3,2,1,0:T(8,128)S(1)}, u32[]{:S(2)}, u32[]{:S(2)}) %collective-permute-start.6) | collective-permute-done | bytes 65568 | tf_op jit(solution)/shard_map/ppermute | solution.py:916
  44.9 1.1 %collective-permute-done.7.refs_2_ = f32[2,4,16,128]{3,2,1,0:T(8,128)S(1)} collective-permute-done((f32[2,4,16,128]{3,2,1,0:T(8,128)S(1)}, f32[2,4,16,128]{3,2,1,0:T(8,128)S(1)}, u32[]{:S(2)}, u32[]{:S(2)}) %collective-permute-start.7) | collective-permute-done | bytes 65568 | tf_op jit(solution)/shard_map/ppermute | solution.py:916
  46.2 0.8 %gather.1 = (f32[4,4,16,128]{3,2,1,0:T(8,128)}, f32[4,4,16,128]{3,2,1,0:T(8,128)}) custom-call(f32[2,4,16,128]{3,2,1,0:T(8,128)S(1)} %get-tuple-element.79.refs_0_, f32[2,4,16,128]{3,2,1,0:T(8,128)S(1)} %collective-permute-done.6.refs_1_, f32[2,4,16,128]{3,2,1,0:T(8,128)S(1)} %collective-permute-done.7.refs_2_, ...), custom_call_target="tpu_custom_call" | custom-call | flops 1024 | bytes 1024 | tf_op jit(solution)/shard_map/gather/pallas_call | solution.py:768
  (17 shorter events, 3.4 us)
Async XLA Ops:
  3.0 12.5 %collective-permute-start.1 = (f32[14,8,512]{2,1,0:T(8,128)S(1)}, f32[14,8,512]{2,1,0:T(8,128)S(1)}, u32[]{:S(2)}, u32[]{:S(2)}) collective-permute-start(f32[14,8,512]{2,1,0:T(8,128)S(1)} %get-tuple-element.50.after), channel_id=1, source_target_pairs={{0,31},{1,2},{2,1},{3,4},{4,3},{5,6},{6,5},{7,8},{8,7},{9,10},{10,... | collective-permute-start | bytes 688136 | tf_op jit(solution)/shard_map/ppermute | solution.py:802
  10.4 11.3 %collective-permute-start = (f32[14,8,512]{2,1,0:T(8,128)S(1)}, f32[14,8,512]{2,1,0:T(8,128)S(1)}, u32[]{:S(2)}, u32[]{:S(2)}) collective-permute-start(f32[14,8,512]{2,1,0:T(8,128)S(1)} %get-tuple-element.55), channel_id=1, source_target_pairs={{0,1},{1,0},{2,3},{3,2},{4,5},{5,4},{6,7},{7,6},{8,9},{9,8},{10,11... | collective-permute-start | bytes 688136 | tf_op jit(solution)/shard_map/ppermute | solution.py:802
  16.2 11.7 %collective-permute-start.3 = (f32[14,8,512]{2,1,0:T(8,128)S(1)}, f32[14,8,512]{2,1,0:T(8,128)S(1)}, u32[]{:S(2)}, u32[]{:S(2)}) collective-permute-start(f32[14,8,512]{2,1,0:T(8,128)S(1)} %get-tuple-element.59.after), channel_id=1, source_target_pairs={{0,31},{1,2},{2,1},{3,4},{4,3},{5,6},{6,5},{7,8},{8,7},{9,10},{10,... | collective-permute-start | bytes 688136 | tf_op jit(solution)/shard_map/ppermute | solution.py:802
  22.4 9.9 %collective-permute-start.2 = (f32[14,8,512]{2,1,0:T(8,128)S(1)}, f32[14,8,512]{2,1,0:T(8,128)S(1)}, u32[]{:S(2)}, u32[]{:S(2)}) collective-permute-start(f32[14,8,512]{2,1,0:T(8,128)S(1)} %get-tuple-element.62.after), channel_id=1, source_target_pairs={{0,1},{1,0},{2,3},{3,2},{4,5},{5,4},{6,7},{7,6},{8,9},{9,8},{10,11... | collective-permute-start | bytes 688136 | tf_op jit(solution)/shard_map/ppermute | solution.py:802
  28.5 7.7 %collective-permute-start.5 = (f32[5,8,512]{2,1,0:T(8,128)S(1)}, f32[5,8,512]{2,1,0:T(8,128)S(1)}, u32[]{:S(2)}, u32[]{:S(2)}) collective-permute-start(f32[5,8,512]{2,1,0:T(8,128)S(1)} %get-tuple-element.67.after), channel_id=1, source_target_pairs={{0,31},{1,2},{2,1},{3,4},{4,3},{5,6},{6,5},{7,8},{8,7},{9,10},{10,... | collective-permute-start | bytes 245768 | tf_op jit(solution)/shard_map/ppermute | solution.py:802
  32.9 4.5 %collective-permute-start.4 = (f32[5,8,512]{2,1,0:T(8,128)S(1)}, f32[5,8,512]{2,1,0:T(8,128)S(1)}, u32[]{:S(2)}, u32[]{:S(2)}) collective-permute-start(f32[5,8,512]{2,1,0:T(8,128)S(1)} %get-tuple-element.77), channel_id=1, source_target_pairs={{0,1},{1,0},{2,3},{3,2},{4,5},{5,4},{6,7},{7,6},{8,9},{9,8},{10,11... | collective-permute-start | bytes 245768 | tf_op jit(solution)/shard_map/ppermute | solution.py:802
  37.8 7.1 %collective-permute-start.6 = (f32[2,4,16,128]{3,2,1,0:T(8,128)S(1)}, f32[2,4,16,128]{3,2,1,0:T(8,128)S(1)}, u32[]{:S(2)}, u32[]{:S(2)}) collective-permute-start(f32[2,4,16,128]{3,2,1,0:T(8,128)S(1)} %get-tuple-element.80), channel_id=1, source_target_pairs={{0,2},{1,3},{2,0},{3,1},{4,6},{5,7},{6,4},{7,5},{8,10},{9,11},{10,... | collective-permute-start | bytes 196616 | tf_op jit(solution)/shard_map/ppermute | solution.py:916
  39.8 6.2 %collective-permute-start.7 = (f32[2,4,16,128]{3,2,1,0:T(8,128)S(1)}, f32[2,4,16,128]{3,2,1,0:T(8,128)S(1)}, u32[]{:S(2)}, u32[]{:S(2)}) collective-permute-start(f32[2,4,16,128]{3,2,1,0:T(8,128)S(1)} %get-tuple-element.81), channel_id=1, source_target_pairs={{0,3},{1,2},{2,1},{3,0},{4,7},{5,6},{6,5},{7,4},{8,11},{9,10},{10,... | collective-permute-start | bytes 196616 | tf_op jit(solution)/shard_map/ppermute | solution.py:916
  40.9 5.3 %collective-permute-start.8 = (f32[2,4,16,128]{3,2,1,0:T(8,128)S(1)}, f32[2,4,16,128]{3,2,1,0:T(8,128)S(1)}, u32[]{:S(2)}, u32[]{:S(2)}) collective-permute-start(f32[2,4,16,128]{3,2,1,0:T(8,128)S(1)} %get-tuple-element.82), channel_id=1, source_target_pairs={{0,1},{1,0},{2,3},{3,2},{4,5},{5,4},{6,7},{7,6},{8,9},{9,8},{10,11... | collective-permute-start | bytes 196616 | tf_op jit(solution)/shard_map/ppermute | solution.py:916
